TPU v7x, 256 devices: a whole 4x4x8 slice. The times are simulated.
256 devices in a mesh: rep: 4 (over z_lo, core), exp: 64 (over z_hi, x, y).
Axes of the slice: x: 4, y: 4, z: 8 (z_hi: 4, z_lo: 2; z = z_hi * 2 + z_lo), core: 2. Of those that a mesh axis runs over, the one named last changes fastest.
Arguments:
- trainer_weight: bfloat16 [4, 64, 4, 64, 3584], P('rep', 'exp'), may hold values from -0.1875 to 0.1875
- owner: int32 [64], replicated, may hold values from 0 to 63, each once
- expert_ids: int32 [16384, 8], P(('rep', 'exp')), may hold values from 0 to 63, all different within a row; in each aligned block of 64 rows (0 to 63, 64 to 127, ...) at most 16 rows name the same one
- gates: float32 [16384, 8], P(('rep', 'exp')), may hold values from 0.1 to 1
- hidden: bfloat16 [16384, 8, 1024], P(('rep', 'exp')), may hold values from -6 to 6
Outputs:
- mixed: bfloat16 [16384, 3584], P(('rep', 'exp'))
Inputs may be any that keep to these rules, and one draw needn't show every extreme that they name: `expert_ids`: each row names 8 different slots; within the rows of one device no slot is named by more than 16 rows, and some slot reaches 16 on some device. `owner`: each slot once.
All inputs are finite; a program needn't handle non-finite values.
Results may differ from a plain program's by a relative error of at most 0.0049.
Values may be sent and summed in bfloat16 or wider, within the bound.
No kernel may reach another device: no remote copies, remote signals or barrier semaphores. Data moves between devices by JAX's collectives and lax.ppermute only.
A program may use at most 128 MiB of HBM per device.

v0:
```python
import jax
import jax.numpy as jnp
from jax import lax
from jax.sharding import PartitionSpec as P


def shifted(value, axis, steps):
    count = lax.axis_size(axis)
    pairs = [(source, (source + steps) % count) for source in range(count)]
    return lax.ppermute(value, axis, pairs)


def per_device(trainer_weight, owner, expert_ids, gates, hidden):
    experts = owner.shape[0]
    rows_dev, fanout = expert_ids.shape
    hidden_width = hidden.shape[2]
    capacity = min(rows_dev, 2 * rows_dev * fanout // experts)
    local_slices = trainer_weight[0, 0]
    exp_train, slice_rows, width = local_slices.shape
    replicas = lax.axis_size("rep")
    tensor_width = hidden_width // slice_rows
    group_count = lax.axis_size("exp") // tensor_width
    block_width = width // replicas
    inverse = jnp.zeros((experts,), jnp.int32).at[owner].set(jnp.arange(experts, dtype=jnp.int32))
    split_blocks = local_slices.reshape(exp_train, slice_rows, replicas, block_width)
    quartered = lax.all_to_all(split_blocks, "rep", split_axis=2, concat_axis=2, tiled=True)
    target_row = inverse // (exp_train * group_count)
    target_group = inverse // exp_train % group_count
    target_local = inverse % exp_train
    my_group = lax.axis_index("exp") // tensor_width
    tiles = quartered[target_local, :, target_row, :]
    outgoing = jnp.where((target_group == my_group)[:, None, None], tiles, jnp.zeros_like(tiles))
    incoming = lax.all_to_all(outgoing, "exp", split_axis=0, concat_axis=0, tiled=True)
    slot_group = jnp.take(target_group, lax.axis_index("exp"))
    columns_local = lax.dynamic_slice_in_dim(incoming, slot_group * tensor_width, tensor_width, 0)
    columns_local = columns_local.reshape(hidden_width, block_width)
    flat_ids = expert_ids.reshape(-1)
    matches = (flat_ids[:, None] == jnp.arange(experts, dtype=jnp.int32)[None, :]).astype(jnp.int32)
    position = jnp.sum(jnp.cumsum(matches, axis=0) * matches, axis=1) - 1
    outbound = jnp.zeros((experts, capacity, hidden_width), jnp.bfloat16)
    outbound = outbound.at[flat_ids, position].set(hidden.reshape(-1, hidden_width))
    arrived = lax.all_to_all(outbound, "exp", split_axis=0, concat_axis=0, tiled=True)
    slot_rows = arrived.reshape(-1, hidden_width)
    replica = lax.axis_index("rep")
    full_weight = jnp.zeros((hidden_width, block_width * replicas), jnp.bfloat16)
    full_weight = lax.dynamic_update_slice_in_dim(
        full_weight, columns_local, replica * block_width, 1
    )
    moving = columns_local
    for hop_index in range(1, replicas):
        moving = shifted(moving, "rep", 1)
        anchor = (replica - hop_index) % replicas
        full_weight = lax.dynamic_update_slice_in_dim(full_weight, moving, anchor * block_width, 1)
    products = jnp.dot(slot_rows, full_weight, preferred_element_type=jnp.float32).astype(
        jnp.bfloat16
    )
    results = lax.all_to_all(
        products.reshape(experts, capacity, -1), "exp", split_axis=0, concat_axis=0, tiled=True
    )
    picked = results[flat_ids, position].astype(jnp.float32).reshape(rows_dev, fanout, -1)
    return jnp.sum(picked * gates[:, :, None], axis=1).astype(jnp.bfloat16)


def solution(mesh):
    return jax.shard_map(
        per_device,
        mesh=mesh,
        in_specs=(
            P("rep", "exp", None, None, None),
            P(),
            P(("rep", "exp"), None),
            P(("rep", "exp"), None),
            P(("rep", "exp"), None, None),
        ),
        out_specs=P(("rep", "exp"), None),
        check_vma=False,
    )
```

profile of v0, /device:TPU:2, one launch (start us, length us, event | category | flops | bytes accessed | tf_op | source)
XLA Modules:
  0.0 614.9 jit_solution(2553176095891859514)
XLA Ops:
  0.0 0.0 copy-start.3
  0.0 3.3 reshape_squeeze.3
  3.3 1.5 copy.22
  4.9 4.4 all-to-all-start.1
  9.3 0.0 copy-done.3
  9.3 0.8 scatter_custom_fusion.1
  10.2 22.1 %all-to-all-done.1 = bf16[4,64,4,896]{3,1,0,2:T(8,128)(2,1)} async-done(((bf16[4,64,4,896]{3,1,0,2:T(8,128)(2,1)}), bf16[4,64,4,896]{3,1,0,2:T(8,128)(2,1)}, u32[]{:S(2)}, u32[]{:S(2)}) %all-to-all-start.1) | async-done | bytes 1835040 | tf_op jit(solution)/shard_map/all_to_all | solution.py:26
  32.2 1.7 copy.23
  33.9 4.4 gather_fusion
  38.3 6.8 %broadcast_select_fusion = bf16[64,64,896]{2,1,0:T(8,128)(2,1)} fusion(bf16[64,64,896]{2,1,0:T(8,128)(2,1)} %gather_fusion, pred[64]{0:T(512)(128)(4,1)S(1)} %get-tuple-element.16), kind=kLoop, calls=%fused_computation.7 | loop fusion | flops 3670016 | bytes 14680128 | tf_op jit(solution)/shard_map/jit(_where)/select_n | solution.py:32
  45.1 0.0 copy-start.1
  45.1 0.0 copy-start
  45.1 14.9 %all-to-all-start.2 = ((bf16[64,64,896]{2,1,0:T(8,128)(2,1)}), bf16[64,64,896]{2,1,0:T(8,128)(2,1)}, u32[]{:S(2)}, u32[]{:S(2)}) async-start(bf16[64,64,896]{2,1,0:T(8,128)(2,1)} %broadcast_select_fusion), calls=%async_computation.2 | async-start | bytes 14680064 | tf_op jit(solution)/shard_map/all_to_all | solution.py:33
  60.1 0.7 dynamic-slice.2
  61.4 160.5 %all-to-all-done.2 = bf16[64,64,896]{2,1,0:T(8,128)(2,1)} async-done(((bf16[64,64,896]{2,1,0:T(8,128)(2,1)}), bf16[64,64,896]{2,1,0:T(8,128)(2,1)}, u32[]{:S(2)}, u32[]{:S(2)}) %all-to-all-start.2) | async-done | bytes 7340064 | tf_op jit(solution)/shard_map/all_to_all | solution.py:33
  221.9 1.6 constant_dynamic-slice_fusion
  223.5 0.1 collective-permute-start
  223.6 0.0 copy-done.1
  223.6 0.1 copy.18
  223.7 0.1 eq.42
  223.8 0.1 eq.38
  223.9 0.1 reshape.87
  224.0 1.2 reduce-window.6
  225.2 0.2 slice_reduce_fusion
  225.5 0.1 fusion.2
  225.7 1.6 broadcast_in_dim.37
  227.3 0.0 copy-done
  227.3 71.6 %scatter_fusion = bf16[64,16,1024]{2,1,0:T(8,128)(2,1)} fusion(bf16[64,16,1024]{2,1,0:T(8,128)(2,1)} %broadcast_in_dim.37, s32[512]{0:T(512)S(1)} %bitcast.33, bf16[512,1024]{1,0:T(8,128)(2,1)S(1)} %bitcast.37), kind=kCustom, calls=%fused_computation.2 | custom fusion | bytes 3149824 | tf_op jit(solution)/shard_map/scatter | solution.py:41
  298.9 14.5 %all-to-all-start = ((bf16[64,16,1024]{2,1,0:T(8,128)(2,1)}), bf16[64,16,1024]{2,1,0:T(8,128)(2,1)}, u32[]{:S(2)}, u32[]{:S(2)}) async-start(bf16[64,16,1024]{2,1,0:T(8,128)(2,1)} %scatter_fusion), calls=%async_computation | async-start | bytes 4194304 | tf_op jit(solution)/shard_map/all_to_all | solution.py:42
  313.4 0.0 collective-permute-done
  313.5 1.9 collective-permute-start.1
  315.3 64.9 %collective-permute-done.1 = bf16[1024,896]{1,0:T(8,128)(2,1)} collective-permute-done((bf16[1024,896]{1,0:T(8,128)(2,1)}, bf16[1024,896]{1,0:T(8,128)(2,1)}, u32[]{:S(2)}, u32[]{:S(2)}) %collective-permute-start.1) | collective-permute-done | bytes 1835040 | tf_op jit(solution)/shard_map/ppermute | solution.py:10
  380.2 0.0 collective-permute-start.2
  380.2 3.5 broadcast_in_dim.38
  383.7 1.5 constant_dynamic-update-slice_fusion.3
  385.2 3.0 constant_dynamic-update-slice_fusion.2
  388.2 3.0 constant_dynamic-update-slice_fusion.1
  391.1 12.0 %collective-permute-done.2 = bf16[1024,896]{1,0:T(8,128)(2,1)} collective-permute-done((bf16[1024,896]{1,0:T(8,128)(2,1)}, bf16[1024,896]{1,0:T(8,128)(2,1)}, u32[]{:S(2)}, u32[]{:S(2)}) %collective-permute-start.2) | collective-permute-done | bytes 1835040 | tf_op jit(solution)/shard_map/ppermute | solution.py:10
  403.2 3.0 constant_dynamic-update-slice_fusion
  406.1 0.0 all-to-all-done
  406.1 12.5 %convolution_convert_fusion = bf16[1024,3584]{1,0:T(8,128)(2,1)} fusion(bf16[1024,1024]{1,0:T(8,128)(2,1)} %bitcast.5, bf16[1024,3584]{1,0:T(8,128)(2,1)} %constant_dynamic-update-slice_fusion), kind=kOutput, calls=%fused_computation.4 | convolution fusion | flops 7519862784 | bytes 16777216 | tf_op jit(solution)/shard_map/dot_general | solution.py:54
  418.6 0.0 copy-start.2
  418.6 12.8 %all-to-all-start.3 = ((bf16[64,16,3584]{2,1,0:T(8,128)(2,1)}), bf16[64,16,3584]{2,1,0:T(8,128)(2,1)}, u32[]{:S(2)}, u32[]{:S(2)}) async-start(bf16[64,16,3584]{2,1,0:T(8,128)(2,1)} %bitcast.34), calls=%async_computation.3 | async-start | bytes 14680064 | tf_op jit(solution)/shard_map/all_to_all | solution.py:57
  431.5 0.0 copy-done.2
  431.5 0.1 copy.24
  431.6 161.3 %all-to-all-done.3 = bf16[64,16,3584]{2,1,0:T(8,128)(2,1)} async-done(((bf16[64,16,3584]{2,1,0:T(8,128)(2,1)}), bf16[64,16,3584]{2,1,0:T(8,128)(2,1)}, u32[]{:S(2)}, u32[]{:S(2)}) %all-to-all-start.3) | async-done | bytes 7340064 | tf_op jit(solution)/shard_map/all_to_all | solution.py:57
  592.9 16.2 %gather_fusion.1 = bf16[512,3584]{1,0:T(8,128)(2,1)} fusion(bf16[64,16,3584]{2,1,0:T(8,128)(2,1)} %all-to-all-done.3, s32[512]{0:T(512)S(1)} %bitcast.32), kind=kCustom, calls=%fused_computation.1 | custom fusion | bytes 7344128 | tf_op jit(solution)/shard_map/gather | solution.py:60
  609.1 5.8 fusion
  (9 shorter events, 0.1 us)
Async XLA Ops:
  0.0 9.3 %copy-start.3 = (s32[64]{0:T(128)S(1)}, s32[64]{0:T(128)}, u32[]{:S(2)}) copy-start(s32[64]{0:T(128)} %param.6) | copy-start | bytes 772
  4.9 27.4 %all-to-all-start.1 = ((bf16[4,64,4,896]{3,1,0,2:T(8,128)(2,1)}), bf16[4,64,4,896]{3,1,0,2:T(8,128)(2,1)}, u32[]{:S(2)}, u32[]{:S(2)}) async-start(bf16[4,64,4,896]{3,1,0,2:T(8,128)(2,1)} %copy.22), calls=%async_computation.1 | async-start | bytes 3670016 | tf_op jit(solution)/shard_map/all_to_all | solution.py:26
  45.1 178.5 %copy-start.1 = (s32[64,8]{0,1:T(8,128)S(1)}, s32[64,8]{0,1:T(8,128)}, u32[]{:S(2)}) copy-start(s32[64,8]{0,1:T(8,128)} %param.7) | copy-start | bytes 6148
  45.1 182.1 %copy-start = (bf16[64,8,1024]{2,1,0:T(8,128)(2,1)S(1)}, bf16[64,8,1024]{2,1,0:T(8,128)(2,1)}, u32[]{:S(2)}) copy-start(bf16[64,8,1024]{2,1,0:T(8,128)(2,1)} %param.9) | copy-start | bytes 3145732
  45.1 176.8 %all-to-all-start.2 = ((bf16[64,64,896]{2,1,0:T(8,128)(2,1)}), bf16[64,64,896]{2,1,0:T(8,128)(2,1)}, u32[]{:S(2)}, u32[]{:S(2)}) async-start(bf16[64,64,896]{2,1,0:T(8,128)(2,1)} %broadcast_select_fusion), calls=%async_computation.2 | async-start | bytes 14680064 | tf_op jit(solution)/shard_map/all_to_all | solution.py:33
  223.5 89.9 %collective-permute-start = (bf16[1024,896]{1,0:T(8,128)(2,1)S(1)}, bf16[1024,896]{1,0:T(8,128)(2,1)}, u32[]{:S(2)}, u32[]{:S(2)}) collective-permute-start(bf16[1024,896]{1,0:T(8,128)(2,1)S(1)} %bitcast.35), channel_id=1, source_target_pairs={{0,64},{64,128},{128,192},{192,0},{1,65},{65,129},{129,193},{193,1... | collective-permute-start | bytes 5505032 | tf_op jit(solution)/shard_map/ppermute | solution.py:10
  298.9 107.2 %all-to-all-start = ((bf16[64,16,1024]{2,1,0:T(8,128)(2,1)}), bf16[64,16,1024]{2,1,0:T(8,128)(2,1)}, u32[]{:S(2)}, u32[]{:S(2)}) async-start(bf16[64,16,1024]{2,1,0:T(8,128)(2,1)} %scatter_fusion), calls=%async_computation | async-start | bytes 4194304 | tf_op jit(solution)/shard_map/all_to_all | solution.py:42
  313.5 66.8 %collective-permute-start.1 = (bf16[1024,896]{1,0:T(8,128)(2,1)}, bf16[1024,896]{1,0:T(8,128)(2,1)}, u32[]{:S(2)}, u32[]{:S(2)}) collective-permute-start(bf16[1024,896]{1,0:T(8,128)(2,1)} %collective-permute-done), channel_id=1, source_target_pairs={{0,64},{64,128},{128,192},{192,0},{1,65},{65,129},{129,193},{193,1... | collective-permute-start | bytes 5505032 | tf_op jit(solution)/shard_map/ppermute | solution.py:10
  380.2 23.0 %collective-permute-start.2 = (bf16[1024,896]{1,0:T(8,128)(2,1)}, bf16[1024,896]{1,0:T(8,128)(2,1)}, u32[]{:S(2)}, u32[]{:S(2)}) collective-permute-start(bf16[1024,896]{1,0:T(8,128)(2,1)} %collective-permute-done.1), channel_id=1, source_target_pairs={{0,64},{64,128},{128,192},{192,0},{1,65},{65,129},{129,193},{193,1... | collective-permute-start | bytes 5505032 | tf_op jit(solution)/shard_map/ppermute | solution.py:10
  418.6 12.9 %copy-start.2 = (f32[64,8]{0,1:T(8,128)S(1)}, f32[64,8]{0,1:T(8,128)}, u32[]{:S(2)}) copy-start(f32[64,8]{0,1:T(8,128)} %param.8) | copy-start | bytes 6148
  418.6 174.2 %all-to-all-start.3 = ((bf16[64,16,3584]{2,1,0:T(8,128)(2,1)}), bf16[64,16,3584]{2,1,0:T(8,128)(2,1)}, u32[]{:S(2)}, u32[]{:S(2)}) async-start(bf16[64,16,3584]{2,1,0:T(8,128)(2,1)} %bitcast.34), calls=%async_computation.3 | async-start | bytes 14680064 | tf_op jit(solution)/shard_map/all_to_all | solution.py:57
where the time goes:
time: 627 us; the launch traced here: 615 us
  waiting for transfers between devices  421 us (67%)
  local copies, waits for them, and re-layouts  118 us (19%)
  starting transfers between devices  48.7 us (8%)
  other arithmetic  14.1 us (2%)
  matrix products  12.5 us (2%)
    all_to_all x1, waiting for transfers between devices, per_device(): lax.all_to_all(products.reshape(experts, capacity, -1), 'exp', split_axis...  161 us
    all_to_all x1, waiting for transfers between devices, per_device(): lax.all_to_all(outgoing, 'exp', split_axis=0, concat_axis=0, tiled=True)  161 us
    ppermute x3, waiting for transfers between devices, shifted(): return lax.ppermute(value, axis, pairs)  76.9 us
    scatter x1, local copies, waits for them, and re-layouts, per_device(): outbound.at[flat_ids, position].set(hidden.reshape(-1, hidden_width))  71.6 us
    all_to_all x1, waiting for transfers between devices, per_device(): lax.all_to_all(split_blocks, 'rep', split_axis=2, concat_axis=2, tiled=True)  22.1 us
    gather x1, local copies, waits for them, and re-layouts, per_device(): results[flat_ids, position].astype(jnp.float32)  16.2 us
    all_to_all x1, starting transfers between devices, per_device(): lax.all_to_all(outgoing, 'exp', split_axis=0, concat_axis=0, tiled=True)  14.9 us
    all_to_all x1, starting transfers between devices, per_device(): lax.all_to_all(outbound, 'exp', split_axis=0, concat_axis=0, tiled=True)  14.5 us
  transfers between devices with their start and end apart: 7, of which 5 were waited for; matrix products, arithmetic and copies ran while one was open for 15% of the time, Pallas kernels for 0%

commit v1 on v0

v1 whole, which is shorter than its diff:
```python
import functools
import jax
import jax.numpy as jnp
from jax import lax
from jax.experimental import pallas as pl
from jax.experimental.pallas import tpu as pltpu
from jax.sharding import Mesh, PartitionSpec as P

AXES = ("zl", "c", "zh", "x", "y")
ZC = ("zh", "zl", "c")


def shifted(value, axis, steps):
    count = lax.axis_size(axis)
    return lax.ppermute(value, axis, [(i, (i + steps) % count) for i in range(count)])


def experts_kernel(x_ref, w_ref, gate_ref, row_ref, out_ref, p_ref):
    sources, slots, hidden_width = x_ref.shape
    blocks, experts, depth, width = w_ref.shape
    rows = out_ref.shape[1]
    capacity = slots // experts
    for k in range(experts):
        block = x_ref[:, k * capacity:(k + 1) * capacity, :].reshape(sources * capacity, hidden_width)
        total = jnp.dot(block[:, :depth], w_ref[0, k], preferred_element_type=jnp.float32)
        for b in range(1, blocks):
            total += jnp.dot(
                block[:, b * depth:(b + 1) * depth], w_ref[b, k], preferred_element_type=jnp.float32
            )
        high = total.astype(jnp.bfloat16)
        low = (total - high.astype(jnp.float32)).astype(jnp.bfloat16)
        p_ref[:, k * capacity:(k + 1) * capacity, :] = high.reshape(sources, capacity, width)
        p_ref[:, slots + k * capacity:slots + (k + 1) * capacity, :] = low.reshape(sources, capacity, width)

    def combine(s, _):
        gate = gate_ref[pl.ds(s, 1), :]
        gate_high = gate.astype(jnp.bfloat16).astype(jnp.float32)
        number = lax.broadcasted_iota(jnp.int32, (rows, slots), 0).astype(jnp.float32)
        mine = number == row_ref[pl.ds(s, 1), :]
        c_high = jnp.where(mine, gate_high, 0.0).astype(jnp.bfloat16)
        c_low = jnp.where(mine, gate - gate_high, 0.0).astype(jnp.bfloat16)
        high, low = p_ref[s, :slots], p_ref[s, slots:]
        mixed = jnp.dot(c_high, high, preferred_element_type=jnp.float32)
        mixed += jnp.dot(c_low, high, preferred_element_type=jnp.float32)
        mixed += jnp.dot(c_high, low, preferred_element_type=jnp.float32)
        out_ref[s] = mixed.astype(out_ref.dtype)
        return 0

    lax.fori_loop(0, sources, combine, 0)


def experts_call(x, w, gate, row, rows):
    sources, slots, hidden_width = x.shape
    width = w.shape[3]
    vmem = pl.BlockSpec(memory_space=pltpu.VMEM)
    flops = 2 * sources * slots * hidden_width * width
    return pl.pallas_call(
        experts_kernel,
        out_shape=jax.ShapeDtypeStruct((sources, rows, width), jnp.bfloat16),
        in_specs=[vmem] * 4,
        out_specs=vmem,
        scratch_shapes=[pltpu.VMEM((sources, 2 * slots, width), jnp.bfloat16)],
        compiler_params=pltpu.CompilerParams(vmem_limit_bytes=48 << 20),
        cost_estimate=pl.CostEstimate(
            flops=flops, bytes_accessed=2 * (x.size + w.size + sources * rows * width), transcendentals=0
        ),
    )(x, w, gate, row)


def per_device(trainer_weight, owner, expert_ids, gates, hidden):
    experts = owner.shape[0]
    rows, fanout = expert_ids.shape
    hidden_width = hidden.shape[2]
    capacity = min(rows, 2 * rows * fanout // experts)
    own = trainer_weight[0, 0]
    exp_train, slice_rows, width = own.shape
    ny, nx = lax.axis_size("y"), lax.axis_size("x")
    groups = experts // exp_train
    block_width = width // ny
    y = lax.axis_index("y")

    blocks = own.reshape(exp_train, slice_rows, ny, block_width).transpose(2, 0, 1, 3)
    blocks = lax.all_to_all(blocks, "y", 0, 0, tiled=True)
    blocks = blocks.transpose(1, 0, 2, 3).reshape(exp_train, ny * slice_rows, block_width)
    weight = lax.all_gather(blocks, "x")

    zl, c, zh = (lax.axis_size(a) for a in ("zl", "c", "zh"))
    slot_of = owner.reshape(zl, c, zh, exp_train).transpose(2, 0, 1, 3).reshape(experts)
    match = expert_ids[:, :, None] == slot_of[None, None, :]
    named = jnp.any(match, axis=1)
    position = jnp.cumsum(named.astype(jnp.int32), axis=0) - 1
    place = jnp.arange(experts, dtype=jnp.int32)[None, :] * capacity + position
    flat = jnp.sum(jnp.where(match, place[:, None, :], 0), axis=2).reshape(-1)
    chosen = jnp.arange(experts * capacity, dtype=jnp.int32)[:, None] == flat[None, :]
    pair_row = jnp.arange(rows * fanout, dtype=jnp.int32) // fanout
    slot_gate = jnp.sum(jnp.where(chosen, gates.reshape(-1)[None, :], 0.0), axis=1)
    slot_row = jnp.sum(jnp.where(chosen, pair_row[None, :] + 1, 0), axis=1) - 1
    outbound = jnp.dot(
        chosen.astype(jnp.bfloat16), hidden.reshape(-1, hidden_width), preferred_element_type=jnp.float32
    ).astype(jnp.bfloat16)
    slots = exp_train * capacity
    info = jnp.stack([slot_gate.reshape(groups, slots), slot_row.astype(jnp.float32).reshape(groups, slots)], 1)
    info = lax.all_to_all(info, ZC, 0, 0, tiled=True)
    arrived = lax.all_to_all(outbound.reshape(groups, slots, hidden_width), ZC, 0, 0, tiled=True)

    partials = []
    for step in range(ny):
        x_step = arrived if step == 0 else shifted(arrived, "y", step)
        info_step = info if step == 0 else shifted(info, "y", step)
        partials.append(experts_call(x_step, weight, info_step[:, 0], info_step[:, 1], rows))
    partial = jnp.stack(partials, 1)
    summed = lax.psum_scatter(partial.reshape(-1, block_width), ZC, scatter_dimension=0, tiled=True)
    summed = summed.reshape(ny, rows, block_width)
    summed = jnp.take(summed, (y - jnp.arange(ny)) % ny, axis=0)
    final = lax.all_to_all(summed, "y", 0, 0, tiled=True)
    return final.transpose(1, 0, 2).reshape(rows, width)


def solution(mesh):
    devices = mesh.devices.reshape(2, 2, 4, 4, 4)
    inner = Mesh(devices, AXES)
    rep, exp = ("zl", "c"), ("zh", "x", "y")
    return jax.shard_map(
        per_device,
        mesh=inner,
        in_specs=(
            P(rep, exp, None, None, None),
            P(),
            P(rep + exp, None),
            P(rep + exp, None),
            P(rep + exp, None, None),
        ),
        out_specs=P(rep + exp, None),
        check_vma=False,
    )
```

time: 627 us -> 330 us (0.53); the launches traced: 615 us -> 330 us
  waiting for transfers between devices: 421 us -> 143 us
  blocking collectives: 0 us -> 109 us
  local copies, waits for them, and re-layouts: 118 us -> 13.3 us
  starting transfers between devices: 48.7 us -> 6.63 us
  Pallas kernels: 0 us -> 38.5 us
  between operations: 0.82 us -> 13.6 us
  matrix products: 12.5 us -> 1.25 us
  other arithmetic: 14.1 us -> 4.14 us
    all_to_all x4 -> x0, waiting for transfers between devices: 344 us -> none  [the longest x1 161 us: per_device(): lax.all_to_all(products.reshape(experts, capacity, -1), 'exp', split_axis...]
    all_to_all x0 -> x4, blocking collectives: none -> 109 us  [the longest x1 58.1 us: per_device(): lax.all_to_all(outbound.reshape(groups, slots, hidden_width), ZC, 0, 0, t...]
    scatter x2 -> x0, local copies, waits for them, and re-layouts: 72.4 us -> none  [the longest x1 71.6 us: per_device(): outbound.at[flat_ids, position].set(hidden.reshape(-1, hidden_width))]
    reduce_scatter x0 -> x1, waiting for transfers between devices: none -> 65.8 us  [per_device(): lax.psum_scatter(partial.reshape(-1, block_width), ZC, scatter_dimension=...]
    all_to_all x4 -> x0, starting transfers between devices: 46.7 us -> none  [the longest x1 14.9 us: per_device(): lax.all_to_all(outgoing, 'exp', split_axis=0, concat_axis=0, tiled=True)]
    pallas_call x0 -> x4, Pallas kernels: none -> 38.5 us  [experts_call(): pl.pallas_call(experts_kernel, out_shape=jax.ShapeDtypeStruct((sources, r...]
    gather x2 -> x1, local copies, waits for them, and re-layouts: 20.7 us -> 1.64 us  [per_device(): summed = jnp.take(summed, (y - jnp.arange(ny)) % ny, axis=0)]
    dot_general x1, matrix products: 12.5 us -> 1.25 us  [per_device(): jnp.dot(chosen.astype(jnp.bfloat16), hidden.reshape(-1, hidden_width), pr...]
  transfers between devices with their start and end apart: 7 -> 8, of which waited for: 5 -> 3; matrix products, arithmetic and copies ran while one was open for 15% -> 2% of each run, Pallas kernels for 0% -> 9%
where the time goes in v1:
time: 330 us
  waiting for transfers between devices  143 us (43%)
  blocking collectives  109 us (33%)
  Pallas kernels  38.5 us (12%)
  between operations  13.6 us (4%)
  local copies, waits for them, and re-layouts  13.3 us (4%)
  starting transfers between devices  6.63 us (2%)
  other arithmetic  4.14 us (1%)
    ppermute x6, waiting for transfers between devices, shifted(): lax.ppermute(value, axis, [(i, (i + steps) % count) for i in range(count)])  77.5 us
    reduce_scatter x1, waiting for transfers between devices, per_device(): lax.psum_scatter(partial.reshape(-1, block_width), ZC, scatter_dimension=...  65.8 us
    all_to_all x1, blocking collectives, per_device(): lax.all_to_all(outbound.reshape(groups, slots, hidden_width), ZC, 0, 0, t...  58.1 us
    pallas_call x4, Pallas kernels, experts_call(): pl.pallas_call(experts_kernel, out_shape=jax.ShapeDtypeStruct((sources, r...  38.5 us
    all_to_all x1, blocking collectives, per_device(): blocks = lax.all_to_all(blocks, 'y', 0, 0, tiled=True)  27.8 us
    all_to_all x1, blocking collectives, per_device(): final = lax.all_to_all(summed, 'y', 0, 0, tiled=True)  11.7 us
    all_to_all x1, blocking collectives, per_device(): info = lax.all_to_all(info, ZC, 0, 0, tiled=True)  11.6 us
  transfers between devices with their start and end apart: 8, of which 3 were waited for; matrix products, arithmetic and copies ran while one was open for 2% of the time, Pallas kernels for 9%

profile of v1, /device:TPU:2, one launch (start us, length us, event | category | flops | bytes accessed | tf_op | source)
XLA Modules:
  0.0 329.8 jit_solution(9137123413956427662)
XLA Ops:
  6.5 0.0 copy-start
  6.5 0.0 all-gather.2.cloned.1.call-start
  6.5 3.4 %reshape_squeeze.3 = bf16[4,64,4,896]{3,2,1,0:T(4,128)(2,1)S(1)} reshape(bf16[1,1,4,64,3584]{4,3,2,1,0:T(8,128)(2,1)} %param.5) | data formatting | bytes 3670016 | tf_op jit(solution)/shard_map/reshape;squeeze | solution.py:82
  9.9 0.3 copy.44
  10.3 27.8 %all_to_all.20 = bf16[4,4,64,896]{3,2,1,0:T(8,128)(2,1)S(1)} all-to-all(bf16[4,4,64,896]{3,2,1,0:T(8,128)(2,1)S(1)} %copy.44), channel_id=1, replica_groups=mesh['zl'=2,'c'=2,'zh'=4,'x'=4,'y'=4] {'y'}, dimensions={0} | all-to-all | bytes 3670016 | tf_op jit(solution)/shard_map/all_to_all | solution.py:83
  38.0 0.0 copy-start.1
  38.0 0.0 copy-start.3
  38.0 1.4 copy.45
  39.4 0.0 all-gather.2.cloned.1.call-update
  39.4 0.0 reduce-scatter.2.cloned.1.call-start
  39.5 0.0 copy-done.1
  39.5 0.1 copy.42
  39.6 0.0 copy-done.3
  39.6 0.1 reshape.133
  39.7 0.1 eq.34
  39.8 0.2 compare_reduce_fusion
  40.0 0.1 reduce_window_sum.11
  40.1 1.2 fusion.4
  41.3 0.1 eq.37
  41.4 0.0 copy-done
  41.4 1.3 fusion.1
  42.7 0.0 copy-start.2
  42.7 58.1 %all_to_all.21.x_ref = bf16[16,64,1024]{2,1,0:T(8,128)(2,1)S(1)} all-to-all(bf16[16,64,1024]{2,1,0:T(8,128)(2,1)S(1)} %bitcast.45), channel_id=1, replica_groups=mesh['zl'=2,'c'=2,'zh'=4,'x'=4,'y'=4] {'zh','zl','c'}, dimensions={0} | all-to-all | bytes 4194304 | tf_op jit(solution)/shard_map/all_to_all | solution.py:104
  100.8 0.6 collective-permute-start
  101.4 2.1 collective-permute-start.2
  103.4 0.0 copy-done.2
  103.5 0.1 copy.46
  103.5 0.1 broadcast_in_dim.56
  103.6 0.9 collective-permute-start.4
  104.5 0.3 select_reduce_fusion.1
  104.8 0.1 stack_reshape.4
  104.9 0.3 select_reduce_fusion
  105.2 0.1 convert_element_type.27
  105.3 0.1 reshape.147
  105.4 11.6 %all_to_all.22 = f32[16,1,128]{2,1,0:T(1,128)S(1)} all-to-all(f32[16,1,128]{2,1,0:T(1,128)S(1)} %reshape.147), channel_id=1, replica_groups=mesh['zl'=2,'c'=2,'zh'=4,'x'=4,'y'=4] {'zh','zl','c'}, dimensions={0} | all-to-all | bytes 16384 | tf_op jit(solution)/shard_map/all_to_all | solution.py:103
  117.0 0.5 broadcast.176
  117.5 0.7 reduce
  118.1 0.1 reshape.148
  118.2 1.3 collective-permute-start.1
  119.5 1.6 collective-permute-start.3
  121.1 73.8 %collective-permute-done.1 = f32[16,2,64]{2,0,1:T(8,128)S(1)} collective-permute-done((f32[16,2,64]{2,0,1:T(8,128)S(1)}, f32[16,2,64]{2,0,1:T(8,128)S(1)}, u32[]{:S(2)}, u32[]{:S(2)}) %collective-permute-start.1) | collective-permute-done | bytes 8224 | tf_op jit(solution)/shard_map/ppermute | solution.py:15
  195.0 0.2 collective-permute-start.5
  195.1 0.0 collective-permute-done.3
  195.1 3.6 %collective-permute-done.5 = f32[16,2,64]{2,0,1:T(8,128)S(1)} collective-permute-done((f32[16,2,64]{2,0,1:T(8,128)S(1)}, f32[16,2,64]{2,0,1:T(8,128)S(1)}, u32[]{:S(2)}, u32[]{:S(2)}) %collective-permute-start.5) | collective-permute-done | bytes 8224 | tf_op jit(solution)/shard_map/ppermute | solution.py:15
  198.8 0.0 all-gather.2.cloned.1.call-done.w_ref
  198.8 9.1 %shard_map.55 = bf16[16,64,896]{2,1,0:T(8,128)(2,1)S(1)} custom-call(bf16[16,64,1024]{2,1,0:T(8,128)(2,1)S(1)} %all_to_all.21.x_ref, bf16[4,4,256,896]{3,2,1,0:T(8,128)(2,1)} %all-gather.2.cloned.1.call-done.w_ref, f32[16,64]{1,0:T(8,128)S(1)} %get-tuple-element.6.gate_ref, f32[16,64]{1,0:T(8,128)S(1)} %get-tuple-element.5.row_ref), custom_call_target="tpu_custom_call" | custom-call | flops 1879048192 | bytes 11272192 | tf_op jit(solution)/shard_map/pallas_call | solution.py:57
  207.9 0.0 collective-permute-done.x_ref
  207.9 9.8 %shard_map.56 = bf16[16,64,896]{2,1,0:T(8,128)(2,1)S(1)} custom-call(bf16[16,64,1024]{2,1,0:T(8,128)(2,1)} %collective-permute-done.x_ref, bf16[4,4,256,896]{3,2,1,0:T(8,128)(2,1)} %all-gather.2.cloned.1.call-done.w_ref, f32[16,64]{1,0:T(8,128)S(1)} %get-tuple-element.8.gate_ref, f32[16,64]{1,0:T(8,128)S(1)} %get-tuple-element.7.row_ref), custom_call_target="tpu_custom_call" | custom-call | flops 1879048192 | bytes 11272192 | tf_op jit(solution)/shard_map/pallas_call | solution.py:57
  217.7 0.0 collective-permute-done.2.x_ref
  217.7 9.8 %shard_map.57 = bf16[16,64,896]{2,1,0:T(8,128)(2,1)S(1)} custom-call(bf16[16,64,1024]{2,1,0:T(8,128)(2,1)} %collective-permute-done.2.x_ref, bf16[4,4,256,896]{3,2,1,0:T(8,128)(2,1)} %all-gather.2.cloned.1.call-done.w_ref, f32[16,64]{1,0:T(8,128)S(1)} %get-tuple-element.10.gate_ref, f32[16,64]{1,0:T(8,128)S(1)} %get-tuple-element.9.row_ref), custom_call_target="tpu_custom_call" | custom-call | flops 1879048192 | bytes 11272192 | tf_op jit(solution)/shard_map/pallas_call | solution.py:57
  227.5 0.0 collective-permute-done.4.x_ref
  227.5 9.8 %shard_map.58 = bf16[16,64,896]{2,1,0:T(8,128)(2,1)S(1)} custom-call(bf16[16,64,1024]{2,1,0:T(8,128)(2,1)} %collective-permute-done.4.x_ref, bf16[4,4,256,896]{3,2,1,0:T(8,128)(2,1)} %all-gather.2.cloned.1.call-done.w_ref, f32[16,64]{1,0:T(8,128)S(1)} %get-tuple-element.12.gate_ref, f32[16,64]{1,0:T(8,128)S(1)} %get-tuple-element.11.row_ref), custom_call_target="tpu_custom_call" | custom-call | flops 1879048192 | bytes 11272192 | tf_op jit(solution)/shard_map/pallas_call | solution.py:57
  237.3 1.2 pad_maximum_fusion
  238.5 4.4 %copy.52 = bf16[16,4,64,896]{3,2,1,0:T(8,128)(2,1)} copy(bf16[16,4,64,896]{3,2,0,1:T(8,128)(2,1)S(1)} %pad_maximum_fusion) | data formatting | bytes 14680064 | tf_op jit(solution)/shard_map/stack | solution.py:111
  242.9 0.0 reduce-scatter.2.cloned.1.call-update
  243.0 65.8 %reduce-scatter.2.cloned.1.call-done = bf16[256,896]{1,0:T(8,128)(2,1)} async-done(((bf16[4096,896]{1,0:T(8,128)(2,1)}), bf16[256,896]{1,0:T(8,128)(2,1)}) %reduce-scatter.2.cloned.1.call-update) | async-done | bytes 458768 | tf_op jit(solution)/shard_map/reduce_scatter | solution.py:112
  308.7 1.6 gather_fusion
  310.4 0.1 broadcast_select_fusion
  310.5 11.7 %all_to_all.23 = bf16[4,64,896]{2,1,0:T(8,128)(2,1)S(1)} all-to-all(bf16[4,64,896]{2,1,0:T(8,128)(2,1)S(1)} %broadcast_select_fusion), channel_id=1, replica_groups=mesh['zl'=2,'c'=2,'zh'=4,'x'=4,'y'=4] {'y'}, dimensions={0} | all-to-all | bytes 917504 | tf_op jit(solution)/shard_map/all_to_all | solution.py:115
  322.2 0.8 copy.54
  (15 shorter events, 0.1 us)
Async XLA Ops:
  6.5 34.9 %copy-start = (bf16[64,8,1024]{2,1,0:T(8,128)(2,1)S(1)}, bf16[64,8,1024]{2,1,0:T(8,128)(2,1)}, u32[]{:S(2)}) copy-start(bf16[64,8,1024]{2,1,0:T(8,128)(2,1)} %param.9) | copy-start | bytes 3145732
  6.5 192.3 %all-gather.2.cloned.1.call-start = ((), (), s32[]{:S(2)}) async-start(), calls=%async_computation.5 | async-start | bytes 9175040 | tf_op jit(solution)/shard_map/all_gather | solution.py:85
  38.0 1.5 copy-start.1
  38.0 1.5 copy-start.3
  39.4 269.3 %reduce-scatter.2.cloned.1.call-start = ((), (), s32[]{:S(2)}) async-start(), calls=%async_computation.6 | async-start | bytes 7798784 | tf_op jit(solution)/shard_map/reduce_scatter | solution.py:112
  42.7 60.7 %copy-start.2 = (f32[64,8]{0,1:T(8,128)S(1)}, f32[64,8]{0,1:T(8,128)}, u32[]{:S(2)}) copy-start(f32[64,8]{0,1:T(8,128)} %param.8) | copy-start | bytes 6148
  100.8 107.1 %collective-permute-start = (bf16[16,64,1024]{2,1,0:T(8,128)(2,1)S(1)}, bf16[16,64,1024]{2,1,0:T(8,128)(2,1)}, u32[]{:S(2)}, u32[]{:S(2)}) collective-permute-start(bf16[16,64,1024]{2,1,0:T(8,128)(2,1)S(1)} %all_to_all.21.x_ref), channel_id=1, source_target_pairs={{0,1},{1,2},{2,3},{3,0},{4,5},{5,6},{6,7},{7,4},{8,9},{9,10},{10,1... | collective-permute-start | bytes 6291464 | tf_op jit(solution)/shard_map/ppermute | solution.py:15
  101.4 116.4 %collective-permute-start.2 = (bf16[16,64,1024]{2,1,0:T(8,128)(2,1)S(1)}, bf16[16,64,1024]{2,1,0:T(8,128)(2,1)}, u32[]{:S(2)}, u32[]{:S(2)}) collective-permute-start(bf16[16,64,1024]{2,1,0:T(8,128)(2,1)S(1)} %all_to_all.21.x_ref), channel_id=1, source_target_pairs={{0,2},{1,3},{2,0},{3,1},{4,6},{5,7},{6,4},{7,5},{8,10},{9,11},{10,... | collective-permute-start | bytes 6291464 | tf_op jit(solution)/shard_map/ppermute | solution.py:15
  103.6 123.9 %collective-permute-start.4 = (bf16[16,64,1024]{2,1,0:T(8,128)(2,1)S(1)}, bf16[16,64,1024]{2,1,0:T(8,128)(2,1)}, u32[]{:S(2)}, u32[]{:S(2)}) collective-permute-start(bf16[16,64,1024]{2,1,0:T(8,128)(2,1)S(1)} %all_to_all.21.x_ref), channel_id=1, source_target_pairs={{0,3},{1,0},{2,1},{3,2},{4,7},{5,4},{6,5},{7,6},{8,11},{9,8},{10,9... | collective-permute-start | bytes 6291464 | tf_op jit(solution)/shard_map/ppermute | solution.py:15
  118.2 76.7 %collective-permute-start.1 = (f32[16,2,64]{2,0,1:T(8,128)S(1)}, f32[16,2,64]{2,0,1:T(8,128)S(1)}, u32[]{:S(2)}, u32[]{:S(2)}) collective-permute-start(f32[16,2,64]{2,0,1:T(8,128)S(1)} %copy.47), channel_id=1, source_target_pairs={{0,1},{1,2},{2,3},{3,0},{4,5},{5,6},{6,7},{7,4},{8,9},{9,10},{10,1... | collective-permute-start | bytes 24584 | tf_op jit(solution)/shard_map/ppermute | solution.py:15
  119.5 75.6 %collective-permute-start.3 = (f32[16,2,64]{2,0,1:T(8,128)S(1)}, f32[16,2,64]{2,0,1:T(8,128)S(1)}, u32[]{:S(2)}, u32[]{:S(2)}) collective-permute-start(f32[16,2,64]{2,0,1:T(8,128)S(1)} %copy.47), channel_id=1, source_target_pairs={{0,2},{1,3},{2,0},{3,1},{4,6},{5,7},{6,4},{7,5},{8,10},{9,11},{10,... | collective-permute-start | bytes 24584 | tf_op jit(solution)/shard_map/ppermute | solution.py:15
  195.0 3.8 %collective-permute-start.5 = (f32[16,2,64]{2,0,1:T(8,128)S(1)}, f32[16,2,64]{2,0,1:T(8,128)S(1)}, u32[]{:S(2)}, u32[]{:S(2)}) collective-permute-start(f32[16,2,64]{2,0,1:T(8,128)S(1)} %copy.47), channel_id=1, source_target_pairs={{0,3},{1,0},{2,1},{3,2},{4,7},{5,4},{6,5},{7,6},{8,11},{9,8},{10,9... | collective-permute-start | bytes 24584 | tf_op jit(solution)/shard_map/ppermute | solution.py:15
Sparse Core Ops, SparseCore 0:
  39.6 77.7 all-gather.1
  243.0 65.6 reduce-scatter.1

commit v2 on v1

v2 whole, which is shorter than its diff:
```python
import functools
import jax
import jax.numpy as jnp
from jax import lax
from jax.experimental import pallas as pl
from jax.experimental.pallas import tpu as pltpu
from jax.sharding import Mesh, PartitionSpec as P

AXES = ("zl", "c", "zh", "x", "y")
Z = ("zh", "zl")
NZ = 8
NEAR = 3
VMEM = pl.BlockSpec(memory_space=pltpu.VMEM)
SMEM = pl.BlockSpec(memory_space=pltpu.SMEM)
PARAMS = pltpu.CompilerParams(vmem_limit_bytes=48 << 20)


def shifted(value, axis, steps):
    count = lax.axis_size(axis)
    return lax.ppermute(value, axis, [(i, (i + steps) % count) for i in range(count)])


def shifted_z(value, steps):
    low, high = lax.axis_size("zl"), lax.axis_size("zh")
    number = lambda z: z % NZ % low * high + z % NZ // low
    return lax.ppermute(value, ("zl", "zh"), [(number(z), number(z + steps)) for z in range(NZ)])


def cost(flops, *arrays):
    size = sum(a.size * a.dtype.itemsize for a in arrays)
    return pl.CostEstimate(flops=flops, bytes_accessed=size, transcendentals=0)


def split_kernel(pos_ref, w_ref, *out_refs):
    count = len(out_refs)
    width = out_refs[0].shape[2]
    for d, out_ref in enumerate(out_refs):
        start = pl.multiple_of(lax.rem(pos_ref[2] + d, count) * width, 128)
        out_ref[...] = w_ref[:, :, pl.ds(start, width)]


def split_blocks(pos, own, count):
    exp_train, depth, width = own.shape
    shape = jax.ShapeDtypeStruct((exp_train, depth, width // count), own.dtype)
    return pl.pallas_call(
        split_kernel, out_shape=[shape] * count, in_specs=[SMEM, VMEM], out_specs=[VMEM] * count,
        compiler_params=PARAMS, cost_estimate=cost(0, own, own),
    )(pos, own)


def join_kernel(pos_ref, *refs):
    in_refs, out_ref = refs[:-1], refs[-1]
    count, depth = len(in_refs), in_refs[0].shape[1]
    for d, in_ref in enumerate(in_refs):
        start = pl.multiple_of(lax.rem(pos_ref[2] + count - d, count) * depth, depth)
        out_ref[:, pl.ds(start, depth), :] = in_ref[...]


def join_blocks(pos, blocks):
    exp_train, depth, width = blocks[0].shape
    shape = jax.ShapeDtypeStruct((exp_train, depth * len(blocks), width), blocks[0].dtype)
    return pl.pallas_call(
        join_kernel, out_shape=shape, in_specs=[SMEM] + [VMEM] * len(blocks), out_specs=VMEM,
        compiler_params=PARAMS, cost_estimate=cost(0, shape, shape),
    )(pos, *blocks)


def dispatch_kernel(pos_ref, flat_ref, hidden_own_ref, hidden_other_ref, *out_refs):
    slots = out_refs[0].shape[1]
    pairs = flat_ref.shape[1]
    numbers = []
    for d in range(NZ):
        base = (lax.rem(pos_ref[0] + d, NZ) * 2 + pos_ref[1]) * slots
        numbers.append(base + lax.broadcasted_iota(jnp.int32, (slots, pairs), 0))
    numbers = jnp.concatenate(numbers, 0)
    for source, ref in enumerate((hidden_own_ref, hidden_other_ref)):
        chosen = jnp.where(numbers == flat_ref[source:source + 1, :], 1.0, 0.0).astype(jnp.bfloat16)
        rows = jnp.dot(chosen, ref[...], preferred_element_type=jnp.float32).astype(jnp.bfloat16)
        for d, out_ref in enumerate(out_refs):
            out_ref[source] = rows[d * slots:(d + 1) * slots]


def dispatch(pos, flat, own, other, slots):
    shape = jax.ShapeDtypeStruct((2, slots, own.shape[1]), own.dtype)
    return pl.pallas_call(
        dispatch_kernel, out_shape=[shape] * NZ, in_specs=[SMEM] + [VMEM] * 3, out_specs=[VMEM] * NZ,
        compiler_params=PARAMS, cost_estimate=cost(4 * NZ * slots * own.size, own, other, own, own, own, own),
    )(pos, flat, own, other)


def experts_kernel(pos_ref, near_ref, far_ref, w_ref, gate_ref, row_ref, mine_ref, other_ref, p_ref):
    _, _, slots, hidden_width = near_ref.shape
    width = w_ref.shape[3]
    experts = w_ref.shape[1]
    rows = mine_ref.shape[1]
    capacity = slots // experts
    planes = NEAR * 2
    for k in range(experts):
        part = slice(k * capacity, (k + 1) * capacity)
        block = jnp.concatenate(
            [ref[:, :, part, :].reshape(-1, hidden_width) for ref in (near_ref, far_ref)], 0
        )
        total = jnp.dot(block, w_ref[:, k].reshape(hidden_width, width), preferred_element_type=jnp.float32)
        high = total.astype(jnp.bfloat16)
        low = (total - high.astype(jnp.float32)).astype(jnp.bfloat16)
        high, low = (v.reshape(-1, capacity, width) for v in (high, low))
        p_ref[:, part, :] = high
        p_ref[:, slots + part.start:slots + part.stop, :] = high
        p_ref[:, 2 * slots + part.start:2 * slots + part.stop, :] = low
    z, c, y = pos_ref[0], pos_ref[1], pos_ref[2]
    number = lax.broadcasted_iota(jnp.int32, (rows, 3 * slots), 0).astype(jnp.float32)
    column = lax.broadcasted_iota(jnp.int32, (rows, 3 * slots), 1)
    middle = (column >= slots) & (column < 2 * slots)

    def combine(plane, _):
        source = lax.rem(z + NZ + 1 - plane, NZ)
        for core, out_ref in enumerate((mine_ref, other_ref)):
            index = (source * 2 + lax.rem(c + core, 2)) * 4 + y
            gate = gate_ref[pl.ds(index, 1), :]
            gate_high = gate.astype(jnp.bfloat16).astype(jnp.float32)
            value = jnp.where(middle, gate - gate_high, gate_high)
            weights = jnp.where(number == row_ref[pl.ds(index, 1), :], value, 0.0).astype(jnp.bfloat16)
            mixed = jnp.dot(weights, p_ref[plane * 2 + core], preferred_element_type=jnp.float32)
            out_ref[source] = mixed.astype(out_ref.dtype)
        return 0

    lax.fori_loop(0, NZ, combine, 0)


def experts_call(pos, near, far, w, gate, row, rows):
    slots, hidden_width = near.shape[2:]
    width = w.shape[3]
    mine = jax.ShapeDtypeStruct((NZ, rows, width), jnp.float32)
    other = jax.ShapeDtypeStruct((NZ, rows, width), jnp.bfloat16)
    return pl.pallas_call(
        experts_kernel,
        out_shape=[mine, other],
        in_specs=[SMEM] + [VMEM] * 5,
        out_specs=[VMEM] * 2,
        scratch_shapes=[pltpu.VMEM((2 * NZ, 3 * slots, width), jnp.bfloat16)],
        compiler_params=PARAMS,
        cost_estimate=cost(4 * NZ * slots * hidden_width * width, near, far, w, mine, other),
    )(pos, near, far, w, gate, row)


def place_kernel(pos_ref, *refs):
    in_refs, out_ref = refs[:-1], refs[-1]
    width = in_refs[0].shape[1]
    for d, in_ref in enumerate(in_refs):
        start = pl.multiple_of(lax.rem(pos_ref[2] + d, len(in_refs)) * width, 128)
        out_ref[:, pl.ds(start, width)] = in_ref[...]


def place_blocks(pos, blocks):
    rows, width = blocks[0].shape
    shape = jax.ShapeDtypeStruct((rows, width * len(blocks)), blocks[0].dtype)
    return pl.pallas_call(
        place_kernel, out_shape=shape, in_specs=[SMEM] + [VMEM] * len(blocks), out_specs=VMEM,
        compiler_params=PARAMS, cost_estimate=cost(0, shape, shape),
    )(pos, *blocks)


def per_device(trainer_weight, owner, expert_ids, gates, hidden):
    experts = owner.shape[0]
    rows, fanout = expert_ids.shape
    hidden_width = hidden.shape[2]
    capacity = min(rows, 2 * rows * fanout // experts)
    own = trainer_weight[0, 0]
    exp_train, slice_rows, width = own.shape
    ny = lax.axis_size("y")
    groups = experts // exp_train
    slots = exp_train * capacity
    block_width = width // ny
    low = lax.axis_size("zl")
    z, c, y = lax.axis_index("zh") * low + lax.axis_index("zl"), lax.axis_index("c"), lax.axis_index("y")
    pos = jnp.stack([z, c, y]).astype(jnp.int32)

    zl, cs, zh = (lax.axis_size(a) for a in ("zl", "c", "zh"))
    slot_of = owner.reshape(zl, cs, zh, exp_train).transpose(2, 0, 1, 3).reshape(experts)
    match = expert_ids[:, :, None] == slot_of[None, None, :]
    named = jnp.any(match, axis=1)
    position = jnp.cumsum(named.astype(jnp.int32), axis=0) - 1
    place = jnp.arange(experts, dtype=jnp.int32)[None, :] * capacity + position
    flat = jnp.sum(jnp.where(match, place[:, None, :], 0), axis=2).reshape(1, -1)
    pairs = hidden.reshape(-1, hidden_width)
    other_pairs = shifted(pairs, "c", 1)
    other_flat = shifted(flat, "c", 1)

    blocks = split_blocks(pos, own, ny)
    blocks = [blocks[0]] + [shifted(blocks[d], "y", d) for d in range(1, ny)]
    weight = lax.all_gather(join_blocks(pos, blocks), "x")

    outbound = dispatch(pos, jnp.concatenate([flat, other_flat], 0), pairs, other_pairs, slots)
    arrived = [outbound[0]] + [shifted_z(outbound[d], d) for d in range(1, NZ)]
    near = jnp.stack([arrived[NZ - 1], arrived[0], arrived[1]])
    far = jnp.stack(arrived[2:NZ - 1])

    chosen = jnp.arange(experts * capacity, dtype=jnp.int32)[:, None] == flat
    pair_row = jnp.arange(rows * fanout, dtype=jnp.int32) // fanout
    slot_gate = jnp.sum(jnp.where(chosen, gates.reshape(-1)[None, :], 0.0), axis=1).reshape(groups, 1, slots)
    slot_row = jnp.sum(jnp.where(chosen, pair_row[None, :] + 1, 0), axis=1).reshape(groups, 1, slots) - 1
    info = jnp.concatenate([slot_gate, slot_row.astype(jnp.float32)], 2)
    info = jnp.broadcast_to(info, (groups, ny, 2 * slots)).reshape(groups * ny, 2 * slots)
    info = lax.all_to_all(info, Z + ("c", "y"), 0, 0, tiled=True)
    gate = jnp.tile(info[:, :slots], (1, 3))
    row = jnp.tile(info[:, slots:], (1, 3))

    partials = []
    for step in (0, 1, ny - 1, 2):
        near_step = near if step == 0 else shifted(near, "y", step)
        far_step = far if step == 0 else shifted(far, "y", step)
        pos_step = jnp.stack([z, c, (y + ny - step) % ny]).astype(jnp.int32)
        mine, other = experts_call(pos_step, near_step, far_step, weight, gate, row, rows)
        other = shifted(other, "c", 1)
        partials.append((mine + other.astype(jnp.float32)).astype(jnp.bfloat16))
    partial = jnp.stack(partials, 1).reshape(-1, block_width)
    summed = lax.psum_scatter(partial, Z, scatter_dimension=0, tiled=True).reshape(ny, rows, block_width)
    final = [summed[0], shifted(summed[1], "y", -1), shifted(summed[3], "y", 2), shifted(summed[2], "y", 1)]
    return place_blocks(pos, final)


def solution(mesh):
    devices = mesh.devices.reshape(2, 2, 4, 4, 4)
    inner = Mesh(devices, AXES)
    rep, exp = ("zl", "c"), ("zh", "x", "y")
    return jax.shard_map(
        per_device,
        mesh=inner,
        in_specs=(
            P(rep, exp, None, None, None),
            P(),
            P(rep + exp, None),
            P(rep + exp, None),
            P(rep + exp, None, None),
        ),
        out_specs=P(rep + exp, None),
        check_vma=False,
    )
```

time: 330 us -> 288 us (0.87)
  blocking collectives: 109 us -> 68.7 us
  waiting for transfers between devices: 143 us -> 105 us
  starting transfers between devices: 6.63 us -> 43.3 us
  other arithmetic: 4.14 us -> 7.86 us
    ppermute x6 -> x18, waiting for transfers between devices: 77.5 us -> 26.5 us  [shifted(): lax.ppermute(value, axis, [(i, (i + steps) % count) for i in range(count)])]
    all_to_all x4 -> x1, blocking collectives: 109 us -> 68.7 us  [per_device(): info = lax.all_to_all(info, Z + ('c', 'y'), 0, 0, tiled=True)]
    ppermute x0 -> x7, waiting for transfers between devices: none -> 31.4 us  [shifted_z(): lax.ppermute(value, ('zl', 'zh'), [(number(z), number(z + steps)) for z i...]
    ppermute x0 -> x7, starting transfers between devices: none -> 21.6 us  [shifted_z(): lax.ppermute(value, ('zl', 'zh'), [(number(z), number(z + steps)) for z i...]
    reduce_scatter x1, waiting for transfers between devices: 65.8 us -> 47.1 us  [per_device(): lax.psum_scatter(partial, Z, scatter_dimension=0, tiled=True)]
    ppermute x6 -> x18, starting transfers between devices: 6.59 us -> 21.7 us  [shifted(): lax.ppermute(value, axis, [(i, (i + steps) % count) for i in range(count)])]
    another operation x2 -> x8, other arithmetic: 1.19 us -> 5.65 us  [the longest x5 3.77 us: per_device(): partial = jnp.stack(partials, 1).reshape(-1, block_width)]
    another operation x3 -> x6, local copies, waits for them, and re-layouts: 7.85 us -> 5.41 us  [the longest x1 2.13 us: per_device(): partial = jnp.stack(partials, 1).reshape(-1, block_width)]
  transfers between devices with their start and end apart: 8 -> 27, of which waited for: 3 -> 10; matrix products, arithmetic and copies ran while one was open for 2% -> 4% of each run, Pallas kernels for 9% -> 12%
where the time goes in v2:
time: 288 us; the launch traced here: 287 us
  waiting for transfers between devices  105 us (36%)
  blocking collectives  68.7 us (24%)
  starting transfers between devices  43.3 us (15%)
  Pallas kernels  37.6 us (13%)
  between operations  13.7 us (5%)
  local copies, waits for them, and re-layouts  10.9 us (4%)
  other arithmetic  7.86 us (3%)
    all_to_all x1, blocking collectives, per_device(): info = lax.all_to_all(info, Z + ('c', 'y'), 0, 0, tiled=True)  68.7 us
    reduce_scatter x1, waiting for transfers between devices, per_device(): lax.psum_scatter(partial, Z, scatter_dimension=0, tiled=True)  47.1 us
    pallas_call x4, Pallas kernels, experts_call(): pl.pallas_call(experts_kernel, out_shape=[mine, other], in_specs=[SMEM] +...  31.8 us
    ppermute x7, waiting for transfers between devices, shifted_z(): lax.ppermute(value, ('zl', 'zh'), [(number(z), number(z + steps)) for z i...  31.4 us
    ppermute x18, waiting for transfers between devices, shifted(): lax.ppermute(value, axis, [(i, (i + steps) % count) for i in range(count)])  26.5 us
    ppermute x18, starting transfers between devices, shifted(): lax.ppermute(value, axis, [(i, (i + steps) % count) for i in range(count)])  21.7 us
    ppermute x7, starting transfers between devices, shifted_z(): lax.ppermute(value, ('zl', 'zh'), [(number(z), number(z + steps)) for z i...  21.6 us
  transfers between devices with their start and end apart: 27, of which 10 were waited for; matrix products, arithmetic and copies ran while one was open for 4% of the time, Pallas kernels for 12%

profile of v2, /device:TPU:2, one launch (start us, length us, event | category | flops | bytes accessed | tf_op | source)
XLA Modules:
  0.0 287.1 jit_solution(9837526085067239208)
XLA Ops:
  6.5 0.6 pad_add_fusion.3
  7.2 1.5 copy-done
  8.7 0.7 shard_map.56
  9.4 3.3 %collective-permute-start.10 = (bf16[4,64,896]{2,1,0:T(8,128)(2,1)S(1)}, bf16[4,64,896]{2,1,0:T(8,128)(2,1)S(1)}, u32[]{:S(2)}, u32[]{:S(2)}) collective-permute-start(bf16[4,64,896]{2,1,0:T(8,128)(2,1)S(1)} %get-tuple-element.35), channel_id=1, source_target_pairs={{0,2},{1,3},{2,0},{3,1},{4,6},{5,7},{6,4},{7,5},{8,10},{9,11},{10,... | collective-permute-start | bytes 1376264 | tf_op jit(solution)/shard_map/ppermute | solution.py:20
  12.7 1.1 collective-permute-start.11
  13.8 1.0 collective-permute-start.9
  14.7 9.7 %collective-permute-done.10.refs_2_ = bf16[4,64,896]{2,1,0:T(8,128)(2,1)S(1)} collective-permute-done((bf16[4,64,896]{2,1,0:T(8,128)(2,1)S(1)}, bf16[4,64,896]{2,1,0:T(8,128)(2,1)S(1)}, u32[]{:S(2)}, u32[]{:S(2)}) %collective-permute-start.10) | collective-permute-done | bytes 458784 | tf_op jit(solution)/shard_map/ppermute | solution.py:20
  24.5 9.0 %collective-permute-done.11.refs_3_ = bf16[4,64,896]{2,1,0:T(8,128)(2,1)S(1)} collective-permute-done((bf16[4,64,896]{2,1,0:T(8,128)(2,1)S(1)}, bf16[4,64,896]{2,1,0:T(8,128)(2,1)S(1)}, u32[]{:S(2)}, u32[]{:S(2)}) %collective-permute-start.11) | collective-permute-done | bytes 458784 | tf_op jit(solution)/shard_map/ppermute | solution.py:20
  33.5 2.0 shard_map.57
  35.6 1.1 copy-done.3
  36.9 0.1 eq.36
  37.0 0.2 compare_reduce_fusion
  37.2 0.1 reduce_window_sum.11
  37.3 1.2 fusion.4
  38.7 0.6 collective-permute-start
  39.3 0.8 collective-permute-done
  40.1 1.8 shard_map.55
  41.9 3.3 %collective-permute-start.4 = (bf16[2,64,1024]{2,1,0:T(8,128)(2,1)S(1)}, bf16[2,64,1024]{2,1,0:T(8,128)(2,1)S(1)}, u32[]{:S(2)}, u32[]{:S(2)}) collective-permute-start(bf16[2,64,1024]{2,1,0:T(8,128)(2,1)S(1)} %get-tuple-element.28), channel_id=1, source_target_pairs={{0,16},{128,144},{16,32},{144,160},{32,48},{160,176},{48,0},{176,1... | collective-permute-start | bytes 786440 | tf_op jit(solution)/shard_map/ppermute | solution.py:26
  45.3 4.9 %collective-permute-start.5 = (bf16[2,64,1024]{2,1,0:T(8,128)(2,1)S(1)}, bf16[2,64,1024]{2,1,0:T(8,128)(2,1)S(1)}, u32[]{:S(2)}, u32[]{:S(2)}) collective-permute-start(bf16[2,64,1024]{2,1,0:T(8,128)(2,1)S(1)} %get-tuple-element.29), channel_id=1, source_target_pairs={{0,144},{128,32},{16,160},{144,48},{32,176},{160,0},{48,128},{176,... | collective-permute-start | bytes 786440 | tf_op jit(solution)/shard_map/ppermute | solution.py:26
  50.2 1.0 collective-permute-start.6
  51.2 4.5 %collective-permute-start.7 = (bf16[2,64,1024]{2,1,0:T(8,128)(2,1)S(1)}, bf16[2,64,1024]{2,1,0:T(8,128)(2,1)S(1)}, u32[]{:S(2)}, u32[]{:S(2)}) collective-permute-start(bf16[2,64,1024]{2,1,0:T(8,128)(2,1)S(1)} %get-tuple-element.31), channel_id=1, source_target_pairs={{0,160},{128,48},{16,176},{144,0},{32,128},{160,16},{48,144},{176,... | collective-permute-start | bytes 786440 | tf_op jit(solution)/shard_map/ppermute | solution.py:26
  55.7 2.7 collective-permute-start.8
  58.4 5.1 %collective-permute-start.2 = (bf16[2,64,1024]{2,1,0:T(8,128)(2,1)S(1)}, bf16[2,64,1024]{2,1,0:T(8,128)(2,1)}, u32[]{:S(2)}, u32[]{:S(2)}) collective-permute-start(bf16[2,64,1024]{2,1,0:T(8,128)(2,1)S(1)} %get-tuple-element.25), channel_id=1, source_target_pairs={{0,176},{128,0},{16,128},{144,16},{32,144},{160,32},{48,160},{176,... | collective-permute-start | bytes 786440 | tf_op jit(solution)/shard_map/ppermute | solution.py:26
  63.5 20.0 %collective-permute-done.5 = bf16[2,64,1024]{2,1,0:T(8,128)(2,1)S(1)} collective-permute-done((bf16[2,64,1024]{2,1,0:T(8,128)(2,1)S(1)}, bf16[2,64,1024]{2,1,0:T(8,128)(2,1)S(1)}, u32[]{:S(2)}, u32[]{:S(2)}) %collective-permute-start.5) | collective-permute-done | bytes 262176 | tf_op jit(solution)/shard_map/ppermute | solution.py:26
  83.6 1.5 collective-permute-done.6
  85.1 9.9 %collective-permute-done.8 = bf16[2,64,1024]{2,1,0:T(8,128)(2,1)S(1)} collective-permute-done((bf16[2,64,1024]{2,1,0:T(8,128)(2,1)S(1)}, bf16[2,64,1024]{2,1,0:T(8,128)(2,1)S(1)}, u32[]{:S(2)}, u32[]{:S(2)}) %collective-permute-start.8) | collective-permute-done | bytes 262176 | tf_op jit(solution)/shard_map/ppermute | solution.py:26
  95.0 1.7 collective-permute-start.14
  97.0 0.3 select_reduce_fusion.1
  97.3 1.9 collective-permute-start.17
  99.2 1.2 pad_maximum_fusion.1.near_ref
  100.4 0.3 collective-permute-start.13
  100.7 0.3 select_reduce_fusion
  101.1 3.0 %collective-permute-start.16 = (bf16[3,2,64,1024]{3,2,1,0:T(8,128)(2,1)S(1)}, bf16[3,2,64,1024]{3,2,1,0:T(8,128)(2,1)}, u32[]{:S(2)}, u32[]{:S(2)}) collective-permute-start(bf16[3,2,64,1024]{3,2,1,0:T(8,128)(2,1)S(1)} %pad_maximum_fusion.1.near_ref), channel_id=1, source_target_pairs={{0,3},{1,0},{2,1},{3,2},{4,7},{5,4},{6,5},{7,6},{8,11},{9,8},{10,9... | collective-permute-start | bytes 2359304 | tf_op jit(solution)/shard_map/ppermute | solution.py:20
  104.1 0.4 collective-permute-start.20
  104.6 68.7 %all_to_all.12 = f32[64,1,128]{2,1,0:T(1,128)S(1)} all-to-all(f32[64,1,128]{2,1,0:T(1,128)S(1)} %bitcast.53), channel_id=1, replica_groups=mesh['zl'=2,'c'=2,'zh'=4,'x'=4,'y'=4] {'zh','zl','c','y'}, dimensions={0} | all-to-all | bytes 65536 | tf_op jit(solution)/shard_map/all_to_all | solution.py:204
  173.5 0.7 tile.8
  174.1 1.0 copy.56.gate_ref
  175.2 0.7 tile.20
  175.9 1.0 copy.57.row_ref
  176.8 2.4 collective-permute-start.19
  179.2 0.6 copy-done.2
  179.8 7.6 %shard_map.58 = (f32[8,64,896]{2,1,0:T(8,128)S(1)}, bf16[8,64,896]{2,1,0:T(8,128)(2,1)S(1)}) custom-call(s32[3]{0:T(128)S(1)} %copy-done.2, bf16[3,2,64,1024]{3,2,1,0:T(8,128)(2,1)S(1)} %pad_maximum_fusion.1.near_ref, bf16[5,2,64,1024]{3,2,1,0:T(8,128)(2,1)S(1)} %bitcast_dynamic-update-slice_fusion.far_ref, bf16[4,4,256,896]{3,2,1,0:T(8,128)(2,1)} %bitcast.45, ...), custom_call_target="tpu_custom_call" | custom-call | flops 1879048192 | bytes 12189696 | tf_op jit(solution)/shard_map/pallas_call | solution.py:135
  187.4 0.1 collective-permute-start.12
  187.5 8.2 %shard_map.59 = (f32[8,64,896]{2,1,0:T(8,128)S(1)}, bf16[8,64,896]{2,1,0:T(8,128)(2,1)S(1)}) custom-call(s32[3]{0:T(128)S(1)} %get-tuple-element.53.pos_ref, bf16[3,2,64,1024]{3,2,1,0:T(8,128)(2,1)} %collective-permute-done.13.near_ref, bf16[5,2,64,1024]{3,2,1,0:T(8,128)(2,1)} %collective-permute-done.14.far_ref, bf16[4,4,256,896]{3,2,1,0:T(8,128)(2,1)} %bitcast.46, ...), custom_call_target="tpu_custom_call" | custom-call | flops 1879048192 | bytes 12189696 | tf_op jit(solution)/shard_map/pallas_call | solution.py:135
  195.7 0.8 collective-permute-start.15
  196.5 7.8 %shard_map.60 = (f32[8,64,896]{2,1,0:T(8,128)S(1)}, bf16[8,64,896]{2,1,0:T(8,128)(2,1)S(1)}) custom-call(s32[3]{0:T(128)S(1)} %get-tuple-element.54.pos_ref, bf16[3,2,64,1024]{3,2,1,0:T(8,128)(2,1)} %collective-permute-done.16.near_ref, bf16[5,2,64,1024]{3,2,1,0:T(8,128)(2,1)S(1)} %collective-permute-done.17.far_ref, bf16[4,4,256,896]{3,2,1,0:T(8,128)(2,1)} %bitcast.47, ...), custom_call_target="tpu_custom_call" | custom-call | flops 1879048192 | bytes 12189696 | tf_op jit(solution)/shard_map/pallas_call | solution.py:135
  204.4 0.1 collective-permute-start.18
  204.5 8.2 %shard_map.61 = (f32[8,64,896]{2,1,0:T(8,128)S(1)}, bf16[8,64,896]{2,1,0:T(8,128)(2,1)S(1)}) custom-call(s32[3]{0:T(128)S(1)} %get-tuple-element.55.pos_ref, bf16[3,2,64,1024]{3,2,1,0:T(8,128)(2,1)} %collective-permute-done.19.near_ref, bf16[5,2,64,1024]{3,2,1,0:T(8,128)(2,1)} %collective-permute-done.20.far_ref, bf16[4,4,256,896]{3,2,1,0:T(8,128)(2,1)} %bitcast.48, ...), custom_call_target="tpu_custom_call" | custom-call | flops 1879048192 | bytes 12189696 | tf_op jit(solution)/shard_map/pallas_call | solution.py:135
  212.7 0.6 collective-permute-start.21
  213.3 1.4 fusion
  214.7 1.4 fusion.1
  216.1 0.2 fusion.2
  216.3 0.2 fusion.3
  216.5 0.6 pad_maximum_fusion
  217.1 2.1 copy.64
  219.3 47.1 %reduce-scatter.2.cloned.1.call-done = bf16[256,896]{1,0:T(8,128)(2,1)} async-done(((bf16[2048,896]{1,0:T(8,128)(2,1)}), bf16[256,896]{1,0:T(8,128)(2,1)}) %reduce-scatter.2.cloned.1.call-update) | async-done | bytes 458768 | tf_op jit(solution)/shard_map/reduce_scatter | solution.py:217
  266.4 1.1 fusion.9
  267.5 2.8 collective-permute-start.22
  270.3 0.8 collective-permute-start.23
  271.1 0.9 collective-permute-start.24
  272.0 3.3 %collective-permute-done.22.refs_1_ = bf16[64,896]{1,0:T(8,128)(2,1)S(1)} collective-permute-done((bf16[64,896]{1,0:T(8,128)(2,1)S(1)}, bf16[64,896]{1,0:T(8,128)(2,1)S(1)}, u32[]{:S(2)}, u32[]{:S(2)}) %collective-permute-start.22) | collective-permute-done | bytes 114720 | tf_op jit(solution)/shard_map/ppermute | solution.py:20
  275.3 2.5 collective-permute-done.23.refs_2_
  277.7 1.2 collective-permute-done.24.refs_3_
  278.9 1.4 shard_map.62
  (60 shorter events, 1.3 us)
Async XLA Ops:
  6.5 172.7 %all-gather.3.cloned.1.call-start = ((), (), s32[]{:S(2)}) async-start(), calls=%async_computation.3 | async-start | bytes 9175040 | tf_op jit(solution)/shard_map/all_gather | solution.py:191
  7.2 1.5 copy-start
  9.4 15.0 %collective-permute-start.10 = (bf16[4,64,896]{2,1,0:T(8,128)(2,1)S(1)}, bf16[4,64,896]{2,1,0:T(8,128)(2,1)S(1)}, u32[]{:S(2)}, u32[]{:S(2)}) collective-permute-start(bf16[4,64,896]{2,1,0:T(8,128)(2,1)S(1)} %get-tuple-element.35), channel_id=1, source_target_pairs={{0,2},{1,3},{2,0},{3,1},{4,6},{5,7},{6,4},{7,5},{8,10},{9,11},{10,... | collective-permute-start | bytes 1376264 | tf_op jit(solution)/shard_map/ppermute | solution.py:20
  12.7 20.8 %collective-permute-start.11 = (bf16[4,64,896]{2,1,0:T(8,128)(2,1)S(1)}, bf16[4,64,896]{2,1,0:T(8,128)(2,1)S(1)}, u32[]{:S(2)}, u32[]{:S(2)}) collective-permute-start(bf16[4,64,896]{2,1,0:T(8,128)(2,1)S(1)} %get-tuple-element.36), channel_id=1, source_target_pairs={{0,3},{1,0},{2,1},{3,2},{4,7},{5,4},{6,5},{7,6},{8,11},{9,8},{10,9... | collective-permute-start | bytes 1376264 | tf_op jit(solution)/shard_map/ppermute | solution.py:20
  13.8 19.7 %collective-permute-start.9 = (bf16[4,64,896]{2,1,0:T(8,128)(2,1)S(1)}, bf16[4,64,896]{2,1,0:T(8,128)(2,1)S(1)}, u32[]{:S(2)}, u32[]{:S(2)}) collective-permute-start(bf16[4,64,896]{2,1,0:T(8,128)(2,1)S(1)} %get-tuple-element.34), channel_id=1, source_target_pairs={{0,1},{1,2},{2,3},{3,0},{4,5},{5,6},{6,7},{7,4},{8,9},{9,10},{10,1... | collective-permute-start | bytes 1376264 | tf_op jit(solution)/shard_map/ppermute | solution.py:20
  35.5 1.2 copy-start.3
  35.5 1.2 copy-start.4
  35.5 1.3 copy-start.6
  35.5 230.9 %reduce-scatter.2.cloned.1.call-start = ((), (), s32[]{:S(2)}) async-start(), calls=%async_computation.2 | async-start | bytes 4128768 | tf_op jit(solution)/shard_map/reduce_scatter | solution.py:217
  36.7 3.4 %collective-permute-start.1 = (bf16[512,1024]{1,0:T(8,128)(2,1)S(1)}, bf16[512,1024]{1,0:T(8,128)(2,1)S(1)}, u32[]{:S(2)}, u32[]{:S(2)}) collective-permute-start(bf16[512,1024]{1,0:T(8,128)(2,1)S(1)} %bitcast.43), channel_id=1, source_target_pairs={{0,64},{64,0},{1,65},{65,1},{2,66},{66,2},{3,67},{67,3},{4,68},{68... | collective-permute-start | bytes 3145736 | tf_op jit(solution)/shard_map/ppermute | solution.py:20
  38.7 1.4 collective-permute-start
  41.9 53.1 %copy-start.1 = (bf16[2,64,1024]{2,1,0:T(8,128)(2,1)}, bf16[2,64,1024]{2,1,0:T(8,128)(2,1)S(1)}, u32[]{:S(2)}) copy-start(bf16[2,64,1024]{2,1,0:T(8,128)(2,1)S(1)} %get-tuple-element.26) | copy-start | bytes 786436
  41.9 54.9 %copy-start.5 = (f32[64,8]{0,1:T(8,128)S(1)}, f32[64,8]{0,1:T(8,128)}, u32[]{:S(2)}) copy-start(f32[64,8]{0,1:T(8,128)} %param.8) | copy-start | bytes 6148
  41.9 16.4 %collective-permute-start.4 = (bf16[2,64,1024]{2,1,0:T(8,128)(2,1)S(1)}, bf16[2,64,1024]{2,1,0:T(8,128)(2,1)S(1)}, u32[]{:S(2)}, u32[]{:S(2)}) collective-permute-start(bf16[2,64,1024]{2,1,0:T(8,128)(2,1)S(1)} %get-tuple-element.28), channel_id=1, source_target_pairs={{0,16},{128,144},{16,32},{144,160},{32,48},{160,176},{48,0},{176,1... | collective-permute-start | bytes 786440 | tf_op jit(solution)/shard_map/ppermute | solution.py:26
  45.3 38.3 %collective-permute-start.5 = (bf16[2,64,1024]{2,1,0:T(8,128)(2,1)S(1)}, bf16[2,64,1024]{2,1,0:T(8,128)(2,1)S(1)}, u32[]{:S(2)}, u32[]{:S(2)}) collective-permute-start(bf16[2,64,1024]{2,1,0:T(8,128)(2,1)S(1)} %get-tuple-element.29), channel_id=1, source_target_pairs={{0,144},{128,32},{16,160},{144,48},{32,176},{160,0},{48,128},{176,... | collective-permute-start | bytes 786440 | tf_op jit(solution)/shard_map/ppermute | solution.py:26
  50.2 34.8 %collective-permute-start.6 = (bf16[2,64,1024]{2,1,0:T(8,128)(2,1)S(1)}, bf16[2,64,1024]{2,1,0:T(8,128)(2,1)S(1)}, u32[]{:S(2)}, u32[]{:S(2)}) collective-permute-start(bf16[2,64,1024]{2,1,0:T(8,128)(2,1)S(1)} %get-tuple-element.30), channel_id=1, source_target_pairs={{0,32},{128,160},{16,48},{144,176},{32,0},{160,128},{48,16},{176,1... | collective-permute-start | bytes 786440 | tf_op jit(solution)/shard_map/ppermute | solution.py:26
  51.2 33.8 %collective-permute-start.7 = (bf16[2,64,1024]{2,1,0:T(8,128)(2,1)S(1)}, bf16[2,64,1024]{2,1,0:T(8,128)(2,1)S(1)}, u32[]{:S(2)}, u32[]{:S(2)}) collective-permute-start(bf16[2,64,1024]{2,1,0:T(8,128)(2,1)S(1)} %get-tuple-element.31), channel_id=1, source_target_pairs={{0,160},{128,48},{16,176},{144,0},{32,128},{160,16},{48,144},{176,... | collective-permute-start | bytes 786440 | tf_op jit(solution)/shard_map/ppermute | solution.py:26
  55.7 39.3 %collective-permute-start.8 = (bf16[2,64,1024]{2,1,0:T(8,128)(2,1)S(1)}, bf16[2,64,1024]{2,1,0:T(8,128)(2,1)S(1)}, u32[]{:S(2)}, u32[]{:S(2)}) collective-permute-start(bf16[2,64,1024]{2,1,0:T(8,128)(2,1)S(1)} %get-tuple-element.32), channel_id=1, source_target_pairs={{0,48},{128,176},{16,0},{144,128},{32,16},{160,144},{48,32},{176,1... | collective-permute-start | bytes 786440 | tf_op jit(solution)/shard_map/ppermute | solution.py:26
  58.4 40.8 %collective-permute-start.2 = (bf16[2,64,1024]{2,1,0:T(8,128)(2,1)S(1)}, bf16[2,64,1024]{2,1,0:T(8,128)(2,1)}, u32[]{:S(2)}, u32[]{:S(2)}) collective-permute-start(bf16[2,64,1024]{2,1,0:T(8,128)(2,1)S(1)} %get-tuple-element.25), channel_id=1, source_target_pairs={{0,176},{128,0},{16,128},{144,16},{32,144},{160,32},{48,160},{176,... | collective-permute-start | bytes 786440 | tf_op jit(solution)/shard_map/ppermute | solution.py:26
  83.5 15.7 %collective-permute-start.3 = (bf16[2,64,1024]{2,1,0:T(8,128)(2,1)S(1)}, bf16[2,64,1024]{2,1,0:T(8,128)(2,1)}, u32[]{:S(2)}, u32[]{:S(2)}) collective-permute-start(bf16[2,64,1024]{2,1,0:T(8,128)(2,1)S(1)} %get-tuple-element.27), channel_id=1, source_target_pairs={{0,128},{128,16},{16,144},{144,32},{32,160},{160,48},{48,176},{176... | collective-permute-start | bytes 786440 | tf_op jit(solution)/shard_map/ppermute | solution.py:26
  95.0 92.4 %collective-permute-start.14 = (bf16[5,2,64,1024]{3,2,1,0:T(8,128)(2,1)S(1)}, bf16[5,2,64,1024]{3,2,1,0:T(8,128)(2,1)}, u32[]{:S(2)}, u32[]{:S(2)}) collective-permute-start(bf16[5,2,64,1024]{3,2,1,0:T(8,128)(2,1)S(1)} %bitcast_dynamic-update-slice_fusion.far_ref), channel_id=1, source_target_pairs={{0,1},{1,2},{2,3},{3,0},{4,5},{5,6},{6,7},{7,4},{8,9},{9,10},{10,1... | collective-permute-start | bytes 3932168 | tf_op jit(solution)/shard_map/ppermute | solution.py:20
  97.3 99.3 %collective-permute-start.17 = (bf16[5,2,64,1024]{3,2,1,0:T(8,128)(2,1)S(1)}, bf16[5,2,64,1024]{3,2,1,0:T(8,128)(2,1)S(1)}, u32[]{:S(2)}, u32[]{:S(2)}) collective-permute-start(bf16[5,2,64,1024]{3,2,1,0:T(8,128)(2,1)S(1)} %bitcast_dynamic-update-slice_fusion.far_ref), channel_id=1, source_target_pairs={{0,3},{1,0},{2,1},{3,2},{4,7},{5,4},{6,5},{7,6},{8,11},{9,8},{10,9... | collective-permute-start | bytes 3932168 | tf_op jit(solution)/shard_map/ppermute | solution.py:20
  100.4 76.5 %collective-permute-start.13 = (bf16[3,2,64,1024]{3,2,1,0:T(8,128)(2,1)S(1)}, bf16[3,2,64,1024]{3,2,1,0:T(8,128)(2,1)}, u32[]{:S(2)}, u32[]{:S(2)}) collective-permute-start(bf16[3,2,64,1024]{3,2,1,0:T(8,128)(2,1)S(1)} %pad_maximum_fusion.1.near_ref), channel_id=1, source_target_pairs={{0,1},{1,2},{2,3},{3,0},{4,5},{5,6},{6,7},{7,4},{8,9},{9,10},{10,1... | collective-permute-start | bytes 2359304 | tf_op jit(solution)/shard_map/ppermute | solution.py:20
  101.1 94.6 %collective-permute-start.16 = (bf16[3,2,64,1024]{3,2,1,0:T(8,128)(2,1)S(1)}, bf16[3,2,64,1024]{3,2,1,0:T(8,128)(2,1)}, u32[]{:S(2)}, u32[]{:S(2)}) collective-permute-start(bf16[3,2,64,1024]{3,2,1,0:T(8,128)(2,1)S(1)} %pad_maximum_fusion.1.near_ref), channel_id=1, source_target_pairs={{0,3},{1,0},{2,1},{3,2},{4,7},{5,4},{6,5},{7,6},{8,11},{9,8},{10,9... | collective-permute-start | bytes 2359304 | tf_op jit(solution)/shard_map/ppermute | solution.py:20
  104.1 100.4 %collective-permute-start.20 = (bf16[5,2,64,1024]{3,2,1,0:T(8,128)(2,1)S(1)}, bf16[5,2,64,1024]{3,2,1,0:T(8,128)(2,1)}, u32[]{:S(2)}, u32[]{:S(2)}) collective-permute-start(bf16[5,2,64,1024]{3,2,1,0:T(8,128)(2,1)S(1)} %bitcast_dynamic-update-slice_fusion.far_ref), channel_id=1, source_target_pairs={{0,2},{1,3},{2,0},{3,1},{4,6},{5,7},{6,4},{7,5},{8,10},{9,11},{10,... | collective-permute-start | bytes 3932168 | tf_op jit(solution)/shard_map/ppermute | solution.py:20
  176.8 27.7 %collective-permute-start.19 = (bf16[3,2,64,1024]{3,2,1,0:T(8,128)(2,1)S(1)}, bf16[3,2,64,1024]{3,2,1,0:T(8,128)(2,1)}, u32[]{:S(2)}, u32[]{:S(2)}) collective-permute-start(bf16[3,2,64,1024]{3,2,1,0:T(8,128)(2,1)S(1)} %pad_maximum_fusion.1.near_ref), channel_id=1, source_target_pairs={{0,2},{1,3},{2,0},{3,1},{4,6},{5,7},{6,4},{7,5},{8,10},{9,11},{10,... | collective-permute-start | bytes 2359304 | tf_op jit(solution)/shard_map/ppermute | solution.py:20
  179.2 0.6 copy-start.2
  187.4 25.9 %collective-permute-start.12 = (bf16[8,64,896]{2,1,0:T(8,128)(2,1)S(1)}, bf16[8,64,896]{2,1,0:T(8,128)(2,1)}, u32[]{:S(2)}, u32[]{:S(2)}) collective-permute-start(bf16[8,64,896]{2,1,0:T(8,128)(2,1)S(1)} %get-tuple-element.38), channel_id=1, source_target_pairs={{0,64},{64,0},{1,65},{65,1},{2,66},{66,2},{3,67},{67,3},{4,68},{68... | collective-permute-start | bytes 2752520 | tf_op jit(solution)/shard_map/ppermute | solution.py:20
  195.7 18.9 %collective-permute-start.15 = (bf16[8,64,896]{2,1,0:T(8,128)(2,1)S(1)}, bf16[8,64,896]{2,1,0:T(8,128)(2,1)}, u32[]{:S(2)}, u32[]{:S(2)}) collective-permute-start(bf16[8,64,896]{2,1,0:T(8,128)(2,1)S(1)} %get-tuple-element.40), channel_id=1, source_target_pairs={{0,64},{64,0},{1,65},{65,1},{2,66},{66,2},{3,67},{67,3},{4,68},{68... | collective-permute-start | bytes 2752520 | tf_op jit(solution)/shard_map/ppermute | solution.py:20
  204.4 11.7 %collective-permute-start.18 = (bf16[8,64,896]{2,1,0:T(8,128)(2,1)S(1)}, bf16[8,64,896]{2,1,0:T(8,128)(2,1)S(1)}, u32[]{:S(2)}, u32[]{:S(2)}) collective-permute-start(bf16[8,64,896]{2,1,0:T(8,128)(2,1)S(1)} %get-tuple-element.42), channel_id=1, source_target_pairs={{0,64},{64,0},{1,65},{65,1},{2,66},{66,2},{3,67},{67,3},{4,68},{68... | collective-permute-start | bytes 2752520 | tf_op jit(solution)/shard_map/ppermute | solution.py:20
  212.7 3.6 %collective-permute-start.21 = (bf16[8,64,896]{2,1,0:T(8,128)(2,1)S(1)}, bf16[8,64,896]{2,1,0:T(8,128)(2,1)S(1)}, u32[]{:S(2)}, u32[]{:S(2)}) collective-permute-start(bf16[8,64,896]{2,1,0:T(8,128)(2,1)S(1)} %get-tuple-element.44), channel_id=1, source_target_pairs={{0,64},{64,0},{1,65},{65,1},{2,66},{66,2},{3,67},{67,3},{4,68},{68... | collective-permute-start | bytes 2752520 | tf_op jit(solution)/shard_map/ppermute | solution.py:20
  267.5 7.8 %collective-permute-start.22 = (bf16[64,896]{1,0:T(8,128)(2,1)S(1)}, bf16[64,896]{1,0:T(8,128)(2,1)S(1)}, u32[]{:S(2)}, u32[]{:S(2)}) collective-permute-start(bf16[64,896]{1,0:T(8,128)(2,1)S(1)} %get-tuple-element.49), channel_id=1, source_target_pairs={{0,3},{1,0},{2,1},{3,2},{4,7},{5,4},{6,5},{7,6},{8,11},{9,8},{10,9... | collective-permute-start | bytes 344072 | tf_op jit(solution)/shard_map/ppermute | solution.py:20
  270.3 7.4 %collective-permute-start.23 = (bf16[64,896]{1,0:T(8,128)(2,1)S(1)}, bf16[64,896]{1,0:T(8,128)(2,1)S(1)}, u32[]{:S(2)}, u32[]{:S(2)}) collective-permute-start(bf16[64,896]{1,0:T(8,128)(2,1)S(1)} %get-tuple-element.48), channel_id=1, source_target_pairs={{0,2},{1,3},{2,0},{3,1},{4,6},{5,7},{6,4},{7,5},{8,10},{9,11},{10,... | collective-permute-start | bytes 344072 | tf_op jit(solution)/shard_map/ppermute | solution.py:20
  271.1 7.8 %collective-permute-start.24 = (bf16[64,896]{1,0:T(8,128)(2,1)S(1)}, bf16[64,896]{1,0:T(8,128)(2,1)S(1)}, u32[]{:S(2)}, u32[]{:S(2)}) collective-permute-start(bf16[64,896]{1,0:T(8,128)(2,1)S(1)} %get-tuple-element.47), channel_id=1, source_target_pairs={{0,1},{1,2},{2,3},{3,0},{4,5},{5,6},{6,7},{7,4},{8,9},{9,10},{10,1... | collective-permute-start | bytes 344072 | tf_op jit(solution)/shard_map/ppermute | solution.py:20
Sparse Core Ops, SparseCore 0:
  35.6 79.3 all-gather.2
  219.4 46.9 reduce-scatter.1

commit v3 on v2

v3 whole, which is shorter than its diff:
```python
import functools
import jax
import jax.numpy as jnp
from jax import lax
from jax.experimental import pallas as pl
from jax.experimental.pallas import tpu as pltpu
from jax.sharding import Mesh, PartitionSpec as P

AXES = ("zl", "c", "zh", "x", "y")
Z = ("zh", "zl")
VMEM = pl.BlockSpec(memory_space=pltpu.VMEM)
SMEM = pl.BlockSpec(memory_space=pltpu.SMEM)
PARAMS = pltpu.CompilerParams(vmem_limit_bytes=48 << 20)


def shifted(value, axis, steps):
    count = lax.axis_size(axis)
    return lax.ppermute(value, axis, [(i, (i + steps) % count) for i in range(count)])


def after(value, *others):
    return lax.optimization_barrier((value, *others))[0]


def cost(flops, *arrays):
    size = sum(a.size * a.dtype.itemsize for a in arrays)
    return pl.CostEstimate(flops=flops, bytes_accessed=size, transcendentals=0)


def split_kernel(pos_ref, w_ref, *out_refs):
    count = len(out_refs)
    width = out_refs[0].shape[2]
    for d, out_ref in enumerate(out_refs):
        start = pl.multiple_of(lax.rem(pos_ref[2] + d, count) * width, 128)
        out_ref[...] = w_ref[:, :, pl.ds(start, width)]


def split_blocks(pos, own, count):
    exp_train, depth, width = own.shape
    shape = jax.ShapeDtypeStruct((exp_train, depth, width // count), own.dtype)
    return pl.pallas_call(
        split_kernel, out_shape=[shape] * count, in_specs=[SMEM, VMEM], out_specs=[VMEM] * count,
        compiler_params=PARAMS, cost_estimate=cost(0, own, own),
    )(pos, own)


def join_kernel(pos_ref, *refs):
    in_refs, out_ref = refs[:-1], refs[-1]
    count, depth = len(in_refs), in_refs[0].shape[1]
    for d, in_ref in enumerate(in_refs):
        start = pl.multiple_of(lax.rem(pos_ref[2] + count - d, count) * depth, depth)
        out_ref[:, pl.ds(start, depth), :] = in_ref[...]


def join_blocks(pos, blocks):
    exp_train, depth, width = blocks[0].shape
    shape = jax.ShapeDtypeStruct((exp_train, depth * len(blocks), width), blocks[0].dtype)
    return pl.pallas_call(
        join_kernel, out_shape=shape, in_specs=[SMEM] + [VMEM] * len(blocks), out_specs=VMEM,
        compiler_params=PARAMS, cost_estimate=cost(0, shape, shape),
    )(pos, *blocks)


def dispatch_kernel(groups, first_ref, flat_ref, hidden_ref, out_ref):
    slots, pairs = out_ref.shape[1], flat_ref.shape[1]
    whole = 2 * slots
    number = lax.broadcasted_iota(jnp.int32, (groups * slots, pairs), 0)
    number = number // slots * whole + lax.rem(number, slots) + first_ref[0]
    chosen = jnp.where(number == flat_ref[...], 1.0, 0.0).astype(jnp.bfloat16)
    rows = jnp.dot(chosen, hidden_ref[...], preferred_element_type=jnp.float32).astype(jnp.bfloat16)
    out_ref[...] = rows.reshape(out_ref.shape)


def dispatch(first, flat, hidden, groups, slots):
    shape = jax.ShapeDtypeStruct((groups, slots, hidden.shape[1]), hidden.dtype)
    return pl.pallas_call(
        functools.partial(dispatch_kernel, groups),
        out_shape=shape, in_specs=[SMEM, VMEM, VMEM], out_specs=VMEM,
        compiler_params=PARAMS, cost_estimate=cost(2 * groups * slots * hidden.size, hidden, shape),
    )(jnp.full((1,), first, jnp.int32), flat, hidden)


def experts_kernel(steps, counts, pos_ref, *refs):
    half = sum(counts)
    x_refs, w_refs = (refs[:half], refs[half:2 * half]), refs[2 * half:2 * half + 5]
    gate_ref, row_ref, mine_ref, other_ref, x_ref, p_ref = refs[2 * half + 5:]
    turn, k = pl.program_id(0), pl.program_id(1)
    capacity, hidden_width = x_refs[0][0].shape[-2:]
    experts = pl.num_programs(1)
    slots = capacity * experts
    depth, width = w_refs[0].shape[1:]
    planes, _, rows, _ = mine_ref.shape
    c, x = pos_ref[1], pos_ref[3]
    first = 0
    for number, count in enumerate(counts):
        for part in range(2):
            @pl.when((turn == number) & (k // 2 == part))
            def _(first=first, count=count, part=part):
                for d in range(4):
                    start = pl.multiple_of(lax.rem(x + 4 - d, 4) * depth, 128)
                    block = [r[:, :, pl.ds(start, depth)].reshape(-1, depth) for r in x_refs[part][first:first + count]]
                    x_ref[:, d * depth:(d + 1) * depth] = jnp.concatenate(block, 0)
        first += count
    opposite = jnp.where(k < 2, w_refs[2][0], w_refs[3][0])
    weights = jnp.concatenate([w_refs[0][0], w_refs[1][0], opposite, w_refs[4][0]], 0)
    total = jnp.dot(x_ref[...], weights, preferred_element_type=jnp.float32)
    high = total.astype(jnp.bfloat16)
    low = (total - high.astype(jnp.float32)).astype(jnp.bfloat16)
    high, low = (v.reshape(-1, capacity, width) for v in (high, low))
    for part, value in enumerate((high, high, low)):
        start = pl.multiple_of(part * slots + k * capacity, capacity)
        p_ref[:, pl.ds(start, capacity), :] = value

    @pl.when(k == experts - 1)
    def _():
        number = lax.broadcasted_iota(jnp.int32, (rows, 3 * slots), 0).astype(jnp.float32)
        column = lax.broadcasted_iota(jnp.int32, (rows, 3 * slots), 1)
        middle = (column >= slots) & (column < 2 * slots)
        step = steps[0] + turn * (steps[-1] - steps[0])
        for plane in range(planes):
            for core, out_ref in enumerate((mine_ref, other_ref)):
                source = plane * 2 + lax.rem(c + core, 2)
                index = source * 4 + step
                gate = gate_ref[pl.ds(index, 1), :]
                gate_high = gate.astype(jnp.bfloat16).astype(jnp.float32)
                value = jnp.where(middle, gate - gate_high, gate_high)
                combine = jnp.where(number == row_ref[pl.ds(index, 1), :], value, 0.0).astype(jnp.bfloat16)
                mixed = jnp.dot(combine, p_ref[source], preferred_element_type=jnp.float32)
                out_ref[plane, 0] = mixed.astype(out_ref.dtype)


def experts_call(steps, pos, xs, ws, gate, row, rows):
    experts, depth, width = ws[0].shape
    half = experts // 2
    hidden_width = xs[0][0][0].shape[2]
    capacity = xs[0][0][0].shape[1] // half
    groups = sum(v.shape[0] for v in xs[0][0])
    turns = len(steps)
    mine = jax.ShapeDtypeStruct((groups // 2, turns, rows, width), jnp.float32)
    other = jax.ShapeDtypeStruct((groups // 2, turns, rows, width), jnp.bfloat16)
    arrays, specs = [], []
    for part in range(2):
        for turn in range(turns):
            for v in xs[turn][part]:
                def index(t, k, part=part, turn=turn):
                    now = jnp.clip(k - part * half, 0, half - 1)
                    return 0, jnp.where(t == turn, now, jnp.where(t < turn, 0, half - 1)), 0

                arrays.append(v)
                specs.append(pl.BlockSpec((v.shape[0], capacity, hidden_width), index))
    kinds = [lambda k: k, lambda k: k, lambda k: jnp.minimum(k, half - 1), lambda k: jnp.maximum(k - half, 0), lambda k: k]
    w_specs = [pl.BlockSpec((1, depth, width), lambda t, k, f=f: (f(k), 0, 0)) for f in kinds]
    whole = pl.BlockSpec((groups // 2, 1, rows, width), lambda t, k: (0, t, 0, 0))
    info = pl.BlockSpec(gate.shape, lambda t, k: (0, 0))
    flops = 2 * turns * groups * capacity * experts * hidden_width * width
    return pl.pallas_call(
        functools.partial(experts_kernel, steps, [len(v[0]) for v in xs]),
        grid=(turns, experts),
        out_shape=[mine, other],
        in_specs=[SMEM] + specs + w_specs + [info] * 2,
        out_specs=[whole] * 2,
        scratch_shapes=[
            pltpu.VMEM((groups * capacity, hidden_width), jnp.bfloat16),
            pltpu.VMEM((groups, 3 * experts * capacity, width), jnp.bfloat16),
        ],
        compiler_params=PARAMS,
        cost_estimate=cost(flops, *arrays, *ws, *ws, mine, other),
    )(pos, *arrays, *ws, gate, row)


def place_kernel(pos_ref, *refs):
    in_refs, out_ref = refs[:-1], refs[-1]
    width = in_refs[0].shape[1]
    for d, in_ref in enumerate(in_refs):
        start = pl.multiple_of(lax.rem(pos_ref[2] + d, len(in_refs)) * width, 128)
        out_ref[:, pl.ds(start, width)] = in_ref[...]


def place_blocks(pos, blocks):
    rows, width = blocks[0].shape
    shape = jax.ShapeDtypeStruct((rows, width * len(blocks)), blocks[0].dtype)
    return pl.pallas_call(
        place_kernel, out_shape=shape, in_specs=[SMEM] + [VMEM] * len(blocks), out_specs=VMEM,
        compiler_params=PARAMS, cost_estimate=cost(0, shape, shape),
    )(pos, *blocks)


def per_device(trainer_weight, owner, expert_ids, gates, hidden):
    experts = owner.shape[0]
    rows, fanout = expert_ids.shape
    hidden_width = hidden.shape[2]
    capacity = min(rows, 2 * rows * fanout // experts)
    own = trainer_weight[0, 0]
    exp_train, slice_rows, width = own.shape
    ny = lax.axis_size("y")
    groups = experts // exp_train
    slots = exp_train * capacity
    block_width = width // ny
    low = lax.axis_size("zl")
    z, c, y = lax.axis_index("zh") * low + lax.axis_index("zl"), lax.axis_index("c"), lax.axis_index("y")
    pos = jnp.stack([z, c, y, lax.axis_index("x")]).astype(jnp.int32)

    zl, cs, zh = (lax.axis_size(a) for a in ("zl", "c", "zh"))
    slot_of = owner.reshape(zl, cs, zh, exp_train).transpose(2, 0, 1, 3).reshape(experts)
    match = expert_ids[:, :, None] == slot_of[None, None, :]
    named = jnp.any(match, axis=1)
    position = jnp.cumsum(named.astype(jnp.int32), axis=0) - 1
    place = jnp.arange(experts, dtype=jnp.int32)[None, :] * capacity + position
    flat = jnp.sum(jnp.where(match, place[:, None, :], 0), axis=2).reshape(1, -1)
    pairs = hidden.reshape(-1, hidden_width)
    group_axes = Z + ("c",)

    blocks = split_blocks(pos, own, ny)
    blocks = [blocks[0]] + [shifted(blocks[d], "y", d) for d in range(1, ny)]

    outbound = dispatch(0, flat, pairs, groups, slots // 2)
    blocks[1] = after(blocks[1], outbound)
    first = lax.all_to_all(outbound, group_axes, 0, 0, tiled=True)

    chosen = jnp.arange(experts * capacity, dtype=jnp.int32)[:, None] == flat
    pair_row = jnp.arange(rows * fanout, dtype=jnp.int32) // fanout
    slot_gate = jnp.sum(jnp.where(chosen, gates.reshape(-1)[None, :], 0.0), axis=1).reshape(groups, slots)
    slot_row = jnp.sum(jnp.where(chosen, pair_row[None, :] + 1, 0), axis=1).reshape(groups, slots) - 1
    info = jnp.concatenate([slot_gate, slot_row.astype(jnp.float32)], 1)
    info = jnp.stack([info] + [shifted(info, "y", d) for d in range(1, ny)], 1)

    weight = join_blocks(pos, blocks)
    weight_up, weight_down = shifted(weight, "x", 1), shifted(weight, "x", -1)

    first_up, first_down = shifted(first, "y", 1), shifted(first, "y", -1)
    outbound = dispatch(slots // 2, flat, pairs, groups, slots // 2)
    second = lax.all_to_all(after(outbound, first, weight, info), group_axes, 0, 0, tiled=True)
    middle = groups // 2
    first_up, first_down, weight_up, weight_down = lax.optimization_barrier(
        (first_up, first_down, weight_up, weight_down)
    )
    first_opposite = [shifted(first_up[:middle], "y", 1), shifted(first_down[middle:], "y", -1)]
    half = exp_train // 2
    weight_opposite = [shifted(weight_up[:half], "x", 1), shifted(weight_down[half:], "x", -1)]
    weights = [weight, weight_up, *weight_opposite, weight_down]
    second_late = after(second, first_up, first_down, weight_up, weight_down)
    second_up, second_down = shifted(second_late, "y", 1), shifted(second_late, "y", -1)
    info = lax.all_to_all(after(info, second), group_axes, 0, 0, tiled=True).reshape(groups * ny, 2 * slots)
    gate = jnp.tile(info[:, :slots], (1, 3))
    row = jnp.tile(info[:, slots:], (1, 3))
    second_opposite = [shifted(second_up[:middle], "y", 1), shifted(second_down[middle:], "y", -1)]

    partials = []
    own_rows, up_rows = ([first], [second]), ([first_up], [second_up])
    down_rows, opposite_rows = ([first_down], [second_down]), (first_opposite, second_opposite)
    for steps, xs in (((0, 1), (own_rows, up_rows)), ((ny - 1, 2), (down_rows, opposite_rows))):
        mine, other = experts_call(steps, pos, xs, weights, gate, row, rows)
        other = shifted(other, "c", 1)
        partials.append((mine + other.astype(jnp.float32)).astype(jnp.bfloat16))
    partial = jnp.concatenate(partials, 1).reshape(-1, block_width)
    summed = lax.psum_scatter(partial, Z, scatter_dimension=0, tiled=True).reshape(ny, rows, block_width)
    final = [summed[0], shifted(summed[1], "y", -1), shifted(summed[3], "y", 2), shifted(summed[2], "y", 1)]
    return place_blocks(pos, final)


def solution(mesh):
    devices = mesh.devices.reshape(2, 2, 4, 4, 4)
    inner = Mesh(devices, AXES)
    rep, exp = ("zl", "c"), ("zh", "x", "y")
    return jax.shard_map(
        per_device,
        mesh=inner,
        in_specs=(
            P(rep, exp, None, None, None),
            P(),
            P(rep + exp, None),
            P(rep + exp, None),
            P(rep + exp, None, None),
        ),
        out_specs=P(rep + exp, None),
        check_vma=False,
    )
```

time: 288 us -> 257 us (0.89)
  blocking collectives: 68.7 us -> 0 us
  waiting for transfers between devices: 105 us -> 118 us
  starting transfers between devices: 43.3 us -> 55.6 us
  local copies, waits for them, and re-layouts: 10.9 us -> 19.3 us
  Pallas kernels: 37.6 us -> 41.1 us
    all_to_all x1 -> x0, blocking collectives: 68.7 us -> none  [per_device(): info = lax.all_to_all(info, Z + ('c', 'y'), 0, 0, tiled=True)]
    ppermute x18 -> x23, waiting for transfers between devices: 26.5 us -> 69.2 us  [shifted(): lax.ppermute(value, axis, [(i, (i + steps) % count) for i in range(count)])]
    ppermute x7 -> x0, waiting for transfers between devices: 31.4 us -> none  [shifted_z(): lax.ppermute(value, ('zl', 'zh'), [(number(z), number(z + steps)) for z i...]
    all_to_all x0 -> x3, starting transfers between devices: none -> 22.7 us  [the longest x1 8.75 us: per_device(): first = lax.all_to_all(outbound, group_axes, 0, 0, tiled=True)]
    ppermute x7 -> x0, starting transfers between devices: 21.6 us -> none  [shifted_z(): lax.ppermute(value, ('zl', 'zh'), [(number(z), number(z + steps)) for z i...]
    ppermute x18 -> x23, starting transfers between devices: 21.7 us -> 32.9 us  [shifted(): lax.ppermute(value, axis, [(i, (i + steps) % count) for i in range(count)])]
    slice x0 -> x6, local copies, waits for them, and re-layouts: none -> 10.7 us  [the longest x1 2.2 us: per_device(): weight_up[:half]]
    another operation x8 -> x2, other arithmetic: 5.65 us -> 0.08 us  [the longest x1 0.08 us: per_device(): pos = jnp.stack([z, c, y, lax.axis_index('x')]).astype(jnp.int32)]
  transfers between devices with their start and end apart: 27 -> 27, of which waited for: 10 -> 10; matrix products, arithmetic and copies ran while one was open for 4% -> 6% of each run, Pallas kernels for 12% -> 15%
where the time goes in v3:
time: 257 us; the launch traced here: 255 us
  waiting for transfers between devices  118 us (46%)
  starting transfers between devices  55.6 us (22%)
  Pallas kernels  41.1 us (16%)
  local copies, waits for them, and re-layouts  19.3 us (8%)
  between operations  13.7 us (5%)
  other arithmetic  7.14 us (3%)
    ppermute x23, waiting for transfers between devices, shifted(): lax.ppermute(value, axis, [(i, (i + steps) % count) for i in range(count)])  69.2 us
    reduce_scatter x1, waiting for transfers between devices, per_device(): lax.psum_scatter(partial, Z, scatter_dimension=0, tiled=True)  49.2 us
    pallas_call x2, Pallas kernels, experts_call(): pl.pallas_call(functools.partial(experts_kernel, steps, [len(v[0]) for v...  33.9 us
    ppermute x23, starting transfers between devices, shifted(): lax.ppermute(value, axis, [(i, (i + steps) % count) for i in range(count)])  32.9 us
    all_to_all x1, starting transfers between devices, per_device(): first = lax.all_to_all(outbound, group_axes, 0, 0, tiled=True)  8.75 us
    all_to_all x1, starting transfers between devices, per_device(): lax.all_to_all(after(outbound, first, weight, info), group_axes, 0, 0, ti...  6.97 us
    all_to_all x1, starting transfers between devices, per_device(): lax.all_to_all(after(info, second), group_axes, 0, 0, tiled=True)  6.96 us
    unnamed x24, local copies, waits for them, and re-layouts  5.19 us
  transfers between devices with their start and end apart: 27, of which 10 were waited for; matrix products, arithmetic and copies ran while one was open for 6% of the time, Pallas kernels for 15%

profile of v3, /device:TPU:2, one launch (start us, length us, event | category | flops | bytes accessed | tf_op | source)
XLA Modules:
  0.0 255.2 jit_solution(587110831736820263)
XLA Ops:
  6.5 0.8 copy.41
  7.3 0.7 reshape.84
  8.1 0.1 eq.31
  8.2 0.2 compare_reduce_fusion
  8.4 0.1 reduce_window_sum.11
  8.5 1.2 fusion
  9.8 1.2 copy-done
  11.0 1.7 shard_map.55
  12.8 8.8 %all-to-all-start = ((bf16[16,32,1024]{2,1,0:T(8,128)(2,1)}), bf16[16,32,1024]{2,1,0:T(8,128)(2,1)}, u32[]{:S(2)}, u32[]{:S(2)}) async-start(bf16[16,32,1024]{2,1,0:T(8,128)(2,1)} %shard_map.55), calls=%async_computation | async-start | bytes 2097152 | tf_op jit(solution)/shard_map/all_to_all | solution.py:218
  21.6 1.7 shard_map.56
  23.3 1.6 collective-permute-start.2
  24.9 2.9 %collective-permute-start.3 = (bf16[4,64,896]{2,1,0:T(8,128)(2,1)}, bf16[4,64,896]{2,1,0:T(8,128)(2,1)S(1)}, u32[]{:S(2)}, u32[]{:S(2)}) collective-permute-start(bf16[4,64,896]{2,1,0:T(8,128)(2,1)} %get-tuple-element.24), channel_id=1, source_target_pairs={{0,2},{1,3},{2,0},{3,1},{4,6},{5,7},{6,4},{7,5},{8,10},{9,11},{10,... | collective-permute-start | bytes 1376264 | tf_op jit(solution)/shard_map/ppermute | solution.py:18
  27.8 1.3 collective-permute-start.4
  29.4 0.1 broadcast_in_dim.45
  29.4 0.3 select_reduce_fusion.1
  29.8 0.3 select_reduce_fusion
  30.3 2.0 collective-permute-start.7
  32.3 15.9 %collective-permute-done.9 = f32[16,128]{1,0:T(8,128)S(1)} collective-permute-done((f32[16,128]{1,0:T(8,128)S(1)}, f32[16,128]{1,0:T(8,128)S(1)}, u32[]{:S(2)}, u32[]{:S(2)}) %collective-permute-start.9) | collective-permute-done | bytes 8224 | tf_op jit(solution)/shard_map/ppermute | solution.py:18
  48.2 3.1 %collective-permute-start.8 = (f32[16,128]{1,0:T(8,128)S(1)}, f32[16,128]{1,0:T(8,128)S(1)}, u32[]{:S(2)}, u32[]{:S(2)}) collective-permute-start(f32[16,128]{1,0:T(8,128)S(1)} %pad_maximum_fusion.2), channel_id=1, source_target_pairs={{0,2},{1,3},{2,0},{3,1},{4,6},{5,7},{6,4},{7,5},{8,10},{9,11},{10,... | collective-permute-start | bytes 24584 | tf_op jit(solution)/shard_map/ppermute | solution.py:18
  51.4 1.7 shard_map.58
  53.1 0.3 collective-permute-done.8
  53.4 0.8 copy-done.4
  54.2 1.0 copy-done.5
  55.2 0.7 shard_map.57.refs_4_.refs_6_
  55.9 7.0 %all-to-all-start.1 = ((bf16[16,32,1024]{2,1,0:T(8,128)(2,1)}), bf16[16,32,1024]{2,1,0:T(8,128)(2,1)S(1)}, u32[]{:S(2)}, u32[]{:S(2)}) async-start(bf16[16,32,1024]{2,1,0:T(8,128)(2,1)} %shard_map.58), calls=%async_computation.1 | async-start | bytes 2097152 | tf_op jit(solution)/shard_map/all_to_all | solution.py:232
  62.9 1.6 collective-permute-start.5
  64.5 0.5 collective-permute-start.6
  65.0 1.7 collective-permute-start
  66.7 1.5 collective-permute-start.1
  68.2 37.1 %collective-permute-done.5.refs_5_.refs_7_ = bf16[4,256,896]{2,1,0:T(8,128)(2,1)} collective-permute-done((bf16[4,256,896]{2,1,0:T(8,128)(2,1)S(1)}, bf16[4,256,896]{2,1,0:T(8,128)(2,1)}, u32[]{:S(2)}, u32[]{:S(2)}) %collective-permute-start.5) | collective-permute-done | bytes 1835040 | tf_op jit(solution)/shard_map/ppermute | solution.py:18
  105.3 1.1 collective-permute-done.6.refs_8_.refs_10_
  106.4 1.3 copy-done.8
  107.8 2.0 collective-permute-start.10
  109.7 1.5 collective-permute-start.16
  111.2 2.2 slice.40
  113.4 1.2 collective-permute-start.11
  114.7 1.0 slice.41
  115.7 0.8 collective-permute-start.12
  116.5 0.6 copy.44
  117.1 7.0 %all-to-all-start.2 = ((f32[16,4,128]{2,1,0:T(4,128)}), f32[16,4,128]{2,1,0:T(4,128)S(1)}, u32[]{:S(2)}, u32[]{:S(2)}) async-start(f32[16,4,128]{2,1,0:T(4,128)} %copy.44), calls=%async_computation.2 | async-start | bytes 65536 | tf_op jit(solution)/shard_map/all_to_all | solution.py:243
  124.1 1.9 slice.44
  126.0 1.9 slice.45
  127.9 0.5 collective-permute-start.14
  128.4 6.4 %collective-permute-done.10.refs_3_ = bf16[16,32,1024]{2,1,0:T(8,128)(2,1)} collective-permute-done((bf16[16,32,1024]{2,1,0:T(8,128)(2,1)S(1)}, bf16[16,32,1024]{2,1,0:T(8,128)(2,1)}, u32[]{:S(2)}, u32[]{:S(2)}) %collective-permute-start.10) | collective-permute-done | bytes 1048608 | tf_op jit(solution)/shard_map/ppermute | solution.py:18
  134.7 2.1 collective-permute-start.15
  136.8 1.9 slice.54
  138.7 1.9 slice.55
  140.6 3.2 %collective-permute-start.18 = (bf16[8,32,1024]{2,1,0:T(8,128)(2,1)}, bf16[8,32,1024]{2,1,0:T(8,128)(2,1)}, u32[]{:S(2)}, u32[]{:S(2)}) collective-permute-start(bf16[8,32,1024]{2,1,0:T(8,128)(2,1)} %slice.55), channel_id=1, source_target_pairs={{0,3},{1,0},{2,1},{3,2},{4,7},{5,4},{6,5},{7,6},{8,11},{9,8},{10,9... | collective-permute-start | bytes 1572872 | tf_op jit(solution)/shard_map/ppermute | solution.py:18
  144.3 17.0 %shard_map.59 = (f32[8,2,64,896]{3,2,1,0:T(8,128)}, bf16[8,2,64,896]{3,2,1,0:T(8,128)(2,1)}) custom-call(s32[4]{0:T(128)S(1)} %pad_add_fusion.pos_ref, bf16[16,32,1024]{2,1,0:T(8,128)(2,1)} %all-to-all-done.refs_0_, bf16[16,32,1024]{2,1,0:T(8,128)(2,1)} %collective-permute-done.refs_1_, bf16[16,32,1024]{2,1,0:T(8,128)(2,1)S(1)} %all-to-all-done.1.refs_2_, ...), custom_call_target="tpu_custom_call" | custom-call | flops 3758096384 | bytes 24379392 | tf_op jit(solution)/shard_map/pallas_call | solution.py:156
  161.4 16.9 %shard_map.60 = (f32[8,2,64,896]{3,2,1,0:T(8,128)}, bf16[8,2,64,896]{3,2,1,0:T(8,128)(2,1)}) custom-call(s32[4]{0:T(128)S(1)} %pad_add_fusion.pos_ref, bf16[16,32,1024]{2,1,0:T(8,128)(2,1)} %collective-permute-done.1.refs_0_, bf16[8,32,1024]{2,1,0:T(8,128)(2,1)S(1)} %collective-permute-done.14.refs_1_, ...), custom_call_target="tpu_custom_call" | custom-call | flops 3758096384 | bytes 24379392 | tf_op jit(solution)/shard_map/pallas_call | solution.py:156
  178.3 0.7 collective-permute-start.19
  179.0 2.2 add_convert_fusion.1
  181.2 1.4 collective-permute-done.19
  182.6 0.5 add_convert_fusion
  183.1 2.1 pad_maximum_fusion
  185.3 49.2 %reduce-scatter.2.cloned.1.call-done = bf16[256,896]{1,0:T(8,128)(2,1)} async-done(((bf16[2048,896]{1,0:T(8,128)(2,1)}), bf16[256,896]{1,0:T(8,128)(2,1)}) %reduce-scatter.2.cloned.1.call-update) | async-done | bytes 458768 | tf_op jit(solution)/shard_map/reduce_scatter | solution.py:256
  234.5 1.1 fusion.5
  235.6 2.8 %collective-permute-start.20 = (bf16[64,896]{1,0:T(8,128)(2,1)S(1)}, bf16[64,896]{1,0:T(8,128)(2,1)S(1)}, u32[]{:S(2)}, u32[]{:S(2)}) collective-permute-start(bf16[64,896]{1,0:T(8,128)(2,1)S(1)} %get-tuple-element.39), channel_id=1, source_target_pairs={{0,3},{1,0},{2,1},{3,2},{4,7},{5,4},{6,5},{7,6},{8,11},{9,8},{10,9... | collective-permute-start | bytes 344072 | tf_op jit(solution)/shard_map/ppermute | solution.py:18
  238.4 0.8 collective-permute-start.21
  239.2 0.9 collective-permute-start.22
  240.1 3.3 %collective-permute-done.20.refs_1_ = bf16[64,896]{1,0:T(8,128)(2,1)S(1)} collective-permute-done((bf16[64,896]{1,0:T(8,128)(2,1)S(1)}, bf16[64,896]{1,0:T(8,128)(2,1)S(1)}, u32[]{:S(2)}, u32[]{:S(2)}) %collective-permute-start.20) | collective-permute-done | bytes 114720 | tf_op jit(solution)/shard_map/ppermute | solution.py:18
  243.4 2.5 collective-permute-done.21.refs_2_
  245.8 1.2 collective-permute-done.22.refs_3_
  247.0 1.4 shard_map.61
  (61 shorter events, 1.2 us)
Async XLA Ops:
  9.8 1.2 copy-start
  11.0 10.6 %copy-start.2 = (bf16[1,1,4,64,3584]{4,3,2,1,0:T(8,128)(2,1)S(1)}, bf16[1,1,4,64,3584]{4,3,2,1,0:T(8,128)(2,1)}, u32[]{:S(2)}) copy-start(bf16[1,1,4,64,3584]{4,3,2,1,0:T(8,128)(2,1)} %param.5) | copy-start | bytes 5505028
  12.8 16.5 %copy-start.10 = (f32[64,8]{0,1:T(8,128)S(1)}, f32[64,8]{0,1:T(8,128)}, u32[]{:S(2)}) copy-start(f32[64,8]{0,1:T(8,128)} %param.8) | copy-start | bytes 6148
  12.8 38.6 %copy-start.1 = (bf16[64,8,1024]{2,1,0:T(8,128)(2,1)S(1)}, bf16[64,8,1024]{2,1,0:T(8,128)(2,1)}, u32[]{:S(2)}) copy-start(bf16[64,8,1024]{2,1,0:T(8,128)(2,1)} %param.9) | copy-start | bytes 3145732
  12.8 43.1 %all-to-all-start = ((bf16[16,32,1024]{2,1,0:T(8,128)(2,1)}), bf16[16,32,1024]{2,1,0:T(8,128)(2,1)}, u32[]{:S(2)}, u32[]{:S(2)}) async-start(bf16[16,32,1024]{2,1,0:T(8,128)(2,1)} %shard_map.55), calls=%async_computation | async-start | bytes 2097152 | tf_op jit(solution)/shard_map/all_to_all | solution.py:218
  23.3 30.0 %collective-permute-start.2 = (bf16[4,64,896]{2,1,0:T(8,128)(2,1)}, bf16[4,64,896]{2,1,0:T(8,128)(2,1)S(1)}, u32[]{:S(2)}, u32[]{:S(2)}) collective-permute-start(bf16[4,64,896]{2,1,0:T(8,128)(2,1)} %get-tuple-element.22), channel_id=1, source_target_pairs={{0,1},{1,2},{2,3},{3,0},{4,5},{5,6},{6,7},{7,4},{8,9},{9,10},{10,1... | collective-permute-start | bytes 1376264 | tf_op jit(solution)/shard_map/ppermute | solution.py:18
  24.9 28.5 %collective-permute-start.3 = (bf16[4,64,896]{2,1,0:T(8,128)(2,1)}, bf16[4,64,896]{2,1,0:T(8,128)(2,1)S(1)}, u32[]{:S(2)}, u32[]{:S(2)}) collective-permute-start(bf16[4,64,896]{2,1,0:T(8,128)(2,1)} %get-tuple-element.24), channel_id=1, source_target_pairs={{0,2},{1,3},{2,0},{3,1},{4,6},{5,7},{6,4},{7,5},{8,10},{9,11},{10,... | collective-permute-start | bytes 1376264 | tf_op jit(solution)/shard_map/ppermute | solution.py:18
  27.8 25.6 %collective-permute-start.4 = (bf16[4,64,896]{2,1,0:T(8,128)(2,1)}, bf16[4,64,896]{2,1,0:T(8,128)(2,1)S(1)}, u32[]{:S(2)}, u32[]{:S(2)}) collective-permute-start(bf16[4,64,896]{2,1,0:T(8,128)(2,1)} %get-tuple-element.25), channel_id=1, source_target_pairs={{0,3},{1,0},{2,1},{3,2},{4,7},{5,4},{6,5},{7,6},{8,11},{9,8},{10,9... | collective-permute-start | bytes 1376264 | tf_op jit(solution)/shard_map/ppermute | solution.py:18
  30.3 18.0 %collective-permute-start.9 = (f32[16,128]{1,0:T(8,128)S(1)}, f32[16,128]{1,0:T(8,128)S(1)}, u32[]{:S(2)}, u32[]{:S(2)}) collective-permute-start(f32[16,128]{1,0:T(8,128)S(1)} %pad_maximum_fusion.2), channel_id=1, source_target_pairs={{0,3},{1,0},{2,1},{3,2},{4,7},{5,4},{6,5},{7,6},{8,11},{9,8},{10,9... | collective-permute-start | bytes 24584 | tf_op jit(solution)/shard_map/ppermute | solution.py:18
  30.3 22.8 %collective-permute-start.7 = (f32[16,128]{1,0:T(8,128)S(1)}, f32[16,128]{1,0:T(8,128)S(1)}, u32[]{:S(2)}, u32[]{:S(2)}) collective-permute-start(f32[16,128]{1,0:T(8,128)S(1)} %pad_maximum_fusion.2), channel_id=1, source_target_pairs={{0,1},{1,2},{2,3},{3,0},{4,5},{5,6},{6,7},{7,4},{8,9},{9,10},{10,1... | collective-permute-start | bytes 24584 | tf_op jit(solution)/shard_map/ppermute | solution.py:18
  48.2 5.2 %collective-permute-start.8 = (f32[16,128]{1,0:T(8,128)S(1)}, f32[16,128]{1,0:T(8,128)S(1)}, u32[]{:S(2)}, u32[]{:S(2)}) collective-permute-start(f32[16,128]{1,0:T(8,128)S(1)} %pad_maximum_fusion.2), channel_id=1, source_target_pairs={{0,2},{1,3},{2,0},{3,1},{4,6},{5,7},{6,4},{7,5},{8,10},{9,11},{10,... | collective-permute-start | bytes 24584 | tf_op jit(solution)/shard_map/ppermute | solution.py:18
  53.4 0.8 copy-start.4
  54.2 1.0 copy-start.5
  55.9 59.8 %copy-start.3 = (bf16[4,256,896]{2,1,0:T(8,128)(2,1)}, bf16[4,256,896]{2,1,0:T(8,128)(2,1)S(1)}, u32[]{:S(2)}) copy-start(bf16[4,256,896]{2,1,0:T(8,128)(2,1)S(1)} %shard_map.57.refs_4_.refs_6_) | copy-start | bytes 5505028
  55.9 51.8 %all-to-all-start.1 = ((bf16[16,32,1024]{2,1,0:T(8,128)(2,1)}), bf16[16,32,1024]{2,1,0:T(8,128)(2,1)S(1)}, u32[]{:S(2)}, u32[]{:S(2)}) async-start(bf16[16,32,1024]{2,1,0:T(8,128)(2,1)} %shard_map.58), calls=%async_computation.1 | async-start | bytes 2097152 | tf_op jit(solution)/shard_map/all_to_all | solution.py:232
  62.9 42.4 %collective-permute-start.5 = (bf16[4,256,896]{2,1,0:T(8,128)(2,1)S(1)}, bf16[4,256,896]{2,1,0:T(8,128)(2,1)}, u32[]{:S(2)}, u32[]{:S(2)}) collective-permute-start(bf16[4,256,896]{2,1,0:T(8,128)(2,1)S(1)} %shard_map.57.refs_4_.refs_6_), channel_id=1, source_target_pairs={{0,4},{4,8},{8,12},{12,0},{1,5},{5,9},{9,13},{13,1},{2,6},{6,10},{... | collective-permute-start | bytes 5505032 | tf_op jit(solution)/shard_map/ppermute | solution.py:18
  64.5 42.0 %collective-permute-start.6 = (bf16[4,256,896]{2,1,0:T(8,128)(2,1)S(1)}, bf16[4,256,896]{2,1,0:T(8,128)(2,1)S(1)}, u32[]{:S(2)}, u32[]{:S(2)}) collective-permute-start(bf16[4,256,896]{2,1,0:T(8,128)(2,1)S(1)} %shard_map.57.refs_4_.refs_6_), channel_id=1, source_target_pairs={{0,12},{4,0},{8,4},{12,8},{1,13},{5,1},{9,5},{13,9},{2,14},{6,2},{... | collective-permute-start | bytes 5505032 | tf_op jit(solution)/shard_map/ppermute | solution.py:18
  65.0 41.4 %collective-permute-start = (bf16[16,32,1024]{2,1,0:T(8,128)(2,1)}, bf16[16,32,1024]{2,1,0:T(8,128)(2,1)}, u32[]{:S(2)}, u32[]{:S(2)}) collective-permute-start(bf16[16,32,1024]{2,1,0:T(8,128)(2,1)} %all-to-all-done.refs_0_), channel_id=1, source_target_pairs={{0,1},{1,2},{2,3},{3,0},{4,5},{5,6},{6,7},{7,4},{8,9},{9,10},{10,1... | collective-permute-start | bytes 3145736 | tf_op jit(solution)/shard_map/ppermute | solution.py:18
  66.7 41.0 %collective-permute-start.1 = (bf16[16,32,1024]{2,1,0:T(8,128)(2,1)}, bf16[16,32,1024]{2,1,0:T(8,128)(2,1)}, u32[]{:S(2)}, u32[]{:S(2)}) collective-permute-start(bf16[16,32,1024]{2,1,0:T(8,128)(2,1)} %all-to-all-done.refs_0_), channel_id=1, source_target_pairs={{0,3},{1,0},{2,1},{3,2},{4,7},{5,4},{6,5},{7,6},{8,11},{9,8},{10,9... | collective-permute-start | bytes 3145736 | tf_op jit(solution)/shard_map/ppermute | solution.py:18
  106.4 1.3 copy-start.8
  107.7 6.9 %copy-start.9 = (bf16[4,256,896]{2,1,0:T(8,128)(2,1)S(1)}, bf16[4,256,896]{2,1,0:T(8,128)(2,1)}, u32[]{:S(2)}) copy-start(bf16[4,256,896]{2,1,0:T(8,128)(2,1)} %copy-done.8) | copy-start | bytes 5505028
  107.8 27.0 %collective-permute-start.10 = (bf16[16,32,1024]{2,1,0:T(8,128)(2,1)S(1)}, bf16[16,32,1024]{2,1,0:T(8,128)(2,1)}, u32[]{:S(2)}, u32[]{:S(2)}) collective-permute-start(bf16[16,32,1024]{2,1,0:T(8,128)(2,1)S(1)} %all-to-all-done.1.refs_2_), channel_id=1, source_target_pairs={{0,1},{1,2},{2,3},{3,0},{4,5},{5,6},{6,7},{7,4},{8,9},{9,10},{10,1... | collective-permute-start | bytes 3145736 | tf_op jit(solution)/shard_map/ppermute | solution.py:18
  109.7 29.0 %collective-permute-start.16 = (bf16[16,32,1024]{2,1,0:T(8,128)(2,1)S(1)}, bf16[16,32,1024]{2,1,0:T(8,128)(2,1)}, u32[]{:S(2)}, u32[]{:S(2)}) collective-permute-start(bf16[16,32,1024]{2,1,0:T(8,128)(2,1)S(1)} %all-to-all-done.1.refs_2_), channel_id=1, source_target_pairs={{0,3},{1,0},{2,1},{3,2},{4,7},{5,4},{6,5},{7,6},{8,11},{9,8},{10,9... | collective-permute-start | bytes 3145736 | tf_op jit(solution)/shard_map/ppermute | solution.py:18
  113.4 27.2 %collective-permute-start.11 = (bf16[2,256,896]{2,1,0:T(8,128)(2,1)}, bf16[2,256,896]{2,1,0:T(8,128)(2,1)}, u32[]{:S(2)}, u32[]{:S(2)}) collective-permute-start(bf16[2,256,896]{2,1,0:T(8,128)(2,1)} %slice.40), channel_id=1, source_target_pairs={{0,4},{4,8},{8,12},{12,0},{1,5},{5,9},{9,13},{13,1},{2,6},{6,10},{... | collective-permute-start | bytes 2752520 | tf_op jit(solution)/shard_map/ppermute | solution.py:18
  115.7 28.7 %collective-permute-start.12 = (bf16[2,256,896]{2,1,0:T(8,128)(2,1)}, bf16[2,256,896]{2,1,0:T(8,128)(2,1)}, u32[]{:S(2)}, u32[]{:S(2)}) collective-permute-start(bf16[2,256,896]{2,1,0:T(8,128)(2,1)} %slice.41), channel_id=1, source_target_pairs={{0,12},{4,0},{8,4},{12,8},{1,13},{5,1},{9,5},{13,9},{2,14},{6,2},{... | collective-permute-start | bytes 2752520 | tf_op jit(solution)/shard_map/ppermute | solution.py:18
  117.1 26.8 %all-to-all-start.2 = ((f32[16,4,128]{2,1,0:T(4,128)}), f32[16,4,128]{2,1,0:T(4,128)S(1)}, u32[]{:S(2)}, u32[]{:S(2)}) async-start(f32[16,4,128]{2,1,0:T(4,128)} %copy.44), calls=%async_computation.2 | async-start | bytes 65536 | tf_op jit(solution)/shard_map/all_to_all | solution.py:243
  124.1 110.4 %reduce-scatter.2.cloned.1.call-start = ((), (), s32[]{:S(2)}) async-start(), calls=%async_computation.4 | async-start | bytes 4128768 | tf_op jit(solution)/shard_map/reduce_scatter | solution.py:256
  127.9 33.5 %collective-permute-start.14 = (bf16[8,32,1024]{2,1,0:T(8,128)(2,1)}, bf16[8,32,1024]{2,1,0:T(8,128)(2,1)S(1)}, u32[]{:S(2)}, u32[]{:S(2)}) collective-permute-start(bf16[8,32,1024]{2,1,0:T(8,128)(2,1)} %slice.44), channel_id=1, source_target_pairs={{0,1},{1,2},{2,3},{3,0},{4,5},{5,6},{6,7},{7,4},{8,9},{9,10},{10,1... | collective-permute-start | bytes 1572872 | tf_op jit(solution)/shard_map/ppermute | solution.py:18
  134.7 26.6 %collective-permute-start.15 = (bf16[8,32,1024]{2,1,0:T(8,128)(2,1)}, bf16[8,32,1024]{2,1,0:T(8,128)(2,1)S(1)}, u32[]{:S(2)}, u32[]{:S(2)}) collective-permute-start(bf16[8,32,1024]{2,1,0:T(8,128)(2,1)} %slice.45), channel_id=1, source_target_pairs={{0,3},{1,0},{2,1},{3,2},{4,7},{5,4},{6,5},{7,6},{8,11},{9,8},{10,9... | collective-permute-start | bytes 1572872 | tf_op jit(solution)/shard_map/ppermute | solution.py:18
  138.7 22.6 %collective-permute-start.17 = (bf16[8,32,1024]{2,1,0:T(8,128)(2,1)}, bf16[8,32,1024]{2,1,0:T(8,128)(2,1)S(1)}, u32[]{:S(2)}, u32[]{:S(2)}) collective-permute-start(bf16[8,32,1024]{2,1,0:T(8,128)(2,1)} %slice.54), channel_id=1, source_target_pairs={{0,1},{1,2},{2,3},{3,0},{4,5},{5,6},{6,7},{7,4},{8,9},{9,10},{10,1... | collective-permute-start | bytes 1572872 | tf_op jit(solution)/shard_map/ppermute | solution.py:18
  140.6 20.7 %collective-permute-start.18 = (bf16[8,32,1024]{2,1,0:T(8,128)(2,1)}, bf16[8,32,1024]{2,1,0:T(8,128)(2,1)}, u32[]{:S(2)}, u32[]{:S(2)}) collective-permute-start(bf16[8,32,1024]{2,1,0:T(8,128)(2,1)} %slice.55), channel_id=1, source_target_pairs={{0,3},{1,0},{2,1},{3,2},{4,7},{5,4},{6,5},{7,6},{8,11},{9,8},{10,9... | collective-permute-start | bytes 1572872 | tf_op jit(solution)/shard_map/ppermute | solution.py:18
  161.3 17.7 %collective-permute-start.13 = (bf16[8,2,64,896]{3,2,1,0:T(8,128)(2,1)}, bf16[8,2,64,896]{3,2,1,0:T(8,128)(2,1)}, u32[]{:S(2)}, u32[]{:S(2)}) collective-permute-start(bf16[8,2,64,896]{3,2,1,0:T(8,128)(2,1)} %get-tuple-element.34), channel_id=1, source_target_pairs={{0,64},{64,0},{1,65},{65,1},{2,66},{66,2},{3,67},{67,3},{4,68},{68... | collective-permute-start | bytes 5505032 | tf_op jit(solution)/shard_map/ppermute | solution.py:18
  161.4 17.6 %copy-start.6 = (f32[8,2,64,896]{3,2,1,0:T(8,128)S(1)}, f32[8,2,64,896]{3,2,1,0:T(8,128)}, u32[]{:S(2)}) copy-start(f32[8,2,64,896]{3,2,1,0:T(8,128)} %get-tuple-element.33) | copy-start | bytes 11010052
  178.3 4.3 %collective-permute-start.19 = (bf16[8,2,64,896]{3,2,1,0:T(8,128)(2,1)}, bf16[8,2,64,896]{3,2,1,0:T(8,128)(2,1)S(1)}, u32[]{:S(2)}, u32[]{:S(2)}) collective-permute-start(bf16[8,2,64,896]{3,2,1,0:T(8,128)(2,1)} %get-tuple-element.36), channel_id=1, source_target_pairs={{0,64},{64,0},{1,65},{65,1},{2,66},{66,2},{3,67},{67,3},{4,68},{68... | collective-permute-start | bytes 5505032 | tf_op jit(solution)/shard_map/ppermute | solution.py:18
  179.0 3.6 %copy-start.7 = (f32[8,2,64,896]{3,2,1,0:T(8,128)S(1)}, f32[8,2,64,896]{3,2,1,0:T(8,128)}, u32[]{:S(2)}) copy-start(f32[8,2,64,896]{3,2,1,0:T(8,128)} %get-tuple-element.35) | copy-start | bytes 11010052
  235.6 7.8 %collective-permute-start.20 = (bf16[64,896]{1,0:T(8,128)(2,1)S(1)}, bf16[64,896]{1,0:T(8,128)(2,1)S(1)}, u32[]{:S(2)}, u32[]{:S(2)}) collective-permute-start(bf16[64,896]{1,0:T(8,128)(2,1)S(1)} %get-tuple-element.39), channel_id=1, source_target_pairs={{0,3},{1,0},{2,1},{3,2},{4,7},{5,4},{6,5},{7,6},{8,11},{9,8},{10,9... | collective-permute-start | bytes 344072 | tf_op jit(solution)/shard_map/ppermute | solution.py:18
  238.4 7.4 %collective-permute-start.21 = (bf16[64,896]{1,0:T(8,128)(2,1)S(1)}, bf16[64,896]{1,0:T(8,128)(2,1)S(1)}, u32[]{:S(2)}, u32[]{:S(2)}) collective-permute-start(bf16[64,896]{1,0:T(8,128)(2,1)S(1)} %get-tuple-element.38), channel_id=1, source_target_pairs={{0,2},{1,3},{2,0},{3,1},{4,6},{5,7},{6,4},{7,5},{8,10},{9,11},{10,... | collective-permute-start | bytes 344072 | tf_op jit(solution)/shard_map/ppermute | solution.py:18
  239.2 7.8 %collective-permute-start.22 = (bf16[64,896]{1,0:T(8,128)(2,1)S(1)}, bf16[64,896]{1,0:T(8,128)(2,1)S(1)}, u32[]{:S(2)}, u32[]{:S(2)}) collective-permute-start(bf16[64,896]{1,0:T(8,128)(2,1)S(1)} %get-tuple-element.37), channel_id=1, source_target_pairs={{0,1},{1,2},{2,3},{3,0},{4,5},{5,6},{6,7},{7,4},{8,9},{9,10},{10,1... | collective-permute-start | bytes 344072 | tf_op jit(solution)/shard_map/ppermute | solution.py:18
Sparse Core Ops, SparseCore 0:
  185.4 49.0 reduce-scatter.1

commit v4 on v3

--- a/solution.py
+++ b/solution.py
@@ -80,36 +80,32 @@
     )(jnp.full((1,), first, jnp.int32), flat, hidden)
 
 
-def experts_kernel(steps, counts, pos_ref, *refs):
-    half = sum(counts)
-    x_refs, w_refs = (refs[:half], refs[half:2 * half]), refs[2 * half:2 * half + 5]
-    gate_ref, row_ref, mine_ref, other_ref, x_ref, p_ref = refs[2 * half + 5:]
-    turn, k = pl.program_id(0), pl.program_id(1)
-    capacity, hidden_width = x_refs[0][0].shape[-2:]
-    experts = pl.num_programs(1)
+def experts_kernel(steps, pos_ref, *refs):
+    turns = len(steps)
+    x_refs = refs[:turns], refs[turns:2 * turns]
+    w_ref, gate_ref, row_ref, mine_ref, other_ref, p_ref = refs[2 * turns:]
+    k, turn = pl.program_id(0), pl.program_id(1)
+    groups, capacity, hidden_width = x_refs[0][0].shape
+    experts = pl.num_programs(0)
     slots = capacity * experts
-    depth, width = w_refs[0].shape[1:]
+    width = w_ref.shape[3]
     planes, _, rows, _ = mine_ref.shape
-    c, x = pos_ref[1], pos_ref[3]
-    first = 0
-    for number, count in enumerate(counts):
+    c = pos_ref[1]
+    for number in range(turns):
         for part in range(2):
             @pl.when((turn == number) & (k // 2 == part))
-            def _(first=first, count=count, part=part):
-                for d in range(4):
-                    start = pl.multiple_of(lax.rem(x + 4 - d, 4) * depth, 128)
-                    block = [r[:, :, pl.ds(start, depth)].reshape(-1, depth) for r in x_refs[part][first:first + count]]
-                    x_ref[:, d * depth:(d + 1) * depth] = jnp.concatenate(block, 0)
-        first += count
-    opposite = jnp.where(k < 2, w_refs[2][0], w_refs[3][0])
-    weights = jnp.concatenate([w_refs[0][0], w_refs[1][0], opposite, w_refs[4][0]], 0)
-    total = jnp.dot(x_ref[...], weights, preferred_element_type=jnp.float32)
-    high = total.astype(jnp.bfloat16)
-    low = (total - high.astype(jnp.float32)).astype(jnp.bfloat16)
-    high, low = (v.reshape(-1, capacity, width) for v in (high, low))
-    for part, value in enumerate((high, high, low)):
-        start = pl.multiple_of(part * slots + k * capacity, capacity)
-        p_ref[:, pl.ds(start, capacity), :] = value
+            def _(number=number, part=part):
+                total = jnp.dot(
+                    x_refs[part][number][...].reshape(groups * capacity, hidden_width),
+                    w_ref[...].reshape(hidden_width, width),
+                    preferred_element_type=jnp.float32,
+                )
+                high = total.astype(jnp.bfloat16)
+                low = (total - high.astype(jnp.float32)).astype(jnp.bfloat16)
+                high, low = (v.reshape(groups, capacity, width) for v in (high, low))
+                for block, value in enumerate((high, high, low)):
+                    start = pl.multiple_of(block * slots + k * capacity, capacity)
+                    p_ref[number, :, pl.ds(start, capacity), :] = value
 
     @pl.when(k == experts - 1)
     def _():
@@ -125,47 +121,40 @@
                 gate_high = gate.astype(jnp.bfloat16).astype(jnp.float32)
                 value = jnp.where(middle, gate - gate_high, gate_high)
                 combine = jnp.where(number == row_ref[pl.ds(index, 1), :], value, 0.0).astype(jnp.bfloat16)
-                mixed = jnp.dot(combine, p_ref[source], preferred_element_type=jnp.float32)
+                mixed = jnp.dot(combine, p_ref[turn, source], preferred_element_type=jnp.float32)
                 out_ref[plane, 0] = mixed.astype(out_ref.dtype)
 
 
-def experts_call(steps, pos, xs, ws, gate, row, rows):
-    experts, depth, width = ws[0].shape
+def experts_call(steps, pos, xs, weight, gate, row, rows):
+    blocks, experts, depth, width = weight.shape
     half = experts // 2
-    hidden_width = xs[0][0][0].shape[2]
-    capacity = xs[0][0][0].shape[1] // half
-    groups = sum(v.shape[0] for v in xs[0][0])
+    groups, slots, hidden_width = xs[0][0].shape
+    capacity = slots // half
     turns = len(steps)
     mine = jax.ShapeDtypeStruct((groups // 2, turns, rows, width), jnp.float32)
     other = jax.ShapeDtypeStruct((groups // 2, turns, rows, width), jnp.bfloat16)
     arrays, specs = [], []
     for part in range(2):
         for turn in range(turns):
-            for v in xs[turn][part]:
-                def index(t, k, part=part, turn=turn):
-                    now = jnp.clip(k - part * half, 0, half - 1)
-                    return 0, jnp.where(t == turn, now, jnp.where(t < turn, 0, half - 1)), 0
-
-                arrays.append(v)
-                specs.append(pl.BlockSpec((v.shape[0], capacity, hidden_width), index))
-    kinds = [lambda k: k, lambda k: k, lambda k: jnp.minimum(k, half - 1), lambda k: jnp.maximum(k - half, 0), lambda k: k]
-    w_specs = [pl.BlockSpec((1, depth, width), lambda t, k, f=f: (f(k), 0, 0)) for f in kinds]
-    whole = pl.BlockSpec((groups // 2, 1, rows, width), lambda t, k: (0, t, 0, 0))
-    info = pl.BlockSpec(gate.shape, lambda t, k: (0, 0))
+            def index(k, t, part=part, turn=turn):
+                now = jnp.where(t > turn, k + 1, k) if turn < turns - 1 else k
+                return 0, jnp.clip(now - part * half, 0, half - 1), 0
+
+            arrays.append(xs[turn][part])
+            specs.append(pl.BlockSpec((groups, capacity, hidden_width), index))
+    whole = pl.BlockSpec((groups // 2, 1, rows, width), lambda k, t: (0, jnp.where(k == experts - 1, t, 0), 0, 0))
+    info = pl.BlockSpec(gate.shape, lambda k, t: (0, 0))
     flops = 2 * turns * groups * capacity * experts * hidden_width * width
     return pl.pallas_call(
-        functools.partial(experts_kernel, steps, [len(v[0]) for v in xs]),
-        grid=(turns, experts),
+        functools.partial(experts_kernel, steps),
+        grid=(experts, turns),
         out_shape=[mine, other],
-        in_specs=[SMEM] + specs + w_specs + [info] * 2,
+        in_specs=[SMEM] + specs + [pl.BlockSpec((blocks, 1, depth, width), lambda k, t: (0, k, 0, 0))] + [info] * 2,
         out_specs=[whole] * 2,
-        scratch_shapes=[
-            pltpu.VMEM((groups * capacity, hidden_width), jnp.bfloat16),
-            pltpu.VMEM((groups, 3 * experts * capacity, width), jnp.bfloat16),
-        ],
+        scratch_shapes=[pltpu.VMEM((turns, groups, 3 * experts * capacity, width), jnp.bfloat16)],
         compiler_params=PARAMS,
-        cost_estimate=cost(flops, *arrays, *ws, *ws, mine, other),
-    )(pos, *arrays, *ws, gate, row)
+        cost_estimate=cost(flops, *arrays, weight, mine, other),
+    )(pos, *arrays, weight, gate, row)
 
 
 def place_kernel(pos_ref, *refs):
@@ -211,6 +200,7 @@
     group_axes = Z + ("c",)
 
     blocks = split_blocks(pos, own, ny)
+    flat = after(flat, blocks[1])
     blocks = [blocks[0]] + [shifted(blocks[d], "y", d) for d in range(1, ny)]
 
     outbound = dispatch(0, flat, pairs, groups, slots // 2)
@@ -222,39 +212,33 @@
     slot_gate = jnp.sum(jnp.where(chosen, gates.reshape(-1)[None, :], 0.0), axis=1).reshape(groups, slots)
     slot_row = jnp.sum(jnp.where(chosen, pair_row[None, :] + 1, 0), axis=1).reshape(groups, slots) - 1
     info = jnp.concatenate([slot_gate, slot_row.astype(jnp.float32)], 1)
-    info = jnp.stack([info] + [shifted(info, "y", d) for d in range(1, ny)], 1)
-
-    weight = join_blocks(pos, blocks)
-    weight_up, weight_down = shifted(weight, "x", 1), shifted(weight, "x", -1)
+    info = [info] + [shifted(info, "y", d) for d in range(1, ny)]
+
+    joined = join_blocks(pos, blocks)
+    weight = lax.all_gather(joined, "x")
 
     first_up, first_down = shifted(first, "y", 1), shifted(first, "y", -1)
     outbound = dispatch(slots // 2, flat, pairs, groups, slots // 2)
-    second = lax.all_to_all(after(outbound, first, weight, info), group_axes, 0, 0, tiled=True)
-    middle = groups // 2
-    first_up, first_down, weight_up, weight_down = lax.optimization_barrier(
-        (first_up, first_down, weight_up, weight_down)
-    )
-    first_opposite = [shifted(first_up[:middle], "y", 1), shifted(first_down[middle:], "y", -1)]
-    half = exp_train // 2
-    weight_opposite = [shifted(weight_up[:half], "x", 1), shifted(weight_down[half:], "x", -1)]
-    weights = [weight, weight_up, *weight_opposite, weight_down]
-    second_late = after(second, first_up, first_down, weight_up, weight_down)
+    second = lax.all_to_all(after(outbound, first, joined, *info[1:]), group_axes, 0, 0, tiled=True)
+    first_opposite = shifted(first_up, "y", 1)
+    second_late = after(second, first_up, first_down)
     second_up, second_down = shifted(second_late, "y", 1), shifted(second_late, "y", -1)
-    info = lax.all_to_all(after(info, second), group_axes, 0, 0, tiled=True).reshape(groups * ny, 2 * slots)
+    second_opposite = shifted(second_down, "y", -1)
+    info = after(jnp.stack(info, 1), second)
+    info = lax.all_to_all(info, group_axes, 0, 0, tiled=True).reshape(groups * ny, 2 * slots)
     gate = jnp.tile(info[:, :slots], (1, 3))
     row = jnp.tile(info[:, slots:], (1, 3))
-    second_opposite = [shifted(second_up[:middle], "y", 1), shifted(second_down[middle:], "y", -1)]
 
     partials = []
-    own_rows, up_rows = ([first], [second]), ([first_up], [second_up])
-    down_rows, opposite_rows = ([first_down], [second_down]), (first_opposite, second_opposite)
-    for steps, xs in (((0, 1), (own_rows, up_rows)), ((ny - 1, 2), (down_rows, opposite_rows))):
-        mine, other = experts_call(steps, pos, xs, weights, gate, row, rows)
+    own_rows, up_rows = (first, second), (first_up, second_up)
+    down_rows, opposite_rows = (first_down, second_down), (first_opposite, second_opposite)
+    for steps, xs in (((0, ny - 1), (own_rows, down_rows)), ((1, 2), (up_rows, opposite_rows))):
+        mine, other = experts_call(steps, pos, xs, weight, gate, row, rows)
         other = shifted(other, "c", 1)
         partials.append((mine + other.astype(jnp.float32)).astype(jnp.bfloat16))
     partial = jnp.concatenate(partials, 1).reshape(-1, block_width)
     summed = lax.psum_scatter(partial, Z, scatter_dimension=0, tiled=True).reshape(ny, rows, block_width)
-    final = [summed[0], shifted(summed[1], "y", -1), shifted(summed[3], "y", 2), shifted(summed[2], "y", 1)]
+    final = [summed[0], shifted(summed[2], "y", -1), shifted(summed[3], "y", 2), shifted(summed[1], "y", 1)]
     return place_blocks(pos, final)
 
 

time: 257 us -> 253 us (0.984)
  starting transfers between devices: 55.6 us -> 39.1 us
  waiting for transfers between devices: 118 us -> 133 us
  blocking collectives: 0 us -> 13.8 us
  local copies, waits for them, and re-layouts: 19.3 us -> 7.32 us
    all_to_all x1, waiting for transfers between devices: 0.01 us -> 18.4 us  [per_device(): first = lax.all_to_all(outbound, group_axes, 0, 0, tiled=True)]
    all_to_all x0 -> x1, blocking collectives: none -> 13.8 us  [per_device(): lax.all_to_all(info, group_axes, 0, 0, tiled=True)]
    slice x7 -> x1, local copies, waits for them, and re-layouts: 11.8 us -> 1.1 us  [per_device(): summed[1]]
    all_to_all x2 -> x1, starting transfers between devices: 13.9 us -> 4.79 us  [per_device(): lax.all_to_all(after(outbound, first, joined, *info[1:]), group_axes, 0,...]
    ppermute x23 -> x17, starting transfers between devices: 32.9 us -> 25.7 us  [shifted(): lax.ppermute(value, axis, [(i, (i + steps) % count) for i in range(count)])]
    reduce_scatter x1, waiting for transfers between devices: 49.2 us -> 44.5 us  [per_device(): lax.psum_scatter(partial, Z, scatter_dimension=0, tiled=True)]
    pallas_call x2, Pallas kernels: 33.9 us -> 30.6 us  [experts_call(): pl.pallas_call(functools.partial(experts_kernel, steps), grid=(experts, t...]
    ppermute x23 -> x17, waiting for transfers between devices: 69.2 us -> 70.2 us  [shifted(): lax.ppermute(value, axis, [(i, (i + steps) % count) for i in range(count)])]
  transfers between devices with their start and end apart: 27 -> 21, of which waited for: 10 -> 11; matrix products, arithmetic and copies ran while one was open for 6% -> 2% of each run, Pallas kernels for 15% -> 14%
where the time goes in v4:
time: 253 us; the launch traced here: 251 us
  waiting for transfers between devices  133 us (53%)
  starting transfers between devices  39.1 us (15%)
  Pallas kernels  38.9 us (15%)
  blocking collectives  13.8 us (5%)
  between operations  13.6 us (5%)
  local copies, waits for them, and re-layouts  7.32 us (3%)
  other arithmetic  5.44 us (2%)
    ppermute x17, waiting for transfers between devices, shifted(): lax.ppermute(value, axis, [(i, (i + steps) % count) for i in range(count)])  70.2 us
    reduce_scatter x1, waiting for transfers between devices, per_device(): lax.psum_scatter(partial, Z, scatter_dimension=0, tiled=True)  44.5 us
    pallas_call x2, Pallas kernels, experts_call(): pl.pallas_call(functools.partial(experts_kernel, steps), grid=(experts, t...  30.6 us
    ppermute x17, starting transfers between devices, shifted(): lax.ppermute(value, axis, [(i, (i + steps) % count) for i in range(count)])  25.7 us
    all_to_all x1, waiting for transfers between devices, per_device(): first = lax.all_to_all(outbound, group_axes, 0, 0, tiled=True)  18.4 us
    all_to_all x1, blocking collectives, per_device(): lax.all_to_all(info, group_axes, 0, 0, tiled=True)  13.8 us
    all_to_all x1, starting transfers between devices, per_device(): first = lax.all_to_all(outbound, group_axes, 0, 0, tiled=True)  8.58 us
  transfers between devices with their start and end apart: 21, of which 11 were waited for; matrix products, arithmetic and copies ran while one was open for 2% of the time, Pallas kernels for 14%

profile of v4, /device:TPU:2, one launch (start us, length us, event | category | flops | bytes accessed | tf_op | source)
XLA Modules:
  0.0 251.4 jit_solution(11564792660551545048)
XLA Ops:
  6.5 0.1 pad_add_fusion.pos_ref
  6.6 1.6 copy-done.1
  8.2 1.6 shard_map.55
  9.8 1.6 collective-permute-start.1
  11.4 2.9 %collective-permute-start.2 = (bf16[4,64,896]{2,1,0:T(8,128)(2,1)}, bf16[4,64,896]{2,1,0:T(8,128)(2,1)S(1)}, u32[]{:S(2)}, u32[]{:S(2)}) collective-permute-start(bf16[4,64,896]{2,1,0:T(8,128)(2,1)} %get-tuple-element.22), channel_id=1, source_target_pairs={{0,2},{1,3},{2,0},{3,1},{4,6},{5,7},{6,4},{7,5},{8,10},{9,11},{10,... | collective-permute-start | bytes 1376264 | tf_op jit(solution)/shard_map/ppermute | solution.py:18
  14.3 1.3 collective-permute-start.3
  15.6 0.8 copy.41
  16.4 0.7 reshape.83
  17.1 0.1 eq.31
  17.2 0.2 compare_reduce_fusion
  17.5 0.1 reduce_window_sum.11
  17.6 1.2 fusion
  18.8 0.1 reshape.84.flat_ref
  18.9 1.7 shard_map.56
  20.6 2.9 %collective-permute-done.1.refs_1_ = bf16[4,64,896]{2,1,0:T(8,128)(2,1)S(1)} collective-permute-done((bf16[4,64,896]{2,1,0:T(8,128)(2,1)}, bf16[4,64,896]{2,1,0:T(8,128)(2,1)S(1)}, u32[]{:S(2)}, u32[]{:S(2)}) %collective-permute-start.1) | collective-permute-done | bytes 458784 | tf_op jit(solution)/shard_map/ppermute | solution.py:18
  23.5 11.0 %collective-permute-done.2.refs_2_ = bf16[4,64,896]{2,1,0:T(8,128)(2,1)S(1)} collective-permute-done((bf16[4,64,896]{2,1,0:T(8,128)(2,1)}, bf16[4,64,896]{2,1,0:T(8,128)(2,1)S(1)}, u32[]{:S(2)}, u32[]{:S(2)}) %collective-permute-start.2) | collective-permute-done | bytes 458784 | tf_op jit(solution)/shard_map/ppermute | solution.py:18
  34.6 2.0 shard_map.58
  36.6 8.6 %all-to-all-start = ((bf16[16,32,1024]{2,1,0:T(8,128)(2,1)}), bf16[16,32,1024]{2,1,0:T(8,128)(2,1)S(1)}, u32[]{:S(2)}, u32[]{:S(2)}) async-start(bf16[16,32,1024]{2,1,0:T(8,128)(2,1)} %shard_map.56), calls=%async_computation | async-start | bytes 2097152 | tf_op jit(solution)/shard_map/all_to_all | solution.py:208
  45.2 0.1 copy.43
  45.2 0.1 broadcast_in_dim.45
  45.3 0.3 select_reduce_fusion.1
  45.6 0.1 reshape.86
  45.7 0.3 select_reduce_fusion
  46.0 0.1 convert_element_type.27
  46.1 0.1 pad_maximum_fusion.2
  46.2 0.9 collective-permute-start.4
  47.1 2.6 %collective-permute-start.5 = (f32[16,128]{1,0:T(8,128)S(1)}, f32[16,128]{1,0:T(8,128)S(1)}, u32[]{:S(2)}, u32[]{:S(2)}) collective-permute-start(f32[16,128]{1,0:T(8,128)S(1)} %pad_maximum_fusion.2), channel_id=1, source_target_pairs={{0,2},{1,3},{2,0},{3,1},{4,6},{5,7},{6,4},{7,5},{8,10},{9,11},{10,... | collective-permute-start | bytes 24584 | tf_op jit(solution)/shard_map/ppermute | solution.py:18
  49.7 1.7 collective-permute-start.6
  51.4 1.7 shard_map.57
  53.1 0.3 collective-permute-done.6
  53.4 18.4 %all-to-all-done.refs_0_ = bf16[16,32,1024]{2,1,0:T(8,128)(2,1)S(1)} async-done(((bf16[16,32,1024]{2,1,0:T(8,128)(2,1)}), bf16[16,32,1024]{2,1,0:T(8,128)(2,1)S(1)}, u32[]{:S(2)}, u32[]{:S(2)}) %all-to-all-start) | async-done | bytes 1048608 | tf_op jit(solution)/shard_map/all_to_all | solution.py:208
  71.8 4.8 %all-to-all-start.1 = ((bf16[16,32,1024]{2,1,0:T(8,128)(2,1)}), bf16[16,32,1024]{2,1,0:T(8,128)(2,1)S(1)}, u32[]{:S(2)}, u32[]{:S(2)}) async-start(bf16[16,32,1024]{2,1,0:T(8,128)(2,1)} %shard_map.57), calls=%async_computation.1 | async-start | bytes 2097152 | tf_op jit(solution)/shard_map/all_to_all | solution.py:222
  76.7 1.0 collective-permute-start.7
  77.7 2.3 collective-permute-start
  80.0 23.5 %collective-permute-done.7.refs_0_ = bf16[16,32,1024]{2,1,0:T(8,128)(2,1)S(1)} collective-permute-done((bf16[16,32,1024]{2,1,0:T(8,128)(2,1)S(1)}, bf16[16,32,1024]{2,1,0:T(8,128)(2,1)S(1)}, u32[]{:S(2)}, u32[]{:S(2)}) %collective-permute-start.7) | collective-permute-done | bytes 1048608 | tf_op jit(solution)/shard_map/ppermute | solution.py:18
  103.5 1.0 copy-done.2
  104.4 3.0 %collective-permute-start.8 = (bf16[16,32,1024]{2,1,0:T(8,128)(2,1)S(1)}, bf16[16,32,1024]{2,1,0:T(8,128)(2,1)}, u32[]{:S(2)}, u32[]{:S(2)}) collective-permute-start(bf16[16,32,1024]{2,1,0:T(8,128)(2,1)S(1)} %all-to-all-done.1.refs_2_), channel_id=1, source_target_pairs={{0,3},{1,0},{2,1},{3,2},{4,7},{5,4},{6,5},{7,6},{8,11},{9,8},{10,9... | collective-permute-start | bytes 3145736 | tf_op jit(solution)/shard_map/ppermute | solution.py:18
  107.4 0.1 collective-permute-start.11
  107.5 22.6 %collective-permute-done.8.refs_3_ = bf16[16,32,1024]{2,1,0:T(8,128)(2,1)} collective-permute-done((bf16[16,32,1024]{2,1,0:T(8,128)(2,1)S(1)}, bf16[16,32,1024]{2,1,0:T(8,128)(2,1)}, u32[]{:S(2)}, u32[]{:S(2)}) %collective-permute-start.8) | collective-permute-done | bytes 1048608 | tf_op jit(solution)/shard_map/ppermute | solution.py:18
  130.1 3.3 %collective-permute-start.12 = (bf16[16,32,1024]{2,1,0:T(8,128)(2,1)}, bf16[16,32,1024]{2,1,0:T(8,128)(2,1)}, u32[]{:S(2)}, u32[]{:S(2)}) collective-permute-start(bf16[16,32,1024]{2,1,0:T(8,128)(2,1)} %collective-permute-done.8.refs_3_), channel_id=1, source_target_pairs={{0,3},{1,0},{2,1},{3,2},{4,7},{5,4},{6,5},{7,6},{8,11},{9,8},{10,9... | collective-permute-start | bytes 3145736 | tf_op jit(solution)/shard_map/ppermute | solution.py:18
  133.4 13.8 %all_to_all.15 = f32[16,4,128]{2,1,0:T(4,128)S(1)} all-to-all(f32[16,4,128]{2,1,0:T(4,128)S(1)} %copy.44), channel_id=1, replica_groups=mesh['zl'=2,'c'=2,'zh'=4,'x'=4,'y'=4] {'zh','zl','c'}, dimensions={0} | all-to-all | bytes 65536 | tf_op jit(solution)/shard_map/all_to_all | solution.py:228
  147.2 0.1 fusion.6
  147.3 0.1 copy.45
  147.4 0.1 copy.47.refs_5_
  147.5 0.1 copy.46
  147.5 0.1 copy.48.refs_6_
  147.7 1.2 copy-done.3
  148.9 15.0 %shard_map.59 = (f32[8,2,64,896]{3,2,1,0:T(8,128)}, bf16[8,2,64,896]{3,2,1,0:T(8,128)(2,1)S(1)}) custom-call(s32[4]{0:T(128)S(1)} %pad_add_fusion.pos_ref, bf16[16,32,1024]{2,1,0:T(8,128)(2,1)S(1)} %all-to-all-done.refs_0_, bf16[16,32,1024]{2,1,0:T(8,128)(2,1)S(1)} %copy-done.3, bf16[16,32,1024]{2,1,0:T(8,128)(2,1)S(1)} %all-to-all-done.1.refs_2_, ...), custom_call_target="tpu_custom_call" | custom-call | flops 3758096384 | bytes 17039360 | tf_op jit(solution)/shard_map/pallas_call | solution.py:148
  163.9 0.1 collective-permute-start.9
  164.0 15.6 %shard_map.60 = (f32[8,2,64,896]{3,2,1,0:T(8,128)}, bf16[8,2,64,896]{3,2,1,0:T(8,128)(2,1)S(1)}) custom-call(s32[4]{0:T(128)S(1)} %pad_add_fusion.pos_ref, bf16[16,32,1024]{2,1,0:T(8,128)(2,1)S(1)} %collective-permute-done.7.refs_0_, bf16[16,32,1024]{2,1,0:T(8,128)(2,1)} %collective-permute-done.10.refs_1_, ...), custom_call_target="tpu_custom_call" | custom-call | flops 3758096384 | bytes 17039360 | tf_op jit(solution)/shard_map/pallas_call | solution.py:148
  179.6 0.4 collective-permute-start.13
  180.0 0.5 add_convert_fusion.1
  180.5 2.9 %collective-permute-done.13 = bf16[8,2,64,896]{3,2,1,0:T(8,128)(2,1)S(1)} collective-permute-done((bf16[8,2,64,896]{3,2,1,0:T(8,128)(2,1)S(1)}, bf16[8,2,64,896]{3,2,1,0:T(8,128)(2,1)S(1)}, u32[]{:S(2)}, u32[]{:S(2)}) %collective-permute-start.13) | collective-permute-done | bytes 1835040 | tf_op jit(solution)/shard_map/ppermute | solution.py:18
  183.4 0.5 add_convert_fusion
  183.9 2.1 pad_maximum_fusion
  186.1 44.5 %reduce-scatter.2.cloned.1.call-done = bf16[256,896]{1,0:T(8,128)(2,1)} async-done(((bf16[2048,896]{1,0:T(8,128)(2,1)}), bf16[256,896]{1,0:T(8,128)(2,1)}) %reduce-scatter.2.cloned.1.call-update) | async-done | bytes 458768 | tf_op jit(solution)/shard_map/reduce_scatter | solution.py:240
  230.6 1.1 fusion.5
  231.7 2.8 %collective-permute-start.14 = (bf16[64,896]{1,0:T(8,128)(2,1)S(1)}, bf16[64,896]{1,0:T(8,128)(2,1)S(1)}, u32[]{:S(2)}, u32[]{:S(2)}) collective-permute-start(bf16[64,896]{1,0:T(8,128)(2,1)S(1)} %get-tuple-element.33), channel_id=1, source_target_pairs={{0,3},{1,0},{2,1},{3,2},{4,7},{5,4},{6,5},{7,6},{8,11},{9,8},{10,9... | collective-permute-start | bytes 344072 | tf_op jit(solution)/shard_map/ppermute | solution.py:18
  234.6 0.8 collective-permute-start.15
  235.4 0.9 collective-permute-start.16
  236.3 3.3 %collective-permute-done.14.refs_1_ = bf16[64,896]{1,0:T(8,128)(2,1)S(1)} collective-permute-done((bf16[64,896]{1,0:T(8,128)(2,1)S(1)}, bf16[64,896]{1,0:T(8,128)(2,1)S(1)}, u32[]{:S(2)}, u32[]{:S(2)}) %collective-permute-start.14) | collective-permute-done | bytes 114720 | tf_op jit(solution)/shard_map/ppermute | solution.py:18
  239.5 2.5 collective-permute-done.15.refs_2_
  242.0 1.2 collective-permute-done.16.refs_3_
  243.2 1.4 shard_map.61
  (36 shorter events, 0.2 us)
Async XLA Ops:
  6.5 12.4 %copy-start = (bf16[64,8,1024]{2,1,0:T(8,128)(2,1)S(1)}, bf16[64,8,1024]{2,1,0:T(8,128)(2,1)}, u32[]{:S(2)}) copy-start(bf16[64,8,1024]{2,1,0:T(8,128)(2,1)} %param.9) | copy-start | bytes 3145732
  6.5 141.1 %all-gather.3.cloned.1.call-start = ((), (), s32[]{:S(2)}) async-start(), calls=%async_computation.5 | async-start | bytes 9175040 | tf_op jit(solution)/shard_map/all_gather | solution.py:218
  6.6 1.6 copy-start.1
  9.8 13.7 %collective-permute-start.1 = (bf16[4,64,896]{2,1,0:T(8,128)(2,1)}, bf16[4,64,896]{2,1,0:T(8,128)(2,1)S(1)}, u32[]{:S(2)}, u32[]{:S(2)}) collective-permute-start(bf16[4,64,896]{2,1,0:T(8,128)(2,1)} %get-tuple-element.18), channel_id=1, source_target_pairs={{0,1},{1,2},{2,3},{3,0},{4,5},{5,6},{6,7},{7,4},{8,9},{9,10},{10,1... | collective-permute-start | bytes 1376264 | tf_op jit(solution)/shard_map/ppermute | solution.py:18
  11.4 23.2 %collective-permute-start.2 = (bf16[4,64,896]{2,1,0:T(8,128)(2,1)}, bf16[4,64,896]{2,1,0:T(8,128)(2,1)S(1)}, u32[]{:S(2)}, u32[]{:S(2)}) collective-permute-start(bf16[4,64,896]{2,1,0:T(8,128)(2,1)} %get-tuple-element.22), channel_id=1, source_target_pairs={{0,2},{1,3},{2,0},{3,1},{4,6},{5,7},{6,4},{7,5},{8,10},{9,11},{10,... | collective-permute-start | bytes 1376264 | tf_op jit(solution)/shard_map/ppermute | solution.py:18
  14.3 20.3 %collective-permute-start.3 = (bf16[4,64,896]{2,1,0:T(8,128)(2,1)S(1)}, bf16[4,64,896]{2,1,0:T(8,128)(2,1)S(1)}, u32[]{:S(2)}, u32[]{:S(2)}) collective-permute-start(bf16[4,64,896]{2,1,0:T(8,128)(2,1)S(1)} %get-tuple-element.23), channel_id=1, source_target_pairs={{0,3},{1,0},{2,1},{3,2},{4,7},{5,4},{6,5},{7,6},{8,11},{9,8},{10,9... | collective-permute-start | bytes 1376264 | tf_op jit(solution)/shard_map/ppermute | solution.py:18
  36.5 8.6 %copy-start.6 = (f32[64,8]{0,1:T(8,128)S(1)}, f32[64,8]{0,1:T(8,128)}, u32[]{:S(2)}) copy-start(f32[64,8]{0,1:T(8,128)} %param.8) | copy-start | bytes 6148
  36.6 35.2 %all-to-all-start = ((bf16[16,32,1024]{2,1,0:T(8,128)(2,1)}), bf16[16,32,1024]{2,1,0:T(8,128)(2,1)S(1)}, u32[]{:S(2)}, u32[]{:S(2)}) async-start(bf16[16,32,1024]{2,1,0:T(8,128)(2,1)} %shard_map.56), calls=%async_computation | async-start | bytes 2097152 | tf_op jit(solution)/shard_map/all_to_all | solution.py:208
  46.2 6.9 %collective-permute-start.4 = (f32[16,128]{1,0:T(8,128)S(1)}, f32[16,128]{1,0:T(8,128)S(1)}, u32[]{:S(2)}, u32[]{:S(2)}) collective-permute-start(f32[16,128]{1,0:T(8,128)S(1)} %pad_maximum_fusion.2), channel_id=1, source_target_pairs={{0,1},{1,2},{2,3},{3,0},{4,5},{5,6},{6,7},{7,4},{8,9},{9,10},{10,1... | collective-permute-start | bytes 24584 | tf_op jit(solution)/shard_map/ppermute | solution.py:18
  47.1 6.0 %collective-permute-start.5 = (f32[16,128]{1,0:T(8,128)S(1)}, f32[16,128]{1,0:T(8,128)S(1)}, u32[]{:S(2)}, u32[]{:S(2)}) collective-permute-start(f32[16,128]{1,0:T(8,128)S(1)} %pad_maximum_fusion.2), channel_id=1, source_target_pairs={{0,2},{1,3},{2,0},{3,1},{4,6},{5,7},{6,4},{7,5},{8,10},{9,11},{10,... | collective-permute-start | bytes 24584 | tf_op jit(solution)/shard_map/ppermute | solution.py:18
  49.7 3.7 %collective-permute-start.6 = (f32[16,128]{1,0:T(8,128)S(1)}, f32[16,128]{1,0:T(8,128)S(1)}, u32[]{:S(2)}, u32[]{:S(2)}) collective-permute-start(f32[16,128]{1,0:T(8,128)S(1)} %pad_maximum_fusion.2), channel_id=1, source_target_pairs={{0,3},{1,0},{2,1},{3,2},{4,7},{5,4},{6,5},{7,6},{8,11},{9,8},{10,9... | collective-permute-start | bytes 24584 | tf_op jit(solution)/shard_map/ppermute | solution.py:18
  71.8 32.6 %all-to-all-start.1 = ((bf16[16,32,1024]{2,1,0:T(8,128)(2,1)}), bf16[16,32,1024]{2,1,0:T(8,128)(2,1)S(1)}, u32[]{:S(2)}, u32[]{:S(2)}) async-start(bf16[16,32,1024]{2,1,0:T(8,128)(2,1)} %shard_map.57), calls=%async_computation.1 | async-start | bytes 2097152 | tf_op jit(solution)/shard_map/all_to_all | solution.py:222
  76.6 154.0 %reduce-scatter.2.cloned.1.call-start = ((), (), s32[]{:S(2)}) async-start(), calls=%async_computation.4 | async-start | bytes 4128768 | tf_op jit(solution)/shard_map/reduce_scatter | solution.py:240
  76.7 26.8 %collective-permute-start.7 = (bf16[16,32,1024]{2,1,0:T(8,128)(2,1)S(1)}, bf16[16,32,1024]{2,1,0:T(8,128)(2,1)S(1)}, u32[]{:S(2)}, u32[]{:S(2)}) collective-permute-start(bf16[16,32,1024]{2,1,0:T(8,128)(2,1)S(1)} %all-to-all-done.refs_0_), channel_id=1, source_target_pairs={{0,1},{1,2},{2,3},{3,0},{4,5},{5,6},{6,7},{7,4},{8,9},{9,10},{10,1... | collective-permute-start | bytes 3145736 | tf_op jit(solution)/shard_map/ppermute | solution.py:18
  77.7 25.8 %collective-permute-start = (bf16[16,32,1024]{2,1,0:T(8,128)(2,1)S(1)}, bf16[16,32,1024]{2,1,0:T(8,128)(2,1)S(1)}, u32[]{:S(2)}, u32[]{:S(2)}) collective-permute-start(bf16[16,32,1024]{2,1,0:T(8,128)(2,1)S(1)} %all-to-all-done.refs_0_), channel_id=1, source_target_pairs={{0,3},{1,0},{2,1},{3,2},{4,7},{5,4},{6,5},{7,6},{8,11},{9,8},{10,9... | collective-permute-start | bytes 3145736 | tf_op jit(solution)/shard_map/ppermute | solution.py:18
  103.5 1.0 copy-start.2
  104.4 25.7 %collective-permute-start.8 = (bf16[16,32,1024]{2,1,0:T(8,128)(2,1)S(1)}, bf16[16,32,1024]{2,1,0:T(8,128)(2,1)}, u32[]{:S(2)}, u32[]{:S(2)}) collective-permute-start(bf16[16,32,1024]{2,1,0:T(8,128)(2,1)S(1)} %all-to-all-done.1.refs_2_), channel_id=1, source_target_pairs={{0,3},{1,0},{2,1},{3,2},{4,7},{5,4},{6,5},{7,6},{8,11},{9,8},{10,9... | collective-permute-start | bytes 3145736 | tf_op jit(solution)/shard_map/ppermute | solution.py:18
  107.4 56.6 %collective-permute-start.10 = (bf16[16,32,1024]{2,1,0:T(8,128)(2,1)S(1)}, bf16[16,32,1024]{2,1,0:T(8,128)(2,1)}, u32[]{:S(2)}, u32[]{:S(2)}) collective-permute-start(bf16[16,32,1024]{2,1,0:T(8,128)(2,1)S(1)} %collective-permute-done.7.refs_0_), channel_id=1, source_target_pairs={{0,1},{1,2},{2,3},{3,0},{4,5},{5,6},{6,7},{7,4},{8,9},{9,10},{10,1... | collective-permute-start | bytes 3145736 | tf_op jit(solution)/shard_map/ppermute | solution.py:18
  107.4 56.6 %collective-permute-start.11 = (bf16[16,32,1024]{2,1,0:T(8,128)(2,1)S(1)}, bf16[16,32,1024]{2,1,0:T(8,128)(2,1)}, u32[]{:S(2)}, u32[]{:S(2)}) collective-permute-start(bf16[16,32,1024]{2,1,0:T(8,128)(2,1)S(1)} %all-to-all-done.1.refs_2_), channel_id=1, source_target_pairs={{0,1},{1,2},{2,3},{3,0},{4,5},{5,6},{6,7},{7,4},{8,9},{9,10},{10,1... | collective-permute-start | bytes 3145736 | tf_op jit(solution)/shard_map/ppermute | solution.py:18
  130.1 33.9 %collective-permute-start.12 = (bf16[16,32,1024]{2,1,0:T(8,128)(2,1)}, bf16[16,32,1024]{2,1,0:T(8,128)(2,1)}, u32[]{:S(2)}, u32[]{:S(2)}) collective-permute-start(bf16[16,32,1024]{2,1,0:T(8,128)(2,1)} %collective-permute-done.8.refs_3_), channel_id=1, source_target_pairs={{0,3},{1,0},{2,1},{3,2},{4,7},{5,4},{6,5},{7,6},{8,11},{9,8},{10,9... | collective-permute-start | bytes 3145736 | tf_op jit(solution)/shard_map/ppermute | solution.py:18
  147.7 1.2 copy-start.3
  163.9 16.1 %collective-permute-start.9 = (bf16[8,2,64,896]{3,2,1,0:T(8,128)(2,1)S(1)}, bf16[8,2,64,896]{3,2,1,0:T(8,128)(2,1)S(1)}, u32[]{:S(2)}, u32[]{:S(2)}) collective-permute-start(bf16[8,2,64,896]{3,2,1,0:T(8,128)(2,1)S(1)} %get-tuple-element.28), channel_id=1, source_target_pairs={{0,64},{64,0},{1,65},{65,1},{2,66},{66,2},{3,67},{67,3},{4,68},{68... | collective-permute-start | bytes 5505032 | tf_op jit(solution)/shard_map/ppermute | solution.py:18
  164.0 16.0 %copy-start.4 = (f32[8,2,64,896]{3,2,1,0:T(8,128)S(1)}, f32[8,2,64,896]{3,2,1,0:T(8,128)}, u32[]{:S(2)}) copy-start(f32[8,2,64,896]{3,2,1,0:T(8,128)} %get-tuple-element.27) | copy-start | bytes 11010052
  179.6 3.8 %collective-permute-start.13 = (bf16[8,2,64,896]{3,2,1,0:T(8,128)(2,1)S(1)}, bf16[8,2,64,896]{3,2,1,0:T(8,128)(2,1)S(1)}, u32[]{:S(2)}, u32[]{:S(2)}) collective-permute-start(bf16[8,2,64,896]{3,2,1,0:T(8,128)(2,1)S(1)} %get-tuple-element.30), channel_id=1, source_target_pairs={{0,64},{64,0},{1,65},{65,1},{2,66},{66,2},{3,67},{67,3},{4,68},{68... | collective-permute-start | bytes 5505032 | tf_op jit(solution)/shard_map/ppermute | solution.py:18
  180.0 3.4 %copy-start.5 = (f32[8,2,64,896]{3,2,1,0:T(8,128)S(1)}, f32[8,2,64,896]{3,2,1,0:T(8,128)}, u32[]{:S(2)}) copy-start(f32[8,2,64,896]{3,2,1,0:T(8,128)} %get-tuple-element.29) | copy-start | bytes 11010052
  231.7 7.8 %collective-permute-start.14 = (bf16[64,896]{1,0:T(8,128)(2,1)S(1)}, bf16[64,896]{1,0:T(8,128)(2,1)S(1)}, u32[]{:S(2)}, u32[]{:S(2)}) collective-permute-start(bf16[64,896]{1,0:T(8,128)(2,1)S(1)} %get-tuple-element.33), channel_id=1, source_target_pairs={{0,3},{1,0},{2,1},{3,2},{4,7},{5,4},{6,5},{7,6},{8,11},{9,8},{10,9... | collective-permute-start | bytes 344072 | tf_op jit(solution)/shard_map/ppermute | solution.py:18
  234.6 7.4 %collective-permute-start.15 = (bf16[64,896]{1,0:T(8,128)(2,1)S(1)}, bf16[64,896]{1,0:T(8,128)(2,1)S(1)}, u32[]{:S(2)}, u32[]{:S(2)}) collective-permute-start(bf16[64,896]{1,0:T(8,128)(2,1)S(1)} %get-tuple-element.32), channel_id=1, source_target_pairs={{0,2},{1,3},{2,0},{3,1},{4,6},{5,7},{6,4},{7,5},{8,10},{9,11},{10,... | collective-permute-start | bytes 344072 | tf_op jit(solution)/shard_map/ppermute | solution.py:18
  235.4 7.8 %collective-permute-start.16 = (bf16[64,896]{1,0:T(8,128)(2,1)S(1)}, bf16[64,896]{1,0:T(8,128)(2,1)S(1)}, u32[]{:S(2)}, u32[]{:S(2)}) collective-permute-start(bf16[64,896]{1,0:T(8,128)(2,1)S(1)} %get-tuple-element.31), channel_id=1, source_target_pairs={{0,1},{1,2},{2,3},{3,0},{4,5},{5,6},{6,7},{7,4},{8,9},{9,10},{10,1... | collective-permute-start | bytes 344072 | tf_op jit(solution)/shard_map/ppermute | solution.py:18
Sparse Core Ops, SparseCore 0:
  36.7 79.1 all-gather.2
  186.2 44.3 reduce-scatter.1

commit v5 on v4

v5 whole, which is shorter than its diff:
```python
import functools
import jax
import jax.numpy as jnp
from jax import lax
from jax.experimental import pallas as pl
from jax.experimental.pallas import tpu as pltpu
from jax.sharding import Mesh, PartitionSpec as P

AXES = ("zl", "c", "zh", "x", "y")
Z = ("zh", "zl")
VMEM = pl.BlockSpec(memory_space=pltpu.VMEM)
SMEM = pl.BlockSpec(memory_space=pltpu.SMEM)
PARAMS = pltpu.CompilerParams(vmem_limit_bytes=48 << 20)


def shifted(value, axis, steps):
    count = lax.axis_size(axis)
    return lax.ppermute(value, axis, [(i, (i + steps) % count) for i in range(count)])


def after(value, *others):
    return lax.optimization_barrier((value, *others))[0]


def cost(flops, *arrays):
    size = sum(a.size * a.dtype.itemsize for a in arrays)
    return pl.CostEstimate(flops=flops, bytes_accessed=size, transcendentals=0)


def split_kernel(pos_ref, w_ref, gate_ref, row_ref, *out_refs):
    count = len(out_refs)
    exp_train, depth, _ = w_ref.shape
    groups, slots = gate_ref.shape
    size, width = exp_train * depth, out_refs[0].shape[1]
    gate = gate_ref[...]
    high = gate.astype(jnp.bfloat16)
    low = (gate - high.astype(jnp.float32)).astype(jnp.bfloat16)
    for d, out_ref in enumerate(out_refs):
        start = pl.multiple_of(lax.rem(pos_ref[2] + d, count) * width, 128)
        out_ref[:size] = w_ref[:, :, pl.ds(start, width)].reshape(size, width)
        out_ref[size:] = jnp.zeros((groups, width), jnp.bfloat16)
        for part, value in enumerate((high, low, row_ref[...].astype(jnp.bfloat16))):
            out_ref[size:, part * slots:(part + 1) * slots] = value


def split_blocks(pos, own, gate, row, count):
    exp_train, depth, width = own.shape
    shape = jax.ShapeDtypeStruct((exp_train * depth + gate.shape[0], width // count), own.dtype)
    return pl.pallas_call(
        split_kernel, out_shape=[shape] * count, in_specs=[SMEM] + [VMEM] * 3, out_specs=[VMEM] * count,
        compiler_params=PARAMS, cost_estimate=cost(0, own, own),
    )(pos, own, gate, row)


def join_kernel(pos_ref, *refs):
    *in_refs, out_ref, info_ref = refs
    count = len(in_refs)
    exp_train, hidden, width = out_ref.shape
    depth = hidden // count
    size, lanes = exp_train * depth, info_ref.shape[2]
    for d, in_ref in enumerate(in_refs):
        start = pl.multiple_of(lax.rem(pos_ref[2] + count - d, count) * depth, depth)
        out_ref[:, pl.ds(start, depth), :] = in_ref[:size].reshape(exp_train, depth, width)
        info_ref[d] = in_ref[size:, :lanes]


def join_blocks(pos, blocks, exp_train, depth, lanes):
    total, width = blocks[0].shape
    count = len(blocks)
    shape = jax.ShapeDtypeStruct((exp_train, depth * count, width), blocks[0].dtype)
    info = jax.ShapeDtypeStruct((count, total - exp_train * depth, lanes), blocks[0].dtype)
    return pl.pallas_call(
        join_kernel, out_shape=[shape, info], in_specs=[SMEM] + [VMEM] * count, out_specs=[VMEM] * 2,
        compiler_params=PARAMS, cost_estimate=cost(0, shape, shape),
    )(pos, *blocks)


def dispatch_kernel(groups, whole, first_ref, flat_ref, hidden_ref, out_ref):
    slots, pairs = out_ref.shape[1], flat_ref.shape[1]
    number = lax.broadcasted_iota(jnp.int32, (groups * slots, pairs), 0)
    number = number // slots * whole + lax.rem(number, slots) + first_ref[0]
    chosen = jnp.where(number == flat_ref[...], 1.0, 0.0).astype(jnp.bfloat16)
    rows = jnp.dot(chosen, hidden_ref[...], preferred_element_type=jnp.float32).astype(jnp.bfloat16)
    out_ref[...] = rows.reshape(out_ref.shape)


def dispatch(first, slots, whole, flat, hidden, groups):
    shape = jax.ShapeDtypeStruct((groups, slots, hidden.shape[1]), hidden.dtype)
    return pl.pallas_call(
        functools.partial(dispatch_kernel, groups, whole),
        out_shape=shape, in_specs=[SMEM, VMEM, VMEM], out_specs=VMEM,
        compiler_params=PARAMS, cost_estimate=cost(2 * groups * slots * hidden.size, hidden, shape),
    )(jnp.full((1,), first, jnp.int32), flat, hidden)


def experts_kernel(counts, pos_ref, *refs):
    *x_refs, w_ref, gate_ref, row_ref, mine_ref, other_ref, p_ref = refs
    k, turn = pl.program_id(0), pl.program_id(1)
    capacity, hidden_width = x_refs[0].shape[1:]
    experts, turns = pl.num_programs(0), pl.num_programs(1)
    slots = capacity * experts
    width = w_ref.shape[3]
    planes, _, rows, _ = mine_ref.shape
    c = pos_ref[1]
    first = 0
    for part, part_counts in enumerate(counts):
        for number, count in enumerate(part_counts):
            @pl.when((turn == number) & (jnp.maximum(k, 1) - 1 == part))
            def _(number=number, sources=x_refs[first:first + count]):
                block = jnp.concatenate([ref[...].reshape(-1, hidden_width) for ref in sources], 0)
                total = jnp.dot(
                    block, w_ref[...].reshape(hidden_width, width), preferred_element_type=jnp.float32
                )
                high = total.astype(jnp.bfloat16)
                low = (total - high.astype(jnp.float32)).astype(jnp.bfloat16)
                high, low = (v.reshape(-1, capacity, width) for v in (high, low))
                for segment, value in enumerate((high, high, low)):
                    start = pl.multiple_of(segment * slots + k * capacity, capacity)
                    p_ref[number, :, pl.ds(start, capacity), :] = value
            first += count

    @pl.when(k == experts - 1)
    def _():
        number = lax.broadcasted_iota(jnp.int32, (rows, 3 * slots), 0).astype(jnp.float32)
        for plane in range(planes):
            for core, out_ref in enumerate((mine_ref, other_ref)):
                source = plane * 2 + lax.rem(c + core, 2)
                index = turn * planes * 2 + source
                mine = number == row_ref[pl.ds(index, 1), :]
                combine = jnp.where(mine, gate_ref[pl.ds(index, 1), :], 0.0).astype(jnp.bfloat16)
                mixed = jnp.dot(combine, p_ref[turn, source], preferred_element_type=jnp.float32)
                out_ref[plane, 0] = mixed.astype(out_ref.dtype)


def experts_call(pos, xs, weight, gate, row, rows):
    blocks, experts, depth, width = weight.shape
    turns = len(xs[0])
    groups, capacity, hidden_width = xs[1][0][0].shape
    mine = jax.ShapeDtypeStruct((groups // 2, turns, rows, width), jnp.float32)
    other = jax.ShapeDtypeStruct((groups // 2, turns, rows, width), jnp.bfloat16)
    arrays, specs = [], []
    for part, part_arrays in enumerate(xs):
        for turn, values in enumerate(part_arrays):
            for v in values:
                def index(k, t, part=part, turn=turn):
                    now = jnp.where(t > turn, k + 1, k) if turn < turns - 1 else k
                    return 0, jnp.clip(now, 0, 1) if part == 0 else 0, 0

                arrays.append(v)
                specs.append(pl.BlockSpec((v.shape[0], capacity, hidden_width), index))
    whole = pl.BlockSpec((groups // 2, 1, rows, width), lambda k, t: (0, jnp.where(k == experts - 1, t, 0), 0, 0))
    info = pl.BlockSpec(gate.shape, lambda k, t: (0, 0))
    flops = 2 * turns * groups * capacity * experts * hidden_width * width
    return pl.pallas_call(
        functools.partial(experts_kernel, [[len(v) for v in part_arrays] for part_arrays in xs]),
        grid=(experts, turns),
        out_shape=[mine, other],
        in_specs=[SMEM] + specs + [pl.BlockSpec((blocks, 1, depth, width), lambda k, t: (0, k, 0, 0))] + [info] * 2,
        out_specs=[whole] * 2,
        scratch_shapes=[pltpu.VMEM((turns, groups, 3 * experts * capacity, width), jnp.bfloat16)],
        compiler_params=PARAMS,
        cost_estimate=cost(flops, *arrays, weight, mine, other),
    )(pos, *arrays, weight, gate, row)


def place_kernel(pos_ref, *refs):
    in_refs, out_ref = refs[:-1], refs[-1]
    width = in_refs[0].shape[1]
    for d, in_ref in enumerate(in_refs):
        start = pl.multiple_of(lax.rem(pos_ref[2] + d, len(in_refs)) * width, 128)
        out_ref[:, pl.ds(start, width)] = in_ref[...]


def place_blocks(pos, blocks):
    rows, width = blocks[0].shape
    shape = jax.ShapeDtypeStruct((rows, width * len(blocks)), blocks[0].dtype)
    return pl.pallas_call(
        place_kernel, out_shape=shape, in_specs=[SMEM] + [VMEM] * len(blocks), out_specs=VMEM,
        compiler_params=PARAMS, cost_estimate=cost(0, shape, shape),
    )(pos, *blocks)


def per_device(trainer_weight, owner, expert_ids, gates, hidden):
    experts = owner.shape[0]
    rows, fanout = expert_ids.shape
    hidden_width = hidden.shape[2]
    capacity = min(rows, 2 * rows * fanout // experts)
    own = trainer_weight[0, 0]
    exp_train, slice_rows, width = own.shape
    ny = lax.axis_size("y")
    groups = experts // exp_train
    slots = exp_train * capacity
    block_width = width // ny
    low = lax.axis_size("zl")
    z, c, y = lax.axis_index("zh") * low + lax.axis_index("zl"), lax.axis_index("c"), lax.axis_index("y")
    pos = jnp.stack([z, c, y, lax.axis_index("x")]).astype(jnp.int32)

    zl, cs, zh = (lax.axis_size(a) for a in ("zl", "c", "zh"))
    slot_of = owner.reshape(zl, cs, zh, exp_train).transpose(2, 0, 1, 3).reshape(experts)
    match = expert_ids[:, :, None] == slot_of[None, None, :]
    named = jnp.any(match, axis=1)
    position = jnp.cumsum(named.astype(jnp.int32), axis=0) - 1
    place = jnp.arange(experts, dtype=jnp.int32)[None, :] * capacity + position
    flat = jnp.sum(jnp.where(match, place[:, None, :], 0), axis=2).reshape(1, -1)
    pairs = hidden.reshape(-1, hidden_width)
    group_axes = Z + ("c",)

    send = lambda first, count: dispatch(first * capacity, count * capacity, slots, flat, pairs, groups)
    exchange = lambda value: lax.all_to_all(value, group_axes, 0, 0, tiled=True)
    first = exchange(send(0, 2))

    chosen = jnp.arange(experts * capacity, dtype=jnp.int32)[:, None] == flat
    pair_row = jnp.arange(rows * fanout, dtype=jnp.int32) // fanout
    slot_gate = jnp.sum(jnp.where(chosen, gates.reshape(-1)[None, :], 0.0), axis=1).reshape(groups, slots)
    slot_row = jnp.sum(jnp.where(chosen, pair_row[None, :] + 1, 0), axis=1).reshape(groups, slots) - 1

    blocks = split_blocks(pos, own, slot_gate, slot_row.astype(jnp.float32), ny)
    blocks = [blocks[0]] + [shifted(blocks[d], "y", d) for d in range(1, ny)]
    blocks[1] = after(blocks[1], first)
    joined, info = join_blocks(pos, blocks, exp_train, slice_rows, 4 * slots)
    weight = lax.all_gather(joined, "x")

    first_up, first_down = shifted(first, "y", 1), shifted(first, "y", -1)
    second = exchange(after(send(2, 1), first))
    third = exchange(after(send(3, 1), first))
    middle = groups // 2
    first_opposite = [shifted(first_up[:middle], "y", 1), shifted(first_down[middle:], "y", -1)]
    second_late = after(second, first_up, first_down)
    second_up, second_down = shifted(second_late, "y", 1), shifted(second_late, "y", -1)
    third_up, third_down = shifted(third, "y", 1), shifted(third, "y", -1)
    info = lax.all_to_all(after(info, third), group_axes, 1, 1, tiled=True).astype(jnp.float32)
    high, low, row = (info[:, :, i * slots:(i + 1) * slots].reshape(ny * groups, slots) for i in range(3))
    gate = jnp.concatenate([high, low, high], 1)
    row = jnp.tile(row, (1, 3))
    second_opposite = shifted(second_up, "y", 1)
    third_opposite = shifted(after(third_down, info), "y", -1)

    xs = [
        [[first], [first_up], first_opposite, [first_down]],
        [[second], [second_up], [second_opposite], [second_down]],
        [[third], [third_up], [third_opposite], [third_down]],
    ]
    mine, other = experts_call(pos, xs, weight, gate, row, rows)
    partial = (mine + shifted(other, "c", 1).astype(jnp.float32)).astype(jnp.bfloat16)
    partial = partial.reshape(-1, block_width)
    summed = lax.psum_scatter(partial, Z, scatter_dimension=0, tiled=True).reshape(ny, rows, block_width)
    final = [summed[0]] + [shifted(summed[d], "y", -d) for d in range(1, ny)]
    return place_blocks(pos, final)


def solution(mesh):
    devices = mesh.devices.reshape(2, 2, 4, 4, 4)
    inner = Mesh(devices, AXES)
    rep, exp = ("zl", "c"), ("zh", "x", "y")
    return jax.shard_map(
        per_device,
        mesh=inner,
        in_specs=(
            P(rep, exp, None, None, None),
            P(),
            P(rep + exp, None),
            P(rep + exp, None),
            P(rep + exp, None, None),
        ),
        out_specs=P(rep + exp, None),
        check_vma=False,
    )
```

time: 253 us -> 254 us (level)
  starting transfers between devices: 39.1 us -> 43.9 us
  other arithmetic: 5.44 us -> 8.45 us
    ppermute x17, waiting for transfers between devices: 70.2 us -> 48 us  [shifted(): lax.ppermute(value, axis, [(i, (i + steps) % count) for i in range(count)])]
    all_to_all x2 -> x3, waiting for transfers between devices: 18.5 us -> 35.4 us  [per_device(): exchange = lambda value: lax.all_to_all(value, group_axes, 0, 0, tiled=True)]
    all_to_all x2 -> x3, starting transfers between devices: 13.4 us -> 19.8 us  [per_device(): exchange = lambda value: lax.all_to_all(value, group_axes, 0, 0, tiled=True)]
    convert_element_type x3, other arithmetic: 1.02 us -> 6.18 us  [the longest x1 6.16 us: per_device(): (mine + shifted(other, 'c', 1).astype(jnp.float32)).astype(jnp.bfloat16)]
    slice x4, local copies, waits for them, and re-layouts: 1.32 us -> 4.9 us  [the longest x1 1.87 us: per_device(): first_down[middle:]]
    reduce_scatter x1, waiting for transfers between devices: 44.5 us -> 47.1 us  [per_device(): lax.psum_scatter(partial, Z, scatter_dimension=0, tiled=True)]
  transfers between devices with their start and end apart: 21 -> 22, of which waited for: 11 -> 11; matrix products, arithmetic and copies ran while one was open for 2% -> 2% of each run, Pallas kernels for 14% -> 2%
where the time goes in v5:
time: 254 us; the launch traced here: 253 us
  waiting for transfers between devices  131 us (52%)
  starting transfers between devices  43.9 us (17%)
  Pallas kernels  36.4 us (14%)
  between operations  13.6 us (5%)
  blocking collectives  11.5 us (5%)
  other arithmetic  8.45 us (3%)
  local copies, waits for them, and re-layouts  8.43 us (3%)
    ppermute x17, waiting for transfers between devices, shifted(): lax.ppermute(value, axis, [(i, (i + steps) % count) for i in range(count)])  48 us
    reduce_scatter x1, waiting for transfers between devices, per_device(): lax.psum_scatter(partial, Z, scatter_dimension=0, tiled=True)  47.1 us
    all_to_all x3, waiting for transfers between devices, per_device(): exchange = lambda value: lax.all_to_all(value, group_axes, 0, 0, tiled=True)  35.4 us
    pallas_call x1, Pallas kernels, experts_call(): pl.pallas_call(functools.partial(experts_kernel, [[len(v) for v in part_a...  27.3 us
    ppermute x17, starting transfers between devices, shifted(): lax.ppermute(value, axis, [(i, (i + steps) % count) for i in range(count)])  24.1 us
    all_to_all x3, starting transfers between devices, per_device(): exchange = lambda value: lax.all_to_all(value, group_axes, 0, 0, tiled=True)  19.8 us
    all_to_all x1, blocking collectives, per_device(): lax.all_to_all(after(info, third), group_axes, 1, 1, tiled=True)  11.5 us
    convert_element_type x1, other arithmetic, per_device(): (mine + shifted(other, 'c', 1).astype(jnp.float32)).astype(jnp.bfloat16)  6.16 us
  transfers between devices with their start and end apart: 22, of which 11 were waited for; matrix products, arithmetic and copies ran while one was open for 2% of the time, Pallas kernels for 2%

profile of v5, /device:TPU:2, one launch (start us, length us, event | category | flops | bytes accessed | tf_op | source)
XLA Modules:
  0.0 252.9 jit_solution(3947857688399253850)
XLA Ops:
  6.5 0.7 reshape.83
  7.3 0.1 eq.31
  7.4 0.8 copy.27
  8.2 0.2 compare_reduce_fusion
  8.4 0.1 reduce_window_sum.11
  8.5 1.2 fusion
  9.7 0.1 reshape.84.flat_ref
  9.8 1.2 copy-done
  11.0 1.7 shard_map.55
  12.7 8.6 %all-to-all-start = ((bf16[16,32,1024]{2,1,0:T(8,128)(2,1)}), bf16[16,32,1024]{2,1,0:T(8,128)(2,1)}, u32[]{:S(2)}, u32[]{:S(2)}) async-start(bf16[16,32,1024]{2,1,0:T(8,128)(2,1)} %shard_map.55), calls=%async_computation | async-start | bytes 2097152 | tf_op jit(solution)/shard_map/all_to_all | solution.py:209
  21.4 0.0 all-gather.3.cloned.1.call-start
  21.4 0.1 eq.35
  21.5 0.3 select_reduce_fusion
  21.8 0.1 convert_element_type.23.row_ref
  21.9 0.1 copy.29
  22.0 0.1 broadcast_in_dim.45
  22.1 0.3 select_reduce_fusion.1
  22.4 0.1 reshape.86.gate_ref
  22.5 0.1 pad_add_fusion.pos_ref
  22.5 1.7 shard_map.58
  24.2 1.6 collective-permute-start.9
  25.8 2.9 %collective-permute-start.10 = (bf16[272,896]{1,0:T(8,128)(2,1)}, bf16[272,896]{1,0:T(8,128)(2,1)S(1)}, u32[]{:S(2)}, u32[]{:S(2)}) collective-permute-start(bf16[272,896]{1,0:T(8,128)(2,1)} %get-tuple-element.25), channel_id=1, source_target_pairs={{0,2},{1,3},{2,0},{3,1},{4,6},{5,7},{6,4},{7,5},{8,10},{9,11},{10,... | collective-permute-start | bytes 1462280 | tf_op jit(solution)/shard_map/ppermute | solution.py:18
  28.7 1.3 collective-permute-start.11
  30.0 8.8 %collective-permute-done.9.refs_1_ = bf16[272,896]{1,0:T(8,128)(2,1)S(1)} collective-permute-done((bf16[272,896]{1,0:T(8,128)(2,1)S(1)}, bf16[272,896]{1,0:T(8,128)(2,1)S(1)}, u32[]{:S(2)}, u32[]{:S(2)}) %collective-permute-start.9) | collective-permute-done | bytes 487456 | tf_op jit(solution)/shard_map/ppermute | solution.py:18
  38.9 9.2 %all-to-all-done.refs_0_ = bf16[16,32,1024]{2,1,0:T(8,128)(2,1)} async-done(((bf16[16,32,1024]{2,1,0:T(8,128)(2,1)}), bf16[16,32,1024]{2,1,0:T(8,128)(2,1)}, u32[]{:S(2)}, u32[]{:S(2)}) %all-to-all-start) | async-done | bytes 1048608 | tf_op jit(solution)/shard_map/all_to_all | solution.py:209
  48.1 2.4 collective-permute-done.10.refs_2_
  50.5 2.0 shard_map.59
  52.5 0.0 all-gather.3.cloned.1.call-update
  52.5 1.2 shard_map.57
  53.7 7.0 %all-to-all-start.2 = ((bf16[16,16,1024]{2,1,0:T(8,128)(2,1)}), bf16[16,16,1024]{2,1,0:T(8,128)(2,1)S(1)}, u32[]{:S(2)}, u32[]{:S(2)}) async-start(bf16[16,16,1024]{2,1,0:T(8,128)(2,1)} %shard_map.57), calls=%async_computation.2 | async-start | bytes 1048576 | tf_op jit(solution)/shard_map/all_to_all | solution.py:209
  60.7 2.4 collective-permute-start.2
  63.1 1.2 shard_map.56
  64.3 12.4 %all-to-all-done.2.refs_9_ = bf16[16,16,1024]{2,1,0:T(8,128)(2,1)S(1)} async-done(((bf16[16,16,1024]{2,1,0:T(8,128)(2,1)}), bf16[16,16,1024]{2,1,0:T(8,128)(2,1)S(1)}, u32[]{:S(2)}, u32[]{:S(2)}) %all-to-all-start.2) | async-done | bytes 524320 | tf_op jit(solution)/shard_map/all_to_all | solution.py:209
  76.7 4.2 %all-to-all-start.1 = ((bf16[16,16,1024]{2,1,0:T(8,128)(2,1)}), bf16[16,16,1024]{2,1,0:T(8,128)(2,1)S(1)}, u32[]{:S(2)}, u32[]{:S(2)}) async-start(bf16[16,16,1024]{2,1,0:T(8,128)(2,1)} %shard_map.56), calls=%async_computation.1 | async-start | bytes 1048576 | tf_op jit(solution)/shard_map/all_to_all | solution.py:209
  80.9 0.0 reduce-scatter.2.cloned.1.call-start
  81.0 2.4 collective-permute-start.8
  83.3 13.8 %all-to-all-done.1.refs_5_ = bf16[16,16,1024]{2,1,0:T(8,128)(2,1)S(1)} async-done(((bf16[16,16,1024]{2,1,0:T(8,128)(2,1)}), bf16[16,16,1024]{2,1,0:T(8,128)(2,1)S(1)}, u32[]{:S(2)}, u32[]{:S(2)}) %all-to-all-start.1) | async-done | bytes 524320 | tf_op jit(solution)/shard_map/all_to_all | solution.py:209
  97.1 1.4 collective-permute-start.4
  98.5 11.5 %all_to_all.20 = bf16[4,16,256]{2,0,1:T(4,128)(2,1)S(1)} all-to-all(bf16[4,16,256]{2,0,1:T(4,128)(2,1)S(1)} %copy.30), channel_id=1, replica_groups=mesh['zl'=2,'c'=2,'zh'=4,'x'=4,'y'=4] {'zh','zl','c'}, dimensions={1} | all-to-all | bytes 65536 | tf_op jit(solution)/shard_map/all_to_all | solution.py:231
  110.0 1.9 collective-permute-start.6
  111.9 1.9 slice.41
  113.8 1.1 collective-permute-start.3
  114.8 1.9 slice.40
  116.7 1.0 collective-permute-start.1
  117.7 2.3 collective-permute-start.12
  119.9 0.1 fusion.6
  120.0 0.1 copy.32
  120.1 0.1 copy.33.refs_15_
  120.2 0.1 pad_maximum_fusion.refs_14_
  120.3 15.8 %collective-permute-done.3.refs_3_ = bf16[8,32,1024]{2,1,0:T(8,128)(2,1)} collective-permute-done((bf16[8,32,1024]{2,1,0:T(8,128)(2,1)}, bf16[8,32,1024]{2,1,0:T(8,128)(2,1)}, u32[]{:S(2)}, u32[]{:S(2)}) %collective-permute-start.3) | collective-permute-done | bytes 524320 | tf_op jit(solution)/shard_map/ppermute | solution.py:18
  136.1 10.4 %collective-permute-done.12.refs_11_ = bf16[16,16,1024]{2,1,0:T(8,128)(2,1)} collective-permute-done((bf16[16,16,1024]{2,1,0:T(8,128)(2,1)S(1)}, bf16[16,16,1024]{2,1,0:T(8,128)(2,1)}, u32[]{:S(2)}, u32[]{:S(2)}) %collective-permute-start.12) | collective-permute-done | bytes 524320 | tf_op jit(solution)/shard_map/ppermute | solution.py:18
  146.5 27.3 %shard_map.60 = (f32[8,4,64,896]{3,2,1,0:T(8,128)}, bf16[8,4,64,896]{3,2,1,0:T(8,128)(2,1)}) custom-call(s32[4]{0:T(128)S(1)} %pad_add_fusion.pos_ref, bf16[16,32,1024]{2,1,0:T(8,128)(2,1)} %all-to-all-done.refs_0_, bf16[16,32,1024]{2,1,0:T(8,128)(2,1)} %collective-permute-done.refs_1_, bf16[8,32,1024]{2,1,0:T(8,128)(2,1)} %collective-permute-done.1.refs_2_, ...), custom_call_target="tpu_custom_call" | custom-call | flops 7516192768 | bytes 26738688 | tf_op jit(solution)/shard_map/pallas_call | solution.py:154
  173.8 0.2 collective-permute-start.13
  174.1 6.6 %collective-permute-done.13 = bf16[8,4,64,896]{3,2,1,0:T(8,128)(2,1)S(1)} collective-permute-done((bf16[8,4,64,896]{3,2,1,0:T(8,128)(2,1)}, bf16[8,4,64,896]{3,2,1,0:T(8,128)(2,1)S(1)}, u32[]{:S(2)}, u32[]{:S(2)}) %collective-permute-start.13) | collective-permute-done | bytes 3670048 | tf_op jit(solution)/shard_map/ppermute | solution.py:18
  180.7 6.2 %add_convert_fusion = bf16[8,4,64,896]{3,2,1,0:T(8,128)(2,1)} fusion(f32[8,4,64,896]{3,2,1,0:T(8,128)} %get-tuple-element.31, bf16[8,4,64,896]{3,2,1,0:T(8,128)(2,1)S(1)} %collective-permute-done.13), kind=kLoop, calls=%fused_computation | loop fusion | flops 5505024 | bytes 14680064 | tf_op jit(solution)/shard_map/convert_element_type | solution.py:244
  186.9 0.0 reduce-scatter.2.cloned.1.call-update
  186.9 47.1 %reduce-scatter.2.cloned.1.call-done = bf16[256,896]{1,0:T(8,128)(2,1)} async-done(((bf16[2048,896]{1,0:T(8,128)(2,1)}), bf16[256,896]{1,0:T(8,128)(2,1)}) %reduce-scatter.2.cloned.1.call-update) | async-done | bytes 458768 | tf_op jit(solution)/shard_map/reduce_scatter | solution.py:246
  233.9 1.1 fusion.5
  235.1 1.6 collective-permute-start.16
  236.6 2.7 %collective-permute-start.15 = (bf16[64,896]{1,0:T(8,128)(2,1)S(1)}, bf16[64,896]{1,0:T(8,128)(2,1)S(1)}, u32[]{:S(2)}, u32[]{:S(2)}) collective-permute-start(bf16[64,896]{1,0:T(8,128)(2,1)S(1)} %get-tuple-element.34), channel_id=1, source_target_pairs={{0,2},{1,3},{2,0},{3,1},{4,6},{5,7},{6,4},{7,5},{8,10},{9,11},{10,... | collective-permute-start | bytes 344072 | tf_op jit(solution)/shard_map/ppermute | solution.py:18
  239.3 1.4 collective-permute-start.14
  240.8 0.6 collective-permute-done.16.refs_3_
  241.4 3.3 %collective-permute-done.15.refs_2_ = bf16[64,896]{1,0:T(8,128)(2,1)S(1)} collective-permute-done((bf16[64,896]{1,0:T(8,128)(2,1)S(1)}, bf16[64,896]{1,0:T(8,128)(2,1)S(1)}, u32[]{:S(2)}, u32[]{:S(2)}) %collective-permute-start.15) | collective-permute-done | bytes 114720 | tf_op jit(solution)/shard_map/ppermute | solution.py:18
  244.7 1.4 shard_map.61
  (30 shorter events, 0.1 us)
Async XLA Ops:
  9.8 1.2 copy-start
  11.0 10.9 %copy-start.3 = (f32[64,8]{0,1:T(8,128)S(1)}, f32[64,8]{0,1:T(8,128)}, u32[]{:S(2)}) copy-start(f32[64,8]{0,1:T(8,128)} %param.8) | copy-start | bytes 6148
  11.0 11.5 %copy-start.2 = (bf16[1,1,4,64,3584]{4,3,2,1,0:T(8,128)(2,1)S(1)}, bf16[1,1,4,64,3584]{4,3,2,1,0:T(8,128)(2,1)}, u32[]{:S(2)}) copy-start(bf16[1,1,4,64,3584]{4,3,2,1,0:T(8,128)(2,1)} %param.5) | copy-start | bytes 5505028
  12.7 35.3 %all-to-all-start = ((bf16[16,32,1024]{2,1,0:T(8,128)(2,1)}), bf16[16,32,1024]{2,1,0:T(8,128)(2,1)}, u32[]{:S(2)}, u32[]{:S(2)}) async-start(bf16[16,32,1024]{2,1,0:T(8,128)(2,1)} %shard_map.55), calls=%async_computation | async-start | bytes 2097152 | tf_op jit(solution)/shard_map/all_to_all | solution.py:209
  21.4 125.2 %all-gather.3.cloned.1.call-start = ((), (), s32[]{:S(2)}) async-start(), calls=%async_computation.6 | async-start | bytes 9175040 | tf_op jit(solution)/shard_map/all_gather | solution.py:221
  24.2 28.3 %copy-start.1 = (bf16[64,8,1024]{2,1,0:T(8,128)(2,1)S(1)}, bf16[64,8,1024]{2,1,0:T(8,128)(2,1)}, u32[]{:S(2)}) copy-start(bf16[64,8,1024]{2,1,0:T(8,128)(2,1)} %param.9) | copy-start | bytes 3145732
  24.2 14.7 %collective-permute-start.9 = (bf16[272,896]{1,0:T(8,128)(2,1)S(1)}, bf16[272,896]{1,0:T(8,128)(2,1)S(1)}, u32[]{:S(2)}, u32[]{:S(2)}) collective-permute-start(bf16[272,896]{1,0:T(8,128)(2,1)S(1)} %get-tuple-element.23), channel_id=1, source_target_pairs={{0,1},{1,2},{2,3},{3,0},{4,5},{5,6},{6,7},{7,4},{8,9},{9,10},{10,1... | collective-permute-start | bytes 1462280 | tf_op jit(solution)/shard_map/ppermute | solution.py:18
  25.8 24.7 %collective-permute-start.10 = (bf16[272,896]{1,0:T(8,128)(2,1)}, bf16[272,896]{1,0:T(8,128)(2,1)S(1)}, u32[]{:S(2)}, u32[]{:S(2)}) collective-permute-start(bf16[272,896]{1,0:T(8,128)(2,1)} %get-tuple-element.25), channel_id=1, source_target_pairs={{0,2},{1,3},{2,0},{3,1},{4,6},{5,7},{6,4},{7,5},{8,10},{9,11},{10,... | collective-permute-start | bytes 1462280 | tf_op jit(solution)/shard_map/ppermute | solution.py:18
  28.7 21.8 %collective-permute-start.11 = (bf16[272,896]{1,0:T(8,128)(2,1)}, bf16[272,896]{1,0:T(8,128)(2,1)S(1)}, u32[]{:S(2)}, u32[]{:S(2)}) collective-permute-start(bf16[272,896]{1,0:T(8,128)(2,1)} %get-tuple-element.26), channel_id=1, source_target_pairs={{0,3},{1,0},{2,1},{3,2},{4,7},{5,4},{6,5},{7,6},{8,11},{9,8},{10,9... | collective-permute-start | bytes 1462280 | tf_op jit(solution)/shard_map/ppermute | solution.py:18
  53.7 23.0 %all-to-all-start.2 = ((bf16[16,16,1024]{2,1,0:T(8,128)(2,1)}), bf16[16,16,1024]{2,1,0:T(8,128)(2,1)S(1)}, u32[]{:S(2)}, u32[]{:S(2)}) async-start(bf16[16,16,1024]{2,1,0:T(8,128)(2,1)} %shard_map.57), calls=%async_computation.2 | async-start | bytes 1048576 | tf_op jit(solution)/shard_map/all_to_all | solution.py:209
  60.7 36.4 %collective-permute-start.2 = (bf16[16,32,1024]{2,1,0:T(8,128)(2,1)}, bf16[16,32,1024]{2,1,0:T(8,128)(2,1)}, u32[]{:S(2)}, u32[]{:S(2)}) collective-permute-start(bf16[16,32,1024]{2,1,0:T(8,128)(2,1)} %all-to-all-done.refs_0_), channel_id=1, source_target_pairs={{0,3},{1,0},{2,1},{3,2},{4,7},{5,4},{6,5},{7,6},{8,11},{9,8},{10,9... | collective-permute-start | bytes 3145736 | tf_op jit(solution)/shard_map/ppermute | solution.py:18
  63.1 34.0 %collective-permute-start = (bf16[16,32,1024]{2,1,0:T(8,128)(2,1)}, bf16[16,32,1024]{2,1,0:T(8,128)(2,1)}, u32[]{:S(2)}, u32[]{:S(2)}) collective-permute-start(bf16[16,32,1024]{2,1,0:T(8,128)(2,1)} %all-to-all-done.refs_0_), channel_id=1, source_target_pairs={{0,1},{1,2},{2,3},{3,0},{4,5},{5,6},{6,7},{7,4},{8,9},{9,10},{10,1... | collective-permute-start | bytes 3145736 | tf_op jit(solution)/shard_map/ppermute | solution.py:18
  76.7 20.4 %all-to-all-start.1 = ((bf16[16,16,1024]{2,1,0:T(8,128)(2,1)}), bf16[16,16,1024]{2,1,0:T(8,128)(2,1)S(1)}, u32[]{:S(2)}, u32[]{:S(2)}) async-start(bf16[16,16,1024]{2,1,0:T(8,128)(2,1)} %shard_map.56), calls=%async_computation.1 | async-start | bytes 1048576 | tf_op jit(solution)/shard_map/all_to_all | solution.py:209
  80.9 153.0 %reduce-scatter.2.cloned.1.call-start = ((), (), s32[]{:S(2)}) async-start(), calls=%async_computation.5 | async-start | bytes 4128768 | tf_op jit(solution)/shard_map/reduce_scatter | solution.py:246
  81.0 35.7 %collective-permute-start.8 = (bf16[16,16,1024]{2,1,0:T(8,128)(2,1)S(1)}, bf16[16,16,1024]{2,1,0:T(8,128)(2,1)S(1)}, u32[]{:S(2)}, u32[]{:S(2)}) collective-permute-start(bf16[16,16,1024]{2,1,0:T(8,128)(2,1)S(1)} %all-to-all-done.2.refs_9_), channel_id=1, source_target_pairs={{0,3},{1,0},{2,1},{3,2},{4,7},{5,4},{6,5},{7,6},{8,11},{9,8},{10,9... | collective-permute-start | bytes 1572872 | tf_op jit(solution)/shard_map/ppermute | solution.py:18
  83.3 34.3 %collective-permute-start.7 = (bf16[16,16,1024]{2,1,0:T(8,128)(2,1)S(1)}, bf16[16,16,1024]{2,1,0:T(8,128)(2,1)S(1)}, u32[]{:S(2)}, u32[]{:S(2)}) collective-permute-start(bf16[16,16,1024]{2,1,0:T(8,128)(2,1)S(1)} %all-to-all-done.2.refs_9_), channel_id=1, source_target_pairs={{0,1},{1,2},{2,3},{3,0},{4,5},{5,6},{6,7},{7,4},{8,9},{9,10},{10,1... | collective-permute-start | bytes 1572872 | tf_op jit(solution)/shard_map/ppermute | solution.py:18
  97.1 22.8 %collective-permute-start.4 = (bf16[16,16,1024]{2,1,0:T(8,128)(2,1)S(1)}, bf16[16,16,1024]{2,1,0:T(8,128)(2,1)S(1)}, u32[]{:S(2)}, u32[]{:S(2)}) collective-permute-start(bf16[16,16,1024]{2,1,0:T(8,128)(2,1)S(1)} %all-to-all-done.1.refs_5_), channel_id=1, source_target_pairs={{0,1},{1,2},{2,3},{3,0},{4,5},{5,6},{6,7},{7,4},{8,9},{9,10},{10,1... | collective-permute-start | bytes 1572872 | tf_op jit(solution)/shard_map/ppermute | solution.py:18
  110.0 26.1 %collective-permute-start.6 = (bf16[16,16,1024]{2,1,0:T(8,128)(2,1)S(1)}, bf16[16,16,1024]{2,1,0:T(8,128)(2,1)}, u32[]{:S(2)}, u32[]{:S(2)}) collective-permute-start(bf16[16,16,1024]{2,1,0:T(8,128)(2,1)S(1)} %all-to-all-done.1.refs_5_), channel_id=1, source_target_pairs={{0,3},{1,0},{2,1},{3,2},{4,7},{5,4},{6,5},{7,6},{8,11},{9,8},{10,9... | collective-permute-start | bytes 1572872 | tf_op jit(solution)/shard_map/ppermute | solution.py:18
  113.8 22.4 %collective-permute-start.3 = (bf16[8,32,1024]{2,1,0:T(8,128)(2,1)}, bf16[8,32,1024]{2,1,0:T(8,128)(2,1)}, u32[]{:S(2)}, u32[]{:S(2)}) collective-permute-start(bf16[8,32,1024]{2,1,0:T(8,128)(2,1)} %slice.41), channel_id=1, source_target_pairs={{0,3},{1,0},{2,1},{3,2},{4,7},{5,4},{6,5},{7,6},{8,11},{9,8},{10,9... | collective-permute-start | bytes 1572872 | tf_op jit(solution)/shard_map/ppermute | solution.py:18
  116.7 19.4 %collective-permute-start.1 = (bf16[8,32,1024]{2,1,0:T(8,128)(2,1)}, bf16[8,32,1024]{2,1,0:T(8,128)(2,1)}, u32[]{:S(2)}, u32[]{:S(2)}) collective-permute-start(bf16[8,32,1024]{2,1,0:T(8,128)(2,1)} %slice.40), channel_id=1, source_target_pairs={{0,1},{1,2},{2,3},{3,0},{4,5},{5,6},{6,7},{7,4},{8,9},{9,10},{10,1... | collective-permute-start | bytes 1572872 | tf_op jit(solution)/shard_map/ppermute | solution.py:18
  117.7 28.9 %collective-permute-start.12 = (bf16[16,16,1024]{2,1,0:T(8,128)(2,1)S(1)}, bf16[16,16,1024]{2,1,0:T(8,128)(2,1)}, u32[]{:S(2)}, u32[]{:S(2)}) collective-permute-start(bf16[16,16,1024]{2,1,0:T(8,128)(2,1)S(1)} %collective-permute-done.8.refs_12_), channel_id=1, source_target_pairs={{0,3},{1,0},{2,1},{3,2},{4,7},{5,4},{6,5},{7,6},{8,11},{9,8},{10,9... | collective-permute-start | bytes 1572872 | tf_op jit(solution)/shard_map/ppermute | solution.py:18
  119.9 26.6 %collective-permute-start.5 = (bf16[16,16,1024]{2,1,0:T(8,128)(2,1)S(1)}, bf16[16,16,1024]{2,1,0:T(8,128)(2,1)}, u32[]{:S(2)}, u32[]{:S(2)}) collective-permute-start(bf16[16,16,1024]{2,1,0:T(8,128)(2,1)S(1)} %collective-permute-done.4.refs_6_), channel_id=1, source_target_pairs={{0,1},{1,2},{2,3},{3,0},{4,5},{5,6},{6,7},{7,4},{8,9},{9,10},{10,1... | collective-permute-start | bytes 1572872 | tf_op jit(solution)/shard_map/ppermute | solution.py:18
  173.8 6.9 %collective-permute-start.13 = (bf16[8,4,64,896]{3,2,1,0:T(8,128)(2,1)}, bf16[8,4,64,896]{3,2,1,0:T(8,128)(2,1)S(1)}, u32[]{:S(2)}, u32[]{:S(2)}) collective-permute-start(bf16[8,4,64,896]{3,2,1,0:T(8,128)(2,1)} %get-tuple-element.32), channel_id=1, source_target_pairs={{0,64},{64,0},{1,65},{65,1},{2,66},{66,2},{3,67},{67,3},{4,68},{68... | collective-permute-start | bytes 11010056 | tf_op jit(solution)/shard_map/ppermute | solution.py:18
  235.1 6.4 %collective-permute-start.16 = (bf16[64,896]{1,0:T(8,128)(2,1)S(1)}, bf16[64,896]{1,0:T(8,128)(2,1)S(1)}, u32[]{:S(2)}, u32[]{:S(2)}) collective-permute-start(bf16[64,896]{1,0:T(8,128)(2,1)S(1)} %get-tuple-element.33), channel_id=1, source_target_pairs={{0,1},{1,2},{2,3},{3,0},{4,5},{5,6},{6,7},{7,4},{8,9},{9,10},{10,1... | collective-permute-start | bytes 344072 | tf_op jit(solution)/shard_map/ppermute | solution.py:18
  236.6 8.1 %collective-permute-start.15 = (bf16[64,896]{1,0:T(8,128)(2,1)S(1)}, bf16[64,896]{1,0:T(8,128)(2,1)S(1)}, u32[]{:S(2)}, u32[]{:S(2)}) collective-permute-start(bf16[64,896]{1,0:T(8,128)(2,1)S(1)} %get-tuple-element.34), channel_id=1, source_target_pairs={{0,2},{1,3},{2,0},{3,1},{4,6},{5,7},{6,4},{7,5},{8,10},{9,11},{10,... | collective-permute-start | bytes 344072 | tf_op jit(solution)/shard_map/ppermute | solution.py:18
  239.3 5.4 %collective-permute-start.14 = (bf16[64,896]{1,0:T(8,128)(2,1)S(1)}, bf16[64,896]{1,0:T(8,128)(2,1)S(1)}, u32[]{:S(2)}, u32[]{:S(2)}) collective-permute-start(bf16[64,896]{1,0:T(8,128)(2,1)S(1)} %get-tuple-element.35), channel_id=1, source_target_pairs={{0,3},{1,0},{2,1},{3,2},{4,7},{5,4},{6,5},{7,6},{8,11},{9,8},{10,9... | collective-permute-start | bytes 344072 | tf_op jit(solution)/shard_map/ppermute | solution.py:18
Sparse Core Ops, SparseCore 0:
  52.6 77.7 all-gather.2
  187.0 46.9 reduce-scatter.1

commit v6 on v5

--- a/solution.py
+++ b/solution.py
@@ -16,6 +16,12 @@
 def shifted(value, axis, steps):
     count = lax.axis_size(axis)
     return lax.ppermute(value, axis, [(i, (i + steps) % count) for i in range(count)])
+
+
+def mirrored(value, axis, steps):
+    cores, count = lax.axis_size("c"), lax.axis_size(axis)
+    pairs = [(c * count + i, c * count + (i + (1 - 2 * c) * steps) % count) for c in range(cores) for i in range(count)]
+    return lax.ppermute(value, ("c", axis), pairs)
 
 
 def after(value, *others):
@@ -93,81 +99,123 @@
     )(jnp.full((1,), first, jnp.int32), flat, hidden)
 
 
-def experts_kernel(counts, pos_ref, *refs):
-    *x_refs, w_ref, gate_ref, row_ref, mine_ref, other_ref, p_ref = refs
-    k, turn = pl.program_id(0), pl.program_id(1)
-    capacity, hidden_width = x_refs[0].shape[1:]
-    experts, turns = pl.num_programs(0), pl.num_programs(1)
-    slots = capacity * experts
-    width = w_ref.shape[3]
-    planes, _, rows, _ = mine_ref.shape
-    c = pos_ref[1]
-    first = 0
-    for part, part_counts in enumerate(counts):
-        for number, count in enumerate(part_counts):
-            @pl.when((turn == number) & (jnp.maximum(k, 1) - 1 == part))
-            def _(number=number, sources=x_refs[first:first + count]):
-                block = jnp.concatenate([ref[...].reshape(-1, hidden_width) for ref in sources], 0)
-                total = jnp.dot(
-                    block, w_ref[...].reshape(hidden_width, width), preferred_element_type=jnp.float32
-                )
-                high = total.astype(jnp.bfloat16)
-                low = (total - high.astype(jnp.float32)).astype(jnp.bfloat16)
-                high, low = (v.reshape(-1, capacity, width) for v in (high, low))
-                for segment, value in enumerate((high, high, low)):
-                    start = pl.multiple_of(segment * slots + k * capacity, capacity)
-                    p_ref[number, :, pl.ds(start, capacity), :] = value
-            first += count
-
-    @pl.when(k == experts - 1)
-    def _():
-        number = lax.broadcasted_iota(jnp.int32, (rows, 3 * slots), 0).astype(jnp.float32)
-        for plane in range(planes):
-            for core, out_ref in enumerate((mine_ref, other_ref)):
-                source = plane * 2 + lax.rem(c + core, 2)
-                index = turn * planes * 2 + source
+def experts_kernel(turns, pos_ref, *refs):
+    x_refs = refs[:turns], refs[turns:2 * turns]
+    w_refs = refs[2 * turns:3 * turns], refs[3 * turns:4 * turns]
+    gate_ref, row_ref, out_ref, x_all, w_all, p_all, sums, out_all, x_sem, w_sem, out_sem = refs[4 * turns:]
+    _, _, planes, part_slots, hidden_width = x_all.shape
+    rows, width = sums.shape[1:]
+    experts, depth, _ = w_refs[0][0].shape
+    capacity = part_slots // experts
+    slots = experts * capacity
+    c, x = pos_ref[1], pos_ref[3]
+
+    def x_copy(part, turn):
+        return pltpu.make_async_copy(x_refs[part][turn], x_all.at[part, turn], x_sem.at[part, turn])
+
+    def w_copy(core, k, d):
+        number = lax.rem(c + core, 2)
+        start = pl.multiple_of(lax.rem(x + d * (3 - 2 * number), turns) * depth, depth)
+        return pltpu.make_async_copy(
+            w_refs[core][d].at[k], w_all.at[core * experts + k, pl.ds(start, depth), :], w_sem.at[core * experts + k, d]
+        )
+
+    for turn in range(turns):
+        x_copy(0, turn).start()
+    for core in range(2):
+        for k in range(experts):
+            for d in range(turns):
+                w_copy(core, k, d).start()
+            if (core, k) == (0, 1):
+                for turn in range(turns):
+                    x_copy(1, turn).start()
+
+    number = lax.broadcasted_iota(jnp.int32, (rows, 3 * slots), 0).astype(jnp.float32)
+    for core in range(2):
+        group = lax.rem(c + core, 2)
+
+        def multiply(k, _, core=core, group=group):
+            if core == 0:
+                for part in range(2):
+                    @pl.when(k == 2 * part)
+                    def _(part=part):
+                        for turn in range(turns):
+                            x_copy(part, turn).wait()
+            for d in range(turns):
+                w_copy(core, k, d).wait()
+            start = pl.multiple_of(group * (part_slots // 2) + lax.rem(k, 2) * capacity, capacity)
+            block = x_all[k // 2, :, :, pl.ds(start, capacity), :].reshape(turns * planes * capacity, hidden_width)
+            total = jnp.dot(block, w_all[core * experts + k], preferred_element_type=jnp.float32)
+            high = total.astype(jnp.bfloat16)
+            low = (total - high.astype(jnp.float32)).astype(jnp.bfloat16)
+            for segment, value in enumerate((high, high, low)):
+                place = pl.multiple_of(segment * slots + k * capacity, capacity)
+                p_all[:, pl.ds(place, capacity), :] = value.reshape(turns * planes, capacity, width)
+            return 0
+
+        lax.fori_loop(0, experts, multiply, 0)
+
+        def combine(turn, _, core=core, group=group):
+            shift = lax.rem(turn * (1 + 2 * c), turns)
+
+            def one(plane, _):
+                index = (shift * planes + plane) * 2 + group
                 mine = number == row_ref[pl.ds(index, 1), :]
-                combine = jnp.where(mine, gate_ref[pl.ds(index, 1), :], 0.0).astype(jnp.bfloat16)
-                mixed = jnp.dot(combine, p_ref[turn, source], preferred_element_type=jnp.float32)
-                out_ref[plane, 0] = mixed.astype(out_ref.dtype)
-
-
-def experts_call(pos, xs, weight, gate, row, rows):
-    blocks, experts, depth, width = weight.shape
-    turns = len(xs[0])
-    groups, capacity, hidden_width = xs[1][0][0].shape
-    mine = jax.ShapeDtypeStruct((groups // 2, turns, rows, width), jnp.float32)
-    other = jax.ShapeDtypeStruct((groups // 2, turns, rows, width), jnp.bfloat16)
-    arrays, specs = [], []
-    for part, part_arrays in enumerate(xs):
-        for turn, values in enumerate(part_arrays):
-            for v in values:
-                def index(k, t, part=part, turn=turn):
-                    now = jnp.where(t > turn, k + 1, k) if turn < turns - 1 else k
-                    return 0, jnp.clip(now, 0, 1) if part == 0 else 0, 0
-
-                arrays.append(v)
-                specs.append(pl.BlockSpec((v.shape[0], capacity, hidden_width), index))
-    whole = pl.BlockSpec((groups // 2, 1, rows, width), lambda k, t: (0, jnp.where(k == experts - 1, t, 0), 0, 0))
-    info = pl.BlockSpec(gate.shape, lambda k, t: (0, 0))
-    flops = 2 * turns * groups * capacity * experts * hidden_width * width
-    return pl.pallas_call(
-        functools.partial(experts_kernel, [[len(v) for v in part_arrays] for part_arrays in xs]),
-        grid=(experts, turns),
-        out_shape=[mine, other],
-        in_specs=[SMEM] + specs + [pl.BlockSpec((blocks, 1, depth, width), lambda k, t: (0, k, 0, 0))] + [info] * 2,
-        out_specs=[whole] * 2,
-        scratch_shapes=[pltpu.VMEM((turns, groups, 3 * experts * capacity, width), jnp.bfloat16)],
-        compiler_params=PARAMS,
-        cost_estimate=cost(flops, *arrays, weight, mine, other),
-    )(pos, *arrays, weight, gate, row)
+                weights = jnp.where(mine, gate_ref[pl.ds(index, 1), :], 0.0).astype(jnp.bfloat16)
+                source = turn * planes + plane
+                mixed = jnp.dot(weights, p_all[source], preferred_element_type=jnp.float32)
+                if core == 0:
+                    sums[source] = mixed
+                else:
+                    out_all[turn, plane] = (sums[source] + mixed).astype(out_all.dtype)
+                return 0
+
+            lax.fori_loop(0, planes, one, 0, unroll=2)
+            if core == 1:
+                pltpu.make_async_copy(out_all.at[turn], out_ref.at[:, turn], out_sem.at[turn]).start()
+            return 0
+
+        lax.fori_loop(0, turns, combine, 0)
+    for turn in range(turns):
+        pltpu.make_async_copy(out_all.at[turn], out_ref.at[:, turn], out_sem.at[turn]).wait()
+
+
+def experts_call(pos, xs, ws, gate, row, rows):
+    turns = len(ws[0])
+    experts, depth, width = ws[0][0].shape
+    planes, part_slots, hidden_width = xs[0][0].shape
+    slots = part_slots
+    out = jax.ShapeDtypeStruct((planes, turns, rows, width), jnp.bfloat16)
+    hbm = pl.BlockSpec(memory_space=pl.ANY)
+    arrays = [*xs[0], *xs[1], *ws[0], *ws[1]]
+    flops = 2 * turns * planes * 2 * part_slots * hidden_width * width
+    bf16 = lambda *shape: pltpu.VMEM(shape, jnp.bfloat16)
+    return pl.pallas_call(
+        functools.partial(experts_kernel, turns),
+        out_shape=out,
+        in_specs=[SMEM] + [hbm] * len(arrays) + [VMEM] * 2,
+        out_specs=hbm,
+        scratch_shapes=[
+            bf16(2, turns, planes, part_slots, hidden_width),
+            bf16(2 * experts, hidden_width, width),
+            bf16(turns * planes, 3 * slots, width),
+            pltpu.VMEM((turns * planes, rows, width), jnp.float32),
+            bf16(turns, planes, rows, width),
+            pltpu.SemaphoreType.DMA((2, turns)),
+            pltpu.SemaphoreType.DMA((2 * experts, turns)),
+            pltpu.SemaphoreType.DMA((turns,)),
+        ],
+        compiler_params=pltpu.CompilerParams(vmem_limit_bytes=56 << 20),
+        cost_estimate=cost(flops, *arrays, out),
+    )(pos, *arrays, gate, row)
 
 
 def place_kernel(pos_ref, *refs):
     in_refs, out_ref = refs[:-1], refs[-1]
     width = in_refs[0].shape[1]
     for d, in_ref in enumerate(in_refs):
-        start = pl.multiple_of(lax.rem(pos_ref[2] + d, len(in_refs)) * width, 128)
+        turned = lax.rem(pos_ref[2] + d * (1 + 2 * pos_ref[1]), len(in_refs))
+        start = pl.multiple_of(turned * width, 128)
         out_ref[:, pl.ds(start, width)] = in_ref[...]
 
 
@@ -203,11 +251,11 @@
     place = jnp.arange(experts, dtype=jnp.int32)[None, :] * capacity + position
     flat = jnp.sum(jnp.where(match, place[:, None, :], 0), axis=2).reshape(1, -1)
     pairs = hidden.reshape(-1, hidden_width)
-    group_axes = Z + ("c",)
-
-    send = lambda first, count: dispatch(first * capacity, count * capacity, slots, flat, pairs, groups)
-    exchange = lambda value: lax.all_to_all(value, group_axes, 0, 0, tiled=True)
-    first = exchange(send(0, 2))
+
+    planes = groups // 2
+    half = exp_train // 2
+    send = lambda first: dispatch(first * capacity, half * capacity, slots, flat, pairs, groups).reshape(planes, -1, hidden_width)
+    first = lax.all_to_all(send(0), Z, 0, 0, tiled=True)
 
     chosen = jnp.arange(experts * capacity, dtype=jnp.int32)[:, None] == flat
     pair_row = jnp.arange(rows * fanout, dtype=jnp.int32) // fanout
@@ -218,33 +266,26 @@
     blocks = [blocks[0]] + [shifted(blocks[d], "y", d) for d in range(1, ny)]
     blocks[1] = after(blocks[1], first)
     joined, info = join_blocks(pos, blocks, exp_train, slice_rows, 4 * slots)
-    weight = lax.all_gather(joined, "x")
-
-    first_up, first_down = shifted(first, "y", 1), shifted(first, "y", -1)
-    second = exchange(after(send(2, 1), first))
-    third = exchange(after(send(3, 1), first))
-    middle = groups // 2
-    first_opposite = [shifted(first_up[:middle], "y", 1), shifted(first_down[middle:], "y", -1)]
+    second = lax.all_to_all(after(send(half), first), Z, 0, 0, tiled=True)
+    weight_up, weight_down = mirrored(joined, "x", 1), mirrored(joined, "x", -1)
+    first_up, first_down = mirrored(first, "y", 1), mirrored(first, "y", -1)
+    first_opposite = mirrored(first_up, "y", 1)
+    weight_opposite = mirrored(weight_up, "x", 1)
+    weights = [joined, weight_up, weight_opposite, weight_down]
+    other_weights = [shifted(v, "c", 1) for v in weights]
     second_late = after(second, first_up, first_down)
-    second_up, second_down = shifted(second_late, "y", 1), shifted(second_late, "y", -1)
-    third_up, third_down = shifted(third, "y", 1), shifted(third, "y", -1)
-    info = lax.all_to_all(after(info, third), group_axes, 1, 1, tiled=True).astype(jnp.float32)
-    high, low, row = (info[:, :, i * slots:(i + 1) * slots].reshape(ny * groups, slots) for i in range(3))
+    second_up, second_down = mirrored(second_late, "y", 1), mirrored(second_late, "y", -1)
+    info = after(info, second).reshape(ny, planes, 2, 4 * slots)
+    info = lax.all_to_all(info, Z, 1, 1, tiled=True).astype(jnp.float32)
+    high, low, row = (info[..., i * slots:(i + 1) * slots].reshape(ny * groups, slots) for i in range(3))
     gate = jnp.concatenate([high, low, high], 1)
     row = jnp.tile(row, (1, 3))
-    second_opposite = shifted(second_up, "y", 1)
-    third_opposite = shifted(after(third_down, info), "y", -1)
-
-    xs = [
-        [[first], [first_up], first_opposite, [first_down]],
-        [[second], [second_up], [second_opposite], [second_down]],
-        [[third], [third_up], [third_opposite], [third_down]],
-    ]
-    mine, other = experts_call(pos, xs, weight, gate, row, rows)
-    partial = (mine + shifted(other, "c", 1).astype(jnp.float32)).astype(jnp.bfloat16)
-    partial = partial.reshape(-1, block_width)
+    second_opposite = mirrored(after(second_up, info), "y", 1)
+
+    xs = [first, first_up, first_opposite, first_down], [second, second_up, second_opposite, second_down]
+    partial = experts_call(pos, xs, (weights, other_weights), gate, row, rows).reshape(-1, block_width)
     summed = lax.psum_scatter(partial, Z, scatter_dimension=0, tiled=True).reshape(ny, rows, block_width)
-    final = [summed[0]] + [shifted(summed[d], "y", -d) for d in range(1, ny)]
+    final = [summed[0]] + [mirrored(summed[d], "y", -d) for d in range(1, ny)]
     return place_blocks(pos, final)
 
 

time: 254 us -> 251 us (0.988)
  other arithmetic: 8.45 us -> 2.92 us
  waiting for transfers between devices: 131 us -> 135 us
  starting transfers between devices: 43.9 us -> 40.6 us
  blocking collectives: 11.5 us -> 14.2 us
    ppermute x0 -> x12, waiting for transfers between devices: none -> 67.8 us  [mirrored(): return lax.ppermute(value, ('c', axis), pairs)]
    ppermute x17 -> x7, waiting for transfers between devices: 48 us -> 8.33 us  [shifted(): lax.ppermute(value, axis, [(i, (i + steps) % count) for i in range(count)])]
    all_to_all x3 -> x2, waiting for transfers between devices: 35.4 us -> 11.9 us  [the longest x1 11.9 us: per_device(): first = lax.all_to_all(send(0), Z, 0, 0, tiled=True)]
    ppermute x0 -> x12, starting transfers between devices: none -> 19.9 us  [mirrored(): return lax.ppermute(value, ('c', axis), pairs)]
    ppermute x17 -> x7, starting transfers between devices: 24.1 us -> 5.84 us  [shifted(): lax.ppermute(value, axis, [(i, (i + steps) % count) for i in range(count)])]
    convert_element_type x2 -> x0, other arithmetic: 6.17 us -> none  [the longest x1 6.16 us: per_device(): (mine + shifted(other, 'c', 1).astype(jnp.float32)).astype(jnp.bfloat16)]
    all_to_all x3 -> x2, starting transfers between devices: 19.8 us -> 14.8 us  [the longest x1 8.47 us: per_device(): first = lax.all_to_all(send(0), Z, 0, 0, tiled=True)]
    slice x4 -> x5, local copies, waits for them, and re-layouts: 4.9 us -> 1.24 us  [the longest x1 1.1 us: per_device(): final = [summed[0]] + [mirrored(summed[d], 'y', -d) for d in range(1, ny)]]
  transfers between devices with their start and end apart: 22 -> 22, of which waited for: 11 -> 10; matrix products, arithmetic and copies ran while one was open for 2% -> 1% of each run, Pallas kernels for 2% -> 1%
where the time goes in v6:
time: 251 us; the launch traced here: 249 us
  waiting for transfers between devices  135 us (54%)
  starting transfers between devices  40.6 us (16%)
  Pallas kernels  36.4 us (15%)
  blocking collectives  14.2 us (6%)
  between operations  13.6 us (5%)
  local copies, waits for them, and re-layouts  6.4 us (3%)
  other arithmetic  2.92 us (1%)
    ppermute x12, waiting for transfers between devices, mirrored(): return lax.ppermute(value, ('c', axis), pairs)  67.8 us
    reduce_scatter x1, waiting for transfers between devices, per_device(): lax.psum_scatter(partial, Z, scatter_dimension=0, tiled=True)  46.9 us
    pallas_call x1, Pallas kernels, experts_call(): pl.pallas_call(functools.partial(experts_kernel, turns), out_shape=out, i...  28 us
    ppermute x12, starting transfers between devices, mirrored(): return lax.ppermute(value, ('c', axis), pairs)  19.9 us
    all_to_all x1, blocking collectives, per_device(): info = lax.all_to_all(info, Z, 1, 1, tiled=True).astype(jnp.float32)  14.2 us
    all_to_all x1, waiting for transfers between devices, per_device(): first = lax.all_to_all(send(0), Z, 0, 0, tiled=True)  11.9 us
    all_to_all x1, starting transfers between devices, per_device(): first = lax.all_to_all(send(0), Z, 0, 0, tiled=True)  8.47 us
    ppermute x7, waiting for transfers between devices, shifted(): lax.ppermute(value, axis, [(i, (i + steps) % count) for i in range(count)])  8.33 us
  transfers between devices with their start and end apart: 22, of which 10 were waited for; matrix products, arithmetic and copies ran while one was open for 1% of the time, Pallas kernels for 1%

profile of v6, /device:TPU:2, one launch (start us, length us, event | category | flops | bytes accessed | tf_op | source)
XLA Modules:
  0.0 249.0 jit_solution(3497295724742698040)
XLA Ops:
  6.5 0.7 reshape.92
  7.3 0.1 eq.31
  7.4 0.8 copy.29
  8.2 0.2 compare_reduce_fusion
  8.4 0.1 reduce_window_sum.11
  8.5 1.2 fusion
  9.7 0.1 reshape.93.flat_ref
  9.8 0.0 copy-start
  9.8 1.2 copy-done
  11.0 1.7 shard_map.55
  12.8 8.5 %all-to-all-start = ((bf16[8,64,1024]{2,1,0:T(8,128)(2,1)}), bf16[8,64,1024]{2,1,0:T(8,128)(2,1)}, u32[]{:S(2)}, u32[]{:S(2)}) async-start(bf16[8,64,1024]{2,1,0:T(8,128)(2,1)} %bitcast.6), calls=%async_computation | async-start | bytes 2097152 | tf_op jit(solution)/shard_map/all_to_all | solution.py:258
  21.2 0.1 eq.35
  21.3 0.3 select_reduce_fusion
  21.6 0.1 convert_element_type.17.row_ref
  21.7 0.1 copy.31
  21.8 0.1 broadcast_in_dim.45
  21.9 0.3 select_reduce_fusion.1
  22.2 0.1 reshape.97.gate_ref
  22.3 0.1 pad_add_fusion.pos_ref
  22.3 1.6 shard_map.57
  24.0 1.6 collective-permute-start.4
  25.6 2.9 %collective-permute-start.5 = (bf16[272,896]{1,0:T(8,128)(2,1)}, bf16[272,896]{1,0:T(8,128)(2,1)S(1)}, u32[]{:S(2)}, u32[]{:S(2)}) collective-permute-start(bf16[272,896]{1,0:T(8,128)(2,1)} %get-tuple-element.21), channel_id=1, source_target_pairs={{0,2},{1,3},{2,0},{3,1},{4,6},{5,7},{6,4},{7,5},{8,10},{9,11},{10,... | collective-permute-start | bytes 1462280 | tf_op jit(solution)/shard_map/ppermute | solution.py:18
  28.5 1.3 collective-permute-start.6
  29.8 8.3 %collective-permute-done.4.refs_1_ = bf16[272,896]{1,0:T(8,128)(2,1)S(1)} collective-permute-done((bf16[272,896]{1,0:T(8,128)(2,1)S(1)}, bf16[272,896]{1,0:T(8,128)(2,1)S(1)}, u32[]{:S(2)}, u32[]{:S(2)}) %collective-permute-start.4) | collective-permute-done | bytes 487456 | tf_op jit(solution)/shard_map/ppermute | solution.py:18
  38.1 11.9 %all-to-all-done.refs_0_ = bf16[8,64,1024]{2,1,0:T(8,128)(2,1)} async-done(((bf16[8,64,1024]{2,1,0:T(8,128)(2,1)}), bf16[8,64,1024]{2,1,0:T(8,128)(2,1)}, u32[]{:S(2)}, u32[]{:S(2)}) %all-to-all-start) | async-done | bytes 1048608 | tf_op jit(solution)/shard_map/all_to_all | solution.py:258
  50.1 0.0 collective-permute-done.5.refs_2_
  50.1 0.0 collective-permute-done.6.refs_3_
  50.1 1.9 shard_map.58
  52.0 1.5 collective-permute-start.9
  53.5 1.7 shard_map.56
  55.2 6.3 %all-to-all-start.1 = ((bf16[8,64,1024]{2,1,0:T(8,128)(2,1)}), bf16[8,64,1024]{2,1,0:T(8,128)(2,1)S(1)}, u32[]{:S(2)}, u32[]{:S(2)}) async-start(bf16[8,64,1024]{2,1,0:T(8,128)(2,1)} %bitcast.7), calls=%async_computation.1 | async-start | bytes 2097152 | tf_op jit(solution)/shard_map/all_to_all | solution.py:269
  61.6 0.0 reduce-scatter.2.cloned.1.call-start
  61.6 2.4 collective-permute-start.2
  64.0 0.5 collective-permute-start.11
  64.5 20.4 %collective-permute-done.9.refs_9_ = bf16[4,256,896]{2,1,0:T(8,128)(2,1)} collective-permute-done((bf16[4,256,896]{2,1,0:T(8,128)(2,1)}, bf16[4,256,896]{2,1,0:T(8,128)(2,1)}, u32[]{:S(2)}, u32[]{:S(2)}) %collective-permute-start.9) | collective-permute-done | bytes 1835040 | tf_op jit(solution)/shard_map/ppermute | solution.py:24
  84.9 2.5 collective-permute-start.10
  87.3 0.0 collective-permute-start.12
  87.3 0.0 collective-permute-done.2.refs_3_
  87.4 1.0 copy-done.8
  88.3 3.4 %collective-permute-start.3 = (bf16[8,64,1024]{2,1,0:T(8,128)(2,1)S(1)}, bf16[8,64,1024]{2,1,0:T(8,128)(2,1)S(1)}, u32[]{:S(2)}, u32[]{:S(2)}) collective-permute-start(bf16[8,64,1024]{2,1,0:T(8,128)(2,1)S(1)} %all-to-all-done.1.refs_4_), channel_id=1, source_target_pairs={{0,1},{1,2},{2,3},{3,0},{64,67},{65,64},{66,65},{67,66},{4,5},{5,6... | collective-permute-start | bytes 3145736 | tf_op jit(solution)/shard_map/ppermute | solution.py:24
  91.7 1.7 collective-permute-start.1
  93.4 10.6 %collective-permute-done.11.refs_11_ = bf16[4,256,896]{2,1,0:T(8,128)(2,1)S(1)} collective-permute-done((bf16[4,256,896]{2,1,0:T(8,128)(2,1)}, bf16[4,256,896]{2,1,0:T(8,128)(2,1)S(1)}, u32[]{:S(2)}, u32[]{:S(2)}) %collective-permute-start.11) | collective-permute-done | bytes 1835040 | tf_op jit(solution)/shard_map/ppermute | solution.py:24
  104.0 0.0 collective-permute-start.15
  104.0 1.6 collective-permute-done.3.refs_5_
  105.6 9.3 %collective-permute-done.10.refs_10_ = bf16[4,256,896]{2,1,0:T(8,128)(2,1)} collective-permute-done((bf16[4,256,896]{2,1,0:T(8,128)(2,1)}, bf16[4,256,896]{2,1,0:T(8,128)(2,1)}, u32[]{:S(2)}, u32[]{:S(2)}) %collective-permute-start.10) | collective-permute-done | bytes 1835040 | tf_op jit(solution)/shard_map/ppermute | solution.py:24
  114.9 0.0 collective-permute-start.14
  114.9 14.2 %all_to_all.15 = bf16[4,8,2,256]{3,2,0,1:T(2,128)(2,1)S(1)} all-to-all(bf16[4,8,2,256]{3,2,0,1:T(2,128)(2,1)S(1)} %copy.32), channel_id=1, replica_groups=mesh['zl'=2,'c'=2,'zh'=4,'x'=4,'y'=4] {'zh','zl'}, dimensions={1} | all-to-all | bytes 65536 | tf_op jit(solution)/shard_map/all_to_all | solution.py:279
  129.1 2.3 collective-permute-start.8
  131.4 0.1 fusion.6
  131.5 0.1 copy.36
  131.6 0.7 copy.37.refs_17_
  132.3 0.7 pad_maximum_fusion.refs_16_
  133.1 21.6 %collective-permute-done.8.refs_7_ = bf16[8,64,1024]{2,1,0:T(8,128)(2,1)} collective-permute-done((bf16[8,64,1024]{2,1,0:T(8,128)(2,1)S(1)}, bf16[8,64,1024]{2,1,0:T(8,128)(2,1)}, u32[]{:S(2)}, u32[]{:S(2)}) %collective-permute-start.8) | collective-permute-done | bytes 1048608 | tf_op jit(solution)/shard_map/ppermute | solution.py:24
  154.6 0.0 collective-permute-done.7.refs_6_
  154.7 28.0 %shard_map.59 = bf16[8,4,64,896]{3,2,1,0:T(8,128)(2,1)} custom-call(s32[4]{0:T(128)} %copy-done.3, bf16[8,64,1024]{2,1,0:T(8,128)(2,1)} %all-to-all-done.refs_0_, bf16[8,64,1024]{2,1,0:T(8,128)(2,1)} %collective-permute-done.refs_1_, bf16[8,64,1024]{2,1,0:T(8,128)(2,1)} %collective-permute-done.1.refs_2_, bf16[8,64,1024]{2,1,0:T(8,128)(2,1)} %copy-done.8, ...), custom_call_target="tpu_custom_call" | custom-call | flops 7516192768 | bytes 26738688 | tf_op jit(solution)/shard_map/pallas_call | solution.py:193
  182.7 0.0 reduce-scatter.2.cloned.1.call-update
  182.7 46.9 %reduce-scatter.2.cloned.1.call-done = bf16[256,896]{1,0:T(8,128)(2,1)} async-done(((bf16[2048,896]{1,0:T(8,128)(2,1)}), bf16[256,896]{1,0:T(8,128)(2,1)}) %reduce-scatter.2.cloned.1.call-update) | async-done | bytes 458768 | tf_op jit(solution)/shard_map/reduce_scatter | solution.py:287
  229.6 1.1 fusion.5
  230.7 1.6 collective-permute-start.18
  232.3 2.7 %collective-permute-start.17 = (bf16[64,896]{1,0:T(8,128)(2,1)S(1)}, bf16[64,896]{1,0:T(8,128)(2,1)S(1)}, u32[]{:S(2)}, u32[]{:S(2)}) collective-permute-start(bf16[64,896]{1,0:T(8,128)(2,1)S(1)} %get-tuple-element.28), channel_id=1, source_target_pairs={{0,2},{1,3},{2,0},{3,1},{64,66},{65,67},{66,64},{67,65},{4,6},{5,7... | collective-permute-start | bytes 344072 | tf_op jit(solution)/shard_map/ppermute | solution.py:24
  235.0 1.5 collective-permute-start.16
  236.5 0.3 collective-permute-done.18.refs_3_
  236.8 4.0 %collective-permute-done.17.refs_2_ = bf16[64,896]{1,0:T(8,128)(2,1)S(1)} collective-permute-done((bf16[64,896]{1,0:T(8,128)(2,1)S(1)}, bf16[64,896]{1,0:T(8,128)(2,1)S(1)}, u32[]{:S(2)}, u32[]{:S(2)}) %collective-permute-start.17) | collective-permute-done | bytes 114720 | tf_op jit(solution)/shard_map/ppermute | solution.py:24
  240.8 1.4 shard_map.60
  (40 shorter events, 0.2 us)
Async XLA Ops:
  9.8 1.2 copy-start
  11.0 10.7 %copy-start.6 = (f32[64,8]{0,1:T(8,128)S(1)}, f32[64,8]{0,1:T(8,128)}, u32[]{:S(2)}) copy-start(f32[64,8]{0,1:T(8,128)} %param.8) | copy-start | bytes 6148
  11.0 11.3 %copy-start.2 = (bf16[1,1,4,64,3584]{4,3,2,1,0:T(8,128)(2,1)S(1)}, bf16[1,1,4,64,3584]{4,3,2,1,0:T(8,128)(2,1)}, u32[]{:S(2)}) copy-start(bf16[1,1,4,64,3584]{4,3,2,1,0:T(8,128)(2,1)} %param.5) | copy-start | bytes 5505028
  12.8 37.3 %all-to-all-start = ((bf16[8,64,1024]{2,1,0:T(8,128)(2,1)}), bf16[8,64,1024]{2,1,0:T(8,128)(2,1)}, u32[]{:S(2)}, u32[]{:S(2)}) async-start(bf16[8,64,1024]{2,1,0:T(8,128)(2,1)} %bitcast.6), calls=%async_computation | async-start | bytes 2097152 | tf_op jit(solution)/shard_map/all_to_all | solution.py:258
  21.2 32.3 %copy-start.1 = (bf16[64,8,1024]{2,1,0:T(8,128)(2,1)S(1)}, bf16[64,8,1024]{2,1,0:T(8,128)(2,1)}, u32[]{:S(2)}) copy-start(bf16[64,8,1024]{2,1,0:T(8,128)(2,1)} %param.9) | copy-start | bytes 3145732
  22.3 32.9 %copy-start.3 = (s32[4]{0:T(128)}, s32[4]{0:T(128)S(1)}, u32[]{:S(2)}) copy-start(s32[4]{0:T(128)S(1)} %pad_add_fusion.pos_ref) | copy-start | bytes 52
  24.0 14.1 %collective-permute-start.4 = (bf16[272,896]{1,0:T(8,128)(2,1)S(1)}, bf16[272,896]{1,0:T(8,128)(2,1)S(1)}, u32[]{:S(2)}, u32[]{:S(2)}) collective-permute-start(bf16[272,896]{1,0:T(8,128)(2,1)S(1)} %get-tuple-element.19), channel_id=1, source_target_pairs={{0,1},{1,2},{2,3},{3,0},{4,5},{5,6},{6,7},{7,4},{8,9},{9,10},{10,1... | collective-permute-start | bytes 1462280 | tf_op jit(solution)/shard_map/ppermute | solution.py:18
  25.6 24.5 %collective-permute-start.5 = (bf16[272,896]{1,0:T(8,128)(2,1)}, bf16[272,896]{1,0:T(8,128)(2,1)S(1)}, u32[]{:S(2)}, u32[]{:S(2)}) collective-permute-start(bf16[272,896]{1,0:T(8,128)(2,1)} %get-tuple-element.21), channel_id=1, source_target_pairs={{0,2},{1,3},{2,0},{3,1},{4,6},{5,7},{6,4},{7,5},{8,10},{9,11},{10,... | collective-permute-start | bytes 1462280 | tf_op jit(solution)/shard_map/ppermute | solution.py:18
  28.5 21.6 %collective-permute-start.6 = (bf16[272,896]{1,0:T(8,128)(2,1)}, bf16[272,896]{1,0:T(8,128)(2,1)S(1)}, u32[]{:S(2)}, u32[]{:S(2)}) collective-permute-start(bf16[272,896]{1,0:T(8,128)(2,1)} %get-tuple-element.22), channel_id=1, source_target_pairs={{0,3},{1,0},{2,1},{3,2},{4,7},{5,4},{6,5},{7,6},{8,11},{9,8},{10,9... | collective-permute-start | bytes 1462280 | tf_op jit(solution)/shard_map/ppermute | solution.py:18
  52.0 32.9 %collective-permute-start.9 = (bf16[4,256,896]{2,1,0:T(8,128)(2,1)}, bf16[4,256,896]{2,1,0:T(8,128)(2,1)}, u32[]{:S(2)}, u32[]{:S(2)}) collective-permute-start(bf16[4,256,896]{2,1,0:T(8,128)(2,1)} %get-tuple-element.26.refs_8_), channel_id=1, source_target_pairs={{0,4},{4,8},{8,12},{12,0},{64,76},{68,64},{72,68},{76,72},{1,5},{5... | collective-permute-start | bytes 5505032 | tf_op jit(solution)/shard_map/ppermute | solution.py:24
  55.2 33.1 %all-to-all-start.1 = ((bf16[8,64,1024]{2,1,0:T(8,128)(2,1)}), bf16[8,64,1024]{2,1,0:T(8,128)(2,1)S(1)}, u32[]{:S(2)}, u32[]{:S(2)}) async-start(bf16[8,64,1024]{2,1,0:T(8,128)(2,1)} %bitcast.7), calls=%async_computation.1 | async-start | bytes 2097152 | tf_op jit(solution)/shard_map/all_to_all | solution.py:269
  61.6 168.1 %reduce-scatter.2.cloned.1.call-start = ((), (), s32[]{:S(2)}) async-start(), calls=%async_computation.4 | async-start | bytes 4128768 | tf_op jit(solution)/shard_map/reduce_scatter | solution.py:287
  61.6 25.7 %collective-permute-start.2 = (bf16[8,64,1024]{2,1,0:T(8,128)(2,1)}, bf16[8,64,1024]{2,1,0:T(8,128)(2,1)S(1)}, u32[]{:S(2)}, u32[]{:S(2)}) collective-permute-start(bf16[8,64,1024]{2,1,0:T(8,128)(2,1)} %all-to-all-done.refs_0_), channel_id=1, source_target_pairs={{0,3},{1,0},{2,1},{3,2},{64,65},{65,66},{66,67},{67,64},{4,7},{5,4... | collective-permute-start | bytes 3145736 | tf_op jit(solution)/shard_map/ppermute | solution.py:24
  64.0 24.4 %collective-permute-start = (bf16[8,64,1024]{2,1,0:T(8,128)(2,1)}, bf16[8,64,1024]{2,1,0:T(8,128)(2,1)}, u32[]{:S(2)}, u32[]{:S(2)}) collective-permute-start(bf16[8,64,1024]{2,1,0:T(8,128)(2,1)} %all-to-all-done.refs_0_), channel_id=1, source_target_pairs={{0,1},{1,2},{2,3},{3,0},{64,67},{65,64},{66,65},{67,66},{4,5},{5,6... | collective-permute-start | bytes 3145736 | tf_op jit(solution)/shard_map/ppermute | solution.py:24
  64.0 40.0 %collective-permute-start.11 = (bf16[4,256,896]{2,1,0:T(8,128)(2,1)}, bf16[4,256,896]{2,1,0:T(8,128)(2,1)S(1)}, u32[]{:S(2)}, u32[]{:S(2)}) collective-permute-start(bf16[4,256,896]{2,1,0:T(8,128)(2,1)} %get-tuple-element.26.refs_8_), channel_id=1, source_target_pairs={{0,12},{4,0},{8,4},{12,8},{64,68},{68,72},{72,76},{76,64},{1,13},{... | collective-permute-start | bytes 5505032 | tf_op jit(solution)/shard_map/ppermute | solution.py:24
  84.9 30.0 %collective-permute-start.10 = (bf16[4,256,896]{2,1,0:T(8,128)(2,1)}, bf16[4,256,896]{2,1,0:T(8,128)(2,1)}, u32[]{:S(2)}, u32[]{:S(2)}) collective-permute-start(bf16[4,256,896]{2,1,0:T(8,128)(2,1)} %collective-permute-done.9.refs_9_), channel_id=1, source_target_pairs={{0,4},{4,8},{8,12},{12,0},{64,76},{68,64},{72,68},{76,72},{1,5},{5... | collective-permute-start | bytes 5505032 | tf_op jit(solution)/shard_map/ppermute | solution.py:24
  87.3 41.7 %collective-permute-start.12 = (bf16[4,256,896]{2,1,0:T(8,128)(2,1)}, bf16[4,256,896]{2,1,0:T(8,128)(2,1)}, u32[]{:S(2)}, u32[]{:S(2)}) collective-permute-start(bf16[4,256,896]{2,1,0:T(8,128)(2,1)} %get-tuple-element.26.refs_8_), channel_id=1, source_target_pairs={{0,64},{64,0},{1,65},{65,1},{2,66},{66,2},{3,67},{67,3},{4,68},{68... | collective-permute-start | bytes 5505032 | tf_op jit(solution)/shard_map/ppermute | solution.py:18
  87.3 1.0 copy-start.8
  88.3 66.3 %copy-start.5 = (bf16[8,64,1024]{2,1,0:T(8,128)(2,1)}, bf16[8,64,1024]{2,1,0:T(8,128)(2,1)S(1)}, u32[]{:S(2)}) copy-start(bf16[8,64,1024]{2,1,0:T(8,128)(2,1)S(1)} %all-to-all-done.1.refs_4_) | copy-start | bytes 3145732
  88.3 17.2 %collective-permute-start.3 = (bf16[8,64,1024]{2,1,0:T(8,128)(2,1)S(1)}, bf16[8,64,1024]{2,1,0:T(8,128)(2,1)S(1)}, u32[]{:S(2)}, u32[]{:S(2)}) collective-permute-start(bf16[8,64,1024]{2,1,0:T(8,128)(2,1)S(1)} %all-to-all-done.1.refs_4_), channel_id=1, source_target_pairs={{0,1},{1,2},{2,3},{3,0},{64,67},{65,64},{66,65},{67,66},{4,5},{5,6... | collective-permute-start | bytes 3145736 | tf_op jit(solution)/shard_map/ppermute | solution.py:24
  91.7 39.7 %collective-permute-start.1 = (bf16[8,64,1024]{2,1,0:T(8,128)(2,1)}, bf16[8,64,1024]{2,1,0:T(8,128)(2,1)}, u32[]{:S(2)}, u32[]{:S(2)}) collective-permute-start(bf16[8,64,1024]{2,1,0:T(8,128)(2,1)} %collective-permute-done.refs_1_), channel_id=1, source_target_pairs={{0,1},{1,2},{2,3},{3,0},{64,67},{65,64},{66,65},{67,66},{4,5},{5,6... | collective-permute-start | bytes 3145736 | tf_op jit(solution)/shard_map/ppermute | solution.py:24
  104.0 50.7 %copy-start.7 = (bf16[4,256,896]{2,1,0:T(8,128)(2,1)}, bf16[4,256,896]{2,1,0:T(8,128)(2,1)S(1)}, u32[]{:S(2)}) copy-start(bf16[4,256,896]{2,1,0:T(8,128)(2,1)S(1)} %collective-permute-done.11.refs_11_) | copy-start | bytes 5505028
  104.0 50.6 %collective-permute-start.15 = (bf16[4,256,896]{2,1,0:T(8,128)(2,1)S(1)}, bf16[4,256,896]{2,1,0:T(8,128)(2,1)}, u32[]{:S(2)}, u32[]{:S(2)}) collective-permute-start(bf16[4,256,896]{2,1,0:T(8,128)(2,1)S(1)} %collective-permute-done.11.refs_11_), channel_id=1, source_target_pairs={{0,64},{64,0},{1,65},{65,1},{2,66},{66,2},{3,67},{67,3},{4,68},{68... | collective-permute-start | bytes 5505032 | tf_op jit(solution)/shard_map/ppermute | solution.py:18
  105.6 9.3 %copy-start.9 = (bf16[8,64,1024]{2,1,0:T(8,128)(2,1)}, bf16[8,64,1024]{2,1,0:T(8,128)(2,1)S(1)}, u32[]{:S(2)}) copy-start(bf16[8,64,1024]{2,1,0:T(8,128)(2,1)S(1)} %collective-permute-done.3.refs_5_) | copy-start | bytes 3145732
  105.6 49.1 %collective-permute-start.13 = (bf16[4,256,896]{2,1,0:T(8,128)(2,1)}, bf16[4,256,896]{2,1,0:T(8,128)(2,1)}, u32[]{:S(2)}, u32[]{:S(2)}) collective-permute-start(bf16[4,256,896]{2,1,0:T(8,128)(2,1)} %collective-permute-done.9.refs_9_), channel_id=1, source_target_pairs={{0,64},{64,0},{1,65},{65,1},{2,66},{66,2},{3,67},{67,3},{4,68},{68... | collective-permute-start | bytes 5505032 | tf_op jit(solution)/shard_map/ppermute | solution.py:18
  114.9 39.8 %collective-permute-start.14 = (bf16[4,256,896]{2,1,0:T(8,128)(2,1)}, bf16[4,256,896]{2,1,0:T(8,128)(2,1)}, u32[]{:S(2)}, u32[]{:S(2)}) collective-permute-start(bf16[4,256,896]{2,1,0:T(8,128)(2,1)} %collective-permute-done.10.refs_10_), channel_id=1, source_target_pairs={{0,64},{64,0},{1,65},{65,1},{2,66},{66,2},{3,67},{67,3},{4,68},{68... | collective-permute-start | bytes 5505032 | tf_op jit(solution)/shard_map/ppermute | solution.py:18
  129.1 25.5 %collective-permute-start.8 = (bf16[8,64,1024]{2,1,0:T(8,128)(2,1)S(1)}, bf16[8,64,1024]{2,1,0:T(8,128)(2,1)}, u32[]{:S(2)}, u32[]{:S(2)}) collective-permute-start(bf16[8,64,1024]{2,1,0:T(8,128)(2,1)S(1)} %all-to-all-done.1.refs_4_), channel_id=1, source_target_pairs={{0,3},{1,0},{2,1},{3,2},{64,65},{65,66},{66,67},{67,64},{4,7},{5,4... | collective-permute-start | bytes 3145736 | tf_op jit(solution)/shard_map/ppermute | solution.py:24
  131.4 23.3 %collective-permute-start.7 = (bf16[8,64,1024]{2,1,0:T(8,128)(2,1)}, bf16[8,64,1024]{2,1,0:T(8,128)(2,1)}, u32[]{:S(2)}, u32[]{:S(2)}) collective-permute-start(bf16[8,64,1024]{2,1,0:T(8,128)(2,1)} %copy-done.9), channel_id=1, source_target_pairs={{0,1},{1,2},{2,3},{3,0},{64,67},{65,64},{66,65},{67,66},{4,5},{5,6... | collective-permute-start | bytes 3145736 | tf_op jit(solution)/shard_map/ppermute | solution.py:24
  182.7 58.2 %copy-start.4 = (s32[4]{0:T(128)S(1)}, s32[4]{0:T(128)}, u32[]{:S(2)}) copy-start(s32[4]{0:T(128)} %copy-done.3) | copy-start | bytes 52
  230.7 6.1 %collective-permute-start.18 = (bf16[64,896]{1,0:T(8,128)(2,1)S(1)}, bf16[64,896]{1,0:T(8,128)(2,1)S(1)}, u32[]{:S(2)}, u32[]{:S(2)}) collective-permute-start(bf16[64,896]{1,0:T(8,128)(2,1)S(1)} %get-tuple-element.27), channel_id=1, source_target_pairs={{0,1},{1,2},{2,3},{3,0},{64,67},{65,64},{66,65},{67,66},{4,5},{5,6... | collective-permute-start | bytes 344072 | tf_op jit(solution)/shard_map/ppermute | solution.py:24
  232.3 8.5 %collective-permute-start.17 = (bf16[64,896]{1,0:T(8,128)(2,1)S(1)}, bf16[64,896]{1,0:T(8,128)(2,1)S(1)}, u32[]{:S(2)}, u32[]{:S(2)}) collective-permute-start(bf16[64,896]{1,0:T(8,128)(2,1)S(1)} %get-tuple-element.28), channel_id=1, source_target_pairs={{0,2},{1,3},{2,0},{3,1},{64,66},{65,67},{66,64},{67,65},{4,6},{5,7... | collective-permute-start | bytes 344072 | tf_op jit(solution)/shard_map/ppermute | solution.py:24
  235.0 5.8 %collective-permute-start.16 = (bf16[64,896]{1,0:T(8,128)(2,1)S(1)}, bf16[64,896]{1,0:T(8,128)(2,1)S(1)}, u32[]{:S(2)}, u32[]{:S(2)}) collective-permute-start(bf16[64,896]{1,0:T(8,128)(2,1)S(1)} %get-tuple-element.29), channel_id=1, source_target_pairs={{0,3},{1,0},{2,1},{3,2},{64,65},{65,66},{66,67},{67,64},{4,7},{5,4... | collective-permute-start | bytes 344072 | tf_op jit(solution)/shard_map/ppermute | solution.py:24
Sparse Core Ops, SparseCore 0:
  182.8 46.7 reduce-scatter.1

commit v7 on v6

v7 whole, which is shorter than its diff:
```python
import functools
import jax
import jax.numpy as jnp
from jax import lax
from jax.experimental import pallas as pl
from jax.experimental.pallas import tpu as pltpu
from jax.sharding import Mesh, PartitionSpec as P

AXES = ("zl", "c", "zh", "x", "y")
Z = ("zh", "zl")
VMEM = pl.BlockSpec(memory_space=pltpu.VMEM)
SMEM = pl.BlockSpec(memory_space=pltpu.SMEM)
BESIDE = 60_000_000_000
PARAMS = pltpu.CompilerParams(vmem_limit_bytes=48 << 20)


def shifted(value, axis, steps):
    count = lax.axis_size(axis)
    return lax.ppermute(value, axis, [(i, (i + steps) % count) for i in range(count)])


def mirrored(value, axis, steps):
    cores, count = lax.axis_size("c"), lax.axis_size(axis)
    pairs = [(c * count + i, c * count + (i + (1 - 2 * c) * steps) % count) for c in range(cores) for i in range(count)]
    return lax.ppermute(value, ("c", axis), pairs)


def after(value, *others):
    return lax.optimization_barrier((value, *others))[0]


def cost(flops, *arrays):
    size = sum(a.size * a.dtype.itemsize for a in arrays)
    return pl.CostEstimate(flops=flops, bytes_accessed=size, transcendentals=0)


def split_kernel(pos_ref, w_ref, gate_ref, row_ref, *out_refs):
    count = len(out_refs)
    exp_train, depth, _ = w_ref.shape
    groups, slots = gate_ref.shape
    size, width = exp_train * depth, out_refs[0].shape[1]
    gate = gate_ref[...]
    high = gate.astype(jnp.bfloat16)
    low = (gate - high.astype(jnp.float32)).astype(jnp.bfloat16)
    for d, out_ref in enumerate(out_refs):
        start = pl.multiple_of(lax.rem(pos_ref[2] + d, count) * width, 128)
        out_ref[:size] = w_ref[:, :, pl.ds(start, width)].reshape(size, width)
        out_ref[size:] = jnp.zeros((groups, width), jnp.bfloat16)
        for part, value in enumerate((high, low, row_ref[...].astype(jnp.bfloat16))):
            out_ref[size:, part * slots:(part + 1) * slots] = value


def split_blocks(pos, own, gate, row, count):
    exp_train, depth, width = own.shape
    shape = jax.ShapeDtypeStruct((exp_train * depth + gate.shape[0], width // count), own.dtype)
    return pl.pallas_call(
        split_kernel, out_shape=[shape] * count, in_specs=[SMEM] + [VMEM] * 3, out_specs=[VMEM] * count,
        compiler_params=PARAMS, cost_estimate=cost(0, own, own),
    )(pos, own, gate, row)


def join_kernel(pos_ref, *refs):
    *in_refs, out_ref, info_ref = refs
    count = len(in_refs)
    exp_train, hidden, width = out_ref.shape
    depth = hidden // count
    size, lanes = exp_train * depth, info_ref.shape[2]
    for d, in_ref in enumerate(in_refs):
        start = pl.multiple_of(lax.rem(pos_ref[2] + count - d, count) * depth, depth)
        out_ref[:, pl.ds(start, depth), :] = in_ref[:size].reshape(exp_train, depth, width)
        info_ref[d] = in_ref[size:, :lanes]


def join_blocks(pos, blocks, exp_train, depth, lanes):
    total, width = blocks[0].shape
    count = len(blocks)
    shape = jax.ShapeDtypeStruct((exp_train, depth * count, width), blocks[0].dtype)
    info = jax.ShapeDtypeStruct((count, total - exp_train * depth, lanes), blocks[0].dtype)
    return pl.pallas_call(
        join_kernel, out_shape=[shape, info], in_specs=[SMEM] + [VMEM] * count, out_specs=[VMEM] * 2,
        compiler_params=PARAMS, cost_estimate=cost(0, shape, shape),
    )(pos, *blocks)


def dispatch_kernel(groups, whole, first_ref, flat_ref, hidden_ref, out_ref):
    slots, pairs = out_ref.shape[1], flat_ref.shape[1]
    number = lax.broadcasted_iota(jnp.int32, (groups * slots, pairs), 0)
    number = number // slots * whole + lax.rem(number, slots) + first_ref[0]
    chosen = jnp.where(number == flat_ref[...], 1.0, 0.0).astype(jnp.bfloat16)
    rows = jnp.dot(chosen, hidden_ref[...], preferred_element_type=jnp.float32).astype(jnp.bfloat16)
    out_ref[...] = rows.reshape(out_ref.shape)


def dispatch(first, slots, whole, flat, hidden, groups, beside=0):
    shape = jax.ShapeDtypeStruct((groups, slots, hidden.shape[1]), hidden.dtype)
    return pl.pallas_call(
        functools.partial(dispatch_kernel, groups, whole),
        out_shape=shape, in_specs=[SMEM, VMEM, VMEM], out_specs=VMEM,
        compiler_params=PARAMS, cost_estimate=cost(2 * groups * slots * hidden.size + beside, hidden, shape),
    )(jnp.full((1,), first, jnp.int32), flat, hidden)


def gates_kernel(info_ref, out_ref):
    shifts, cores, planes, _ = info_ref.shape
    slots = out_ref.shape[3] // 2
    out_ref[...] = jnp.zeros_like(out_ref)
    for d in range(shifts):
        for core in range(cores):
            info = info_ref[d, core].astype(jnp.float32)
            high, low, row = (info[:, i * slots:(i + 1) * slots] for i in range(3))
            for part, place, value in ((0, 0, high), (0, 1, high), (1, 0, low), (2, 0, row), (2, 1, row)):
                out_ref[core, part, d * planes:(d + 1) * planes, place * slots:(place + 1) * slots] = value


def gates_call(info, slots):
    shifts, cores, planes, _ = info.shape
    shape = jax.ShapeDtypeStruct((cores, 3, shifts * planes, 2 * slots), jnp.float32)
    return pl.pallas_call(
        gates_kernel, out_shape=shape, in_specs=[VMEM], out_specs=VMEM,
        compiler_params=PARAMS, cost_estimate=cost(BESIDE, info, shape),
    )(info)


def experts_kernel(core, turns, pos_ref, *refs):
    x_refs = refs[:turns], refs[turns:2 * turns]
    w_ref, gate_ref, *refs = refs[2 * turns:]
    last = core == 1
    sums_ref, out_ref = refs[:2] if last else (None, refs[0])
    x_all, w_all, p_all, sums, out_all, x_sem, w_sem, sum_sem, out_sem = refs[1 + last:]
    _, _, planes, part_slots, hidden_width = x_all.shape
    blocks, experts, depth, width = w_ref.shape
    rows = sums.shape[2]
    slots = p_all.shape[1] // 2
    capacity = slots // experts
    c = pos_ref[1]
    group = lax.rem(c + core, 2)

    def x_copy(part, turn):
        source = x_refs[part][turn].at[:, pl.ds(pl.multiple_of(group * part_slots, part_slots), part_slots), :]
        return pltpu.make_async_copy(source, x_all.at[part, turn], x_sem.at[part, turn])

    def w_copy(k, d):
        return pltpu.make_async_copy(w_ref.at[d, k], w_all.at[k, pl.ds(d * depth, depth), :], w_sem.at[k, d])

    def sum_copy(turn):
        return pltpu.make_async_copy(sums_ref.at[turn], sums.at[turn], sum_sem.at[turn])

    def out_copy(turn):
        if last:
            return pltpu.make_async_copy(out_all.at[turn], out_ref.at[:, turn], out_sem.at[turn])
        return pltpu.make_async_copy(sums.at[turn], out_ref.at[turn], out_sem.at[turn])

    for k in range(experts):
        if k % 2 == 0:
            for turn in range(turns):
                x_copy(k // 2, turn).start()
        for d in range(blocks):
            w_copy(k, d).start()
    if last:
        for turn in range(turns):
            sum_copy(turn).start()

    def multiply(k, _):
        for part in range(2):
            @pl.when(k == 2 * part)
            def _(part=part):
                for turn in range(turns):
                    x_copy(part, turn).wait()
        for d in range(blocks):
            w_copy(k, d).wait()
        start = pl.multiple_of(lax.rem(k, 2) * capacity, capacity)
        block = x_all[k // 2, :, :, pl.ds(start, capacity), :].reshape(turns * planes * capacity, hidden_width)
        total = jnp.dot(block, w_all[k], preferred_element_type=jnp.float32)
        high = total.astype(jnp.bfloat16)
        low = (total - high.astype(jnp.float32)).astype(jnp.bfloat16)
        for segment, value in enumerate((high, low)):
            place = pl.multiple_of(segment * slots + k * capacity, capacity)
            p_all[:, pl.ds(place, capacity), :] = value.reshape(turns * planes, capacity, width)
        return 0

    lax.fori_loop(0, experts, multiply, 0)
    number = lax.broadcasted_iota(jnp.int32, (rows, 2 * slots), 0).astype(jnp.float32)

    def combine(turn, _):
        shift = lax.rem(turn * (1 + 2 * c), turns)
        if last:
            sum_copy(turn).wait()

        def one(plane, _):
            index = pl.ds(shift * planes + plane, 1)
            mine = number == gate_ref[group, 2, index, :]
            high, low = (jnp.where(mine, gate_ref[group, part, index, :], 0.0) for part in range(2))
            weights = jnp.concatenate([high, low], 0).astype(jnp.bfloat16)
            mixed = jnp.dot(weights, p_all[turn * planes + plane], preferred_element_type=jnp.float32)
            mixed = mixed[:rows] + mixed[rows:]
            if last:
                out_all[turn, plane] = (sums[turn, plane] + mixed).astype(out_all.dtype)
            else:
                sums[turn, plane] = mixed
            return 0

        lax.fori_loop(0, planes, one, 0, unroll=2)
        out_copy(turn).start()
        return 0

    lax.fori_loop(0, turns, combine, 0)
    for turn in range(turns):
        out_copy(turn).wait()


def experts_call(core, pos, xs, weight, gate, rows, sums=None):
    turns = len(xs[0])
    blocks, experts, depth, width = weight.shape
    planes, part_slots, hidden_width = xs[0][0].shape
    part_slots = part_slots // 2
    slots = 2 * part_slots
    total = jax.ShapeDtypeStruct((turns, planes, rows, width), jnp.float32)
    out = jax.ShapeDtypeStruct((planes, turns, rows, width), jnp.bfloat16) if core else total
    hbm = pl.BlockSpec(memory_space=pl.ANY)
    arrays = [*xs[0], *xs[1], weight]
    flops = 2 * turns * planes * slots * hidden_width * width
    bf16 = lambda *shape: pltpu.VMEM(shape, jnp.bfloat16)
    given = [] if sums is None else [sums]
    return pl.pallas_call(
        functools.partial(experts_kernel, core, turns),
        out_shape=out,
        in_specs=[SMEM] + [hbm] * len(arrays) + [VMEM] + [hbm] * len(given),
        out_specs=hbm,
        scratch_shapes=[
            bf16(2, turns, planes, part_slots, hidden_width),
            bf16(experts, blocks * depth, width),
            bf16(turns * planes, 2 * slots, width),
            pltpu.VMEM(total.shape, jnp.float32),
            bf16(turns, planes, rows, width),
            pltpu.SemaphoreType.DMA((2, turns)),
            pltpu.SemaphoreType.DMA((experts, blocks)),
            pltpu.SemaphoreType.DMA((turns,)),
            pltpu.SemaphoreType.DMA((turns,)),
        ],
        compiler_params=PARAMS,
        cost_estimate=cost(flops, *arrays, total, out),
    )(pos, *arrays, gate, *given)


def place_kernel(pos_ref, *refs):
    in_refs, out_ref = refs[:-1], refs[-1]
    width = in_refs[0].shape[1]
    for d, in_ref in enumerate(in_refs):
        turned = lax.rem(pos_ref[2] + d * (1 + 2 * pos_ref[1]), len(in_refs))
        start = pl.multiple_of(turned * width, 128)
        out_ref[:, pl.ds(start, width)] = in_ref[...]


def place_blocks(pos, blocks):
    rows, width = blocks[0].shape
    shape = jax.ShapeDtypeStruct((rows, width * len(blocks)), blocks[0].dtype)
    return pl.pallas_call(
        place_kernel, out_shape=shape, in_specs=[SMEM] + [VMEM] * len(blocks), out_specs=VMEM,
        compiler_params=PARAMS, cost_estimate=cost(0, shape, shape),
    )(pos, *blocks)


def per_device(trainer_weight, owner, expert_ids, gates, hidden):
    experts = owner.shape[0]
    rows, fanout = expert_ids.shape
    hidden_width = hidden.shape[2]
    capacity = min(rows, 2 * rows * fanout // experts)
    own = trainer_weight[0, 0]
    exp_train, slice_rows, width = own.shape
    ny = lax.axis_size("y")
    groups = experts // exp_train
    slots = exp_train * capacity
    block_width = width // ny
    low = lax.axis_size("zl")
    z, c, y = lax.axis_index("zh") * low + lax.axis_index("zl"), lax.axis_index("c"), lax.axis_index("y")
    pos = jnp.stack([z, c, y, lax.axis_index("x")]).astype(jnp.int32)

    zl, cs, zh = (lax.axis_size(a) for a in ("zl", "c", "zh"))
    slot_of = owner.reshape(zl, cs, zh, exp_train).transpose(2, 0, 1, 3).reshape(experts)
    match = expert_ids[:, :, None] == slot_of[None, None, :]
    named = jnp.any(match, axis=1)
    position = jnp.cumsum(named.astype(jnp.int32), axis=0) - 1
    place = jnp.arange(experts, dtype=jnp.int32)[None, :] * capacity + position
    flat = jnp.sum(jnp.where(match, place[:, None, :], 0), axis=2).reshape(1, -1)
    pairs = hidden.reshape(-1, hidden_width)

    planes = groups // 2
    half = exp_train // 2
    send = lambda first, flat, beside=0: dispatch(
        first * capacity, half * capacity, slots, flat, pairs, groups, beside
    ).reshape(planes, -1, hidden_width)
    first = lax.all_to_all(send(0, flat), Z, 0, 0, tiled=True)

    chosen = jnp.arange(experts * capacity, dtype=jnp.int32)[:, None] == flat
    pair_row = jnp.arange(rows * fanout, dtype=jnp.int32) // fanout
    slot_gate = jnp.sum(jnp.where(chosen, gates.reshape(-1)[None, :], 0.0), axis=1).reshape(groups, slots)
    slot_row = jnp.sum(jnp.where(chosen, pair_row[None, :] + 1, 0), axis=1).reshape(groups, slots) - 1

    by_core = lambda v: v.astype(jnp.float32).reshape(planes, 2, slots).transpose(1, 0, 2).reshape(groups, slots)
    blocks = split_blocks(pos, own, by_core(slot_gate), by_core(slot_row), ny)
    blocks = [blocks[0]] + [shifted(blocks[d], "y", d) for d in range(1, ny)]
    blocks[1] = after(blocks[1], first)
    joined, info = join_blocks(pos, blocks, exp_train, slice_rows, 4 * slots)
    weight = lax.all_gather(joined, "x")

    first_up, first_down = mirrored(first, "y", 1), mirrored(first, "y", -1)
    second = lax.all_to_all(send(half, after(flat, first, joined), BESIDE), Z, 0, 0, tiled=True)
    first_opposite = mirrored(after(first_up, first_down), "y", 1)
    second_late = after(second, first_opposite)
    second_up, second_down = mirrored(second_late, "y", 1), mirrored(second_late, "y", -1)
    info = lax.all_to_all(after(info, second).reshape(ny, 2, planes, 4 * slots), Z, 2, 2, tiled=True)
    gate = gates_call(info, slots)
    second_opposite = mirrored(after(second_up, second_down), "y", 1)
    other_weight = shifted(after(weight, second_opposite, gate), "c", 1)

    xs = [first, first_up, first_opposite, first_down], [second, second_up, second_opposite, second_down]
    sums = experts_call(0, pos, xs, weight, gate, rows)
    partial = experts_call(1, pos, xs, other_weight, gate, rows, sums).reshape(-1, block_width)
    summed = lax.psum_scatter(partial, Z, scatter_dimension=0, tiled=True).reshape(ny, rows, block_width)
    final = [summed[0]] + [mirrored(summed[d], "y", -d) for d in range(1, ny)]
    return place_blocks(pos, final)


def solution(mesh):
    devices = mesh.devices.reshape(2, 2, 4, 4, 4)
    inner = Mesh(devices, AXES)
    rep, exp = ("zl", "c"), ("zh", "x", "y")
    return jax.shard_map(
        per_device,
        mesh=inner,
        in_specs=(
            P(rep, exp, None, None, None),
            P(),
            P(rep + exp, None),
            P(rep + exp, None),
            P(rep + exp, None, None),
        ),
        out_specs=P(rep + exp, None),
        check_vma=False,
    )
```

time: 251 us -> 243 us (0.968)
  waiting for transfers between devices: 135 us -> 126 us
  local copies, waits for them, and re-layouts: 6.4 us -> 15 us
  starting transfers between devices: 40.6 us -> 33.4 us
    ppermute x12 -> x9, waiting for transfers between devices: 67.8 us -> 45.7 us  [mirrored(): return lax.ppermute(value, ('c', axis), pairs)]
    all_to_all x2, waiting for transfers between devices: 11.9 us -> 22.1 us  [the longest x1 12 us: per_device(): lax.all_to_all(send(half, after(flat, first, joined), BESIDE), Z, 0, 0, t...]
    unnamed x22 -> x30, local copies, waits for them, and re-layouts: 3.08 us -> 12.6 us
    ppermute x12 -> x9, starting transfers between devices: 19.9 us -> 12.2 us  [mirrored(): return lax.ppermute(value, ('c', axis), pairs)]
    pallas_call x1 -> x3, Pallas kernels: 28 us -> 28.4 us  [the longest x2 28.4 us: experts_call(): pl.pallas_call(functools.partial(experts_kernel, core, turns), out_shape=...]
    ppermute x7 -> x4, waiting for transfers between devices: 8.33 us -> 8.71 us  [shifted(): lax.ppermute(value, axis, [(i, (i + steps) % count) for i in range(count)])]
    ppermute x7 -> x4, starting transfers between devices: 5.84 us -> 5.83 us  [shifted(): lax.ppermute(value, axis, [(i, (i + steps) % count) for i in range(count)])]
  transfers between devices with their start and end apart: 22 -> 17, of which waited for: 10 -> 12; matrix products, arithmetic and copies ran while one was open for 1% -> 0% of each run, Pallas kernels for 1% -> 7%
where the time goes in v7:
time: 243 us; the launch traced here: 242 us
  waiting for transfers between devices  126 us (52%)
  Pallas kernels  36.4 us (15%)
  starting transfers between devices  33.4 us (14%)
  blocking collectives  15.8 us (7%)
  local copies, waits for them, and re-layouts  15 us (6%)
  between operations  13.6 us (6%)
    reduce_scatter x1, waiting for transfers between devices, per_device(): lax.psum_scatter(partial, Z, scatter_dimension=0, tiled=True)  49.2 us
    ppermute x9, waiting for transfers between devices, mirrored(): return lax.ppermute(value, ('c', axis), pairs)  45.7 us
    pallas_call x2, Pallas kernels, experts_call(): pl.pallas_call(functools.partial(experts_kernel, core, turns), out_shape=...  28.4 us
    all_to_all x1, blocking collectives, per_device(): lax.all_to_all(after(info, second).reshape(ny, 2, planes, 4 * slots), Z,...  15.8 us
    unnamed x30, local copies, waits for them, and re-layouts  12.6 us
    ppermute x9, starting transfers between devices, mirrored(): return lax.ppermute(value, ('c', axis), pairs)  12.2 us
    all_to_all x1, waiting for transfers between devices, per_device(): lax.all_to_all(send(half, after(flat, first, joined), BESIDE), Z, 0, 0, t...  12 us
    all_to_all x1, waiting for transfers between devices, per_device(): first = lax.all_to_all(send(0, flat), Z, 0, 0, tiled=True)  10.2 us
  transfers between devices with their start and end apart: 17, of which 12 were waited for; matrix products, arithmetic and copies ran while one was open for 0% of the time, Pallas kernels for 7%

profile of v7, /device:TPU:2, one launch (start us, length us, event | category | flops | bytes accessed | tf_op | source)
XLA Modules:
  0.0 242.2 jit_solution(12014041831647021761)
XLA Ops:
  6.5 0.7 reshape.87
  7.3 0.1 eq.31
  7.4 0.8 copy.20
  8.2 0.2 compare_reduce_fusion
  8.4 0.1 reduce_window_sum.11
  8.5 1.2 fusion
  9.7 0.1 reshape.88.flat_ref
  9.8 1.2 copy-done.1
  11.0 1.7 shard_map.55
  12.7 8.5 %all-to-all-start = ((bf16[8,64,1024]{2,1,0:T(8,128)(2,1)}), bf16[8,64,1024]{2,1,0:T(8,128)(2,1)S(1)}, u32[]{:S(2)}, u32[]{:S(2)}) async-start(bf16[8,64,1024]{2,1,0:T(8,128)(2,1)} %bitcast.6), calls=%async_computation | async-start | bytes 2097152 | tf_op jit(solution)/shard_map/all_to_all | solution.py:292
  21.2 0.0 all-gather.3.cloned.1.call-start
  21.3 0.1 eq.35
  21.4 0.3 select_reduce_fusion
  21.7 0.1 convert_element_type.16
  21.8 0.1 copy.22
  21.8 0.1 broadcast_in_dim.45
  21.9 0.3 select_reduce_fusion.1
  22.2 0.1 reshape_reshape.3
  22.3 0.1 pad_add_fusion.pos_ref
  22.4 1.7 shard_map.56
  24.0 0.8 copy-done.4
  24.8 1.6 collective-permute-start.3
  26.4 2.9 %collective-permute-start.4 = (bf16[272,896]{1,0:T(8,128)(2,1)}, bf16[272,896]{1,0:T(8,128)(2,1)S(1)}, u32[]{:S(2)}, u32[]{:S(2)}) collective-permute-start(bf16[272,896]{1,0:T(8,128)(2,1)} %get-tuple-element.22), channel_id=1, source_target_pairs={{0,2},{1,3},{2,0},{3,1},{4,6},{5,7},{6,4},{7,5},{8,10},{9,11},{10,... | collective-permute-start | bytes 1462280 | tf_op jit(solution)/shard_map/ppermute | solution.py:19
  29.3 1.3 collective-permute-start.5
  30.7 8.3 %collective-permute-done.3.refs_1_ = bf16[272,896]{1,0:T(8,128)(2,1)S(1)} collective-permute-done((bf16[272,896]{1,0:T(8,128)(2,1)S(1)}, bf16[272,896]{1,0:T(8,128)(2,1)S(1)}, u32[]{:S(2)}, u32[]{:S(2)}) %collective-permute-start.3) | collective-permute-done | bytes 487456 | tf_op jit(solution)/shard_map/ppermute | solution.py:19
  39.0 0.8 copy-done.6
  39.8 10.2 %all-to-all-done.refs_0_ = bf16[8,64,1024]{2,1,0:T(8,128)(2,1)S(1)} async-done(((bf16[8,64,1024]{2,1,0:T(8,128)(2,1)}), bf16[8,64,1024]{2,1,0:T(8,128)(2,1)S(1)}, u32[]{:S(2)}, u32[]{:S(2)}) %all-to-all-start) | async-done | bytes 1048608 | tf_op jit(solution)/shard_map/all_to_all | solution.py:292
  49.9 0.4 collective-permute-done.4.refs_2_
  50.3 0.8 copy-done.8
  51.1 1.0 copy-done.5
  52.2 1.0 copy-done.7
  53.2 1.0 copy-done.9
  54.2 2.5 %shard_map.57 = (bf16[4,256,896]{2,1,0:T(8,128)(2,1)}, bf16[4,16,256]{2,1,0:T(8,128)(2,1)S(1)}) custom-call(s32[4]{0:T(128)S(1)} %pad_add_fusion.pos_ref, bf16[272,896]{1,0:T(8,128)(2,1)S(1)} %copy-done.5, bf16[272,896]{1,0:T(8,128)(2,1)S(1)} %copy-done.7, bf16[272,896]{1,0:T(8,128)(2,1)S(1)} %copy-done.9, bf16[272,896]{1,0:T(8,128)(2,1)} %collective-permute-done.5.refs_3_), custom_call_target="tpu_custom_call" | custom-call | bytes 3670016 | tf_op jit(solution)/shard_map/pallas_call | solution.py:79
  56.7 1.3 collective-permute-start
  58.0 2.0 collective-permute-start.1
  60.1 0.7 shard_map.58
  60.8 1.0 copy-done.3
  61.8 6.9 %all-to-all-start.1 = ((bf16[8,64,1024]{2,1,0:T(8,128)(2,1)}), bf16[8,64,1024]{2,1,0:T(8,128)(2,1)S(1)}, u32[]{:S(2)}, u32[]{:S(2)}) async-start(bf16[8,64,1024]{2,1,0:T(8,128)(2,1)} %bitcast.21), calls=%async_computation.1 | async-start | bytes 2097152 | tf_op jit(solution)/shard_map/all_to_all | solution.py:307
  68.6 0.0 reduce-scatter.2.cloned.1.call-start
  68.7 13.9 %collective-permute-done.refs_1_ = bf16[8,64,1024]{2,1,0:T(8,128)(2,1)S(1)} collective-permute-done((bf16[8,64,1024]{2,1,0:T(8,128)(2,1)S(1)}, bf16[8,64,1024]{2,1,0:T(8,128)(2,1)S(1)}, u32[]{:S(2)}, u32[]{:S(2)}) %collective-permute-start) | collective-permute-done | bytes 1048608 | tf_op jit(solution)/shard_map/ppermute | solution.py:25
  82.6 1.0 collective-permute-start.2
  83.6 12.0 %all-to-all-done.1.refs_4_ = bf16[8,64,1024]{2,1,0:T(8,128)(2,1)S(1)} async-done(((bf16[8,64,1024]{2,1,0:T(8,128)(2,1)}), bf16[8,64,1024]{2,1,0:T(8,128)(2,1)S(1)}, u32[]{:S(2)}, u32[]{:S(2)}) %all-to-all-start.1) | async-done | bytes 1048608 | tf_op jit(solution)/shard_map/all_to_all | solution.py:307
  95.6 3.1 %collective-permute-done.2.refs_2_ = bf16[8,64,1024]{2,1,0:T(8,128)(2,1)} collective-permute-done((bf16[8,64,1024]{2,1,0:T(8,128)(2,1)S(1)}, bf16[8,64,1024]{2,1,0:T(8,128)(2,1)}, u32[]{:S(2)}, u32[]{:S(2)}) %collective-permute-start.2) | collective-permute-done | bytes 1048608 | tf_op jit(solution)/shard_map/ppermute | solution.py:25
  98.7 3.2 %collective-permute-start.7 = (bf16[8,64,1024]{2,1,0:T(8,128)(2,1)S(1)}, bf16[8,64,1024]{2,1,0:T(8,128)(2,1)S(1)}, u32[]{:S(2)}, u32[]{:S(2)}) collective-permute-start(bf16[8,64,1024]{2,1,0:T(8,128)(2,1)S(1)} %all-to-all-done.1.refs_4_), channel_id=1, source_target_pairs={{0,3},{1,0},{2,1},{3,2},{64,65},{65,66},{66,67},{67,64},{4,7},{5,4... | collective-permute-start | bytes 3145736 | tf_op jit(solution)/shard_map/ppermute | solution.py:25
  102.0 15.8 %all_to_all.15 = bf16[4,2,8,256]{3,1,0,2:T(2,128)(2,1)S(1)} all-to-all(bf16[4,2,8,256]{3,1,0,2:T(2,128)(2,1)S(1)} %copy.25), channel_id=1, replica_groups=mesh['zl'=2,'c'=2,'zh'=4,'x'=4,'y'=4] {'zh','zl'}, dimensions={2} | all-to-all | bytes 65536 | tf_op jit(solution)/shard_map/all_to_all | solution.py:311
  117.8 7.9 %collective-permute-done.6.refs_5_ = bf16[8,64,1024]{2,1,0:T(8,128)(2,1)S(1)} collective-permute-done((bf16[8,64,1024]{2,1,0:T(8,128)(2,1)S(1)}, bf16[8,64,1024]{2,1,0:T(8,128)(2,1)S(1)}, u32[]{:S(2)}, u32[]{:S(2)}) %collective-permute-start.6) | collective-permute-done | bytes 1048608 | tf_op jit(solution)/shard_map/ppermute | solution.py:25
  125.8 0.1 collective-permute-start.8
  125.9 0.1 shard_map.59.refs_9_
  125.9 0.8 copy-done.11
  126.7 0.3 copy-done.12
  127.1 14.9 %collective-permute-done.8.refs_6_ = bf16[8,64,1024]{2,1,0:T(8,128)(2,1)} collective-permute-done((bf16[8,64,1024]{2,1,0:T(8,128)(2,1)S(1)}, bf16[8,64,1024]{2,1,0:T(8,128)(2,1)}, u32[]{:S(2)}, u32[]{:S(2)}) %collective-permute-start.8) | collective-permute-done | bytes 1048608 | tf_op jit(solution)/shard_map/ppermute | solution.py:25
  142.0 14.1 %shard_map.60.refs_10_ = f32[4,8,64,896]{3,2,1,0:T(8,128)} custom-call(s32[4]{0:T(128)S(1)} %pad_add_fusion.pos_ref, bf16[8,64,1024]{2,1,0:T(8,128)(2,1)S(1)} %all-to-all-done.refs_0_, bf16[8,64,1024]{2,1,0:T(8,128)(2,1)S(1)} %collective-permute-done.refs_1_, bf16[8,64,1024]{2,1,0:T(8,128)(2,1)} %collective-permute-done.2.refs_2_, ...), custom_call_target="tpu_custom_call" | custom-call | flops 3758096384 | bytes 30408704 | tf_op jit(solution)/shard_map/pallas_call | solution.py:224
  156.1 2.9 %copy-done.10 = bf16[4,4,256,896]{3,2,1,0:T(8,128)(2,1)} copy-done((bf16[4,4,256,896]{3,2,1,0:T(8,128)(2,1)}, bf16[4,4,256,896]{3,2,1,0:T(8,128)(2,1)S(1)}, u32[]{:S(2)}) %copy-start.10) | copy-done | bytes 7340056
  159.0 14.3 %shard_map.61 = bf16[8,4,64,896]{3,2,1,0:T(8,128)(2,1)} custom-call(s32[4]{0:T(128)S(1)} %pad_add_fusion.pos_ref, bf16[8,64,1024]{2,1,0:T(8,128)(2,1)S(1)} %all-to-all-done.refs_0_, bf16[8,64,1024]{2,1,0:T(8,128)(2,1)S(1)} %collective-permute-done.refs_1_, bf16[8,64,1024]{2,1,0:T(8,128)(2,1)} %collective-permute-done.2.refs_2_, ...), custom_call_target="tpu_custom_call" | custom-call | flops 3758096384 | bytes 26738688 | tf_op jit(solution)/shard_map/pallas_call | solution.py:224
  173.3 0.0 reduce-scatter.2.cloned.1.call-update
  173.3 49.2 %reduce-scatter.2.cloned.1.call-done = bf16[256,896]{1,0:T(8,128)(2,1)} async-done(((bf16[2048,896]{1,0:T(8,128)(2,1)}), bf16[256,896]{1,0:T(8,128)(2,1)}) %reduce-scatter.2.cloned.1.call-update) | async-done | bytes 458768 | tf_op jit(solution)/shard_map/reduce_scatter | solution.py:319
  222.5 1.1 fusion.5
  223.6 2.8 %collective-permute-start.10 = (bf16[64,896]{1,0:T(8,128)(2,1)S(1)}, bf16[64,896]{1,0:T(8,128)(2,1)S(1)}, u32[]{:S(2)}, u32[]{:S(2)}) collective-permute-start(bf16[64,896]{1,0:T(8,128)(2,1)S(1)} %get-tuple-element.33), channel_id=1, source_target_pairs={{0,3},{1,0},{2,1},{3,2},{64,65},{65,66},{66,67},{67,64},{4,7},{5,4... | collective-permute-start | bytes 344072 | tf_op jit(solution)/shard_map/ppermute | solution.py:25
  226.4 0.8 collective-permute-start.11
  227.3 0.9 collective-permute-start.12
  228.1 3.5 %collective-permute-done.10.refs_1_ = bf16[64,896]{1,0:T(8,128)(2,1)S(1)} collective-permute-done((bf16[64,896]{1,0:T(8,128)(2,1)S(1)}, bf16[64,896]{1,0:T(8,128)(2,1)S(1)}, u32[]{:S(2)}, u32[]{:S(2)}) %collective-permute-start.10) | collective-permute-done | bytes 114720 | tf_op jit(solution)/shard_map/ppermute | solution.py:25
  231.7 1.2 collective-permute-done.11.refs_2_
  232.8 1.2 collective-permute-done.12.refs_3_
  234.0 1.3 shard_map.62
  (34 shorter events, 0.1 us)
Async XLA Ops:
  9.8 1.2 copy-start.1
  11.0 10.7 %copy-start.13 = (f32[64,8]{0,1:T(8,128)S(1)}, f32[64,8]{0,1:T(8,128)}, u32[]{:S(2)}) copy-start(f32[64,8]{0,1:T(8,128)} %param.8) | copy-start | bytes 6148
  11.0 11.4 %copy-start = (bf16[1,1,4,64,3584]{4,3,2,1,0:T(8,128)(2,1)S(1)}, bf16[1,1,4,64,3584]{4,3,2,1,0:T(8,128)(2,1)}, u32[]{:S(2)}) copy-start(bf16[1,1,4,64,3584]{4,3,2,1,0:T(8,128)(2,1)} %param.5) | copy-start | bytes 5505028
  12.7 37.2 %all-to-all-start = ((bf16[8,64,1024]{2,1,0:T(8,128)(2,1)}), bf16[8,64,1024]{2,1,0:T(8,128)(2,1)S(1)}, u32[]{:S(2)}, u32[]{:S(2)}) async-start(bf16[8,64,1024]{2,1,0:T(8,128)(2,1)} %bitcast.6), calls=%async_computation | async-start | bytes 2097152 | tf_op jit(solution)/shard_map/all_to_all | solution.py:292
  21.2 120.7 %all-gather.3.cloned.1.call-start = ((), (), s32[]{:S(2)}) async-start(), calls=%async_computation.5 | async-start | bytes 9175040 | tf_op jit(solution)/shard_map/all_gather | solution.py:304
  24.0 0.8 copy-start.4
  24.8 35.2 %copy-start.2 = (bf16[64,8,1024]{2,1,0:T(8,128)(2,1)S(1)}, bf16[64,8,1024]{2,1,0:T(8,128)(2,1)}, u32[]{:S(2)}) copy-start(bf16[64,8,1024]{2,1,0:T(8,128)(2,1)} %param.9) | copy-start | bytes 3145732
  24.8 14.1 %collective-permute-start.3 = (bf16[272,896]{1,0:T(8,128)(2,1)S(1)}, bf16[272,896]{1,0:T(8,128)(2,1)S(1)}, u32[]{:S(2)}, u32[]{:S(2)}) collective-permute-start(bf16[272,896]{1,0:T(8,128)(2,1)S(1)} %get-tuple-element.20), channel_id=1, source_target_pairs={{0,1},{1,2},{2,3},{3,0},{4,5},{5,6},{6,7},{7,4},{8,9},{9,10},{10,1... | collective-permute-start | bytes 1462280 | tf_op jit(solution)/shard_map/ppermute | solution.py:19
  26.4 23.9 %collective-permute-start.4 = (bf16[272,896]{1,0:T(8,128)(2,1)}, bf16[272,896]{1,0:T(8,128)(2,1)S(1)}, u32[]{:S(2)}, u32[]{:S(2)}) collective-permute-start(bf16[272,896]{1,0:T(8,128)(2,1)} %get-tuple-element.22), channel_id=1, source_target_pairs={{0,2},{1,3},{2,0},{3,1},{4,6},{5,7},{6,4},{7,5},{8,10},{9,11},{10,... | collective-permute-start | bytes 1462280 | tf_op jit(solution)/shard_map/ppermute | solution.py:19
  29.3 21.8 %collective-permute-start.5 = (bf16[272,896]{1,0:T(8,128)(2,1)}, bf16[272,896]{1,0:T(8,128)(2,1)}, u32[]{:S(2)}, u32[]{:S(2)}) collective-permute-start(bf16[272,896]{1,0:T(8,128)(2,1)} %get-tuple-element.23), channel_id=1, source_target_pairs={{0,3},{1,0},{2,1},{3,2},{4,7},{5,4},{6,5},{7,6},{8,11},{9,8},{10,9... | collective-permute-start | bytes 1462280 | tf_op jit(solution)/shard_map/ppermute | solution.py:19
  39.0 0.8 copy-start.6
  50.3 0.8 copy-start.8
  51.1 1.0 copy-start.5
  52.2 1.0 copy-start.7
  53.2 1.0 copy-start.9
  56.7 25.9 %collective-permute-start = (bf16[8,64,1024]{2,1,0:T(8,128)(2,1)S(1)}, bf16[8,64,1024]{2,1,0:T(8,128)(2,1)S(1)}, u32[]{:S(2)}, u32[]{:S(2)}) collective-permute-start(bf16[8,64,1024]{2,1,0:T(8,128)(2,1)S(1)} %all-to-all-done.refs_0_), channel_id=1, source_target_pairs={{0,1},{1,2},{2,3},{3,0},{64,67},{65,64},{66,65},{67,66},{4,5},{5,6... | collective-permute-start | bytes 3145736 | tf_op jit(solution)/shard_map/ppermute | solution.py:25
  58.0 24.6 %collective-permute-start.1 = (bf16[8,64,1024]{2,1,0:T(8,128)(2,1)S(1)}, bf16[8,64,1024]{2,1,0:T(8,128)(2,1)}, u32[]{:S(2)}, u32[]{:S(2)}) collective-permute-start(bf16[8,64,1024]{2,1,0:T(8,128)(2,1)S(1)} %all-to-all-done.refs_0_), channel_id=1, source_target_pairs={{0,3},{1,0},{2,1},{3,2},{64,65},{65,66},{66,67},{67,64},{4,7},{5,4... | collective-permute-start | bytes 3145736 | tf_op jit(solution)/shard_map/ppermute | solution.py:25
  60.8 1.0 copy-start.3
  61.8 33.9 %all-to-all-start.1 = ((bf16[8,64,1024]{2,1,0:T(8,128)(2,1)}), bf16[8,64,1024]{2,1,0:T(8,128)(2,1)S(1)}, u32[]{:S(2)}, u32[]{:S(2)}) async-start(bf16[8,64,1024]{2,1,0:T(8,128)(2,1)} %bitcast.21), calls=%async_computation.1 | async-start | bytes 2097152 | tf_op jit(solution)/shard_map/all_to_all | solution.py:307
  68.6 153.9 %reduce-scatter.2.cloned.1.call-start = ((), (), s32[]{:S(2)}) async-start(), calls=%async_computation.4 | async-start | bytes 4128768 | tf_op jit(solution)/shard_map/reduce_scatter | solution.py:319
  82.6 16.1 %collective-permute-start.2 = (bf16[8,64,1024]{2,1,0:T(8,128)(2,1)S(1)}, bf16[8,64,1024]{2,1,0:T(8,128)(2,1)}, u32[]{:S(2)}, u32[]{:S(2)}) collective-permute-start(bf16[8,64,1024]{2,1,0:T(8,128)(2,1)S(1)} %collective-permute-done.refs_1_), channel_id=1, source_target_pairs={{0,1},{1,2},{2,3},{3,0},{64,67},{65,64},{66,65},{67,66},{4,5},{5,6... | collective-permute-start | bytes 3145736 | tf_op jit(solution)/shard_map/ppermute | solution.py:25
  98.7 27.0 %collective-permute-start.6 = (bf16[8,64,1024]{2,1,0:T(8,128)(2,1)S(1)}, bf16[8,64,1024]{2,1,0:T(8,128)(2,1)S(1)}, u32[]{:S(2)}, u32[]{:S(2)}) collective-permute-start(bf16[8,64,1024]{2,1,0:T(8,128)(2,1)S(1)} %all-to-all-done.1.refs_4_), channel_id=1, source_target_pairs={{0,1},{1,2},{2,3},{3,0},{64,67},{65,64},{66,65},{67,66},{4,5},{5,6... | collective-permute-start | bytes 3145736 | tf_op jit(solution)/shard_map/ppermute | solution.py:25
  98.7 27.0 %collective-permute-start.7 = (bf16[8,64,1024]{2,1,0:T(8,128)(2,1)S(1)}, bf16[8,64,1024]{2,1,0:T(8,128)(2,1)S(1)}, u32[]{:S(2)}, u32[]{:S(2)}) collective-permute-start(bf16[8,64,1024]{2,1,0:T(8,128)(2,1)S(1)} %all-to-all-done.1.refs_4_), channel_id=1, source_target_pairs={{0,3},{1,0},{2,1},{3,2},{64,65},{65,66},{66,67},{67,64},{4,7},{5,4... | collective-permute-start | bytes 3145736 | tf_op jit(solution)/shard_map/ppermute | solution.py:25
  125.8 1.0 copy-start.11
  125.8 1.3 copy-start.12
  125.8 16.2 %collective-permute-start.8 = (bf16[8,64,1024]{2,1,0:T(8,128)(2,1)S(1)}, bf16[8,64,1024]{2,1,0:T(8,128)(2,1)}, u32[]{:S(2)}, u32[]{:S(2)}) collective-permute-start(bf16[8,64,1024]{2,1,0:T(8,128)(2,1)S(1)} %collective-permute-done.6.refs_5_), channel_id=1, source_target_pairs={{0,1},{1,2},{2,3},{3,0},{64,67},{65,64},{66,65},{67,66},{4,5},{5,6... | collective-permute-start | bytes 3145736 | tf_op jit(solution)/shard_map/ppermute | solution.py:25
  142.0 14.1 %collective-permute-start.9 = (bf16[4,4,256,896]{3,2,1,0:T(8,128)(2,1)}, bf16[4,4,256,896]{3,2,1,0:T(8,128)(2,1)S(1)}, u32[]{:S(2)}, u32[]{:S(2)}) collective-permute-start(bf16[4,4,256,896]{3,2,1,0:T(8,128)(2,1)} %bitcast.24), channel_id=1, source_target_pairs={{0,64},{64,0},{1,65},{65,1},{2,66},{66,2},{3,67},{67,3},{4,68},{68... | collective-permute-start | bytes 22020104 | tf_op jit(solution)/shard_map/ppermute | solution.py:19
  156.1 2.9 %copy-start.10 = (bf16[4,4,256,896]{3,2,1,0:T(8,128)(2,1)}, bf16[4,4,256,896]{3,2,1,0:T(8,128)(2,1)S(1)}, u32[]{:S(2)}) copy-start(bf16[4,4,256,896]{3,2,1,0:T(8,128)(2,1)S(1)} %collective-permute-done.9.refs_8_) | copy-start | bytes 22020100
  223.6 8.0 %collective-permute-start.10 = (bf16[64,896]{1,0:T(8,128)(2,1)S(1)}, bf16[64,896]{1,0:T(8,128)(2,1)S(1)}, u32[]{:S(2)}, u32[]{:S(2)}) collective-permute-start(bf16[64,896]{1,0:T(8,128)(2,1)S(1)} %get-tuple-element.33), channel_id=1, source_target_pairs={{0,3},{1,0},{2,1},{3,2},{64,65},{65,66},{66,67},{67,64},{4,7},{5,4... | collective-permute-start | bytes 344072 | tf_op jit(solution)/shard_map/ppermute | solution.py:25
  226.4 6.4 %collective-permute-start.11 = (bf16[64,896]{1,0:T(8,128)(2,1)S(1)}, bf16[64,896]{1,0:T(8,128)(2,1)S(1)}, u32[]{:S(2)}, u32[]{:S(2)}) collective-permute-start(bf16[64,896]{1,0:T(8,128)(2,1)S(1)} %get-tuple-element.32), channel_id=1, source_target_pairs={{0,2},{1,3},{2,0},{3,1},{64,66},{65,67},{66,64},{67,65},{4,6},{5,7... | collective-permute-start | bytes 344072 | tf_op jit(solution)/shard_map/ppermute | solution.py:25
  227.3 6.7 %collective-permute-start.12 = (bf16[64,896]{1,0:T(8,128)(2,1)S(1)}, bf16[64,896]{1,0:T(8,128)(2,1)S(1)}, u32[]{:S(2)}, u32[]{:S(2)}) collective-permute-start(bf16[64,896]{1,0:T(8,128)(2,1)S(1)} %get-tuple-element.31), channel_id=1, source_target_pairs={{0,1},{1,2},{2,3},{3,0},{64,67},{65,64},{66,65},{67,66},{4,5},{5,6... | collective-permute-start | bytes 344072 | tf_op jit(solution)/shard_map/ppermute | solution.py:25
Sparse Core Ops, SparseCore 0:
  56.9 77.0 all-gather.2
  173.4 49.0 reduce-scatter.1

commit v8 on v7

--- a/solution.py
+++ b/solution.py
@@ -78,7 +78,7 @@
     info = jax.ShapeDtypeStruct((count, total - exp_train * depth, lanes), blocks[0].dtype)
     return pl.pallas_call(
         join_kernel, out_shape=[shape, info], in_specs=[SMEM] + [VMEM] * count, out_specs=[VMEM] * 2,
-        compiler_params=PARAMS, cost_estimate=cost(0, shape, shape),
+        compiler_params=PARAMS, cost_estimate=cost(BESIDE // 8, shape, shape),
     )(pos, *blocks)
 
 
@@ -237,7 +237,7 @@
             pltpu.SemaphoreType.DMA((turns,)),
             pltpu.SemaphoreType.DMA((turns,)),
         ],
-        compiler_params=PARAMS,
+        compiler_params=pltpu.CompilerParams(vmem_limit_bytes=60 << 20),
         cost_estimate=cost(flops, *arrays, total, out),
     )(pos, *arrays, gate, *given)
 
@@ -289,7 +289,8 @@
     send = lambda first, flat, beside=0: dispatch(
         first * capacity, half * capacity, slots, flat, pairs, groups, beside
     ).reshape(planes, -1, hidden_width)
-    first = lax.all_to_all(send(0, flat), Z, 0, 0, tiled=True)
+    outbound = send(0, flat)
+    first = lax.all_to_all(outbound, Z, 0, 0, tiled=True)
 
     chosen = jnp.arange(experts * capacity, dtype=jnp.int32)[:, None] == flat
     pair_row = jnp.arange(rows * fanout, dtype=jnp.int32) // fanout
@@ -297,9 +298,8 @@
     slot_row = jnp.sum(jnp.where(chosen, pair_row[None, :] + 1, 0), axis=1).reshape(groups, slots) - 1
 
     by_core = lambda v: v.astype(jnp.float32).reshape(planes, 2, slots).transpose(1, 0, 2).reshape(groups, slots)
-    blocks = split_blocks(pos, own, by_core(slot_gate), by_core(slot_row), ny)
+    blocks = split_blocks(pos, own, after(by_core(slot_gate), outbound), by_core(slot_row), ny)
     blocks = [blocks[0]] + [shifted(blocks[d], "y", d) for d in range(1, ny)]
-    blocks[1] = after(blocks[1], first)
     joined, info = join_blocks(pos, blocks, exp_train, slice_rows, 4 * slots)
     weight = lax.all_gather(joined, "x")
 

time: 243 us -> 235 us (0.967)
  local copies, waits for them, and re-layouts: 15 us -> 6.35 us
    ppermute x4, waiting for transfers between devices: 8.71 us -> 19.7 us  [shifted(): lax.ppermute(value, axis, [(i, (i + steps) % count) for i in range(count)])]
    all_to_all x1, waiting for transfers between devices: 10.2 us -> 0.01 us  [per_device(): first = lax.all_to_all(outbound, Z, 0, 0, tiled=True)]
    unnamed x30 -> x28, local copies, waits for them, and re-layouts: 12.6 us -> 3.93 us
  transfers between devices with their start and end apart: 17 -> 17, of which waited for: 12 -> 11; matrix products, arithmetic and copies ran while one was open for 0% -> 0% of each run, Pallas kernels for 7% -> 8%
where the time goes in v8:
time: 235 us
  waiting for transfers between devices  127 us (54%)
  Pallas kernels  37.7 us (16%)
  starting transfers between devices  33.4 us (14%)
  blocking collectives  14.7 us (6%)
  between operations  13.6 us (6%)
  local copies, waits for them, and re-layouts  6.35 us (3%)
    reduce_scatter x1, waiting for transfers between devices, per_device(): lax.psum_scatter(partial, Z, scatter_dimension=0, tiled=True)  49.6 us
    ppermute x9, waiting for transfers between devices, mirrored(): return lax.ppermute(value, ('c', axis), pairs)  45.6 us
    pallas_call x2, Pallas kernels, experts_call(): pl.pallas_call(functools.partial(experts_kernel, core, turns), out_shape=...  30.3 us
    ppermute x4, waiting for transfers between devices, shifted(): lax.ppermute(value, axis, [(i, (i + steps) % count) for i in range(count)])  19.7 us
    all_to_all x1, blocking collectives, per_device(): lax.all_to_all(after(info, second).reshape(ny, 2, planes, 4 * slots), Z,...  14.7 us
    all_to_all x1, waiting for transfers between devices, per_device(): lax.all_to_all(send(half, after(flat, first, joined), BESIDE), Z, 0, 0, t...  12.1 us
    ppermute x9, starting transfers between devices, mirrored(): return lax.ppermute(value, ('c', axis), pairs)  12.1 us
    all_to_all x1, starting transfers between devices, per_device(): first = lax.all_to_all(outbound, Z, 0, 0, tiled=True)  8.47 us
  transfers between devices with their start and end apart: 17, of which 11 were waited for; matrix products, arithmetic and copies ran while one was open for 0% of the time, Pallas kernels for 8%

profile of v8, /device:TPU:2, one launch (start us, length us, event | category | flops | bytes accessed | tf_op | source)
XLA Modules:
  0.0 235.1 jit_solution(2357930003045379883)
XLA Ops:
  6.5 0.7 reshape.87
  7.3 0.1 eq.31
  7.4 0.8 copy.20
  8.2 0.2 compare_reduce_fusion
  8.4 0.1 reduce_window_sum.11
  8.5 1.2 fusion
  9.7 0.1 reshape.88.flat_ref
  9.8 0.0 copy-start.1
  9.8 1.2 copy-done.1
  11.0 1.7 shard_map.55
  12.7 8.5 %all-to-all-start = ((bf16[8,64,1024]{2,1,0:T(8,128)(2,1)}), bf16[8,64,1024]{2,1,0:T(8,128)(2,1)S(1)}, u32[]{:S(2)}, u32[]{:S(2)}) async-start(bf16[8,64,1024]{2,1,0:T(8,128)(2,1)} %bitcast.6), calls=%async_computation | async-start | bytes 2097152 | tf_op jit(solution)/shard_map/all_to_all | solution.py:293
  21.2 0.0 all-gather.3.cloned.1.call-start
  21.2 0.1 eq.35
  21.3 0.1 copy.22
  21.4 0.1 broadcast_in_dim.45
  21.5 0.3 select_reduce_fusion.1
  21.8 0.1 reshape_reshape.3
  21.9 0.3 select_reduce_fusion
  22.2 0.1 convert_element_type.16
  22.3 0.1 pad_add_fusion.pos_ref
  22.4 0.7 shard_map.56
  23.1 1.7 collective-permute-start.3
  24.7 2.9 %collective-permute-start.4 = (bf16[272,896]{1,0:T(8,128)(2,1)S(1)}, bf16[272,896]{1,0:T(8,128)(2,1)S(1)}, u32[]{:S(2)}, u32[]{:S(2)}) collective-permute-start(bf16[272,896]{1,0:T(8,128)(2,1)S(1)} %get-tuple-element.22), channel_id=1, source_target_pairs={{0,2},{1,3},{2,0},{3,1},{4,6},{5,7},{6,4},{7,5},{8,10},{9,11},{10,... | collective-permute-start | bytes 1462280 | tf_op jit(solution)/shard_map/ppermute | solution.py:19
  27.6 1.3 collective-permute-start.5
  29.0 8.3 %collective-permute-done.3.refs_1_ = bf16[272,896]{1,0:T(8,128)(2,1)S(1)} collective-permute-done((bf16[272,896]{1,0:T(8,128)(2,1)S(1)}, bf16[272,896]{1,0:T(8,128)(2,1)S(1)}, u32[]{:S(2)}, u32[]{:S(2)}) %collective-permute-start.3) | collective-permute-done | bytes 487456 | tf_op jit(solution)/shard_map/ppermute | solution.py:19
  37.3 11.3 %collective-permute-done.4.refs_2_ = bf16[272,896]{1,0:T(8,128)(2,1)S(1)} collective-permute-done((bf16[272,896]{1,0:T(8,128)(2,1)S(1)}, bf16[272,896]{1,0:T(8,128)(2,1)S(1)}, u32[]{:S(2)}, u32[]{:S(2)}) %collective-permute-start.4) | collective-permute-done | bytes 487456 | tf_op jit(solution)/shard_map/ppermute | solution.py:19
  48.6 0.0 collective-permute-done.5.refs_3_
  48.6 2.0 shard_map.57
  50.6 0.0 all-gather.3.cloned.1.call-update
  50.7 0.0 all-to-all-done.refs_0_
  50.7 1.3 collective-permute-start
  52.0 2.0 collective-permute-start.1
  54.0 1.7 shard_map.58
  55.7 6.9 %all-to-all-start.1 = ((bf16[8,64,1024]{2,1,0:T(8,128)(2,1)}), bf16[8,64,1024]{2,1,0:T(8,128)(2,1)S(1)}, u32[]{:S(2)}, u32[]{:S(2)}) async-start(bf16[8,64,1024]{2,1,0:T(8,128)(2,1)} %bitcast.12), calls=%async_computation.1 | async-start | bytes 2097152 | tf_op jit(solution)/shard_map/all_to_all | solution.py:307
  62.6 0.0 reduce-scatter.2.cloned.1.call-start
  62.6 14.4 %collective-permute-done.refs_1_ = bf16[8,64,1024]{2,1,0:T(8,128)(2,1)S(1)} collective-permute-done((bf16[8,64,1024]{2,1,0:T(8,128)(2,1)S(1)}, bf16[8,64,1024]{2,1,0:T(8,128)(2,1)S(1)}, u32[]{:S(2)}, u32[]{:S(2)}) %collective-permute-start) | collective-permute-done | bytes 1048608 | tf_op jit(solution)/shard_map/ppermute | solution.py:25
  77.1 0.0 collective-permute-done.1.refs_3_
  77.1 1.0 collective-permute-start.2
  78.0 12.1 %all-to-all-done.1.refs_4_ = bf16[8,64,1024]{2,1,0:T(8,128)(2,1)S(1)} async-done(((bf16[8,64,1024]{2,1,0:T(8,128)(2,1)}), bf16[8,64,1024]{2,1,0:T(8,128)(2,1)S(1)}, u32[]{:S(2)}, u32[]{:S(2)}) %all-to-all-start.1) | async-done | bytes 1048608 | tf_op jit(solution)/shard_map/all_to_all | solution.py:307
  90.1 2.9 %collective-permute-done.2.refs_2_ = bf16[8,64,1024]{2,1,0:T(8,128)(2,1)S(1)} collective-permute-done((bf16[8,64,1024]{2,1,0:T(8,128)(2,1)S(1)}, bf16[8,64,1024]{2,1,0:T(8,128)(2,1)S(1)}, u32[]{:S(2)}, u32[]{:S(2)}) %collective-permute-start.2) | collective-permute-done | bytes 1048608 | tf_op jit(solution)/shard_map/ppermute | solution.py:25
  93.1 0.0 collective-permute-start.6
  93.1 3.2 %collective-permute-start.7 = (bf16[8,64,1024]{2,1,0:T(8,128)(2,1)S(1)}, bf16[8,64,1024]{2,1,0:T(8,128)(2,1)S(1)}, u32[]{:S(2)}, u32[]{:S(2)}) collective-permute-start(bf16[8,64,1024]{2,1,0:T(8,128)(2,1)S(1)} %all-to-all-done.1.refs_4_), channel_id=1, source_target_pairs={{0,3},{1,0},{2,1},{3,2},{64,65},{65,66},{66,67},{67,64},{4,7},{5,4... | collective-permute-start | bytes 3145736 | tf_op jit(solution)/shard_map/ppermute | solution.py:25
  96.3 14.7 %all_to_all.15 = bf16[4,2,8,256]{3,1,0,2:T(2,128)(2,1)S(1)} all-to-all(bf16[4,2,8,256]{3,1,0,2:T(2,128)(2,1)S(1)} %copy.25), channel_id=1, replica_groups=mesh['zl'=2,'c'=2,'zh'=4,'x'=4,'y'=4] {'zh','zl'}, dimensions={2} | all-to-all | bytes 65536 | tf_op jit(solution)/shard_map/all_to_all | solution.py:311
  111.1 8.2 %collective-permute-done.6.refs_5_ = bf16[8,64,1024]{2,1,0:T(8,128)(2,1)S(1)} collective-permute-done((bf16[8,64,1024]{2,1,0:T(8,128)(2,1)S(1)}, bf16[8,64,1024]{2,1,0:T(8,128)(2,1)S(1)}, u32[]{:S(2)}, u32[]{:S(2)}) %collective-permute-start.6) | collective-permute-done | bytes 1048608 | tf_op jit(solution)/shard_map/ppermute | solution.py:25
  119.3 0.0 collective-permute-done.7.refs_7_
  119.3 0.1 collective-permute-start.8
  119.4 0.1 shard_map.59.refs_9_
  119.5 0.8 copy-done.10
  120.2 0.4 copy-done.11
  120.6 0.6 copy-done.3
  121.3 14.2 %collective-permute-done.8.refs_6_ = bf16[8,64,1024]{2,1,0:T(8,128)(2,1)} collective-permute-done((bf16[8,64,1024]{2,1,0:T(8,128)(2,1)S(1)}, bf16[8,64,1024]{2,1,0:T(8,128)(2,1)}, u32[]{:S(2)}, u32[]{:S(2)}) %collective-permute-start.8) | collective-permute-done | bytes 1048608 | tf_op jit(solution)/shard_map/ppermute | solution.py:25
  135.5 0.0 collective-permute-start.9
  135.5 15.3 %shard_map.60.refs_10_ = f32[4,8,64,896]{3,2,1,0:T(8,128)} custom-call(s32[4]{0:T(128)} %copy-done.4, bf16[8,64,1024]{2,1,0:T(8,128)(2,1)} %copy-done.6, bf16[8,64,1024]{2,1,0:T(8,128)(2,1)} %copy-done.8, bf16[8,64,1024]{2,1,0:T(8,128)(2,1)} %copy-done.9, bf16[8,64,1024]{2,1,0:T(8,128)(2,1)} %collective-permute-done.1.refs_3_, ...), custom_call_target="tpu_custom_call" | custom-call | flops 3758096384 | bytes 30408704 | tf_op jit(solution)/shard_map/pallas_call | solution.py:224
  150.7 15.0 %shard_map.61 = bf16[8,4,64,896]{3,2,1,0:T(8,128)(2,1)} custom-call(s32[4]{0:T(128)} %copy-done.4, bf16[8,64,1024]{2,1,0:T(8,128)(2,1)} %copy-done.6, bf16[8,64,1024]{2,1,0:T(8,128)(2,1)} %copy-done.8, bf16[8,64,1024]{2,1,0:T(8,128)(2,1)} %copy-done.9, bf16[8,64,1024]{2,1,0:T(8,128)(2,1)} %collective-permute-done.1.refs_3_, bf16[8,64,1024]{2,1,0:T(8,128)(2,1)} %copy-done.7, ...), custom_call_target="tpu_custom_call" | custom-call | flops 3758096384 | bytes 26738688 | tf_op jit(solution)/shard_map/pallas_call | solution.py:224
  165.8 0.0 reduce-scatter.2.cloned.1.call-update
  165.8 49.6 %reduce-scatter.2.cloned.1.call-done = bf16[256,896]{1,0:T(8,128)(2,1)} async-done(((bf16[2048,896]{1,0:T(8,128)(2,1)}), bf16[256,896]{1,0:T(8,128)(2,1)}) %reduce-scatter.2.cloned.1.call-update) | async-done | bytes 458768 | tf_op jit(solution)/shard_map/reduce_scatter | solution.py:319
  215.4 1.1 fusion.5
  216.5 2.8 %collective-permute-start.10 = (bf16[64,896]{1,0:T(8,128)(2,1)S(1)}, bf16[64,896]{1,0:T(8,128)(2,1)S(1)}, u32[]{:S(2)}, u32[]{:S(2)}) collective-permute-start(bf16[64,896]{1,0:T(8,128)(2,1)S(1)} %get-tuple-element.33), channel_id=1, source_target_pairs={{0,3},{1,0},{2,1},{3,2},{64,65},{65,66},{66,67},{67,64},{4,7},{5,4... | collective-permute-start | bytes 344072 | tf_op jit(solution)/shard_map/ppermute | solution.py:25
  219.3 0.8 collective-permute-start.11
  220.1 0.9 collective-permute-start.12
  221.0 3.5 %collective-permute-done.10.refs_1_ = bf16[64,896]{1,0:T(8,128)(2,1)S(1)} collective-permute-done((bf16[64,896]{1,0:T(8,128)(2,1)S(1)}, bf16[64,896]{1,0:T(8,128)(2,1)S(1)}, u32[]{:S(2)}, u32[]{:S(2)}) %collective-permute-start.10) | collective-permute-done | bytes 114720 | tf_op jit(solution)/shard_map/ppermute | solution.py:25
  224.5 1.2 collective-permute-done.11.refs_2_
  225.7 1.2 collective-permute-done.12.refs_3_
  226.9 1.4 shard_map.62
  (33 shorter events, 0.1 us)
Async XLA Ops:
  9.8 1.2 copy-start.1
  11.0 10.3 %copy-start.12 = (f32[64,8]{0,1:T(8,128)S(1)}, f32[64,8]{0,1:T(8,128)}, u32[]{:S(2)}) copy-start(f32[64,8]{0,1:T(8,128)} %param.8) | copy-start | bytes 6148
  11.0 11.3 %copy-start = (bf16[1,1,4,64,3584]{4,3,2,1,0:T(8,128)(2,1)S(1)}, bf16[1,1,4,64,3584]{4,3,2,1,0:T(8,128)(2,1)}, u32[]{:S(2)}) copy-start(bf16[1,1,4,64,3584]{4,3,2,1,0:T(8,128)(2,1)} %param.5) | copy-start | bytes 5505028
  12.7 37.9 %all-to-all-start = ((bf16[8,64,1024]{2,1,0:T(8,128)(2,1)}), bf16[8,64,1024]{2,1,0:T(8,128)(2,1)S(1)}, u32[]{:S(2)}, u32[]{:S(2)}) async-start(bf16[8,64,1024]{2,1,0:T(8,128)(2,1)} %bitcast.6), calls=%async_computation | async-start | bytes 2097152 | tf_op jit(solution)/shard_map/all_to_all | solution.py:293
  21.2 114.3 %all-gather.3.cloned.1.call-start = ((), (), s32[]{:S(2)}) async-start(), calls=%async_computation.5 | async-start | bytes 9175040 | tf_op jit(solution)/shard_map/all_gather | solution.py:304
  22.4 28.3 %copy-start.4 = (s32[4]{0:T(128)}, s32[4]{0:T(128)S(1)}, u32[]{:S(2)}) copy-start(s32[4]{0:T(128)S(1)} %pad_add_fusion.pos_ref) | copy-start | bytes 52
  23.1 14.2 %collective-permute-start.3 = (bf16[272,896]{1,0:T(8,128)(2,1)S(1)}, bf16[272,896]{1,0:T(8,128)(2,1)S(1)}, u32[]{:S(2)}, u32[]{:S(2)}) collective-permute-start(bf16[272,896]{1,0:T(8,128)(2,1)S(1)} %get-tuple-element.21), channel_id=1, source_target_pairs={{0,1},{1,2},{2,3},{3,0},{4,5},{5,6},{6,7},{7,4},{8,9},{9,10},{10,1... | collective-permute-start | bytes 1462280 | tf_op jit(solution)/shard_map/ppermute | solution.py:19
  24.7 23.9 %collective-permute-start.4 = (bf16[272,896]{1,0:T(8,128)(2,1)S(1)}, bf16[272,896]{1,0:T(8,128)(2,1)S(1)}, u32[]{:S(2)}, u32[]{:S(2)}) collective-permute-start(bf16[272,896]{1,0:T(8,128)(2,1)S(1)} %get-tuple-element.22), channel_id=1, source_target_pairs={{0,2},{1,3},{2,0},{3,1},{4,6},{5,7},{6,4},{7,5},{8,10},{9,11},{10,... | collective-permute-start | bytes 1462280 | tf_op jit(solution)/shard_map/ppermute | solution.py:19
  27.6 21.0 %collective-permute-start.5 = (bf16[272,896]{1,0:T(8,128)(2,1)S(1)}, bf16[272,896]{1,0:T(8,128)(2,1)S(1)}, u32[]{:S(2)}, u32[]{:S(2)}) collective-permute-start(bf16[272,896]{1,0:T(8,128)(2,1)S(1)} %get-tuple-element.23), channel_id=1, source_target_pairs={{0,3},{1,0},{2,1},{3,2},{4,7},{5,4},{6,5},{7,6},{8,11},{9,8},{10,9... | collective-permute-start | bytes 1462280 | tf_op jit(solution)/shard_map/ppermute | solution.py:19
  48.6 5.4 %copy-start.2 = (bf16[64,8,1024]{2,1,0:T(8,128)(2,1)S(1)}, bf16[64,8,1024]{2,1,0:T(8,128)(2,1)}, u32[]{:S(2)}) copy-start(bf16[64,8,1024]{2,1,0:T(8,128)(2,1)} %param.9) | copy-start | bytes 3145732
  50.7 5.0 %copy-start.6 = (bf16[8,64,1024]{2,1,0:T(8,128)(2,1)}, bf16[8,64,1024]{2,1,0:T(8,128)(2,1)S(1)}, u32[]{:S(2)}) copy-start(bf16[8,64,1024]{2,1,0:T(8,128)(2,1)S(1)} %all-to-all-done.refs_0_) | copy-start | bytes 3145732
  50.7 26.4 %collective-permute-start = (bf16[8,64,1024]{2,1,0:T(8,128)(2,1)S(1)}, bf16[8,64,1024]{2,1,0:T(8,128)(2,1)S(1)}, u32[]{:S(2)}, u32[]{:S(2)}) collective-permute-start(bf16[8,64,1024]{2,1,0:T(8,128)(2,1)S(1)} %all-to-all-done.refs_0_), channel_id=1, source_target_pairs={{0,1},{1,2},{2,3},{3,0},{64,67},{65,64},{66,65},{67,66},{4,5},{5,6... | collective-permute-start | bytes 3145736 | tf_op jit(solution)/shard_map/ppermute | solution.py:25
  52.0 25.1 %collective-permute-start.1 = (bf16[8,64,1024]{2,1,0:T(8,128)(2,1)S(1)}, bf16[8,64,1024]{2,1,0:T(8,128)(2,1)}, u32[]{:S(2)}, u32[]{:S(2)}) collective-permute-start(bf16[8,64,1024]{2,1,0:T(8,128)(2,1)S(1)} %all-to-all-done.refs_0_), channel_id=1, source_target_pairs={{0,3},{1,0},{2,1},{3,2},{64,65},{65,66},{66,67},{67,64},{4,7},{5,4... | collective-permute-start | bytes 3145736 | tf_op jit(solution)/shard_map/ppermute | solution.py:25
  55.7 34.4 %all-to-all-start.1 = ((bf16[8,64,1024]{2,1,0:T(8,128)(2,1)}), bf16[8,64,1024]{2,1,0:T(8,128)(2,1)S(1)}, u32[]{:S(2)}, u32[]{:S(2)}) async-start(bf16[8,64,1024]{2,1,0:T(8,128)(2,1)} %bitcast.12), calls=%async_computation.1 | async-start | bytes 2097152 | tf_op jit(solution)/shard_map/all_to_all | solution.py:307
  62.6 152.8 %reduce-scatter.2.cloned.1.call-start = ((), (), s32[]{:S(2)}) async-start(), calls=%async_computation.4 | async-start | bytes 4128768 | tf_op jit(solution)/shard_map/reduce_scatter | solution.py:319
  77.1 42.4 %copy-start.8 = (bf16[8,64,1024]{2,1,0:T(8,128)(2,1)}, bf16[8,64,1024]{2,1,0:T(8,128)(2,1)S(1)}, u32[]{:S(2)}) copy-start(bf16[8,64,1024]{2,1,0:T(8,128)(2,1)S(1)} %collective-permute-done.refs_1_) | copy-start | bytes 3145732
  77.1 16.0 %collective-permute-start.2 = (bf16[8,64,1024]{2,1,0:T(8,128)(2,1)S(1)}, bf16[8,64,1024]{2,1,0:T(8,128)(2,1)S(1)}, u32[]{:S(2)}, u32[]{:S(2)}) collective-permute-start(bf16[8,64,1024]{2,1,0:T(8,128)(2,1)S(1)} %collective-permute-done.refs_1_), channel_id=1, source_target_pairs={{0,1},{1,2},{2,3},{3,0},{64,67},{65,64},{66,65},{67,66},{4,5},{5,6... | collective-permute-start | bytes 3145736 | tf_op jit(solution)/shard_map/ppermute | solution.py:25
  90.1 29.3 %copy-start.7 = (bf16[8,64,1024]{2,1,0:T(8,128)(2,1)}, bf16[8,64,1024]{2,1,0:T(8,128)(2,1)S(1)}, u32[]{:S(2)}) copy-start(bf16[8,64,1024]{2,1,0:T(8,128)(2,1)S(1)} %all-to-all-done.1.refs_4_) | copy-start | bytes 3145732
  93.1 26.4 %copy-start.9 = (bf16[8,64,1024]{2,1,0:T(8,128)(2,1)}, bf16[8,64,1024]{2,1,0:T(8,128)(2,1)S(1)}, u32[]{:S(2)}) copy-start(bf16[8,64,1024]{2,1,0:T(8,128)(2,1)S(1)} %collective-permute-done.2.refs_2_) | copy-start | bytes 3145732
  93.1 26.2 %collective-permute-start.6 = (bf16[8,64,1024]{2,1,0:T(8,128)(2,1)S(1)}, bf16[8,64,1024]{2,1,0:T(8,128)(2,1)S(1)}, u32[]{:S(2)}, u32[]{:S(2)}) collective-permute-start(bf16[8,64,1024]{2,1,0:T(8,128)(2,1)S(1)} %all-to-all-done.1.refs_4_), channel_id=1, source_target_pairs={{0,1},{1,2},{2,3},{3,0},{64,67},{65,64},{66,65},{67,66},{4,5},{5,6... | collective-permute-start | bytes 3145736 | tf_op jit(solution)/shard_map/ppermute | solution.py:25
  93.1 26.2 %collective-permute-start.7 = (bf16[8,64,1024]{2,1,0:T(8,128)(2,1)S(1)}, bf16[8,64,1024]{2,1,0:T(8,128)(2,1)S(1)}, u32[]{:S(2)}, u32[]{:S(2)}) collective-permute-start(bf16[8,64,1024]{2,1,0:T(8,128)(2,1)S(1)} %all-to-all-done.1.refs_4_), channel_id=1, source_target_pairs={{0,3},{1,0},{2,1},{3,2},{64,65},{65,66},{66,67},{67,64},{4,7},{5,4... | collective-permute-start | bytes 3145736 | tf_op jit(solution)/shard_map/ppermute | solution.py:25
  119.3 1.0 copy-start.10
  119.3 1.4 copy-start.11
  119.3 16.2 %collective-permute-start.8 = (bf16[8,64,1024]{2,1,0:T(8,128)(2,1)S(1)}, bf16[8,64,1024]{2,1,0:T(8,128)(2,1)}, u32[]{:S(2)}, u32[]{:S(2)}) collective-permute-start(bf16[8,64,1024]{2,1,0:T(8,128)(2,1)S(1)} %collective-permute-done.6.refs_5_), channel_id=1, source_target_pairs={{0,1},{1,2},{2,3},{3,0},{64,67},{65,64},{66,65},{67,66},{4,5},{5,6... | collective-permute-start | bytes 3145736 | tf_op jit(solution)/shard_map/ppermute | solution.py:25
  120.6 0.6 copy-start.3
  135.5 15.3 %collective-permute-start.9 = (bf16[4,4,256,896]{3,2,1,0:T(8,128)(2,1)}, bf16[4,4,256,896]{3,2,1,0:T(8,128)(2,1)}, u32[]{:S(2)}, u32[]{:S(2)}) collective-permute-start(bf16[4,4,256,896]{3,2,1,0:T(8,128)(2,1)} %bitcast.27), channel_id=1, source_target_pairs={{0,64},{64,0},{1,65},{65,1},{2,66},{66,2},{3,67},{67,3},{4,68},{68... | collective-permute-start | bytes 22020104 | tf_op jit(solution)/shard_map/ppermute | solution.py:19
  165.7 61.1 %copy-start.5 = (s32[4]{0:T(128)S(1)}, s32[4]{0:T(128)}, u32[]{:S(2)}) copy-start(s32[4]{0:T(128)} %copy-done.4) | copy-start | bytes 52
  216.5 8.0 %collective-permute-start.10 = (bf16[64,896]{1,0:T(8,128)(2,1)S(1)}, bf16[64,896]{1,0:T(8,128)(2,1)S(1)}, u32[]{:S(2)}, u32[]{:S(2)}) collective-permute-start(bf16[64,896]{1,0:T(8,128)(2,1)S(1)} %get-tuple-element.33), channel_id=1, source_target_pairs={{0,3},{1,0},{2,1},{3,2},{64,65},{65,66},{66,67},{67,64},{4,7},{5,4... | collective-permute-start | bytes 344072 | tf_op jit(solution)/shard_map/ppermute | solution.py:25
  219.3 6.4 %collective-permute-start.11 = (bf16[64,896]{1,0:T(8,128)(2,1)S(1)}, bf16[64,896]{1,0:T(8,128)(2,1)S(1)}, u32[]{:S(2)}, u32[]{:S(2)}) collective-permute-start(bf16[64,896]{1,0:T(8,128)(2,1)S(1)} %get-tuple-element.32), channel_id=1, source_target_pairs={{0,2},{1,3},{2,0},{3,1},{64,66},{65,67},{66,64},{67,65},{4,6},{5,7... | collective-permute-start | bytes 344072 | tf_op jit(solution)/shard_map/ppermute | solution.py:25
  220.1 6.7 %collective-permute-start.12 = (bf16[64,896]{1,0:T(8,128)(2,1)S(1)}, bf16[64,896]{1,0:T(8,128)(2,1)S(1)}, u32[]{:S(2)}, u32[]{:S(2)}) collective-permute-start(bf16[64,896]{1,0:T(8,128)(2,1)S(1)} %get-tuple-element.31), channel_id=1, source_target_pairs={{0,1},{1,2},{2,3},{3,0},{64,67},{65,64},{66,65},{67,66},{4,5},{5,6... | collective-permute-start | bytes 344072 | tf_op jit(solution)/shard_map/ppermute | solution.py:25
Sparse Core Ops, SparseCore 0:
  50.8 77.5 all-gather.2
  165.9 49.4 reduce-scatter.1

commit v9 on v8

--- a/solution.py
+++ b/solution.py
@@ -178,7 +178,7 @@
             p_all[:, pl.ds(place, capacity), :] = value.reshape(turns * planes, capacity, width)
         return 0
 
-    lax.fori_loop(0, experts, multiply, 0)
+    lax.fori_loop(0, experts, multiply, 0, unroll=True)
     number = lax.broadcasted_iota(jnp.int32, (rows, 2 * slots), 0).astype(jnp.float32)
 
     def combine(turn, _):
@@ -199,7 +199,7 @@
                 sums[turn, plane] = mixed
             return 0
 
-        lax.fori_loop(0, planes, one, 0, unroll=2)
+        lax.fori_loop(0, planes, one, 0, unroll=8)
         out_copy(turn).start()
         return 0
 

time: 235 us -> 231 us (0.983)
  Pallas kernels: 37.7 us -> 33.4 us
    pallas_call x2, Pallas kernels: 30.3 us -> 26 us  [experts_call(): pl.pallas_call(functools.partial(experts_kernel, core, turns), out_shape=...]
where the time goes in v9:
time: 231 us
  waiting for transfers between devices  127 us (55%)
  Pallas kernels  33.4 us (14%)
  starting transfers between devices  33.4 us (14%)
  blocking collectives  14.7 us (6%)
  between operations  13.6 us (6%)
  local copies, waits for them, and re-layouts  6.35 us (3%)
    reduce_scatter x1, waiting for transfers between devices, per_device(): lax.psum_scatter(partial, Z, scatter_dimension=0, tiled=True)  49.6 us
    ppermute x9, waiting for transfers between devices, mirrored(): return lax.ppermute(value, ('c', axis), pairs)  45.6 us
    pallas_call x2, Pallas kernels, experts_call(): pl.pallas_call(functools.partial(experts_kernel, core, turns), out_shape=...  26 us
    ppermute x4, waiting for transfers between devices, shifted(): lax.ppermute(value, axis, [(i, (i + steps) % count) for i in range(count)])  19.7 us
    all_to_all x1, blocking collectives, per_device(): lax.all_to_all(after(info, second).reshape(ny, 2, planes, 4 * slots), Z,...  14.7 us
    all_to_all x1, waiting for transfers between devices, per_device(): lax.all_to_all(send(half, after(flat, first, joined), BESIDE), Z, 0, 0, t...  12.1 us
    ppermute x9, starting transfers between devices, mirrored(): return lax.ppermute(value, ('c', axis), pairs)  12.1 us
    all_to_all x1, starting transfers between devices, per_device(): first = lax.all_to_all(outbound, Z, 0, 0, tiled=True)  8.47 us
  transfers between devices with their start and end apart: 17, of which 11 were waited for; matrix products, arithmetic and copies ran while one was open for 0% of the time, Pallas kernels for 8%

profile of v9, /device:TPU:2, one launch (start us, length us, event | category | flops | bytes accessed | tf_op | source)
XLA Modules:
  0.0 230.7 jit_solution(6237603608264278971)
XLA Ops:
  6.5 0.7 reshape.87
  7.3 0.1 eq.31
  7.4 0.8 copy.20
  8.2 0.2 compare_reduce_fusion
  8.4 0.1 reduce_window_sum.11
  8.5 1.2 fusion
  9.7 0.1 reshape.88.flat_ref
  9.8 0.0 copy-start.1
  9.8 1.2 copy-done.1
  11.0 1.7 shard_map.55
  12.7 8.5 %all-to-all-start = ((bf16[8,64,1024]{2,1,0:T(8,128)(2,1)}), bf16[8,64,1024]{2,1,0:T(8,128)(2,1)S(1)}, u32[]{:S(2)}, u32[]{:S(2)}) async-start(bf16[8,64,1024]{2,1,0:T(8,128)(2,1)} %bitcast.6), calls=%async_computation | async-start | bytes 2097152 | tf_op jit(solution)/shard_map/all_to_all | solution.py:293
  21.2 0.0 all-gather.3.cloned.1.call-start
  21.2 0.1 eq.35
  21.3 0.1 copy.22
  21.4 0.1 broadcast_in_dim.45
  21.5 0.3 select_reduce_fusion.1
  21.8 0.1 reshape_reshape.3
  21.9 0.3 select_reduce_fusion
  22.2 0.1 convert_element_type.16
  22.3 0.1 pad_add_fusion.pos_ref
  22.4 0.7 shard_map.56
  23.1 1.7 collective-permute-start.3
  24.7 2.9 %collective-permute-start.4 = (bf16[272,896]{1,0:T(8,128)(2,1)S(1)}, bf16[272,896]{1,0:T(8,128)(2,1)S(1)}, u32[]{:S(2)}, u32[]{:S(2)}) collective-permute-start(bf16[272,896]{1,0:T(8,128)(2,1)S(1)} %get-tuple-element.22), channel_id=1, source_target_pairs={{0,2},{1,3},{2,0},{3,1},{4,6},{5,7},{6,4},{7,5},{8,10},{9,11},{10,... | collective-permute-start | bytes 1462280 | tf_op jit(solution)/shard_map/ppermute | solution.py:19
  27.6 1.3 collective-permute-start.5
  29.0 8.3 %collective-permute-done.3.refs_1_ = bf16[272,896]{1,0:T(8,128)(2,1)S(1)} collective-permute-done((bf16[272,896]{1,0:T(8,128)(2,1)S(1)}, bf16[272,896]{1,0:T(8,128)(2,1)S(1)}, u32[]{:S(2)}, u32[]{:S(2)}) %collective-permute-start.3) | collective-permute-done | bytes 487456 | tf_op jit(solution)/shard_map/ppermute | solution.py:19
  37.3 11.3 %collective-permute-done.4.refs_2_ = bf16[272,896]{1,0:T(8,128)(2,1)S(1)} collective-permute-done((bf16[272,896]{1,0:T(8,128)(2,1)S(1)}, bf16[272,896]{1,0:T(8,128)(2,1)S(1)}, u32[]{:S(2)}, u32[]{:S(2)}) %collective-permute-start.4) | collective-permute-done | bytes 487456 | tf_op jit(solution)/shard_map/ppermute | solution.py:19
  48.6 0.0 collective-permute-done.5.refs_3_
  48.6 2.0 shard_map.57
  50.6 0.0 all-gather.3.cloned.1.call-update
  50.7 0.0 all-to-all-done.refs_0_
  50.7 1.3 collective-permute-start
  52.0 2.0 collective-permute-start.1
  54.0 1.7 shard_map.58
  55.7 6.9 %all-to-all-start.1 = ((bf16[8,64,1024]{2,1,0:T(8,128)(2,1)}), bf16[8,64,1024]{2,1,0:T(8,128)(2,1)S(1)}, u32[]{:S(2)}, u32[]{:S(2)}) async-start(bf16[8,64,1024]{2,1,0:T(8,128)(2,1)} %bitcast.12), calls=%async_computation.1 | async-start | bytes 2097152 | tf_op jit(solution)/shard_map/all_to_all | solution.py:307
  62.6 0.0 reduce-scatter.2.cloned.1.call-start
  62.6 14.4 %collective-permute-done.refs_1_ = bf16[8,64,1024]{2,1,0:T(8,128)(2,1)S(1)} collective-permute-done((bf16[8,64,1024]{2,1,0:T(8,128)(2,1)S(1)}, bf16[8,64,1024]{2,1,0:T(8,128)(2,1)S(1)}, u32[]{:S(2)}, u32[]{:S(2)}) %collective-permute-start) | collective-permute-done | bytes 1048608 | tf_op jit(solution)/shard_map/ppermute | solution.py:25
  77.1 0.0 collective-permute-done.1.refs_3_
  77.1 1.0 collective-permute-start.2
  78.0 12.1 %all-to-all-done.1.refs_4_ = bf16[8,64,1024]{2,1,0:T(8,128)(2,1)S(1)} async-done(((bf16[8,64,1024]{2,1,0:T(8,128)(2,1)}), bf16[8,64,1024]{2,1,0:T(8,128)(2,1)S(1)}, u32[]{:S(2)}, u32[]{:S(2)}) %all-to-all-start.1) | async-done | bytes 1048608 | tf_op jit(solution)/shard_map/all_to_all | solution.py:307
  90.1 2.9 %collective-permute-done.2.refs_2_ = bf16[8,64,1024]{2,1,0:T(8,128)(2,1)S(1)} collective-permute-done((bf16[8,64,1024]{2,1,0:T(8,128)(2,1)S(1)}, bf16[8,64,1024]{2,1,0:T(8,128)(2,1)S(1)}, u32[]{:S(2)}, u32[]{:S(2)}) %collective-permute-start.2) | collective-permute-done | bytes 1048608 | tf_op jit(solution)/shard_map/ppermute | solution.py:25
  93.1 0.0 collective-permute-start.6
  93.1 3.2 %collective-permute-start.7 = (bf16[8,64,1024]{2,1,0:T(8,128)(2,1)S(1)}, bf16[8,64,1024]{2,1,0:T(8,128)(2,1)S(1)}, u32[]{:S(2)}, u32[]{:S(2)}) collective-permute-start(bf16[8,64,1024]{2,1,0:T(8,128)(2,1)S(1)} %all-to-all-done.1.refs_4_), channel_id=1, source_target_pairs={{0,3},{1,0},{2,1},{3,2},{64,65},{65,66},{66,67},{67,64},{4,7},{5,4... | collective-permute-start | bytes 3145736 | tf_op jit(solution)/shard_map/ppermute | solution.py:25
  96.3 14.7 %all_to_all.15 = bf16[4,2,8,256]{3,1,0,2:T(2,128)(2,1)S(1)} all-to-all(bf16[4,2,8,256]{3,1,0,2:T(2,128)(2,1)S(1)} %copy.25), channel_id=1, replica_groups=mesh['zl'=2,'c'=2,'zh'=4,'x'=4,'y'=4] {'zh','zl'}, dimensions={2} | all-to-all | bytes 65536 | tf_op jit(solution)/shard_map/all_to_all | solution.py:311
  111.1 8.2 %collective-permute-done.6.refs_5_ = bf16[8,64,1024]{2,1,0:T(8,128)(2,1)S(1)} collective-permute-done((bf16[8,64,1024]{2,1,0:T(8,128)(2,1)S(1)}, bf16[8,64,1024]{2,1,0:T(8,128)(2,1)S(1)}, u32[]{:S(2)}, u32[]{:S(2)}) %collective-permute-start.6) | collective-permute-done | bytes 1048608 | tf_op jit(solution)/shard_map/ppermute | solution.py:25
  119.3 0.1 collective-permute-start.8
  119.4 0.1 shard_map.59.refs_9_
  119.5 0.8 copy-done.10
  120.2 0.4 copy-done.11
  120.6 0.6 copy-done.3
  121.3 14.2 %collective-permute-done.8.refs_6_ = bf16[8,64,1024]{2,1,0:T(8,128)(2,1)} collective-permute-done((bf16[8,64,1024]{2,1,0:T(8,128)(2,1)S(1)}, bf16[8,64,1024]{2,1,0:T(8,128)(2,1)}, u32[]{:S(2)}, u32[]{:S(2)}) %collective-permute-start.8) | collective-permute-done | bytes 1048608 | tf_op jit(solution)/shard_map/ppermute | solution.py:25
  135.5 0.0 collective-permute-start.9
  135.5 13.1 %shard_map.60.refs_10_ = f32[4,8,64,896]{3,2,1,0:T(8,128)} custom-call(s32[4]{0:T(128)} %copy-done.4, bf16[8,64,1024]{2,1,0:T(8,128)(2,1)} %copy-done.6, bf16[8,64,1024]{2,1,0:T(8,128)(2,1)} %copy-done.8, bf16[8,64,1024]{2,1,0:T(8,128)(2,1)} %copy-done.9, bf16[8,64,1024]{2,1,0:T(8,128)(2,1)} %collective-permute-done.1.refs_3_, ...), custom_call_target="tpu_custom_call" | custom-call | flops 3758096384 | bytes 30408704 | tf_op jit(solution)/shard_map/pallas_call | solution.py:224
  148.5 0.0 collective-permute-done.9.refs_8_
  148.5 12.9 %shard_map.61 = bf16[8,4,64,896]{3,2,1,0:T(8,128)(2,1)} custom-call(s32[4]{0:T(128)} %copy-done.4, bf16[8,64,1024]{2,1,0:T(8,128)(2,1)} %copy-done.6, bf16[8,64,1024]{2,1,0:T(8,128)(2,1)} %copy-done.8, bf16[8,64,1024]{2,1,0:T(8,128)(2,1)} %copy-done.9, bf16[8,64,1024]{2,1,0:T(8,128)(2,1)} %collective-permute-done.1.refs_3_, bf16[8,64,1024]{2,1,0:T(8,128)(2,1)} %copy-done.7, ...), custom_call_target="tpu_custom_call" | custom-call | flops 3758096384 | bytes 26738688 | tf_op jit(solution)/shard_map/pallas_call | solution.py:224
  161.5 0.0 reduce-scatter.2.cloned.1.call-update
  161.5 49.6 %reduce-scatter.2.cloned.1.call-done = bf16[256,896]{1,0:T(8,128)(2,1)} async-done(((bf16[2048,896]{1,0:T(8,128)(2,1)}), bf16[256,896]{1,0:T(8,128)(2,1)}) %reduce-scatter.2.cloned.1.call-update) | async-done | bytes 458768 | tf_op jit(solution)/shard_map/reduce_scatter | solution.py:319
  211.1 1.1 fusion.5
  212.2 2.8 %collective-permute-start.10 = (bf16[64,896]{1,0:T(8,128)(2,1)S(1)}, bf16[64,896]{1,0:T(8,128)(2,1)S(1)}, u32[]{:S(2)}, u32[]{:S(2)}) collective-permute-start(bf16[64,896]{1,0:T(8,128)(2,1)S(1)} %get-tuple-element.33), channel_id=1, source_target_pairs={{0,3},{1,0},{2,1},{3,2},{64,65},{65,66},{66,67},{67,64},{4,7},{5,4... | collective-permute-start | bytes 344072 | tf_op jit(solution)/shard_map/ppermute | solution.py:25
  215.0 0.8 collective-permute-start.11
  215.8 0.9 collective-permute-start.12
  216.7 3.5 %collective-permute-done.10.refs_1_ = bf16[64,896]{1,0:T(8,128)(2,1)S(1)} collective-permute-done((bf16[64,896]{1,0:T(8,128)(2,1)S(1)}, bf16[64,896]{1,0:T(8,128)(2,1)S(1)}, u32[]{:S(2)}, u32[]{:S(2)}) %collective-permute-start.10) | collective-permute-done | bytes 114720 | tf_op jit(solution)/shard_map/ppermute | solution.py:25
  220.2 1.2 collective-permute-done.11.refs_2_
  221.4 1.2 collective-permute-done.12.refs_3_
  222.5 1.4 shard_map.62
  (33 shorter events, 0.1 us)
Async XLA Ops:
  9.8 1.2 copy-start.1
  11.0 10.3 %copy-start.12 = (f32[64,8]{0,1:T(8,128)S(1)}, f32[64,8]{0,1:T(8,128)}, u32[]{:S(2)}) copy-start(f32[64,8]{0,1:T(8,128)} %param.8) | copy-start | bytes 6148
  11.0 11.3 %copy-start = (bf16[1,1,4,64,3584]{4,3,2,1,0:T(8,128)(2,1)S(1)}, bf16[1,1,4,64,3584]{4,3,2,1,0:T(8,128)(2,1)}, u32[]{:S(2)}) copy-start(bf16[1,1,4,64,3584]{4,3,2,1,0:T(8,128)(2,1)} %param.5) | copy-start | bytes 5505028
  12.7 37.9 %all-to-all-start = ((bf16[8,64,1024]{2,1,0:T(8,128)(2,1)}), bf16[8,64,1024]{2,1,0:T(8,128)(2,1)S(1)}, u32[]{:S(2)}, u32[]{:S(2)}) async-start(bf16[8,64,1024]{2,1,0:T(8,128)(2,1)} %bitcast.6), calls=%async_computation | async-start | bytes 2097152 | tf_op jit(solution)/shard_map/all_to_all | solution.py:293
  21.2 114.3 %all-gather.3.cloned.1.call-start = ((), (), s32[]{:S(2)}) async-start(), calls=%async_computation.5 | async-start | bytes 9175040 | tf_op jit(solution)/shard_map/all_gather | solution.py:304
  22.4 28.3 %copy-start.4 = (s32[4]{0:T(128)}, s32[4]{0:T(128)S(1)}, u32[]{:S(2)}) copy-start(s32[4]{0:T(128)S(1)} %pad_add_fusion.pos_ref) | copy-start | bytes 52
  23.1 14.2 %collective-permute-start.3 = (bf16[272,896]{1,0:T(8,128)(2,1)S(1)}, bf16[272,896]{1,0:T(8,128)(2,1)S(1)}, u32[]{:S(2)}, u32[]{:S(2)}) collective-permute-start(bf16[272,896]{1,0:T(8,128)(2,1)S(1)} %get-tuple-element.21), channel_id=1, source_target_pairs={{0,1},{1,2},{2,3},{3,0},{4,5},{5,6},{6,7},{7,4},{8,9},{9,10},{10,1... | collective-permute-start | bytes 1462280 | tf_op jit(solution)/shard_map/ppermute | solution.py:19
  24.7 23.9 %collective-permute-start.4 = (bf16[272,896]{1,0:T(8,128)(2,1)S(1)}, bf16[272,896]{1,0:T(8,128)(2,1)S(1)}, u32[]{:S(2)}, u32[]{:S(2)}) collective-permute-start(bf16[272,896]{1,0:T(8,128)(2,1)S(1)} %get-tuple-element.22), channel_id=1, source_target_pairs={{0,2},{1,3},{2,0},{3,1},{4,6},{5,7},{6,4},{7,5},{8,10},{9,11},{10,... | collective-permute-start | bytes 1462280 | tf_op jit(solution)/shard_map/ppermute | solution.py:19
  27.6 21.0 %collective-permute-start.5 = (bf16[272,896]{1,0:T(8,128)(2,1)S(1)}, bf16[272,896]{1,0:T(8,128)(2,1)S(1)}, u32[]{:S(2)}, u32[]{:S(2)}) collective-permute-start(bf16[272,896]{1,0:T(8,128)(2,1)S(1)} %get-tuple-element.23), channel_id=1, source_target_pairs={{0,3},{1,0},{2,1},{3,2},{4,7},{5,4},{6,5},{7,6},{8,11},{9,8},{10,9... | collective-permute-start | bytes 1462280 | tf_op jit(solution)/shard_map/ppermute | solution.py:19
  48.6 5.4 %copy-start.2 = (bf16[64,8,1024]{2,1,0:T(8,128)(2,1)S(1)}, bf16[64,8,1024]{2,1,0:T(8,128)(2,1)}, u32[]{:S(2)}) copy-start(bf16[64,8,1024]{2,1,0:T(8,128)(2,1)} %param.9) | copy-start | bytes 3145732
  50.7 5.0 %copy-start.6 = (bf16[8,64,1024]{2,1,0:T(8,128)(2,1)}, bf16[8,64,1024]{2,1,0:T(8,128)(2,1)S(1)}, u32[]{:S(2)}) copy-start(bf16[8,64,1024]{2,1,0:T(8,128)(2,1)S(1)} %all-to-all-done.refs_0_) | copy-start | bytes 3145732
  50.7 26.4 %collective-permute-start = (bf16[8,64,1024]{2,1,0:T(8,128)(2,1)S(1)}, bf16[8,64,1024]{2,1,0:T(8,128)(2,1)S(1)}, u32[]{:S(2)}, u32[]{:S(2)}) collective-permute-start(bf16[8,64,1024]{2,1,0:T(8,128)(2,1)S(1)} %all-to-all-done.refs_0_), channel_id=1, source_target_pairs={{0,1},{1,2},{2,3},{3,0},{64,67},{65,64},{66,65},{67,66},{4,5},{5,6... | collective-permute-start | bytes 3145736 | tf_op jit(solution)/shard_map/ppermute | solution.py:25
  52.0 25.1 %collective-permute-start.1 = (bf16[8,64,1024]{2,1,0:T(8,128)(2,1)S(1)}, bf16[8,64,1024]{2,1,0:T(8,128)(2,1)}, u32[]{:S(2)}, u32[]{:S(2)}) collective-permute-start(bf16[8,64,1024]{2,1,0:T(8,128)(2,1)S(1)} %all-to-all-done.refs_0_), channel_id=1, source_target_pairs={{0,3},{1,0},{2,1},{3,2},{64,65},{65,66},{66,67},{67,64},{4,7},{5,4... | collective-permute-start | bytes 3145736 | tf_op jit(solution)/shard_map/ppermute | solution.py:25
  55.7 34.4 %all-to-all-start.1 = ((bf16[8,64,1024]{2,1,0:T(8,128)(2,1)}), bf16[8,64,1024]{2,1,0:T(8,128)(2,1)S(1)}, u32[]{:S(2)}, u32[]{:S(2)}) async-start(bf16[8,64,1024]{2,1,0:T(8,128)(2,1)} %bitcast.12), calls=%async_computation.1 | async-start | bytes 2097152 | tf_op jit(solution)/shard_map/all_to_all | solution.py:307
  62.6 148.5 %reduce-scatter.2.cloned.1.call-start = ((), (), s32[]{:S(2)}) async-start(), calls=%async_computation.4 | async-start | bytes 4128768 | tf_op jit(solution)/shard_map/reduce_scatter | solution.py:319
  77.1 42.4 %copy-start.8 = (bf16[8,64,1024]{2,1,0:T(8,128)(2,1)}, bf16[8,64,1024]{2,1,0:T(8,128)(2,1)S(1)}, u32[]{:S(2)}) copy-start(bf16[8,64,1024]{2,1,0:T(8,128)(2,1)S(1)} %collective-permute-done.refs_1_) | copy-start | bytes 3145732
  77.1 16.0 %collective-permute-start.2 = (bf16[8,64,1024]{2,1,0:T(8,128)(2,1)S(1)}, bf16[8,64,1024]{2,1,0:T(8,128)(2,1)S(1)}, u32[]{:S(2)}, u32[]{:S(2)}) collective-permute-start(bf16[8,64,1024]{2,1,0:T(8,128)(2,1)S(1)} %collective-permute-done.refs_1_), channel_id=1, source_target_pairs={{0,1},{1,2},{2,3},{3,0},{64,67},{65,64},{66,65},{67,66},{4,5},{5,6... | collective-permute-start | bytes 3145736 | tf_op jit(solution)/shard_map/ppermute | solution.py:25
  90.1 29.3 %copy-start.7 = (bf16[8,64,1024]{2,1,0:T(8,128)(2,1)}, bf16[8,64,1024]{2,1,0:T(8,128)(2,1)S(1)}, u32[]{:S(2)}) copy-start(bf16[8,64,1024]{2,1,0:T(8,128)(2,1)S(1)} %all-to-all-done.1.refs_4_) | copy-start | bytes 3145732
  93.1 26.4 %copy-start.9 = (bf16[8,64,1024]{2,1,0:T(8,128)(2,1)}, bf16[8,64,1024]{2,1,0:T(8,128)(2,1)S(1)}, u32[]{:S(2)}) copy-start(bf16[8,64,1024]{2,1,0:T(8,128)(2,1)S(1)} %collective-permute-done.2.refs_2_) | copy-start | bytes 3145732
  93.1 26.2 %collective-permute-start.6 = (bf16[8,64,1024]{2,1,0:T(8,128)(2,1)S(1)}, bf16[8,64,1024]{2,1,0:T(8,128)(2,1)S(1)}, u32[]{:S(2)}, u32[]{:S(2)}) collective-permute-start(bf16[8,64,1024]{2,1,0:T(8,128)(2,1)S(1)} %all-to-all-done.1.refs_4_), channel_id=1, source_target_pairs={{0,1},{1,2},{2,3},{3,0},{64,67},{65,64},{66,65},{67,66},{4,5},{5,6... | collective-permute-start | bytes 3145736 | tf_op jit(solution)/shard_map/ppermute | solution.py:25
  93.1 26.2 %collective-permute-start.7 = (bf16[8,64,1024]{2,1,0:T(8,128)(2,1)S(1)}, bf16[8,64,1024]{2,1,0:T(8,128)(2,1)S(1)}, u32[]{:S(2)}, u32[]{:S(2)}) collective-permute-start(bf16[8,64,1024]{2,1,0:T(8,128)(2,1)S(1)} %all-to-all-done.1.refs_4_), channel_id=1, source_target_pairs={{0,3},{1,0},{2,1},{3,2},{64,65},{65,66},{66,67},{67,64},{4,7},{5,4... | collective-permute-start | bytes 3145736 | tf_op jit(solution)/shard_map/ppermute | solution.py:25
  119.3 1.0 copy-start.10
  119.3 1.4 copy-start.11
  119.3 16.2 %collective-permute-start.8 = (bf16[8,64,1024]{2,1,0:T(8,128)(2,1)S(1)}, bf16[8,64,1024]{2,1,0:T(8,128)(2,1)}, u32[]{:S(2)}, u32[]{:S(2)}) collective-permute-start(bf16[8,64,1024]{2,1,0:T(8,128)(2,1)S(1)} %collective-permute-done.6.refs_5_), channel_id=1, source_target_pairs={{0,1},{1,2},{2,3},{3,0},{64,67},{65,64},{66,65},{67,66},{4,5},{5,6... | collective-permute-start | bytes 3145736 | tf_op jit(solution)/shard_map/ppermute | solution.py:25
  120.6 0.6 copy-start.3
  135.5 13.1 %collective-permute-start.9 = (bf16[4,4,256,896]{3,2,1,0:T(8,128)(2,1)}, bf16[4,4,256,896]{3,2,1,0:T(8,128)(2,1)}, u32[]{:S(2)}, u32[]{:S(2)}) collective-permute-start(bf16[4,4,256,896]{3,2,1,0:T(8,128)(2,1)} %bitcast.27), channel_id=1, source_target_pairs={{0,64},{64,0},{1,65},{65,1},{2,66},{66,2},{3,67},{67,3},{4,68},{68... | collective-permute-start | bytes 22020104 | tf_op jit(solution)/shard_map/ppermute | solution.py:19
  161.5 61.1 %copy-start.5 = (s32[4]{0:T(128)S(1)}, s32[4]{0:T(128)}, u32[]{:S(2)}) copy-start(s32[4]{0:T(128)} %copy-done.4) | copy-start | bytes 52
  212.2 8.0 %collective-permute-start.10 = (bf16[64,896]{1,0:T(8,128)(2,1)S(1)}, bf16[64,896]{1,0:T(8,128)(2,1)S(1)}, u32[]{:S(2)}, u32[]{:S(2)}) collective-permute-start(bf16[64,896]{1,0:T(8,128)(2,1)S(1)} %get-tuple-element.33), channel_id=1, source_target_pairs={{0,3},{1,0},{2,1},{3,2},{64,65},{65,66},{66,67},{67,64},{4,7},{5,4... | collective-permute-start | bytes 344072 | tf_op jit(solution)/shard_map/ppermute | solution.py:25
  215.0 6.4 %collective-permute-start.11 = (bf16[64,896]{1,0:T(8,128)(2,1)S(1)}, bf16[64,896]{1,0:T(8,128)(2,1)S(1)}, u32[]{:S(2)}, u32[]{:S(2)}) collective-permute-start(bf16[64,896]{1,0:T(8,128)(2,1)S(1)} %get-tuple-element.32), channel_id=1, source_target_pairs={{0,2},{1,3},{2,0},{3,1},{64,66},{65,67},{66,64},{67,65},{4,6},{5,7... | collective-permute-start | bytes 344072 | tf_op jit(solution)/shard_map/ppermute | solution.py:25
  215.8 6.7 %collective-permute-start.12 = (bf16[64,896]{1,0:T(8,128)(2,1)S(1)}, bf16[64,896]{1,0:T(8,128)(2,1)S(1)}, u32[]{:S(2)}, u32[]{:S(2)}) collective-permute-start(bf16[64,896]{1,0:T(8,128)(2,1)S(1)} %get-tuple-element.31), channel_id=1, source_target_pairs={{0,1},{1,2},{2,3},{3,0},{64,67},{65,64},{66,65},{67,66},{4,5},{5,6... | collective-permute-start | bytes 344072 | tf_op jit(solution)/shard_map/ppermute | solution.py:25
Sparse Core Ops, SparseCore 0:
  50.8 77.5 all-gather.2
  161.6 49.4 reduce-scatter.1

commit v10 on v9

--- a/solution.py
+++ b/solution.py
@@ -121,82 +121,111 @@
     )(info)
 
 
-def experts_kernel(core, turns, pos_ref, *refs):
-    x_refs = refs[:turns], refs[turns:2 * turns]
-    w_ref, gate_ref, *refs = refs[2 * turns:]
+def experts_kernel(core, shifts, given, early, pos_ref, *refs):
+    turns = len(shifts)
     last = core == 1
-    sums_ref, out_ref = refs[:2] if last else (None, refs[0])
-    x_all, w_all, p_all, sums, out_all, x_sem, w_sem, sum_sem, out_sem = refs[1 + last:]
+    operands = []
+    for count in (turns, len(early)):
+        if count:
+            operands.append((refs[:count], refs[count:2 * count], refs[2 * count]))
+            refs = refs[2 * count + 1:]
+    gate_ref, *refs = refs
+    given_refs, out_ref = refs[:len(given)], refs[2 * len(given)]
+    x_all, w_all, p_all, sums, out_all, x_sem, w_sem, sum_sem, out_sem = refs[1 + 2 * len(given):]
     _, _, planes, part_slots, hidden_width = x_all.shape
-    blocks, experts, depth, width = w_ref.shape
+    blocks, experts, depth, width = operands[0][2].shape
     rows = sums.shape[2]
     slots = p_all.shape[1] // 2
     capacity = slots // experts
     c = pos_ref[1]
-    group = lax.rem(c + core, 2)
-
-    def x_copy(part, turn):
-        source = x_refs[part][turn].at[:, pl.ds(pl.multiple_of(group * part_slots, part_slots), part_slots), :]
-        return pltpu.make_async_copy(source, x_all.at[part, turn], x_sem.at[part, turn])
-
-    def w_copy(k, d):
-        return pltpu.make_async_copy(w_ref.at[d, k], w_all.at[k, pl.ds(d * depth, depth), :], w_sem.at[k, d])
+    number = lax.broadcasted_iota(jnp.int32, (rows, 2 * slots), 0).astype(jnp.float32)
+
+    def stage(place, group, count):
+        *x_refs, w_ref = operands[place]
+        first, base = place * turns, place * experts
+
+        def x_copy(part, turn):
+            source = x_refs[part][turn].at[:, pl.ds(pl.multiple_of(group * part_slots, part_slots), part_slots), :]
+            return pltpu.make_async_copy(source, x_all.at[part, first + turn], x_sem.at[part, first + turn])
+
+        def w_copy(k, d):
+            target = w_all.at[base + k, pl.ds(d * depth, depth), :]
+            return pltpu.make_async_copy(w_ref.at[d, k], target, w_sem.at[base + k, d])
+
+        def start():
+            for k in range(experts):
+                if k % 2 == 0:
+                    for turn in range(count):
+                        x_copy(k // 2, turn).start()
+                for d in range(blocks):
+                    w_copy(k, d).start()
+
+        def multiply():
+            for k in range(experts):
+                if k % 2 == 0:
+                    for turn in range(count):
+                        x_copy(k // 2, turn).wait()
+                for d in range(blocks):
+                    w_copy(k, d).wait()
+                held = k % 2 * capacity
+                block = x_all[k // 2, first:first + count, :, held:held + capacity, :].reshape(-1, hidden_width)
+                total = jnp.dot(block, w_all[base + k], preferred_element_type=jnp.float32)
+                high = total.astype(jnp.bfloat16)
+                low = (total - high.astype(jnp.float32)).astype(jnp.bfloat16)
+                for segment, value in enumerate((high, low)):
+                    start = segment * slots + k * capacity
+                    p_all[:count * planes, start:start + capacity, :] = value.reshape(-1, capacity, width)
+
+        def mixed(shift, source, plane):
+            index = pl.ds(lax.rem(shift * (1 + 2 * c), 4) * planes + plane, 1)
+            mine = number == gate_ref[group, 2, index, :]
+            high, low = (jnp.where(mine, gate_ref[group, part, index, :], 0.0) for part in range(2))
+            weights = jnp.concatenate([high, low], 0).astype(jnp.bfloat16)
+            value = jnp.dot(weights, p_all[source], preferred_element_type=jnp.float32)
+            return value[:rows] + value[rows:]
+
+        return start, multiply, mixed
 
     def sum_copy(turn):
-        return pltpu.make_async_copy(sums_ref.at[turn], sums.at[turn], sum_sem.at[turn])
+        source = given_refs[0].at[given[0].index(shifts[turn])]
+        return pltpu.make_async_copy(source, sums.at[turn], sum_sem.at[turn])
 
     def out_copy(turn):
         if last:
             return pltpu.make_async_copy(out_all.at[turn], out_ref.at[:, turn], out_sem.at[turn])
         return pltpu.make_async_copy(sums.at[turn], out_ref.at[turn], out_sem.at[turn])
 
-    for k in range(experts):
-        if k % 2 == 0:
-            for turn in range(turns):
-                x_copy(k // 2, turn).start()
-        for d in range(blocks):
-            w_copy(k, d).start()
-    if last:
-        for turn in range(turns):
-            sum_copy(turn).start()
-
-    def multiply(k, _):
-        for part in range(2):
-            @pl.when(k == 2 * part)
-            def _(part=part):
-                for turn in range(turns):
-                    x_copy(part, turn).wait()
-        for d in range(blocks):
-            w_copy(k, d).wait()
-        start = pl.multiple_of(lax.rem(k, 2) * capacity, capacity)
-        block = x_all[k // 2, :, :, pl.ds(start, capacity), :].reshape(turns * planes * capacity, hidden_width)
-        total = jnp.dot(block, w_all[k], preferred_element_type=jnp.float32)
-        high = total.astype(jnp.bfloat16)
-        low = (total - high.astype(jnp.float32)).astype(jnp.bfloat16)
-        for segment, value in enumerate((high, low)):
-            place = pl.multiple_of(segment * slots + k * capacity, capacity)
-            p_all[:, pl.ds(place, capacity), :] = value.reshape(turns * planes, capacity, width)
-        return 0
-
-    lax.fori_loop(0, experts, multiply, 0, unroll=True)
-    number = lax.broadcasted_iota(jnp.int32, (rows, 2 * slots), 0).astype(jnp.float32)
+    start, multiply, mixed = stage(0, lax.rem(c + core, 2), turns)
+    added = [turn for turn in range(turns) if given and shifts[turn] in given[0]]
+    if early:
+        start_early, multiply_early, mixed_early = stage(1, c, len(early))
+        start_early()
+    start()
+    for turn in added:
+        sum_copy(turn).start()
+    if early:
+        multiply_early()
+        for place, shift in enumerate(early):
+            turn = shifts.index(shift)
+
+            def one(plane, _, place=place, shift=shift, turn=turn):
+                sums[turn, plane] = mixed_early(shift, place * planes + plane, plane)
+                return 0
+
+            lax.fori_loop(0, planes, one, 0, unroll=8)
+    multiply()
+    for turn in added:
+        sum_copy(turn).wait()
 
     def combine(turn, _):
-        shift = lax.rem(turn * (1 + 2 * c), turns)
-        if last:
-            sum_copy(turn).wait()
+        shift = shifts[0] + turn + turn // 2 * (shifts[-1] - shifts[0] + 1 - turns)
 
         def one(plane, _):
-            index = pl.ds(shift * planes + plane, 1)
-            mine = number == gate_ref[group, 2, index, :]
-            high, low = (jnp.where(mine, gate_ref[group, part, index, :], 0.0) for part in range(2))
-            weights = jnp.concatenate([high, low], 0).astype(jnp.bfloat16)
-            mixed = jnp.dot(weights, p_all[turn * planes + plane], preferred_element_type=jnp.float32)
-            mixed = mixed[:rows] + mixed[rows:]
+            value = mixed(shift, turn * planes + plane, plane)
             if last:
-                out_all[turn, plane] = (sums[turn, plane] + mixed).astype(out_all.dtype)
+                out_all[turn, plane] = (sums[turn, plane] + value).astype(out_all.dtype)
             else:
-                sums[turn, plane] = mixed
+                sums[turn, plane] = value
             return 0
 
         lax.fori_loop(0, planes, one, 0, unroll=8)
@@ -208,8 +237,21 @@
         out_copy(turn).wait()
 
 
-def experts_call(core, pos, xs, weight, gate, rows, sums=None):
-    turns = len(xs[0])
+def wait_for_kernel(in_ref, sums_ref, out_ref):
+    out_ref[...] = in_ref[0]
+
+
+def wait_for(value, sums):
+    lanes = value.shape[2] // 8
+    return pl.pallas_call(
+        wait_for_kernel, grid=(1,), out_shape=jax.ShapeDtypeStruct((16, lanes), value.dtype),
+        in_specs=[pl.BlockSpec((1, 16, lanes), lambda i: (0, 0, 0)), pl.BlockSpec(memory_space=pl.ANY)], out_specs=pl.BlockSpec((16, lanes), lambda i: (0, 0)),
+        cost_estimate=pl.CostEstimate(flops=BESIDE, bytes_accessed=8192, transcendentals=0),
+    )(value, sums)
+
+
+def experts_call(core, shifts, pos, xs, weight, gate, rows, given=(), early=(), early_weight=None):
+    turns = len(shifts)
     blocks, experts, depth, width = weight.shape
     planes, part_slots, hidden_width = xs[0][0].shape
     part_slots = part_slots // 2
@@ -217,29 +259,31 @@
     total = jax.ShapeDtypeStruct((turns, planes, rows, width), jnp.float32)
     out = jax.ShapeDtypeStruct((planes, turns, rows, width), jnp.bfloat16) if core else total
     hbm = pl.BlockSpec(memory_space=pl.ANY)
-    arrays = [*xs[0], *xs[1], weight]
+    arrays = [xs[part][shift] for part in range(2) for shift in shifts] + [weight]
+    if early:
+        arrays += [xs[part][shift] for part in range(2) for shift in early] + [early_weight]
+    stages = 1 + bool(early)
     flops = 2 * turns * planes * slots * hidden_width * width
     bf16 = lambda *shape: pltpu.VMEM(shape, jnp.bfloat16)
-    given = [] if sums is None else [sums]
-    return pl.pallas_call(
-        functools.partial(experts_kernel, core, turns),
+    return pl.pallas_call(
+        functools.partial(experts_kernel, core, shifts, [v[0] for v in given], early),
         out_shape=out,
-        in_specs=[SMEM] + [hbm] * len(arrays) + [VMEM] + [hbm] * len(given),
+        in_specs=[SMEM] + [hbm] * len(arrays) + [VMEM] + [hbm] * (2 * len(given)),
         out_specs=hbm,
         scratch_shapes=[
-            bf16(2, turns, planes, part_slots, hidden_width),
-            bf16(experts, blocks * depth, width),
+            bf16(2, turns + len(early), planes, part_slots, hidden_width),
+            bf16(stages * experts, blocks * depth, width),
             bf16(turns * planes, 2 * slots, width),
             pltpu.VMEM(total.shape, jnp.float32),
             bf16(turns, planes, rows, width),
-            pltpu.SemaphoreType.DMA((2, turns)),
-            pltpu.SemaphoreType.DMA((experts, blocks)),
+            pltpu.SemaphoreType.DMA((2, turns + len(early))),
+            pltpu.SemaphoreType.DMA((stages * experts, blocks)),
             pltpu.SemaphoreType.DMA((turns,)),
             pltpu.SemaphoreType.DMA((turns,)),
         ],
         compiler_params=pltpu.CompilerParams(vmem_limit_bytes=60 << 20),
-        cost_estimate=cost(flops, *arrays, total, out),
-    )(pos, *arrays, gate, *given)
+        cost_estimate=cost(flops, *arrays, total, out) if core else cost(BESIDE, gate),
+    )(pos, *arrays, gate, *[v[1] for v in given], *[v[2] for v in given])
 
 
 def place_kernel(pos_ref, *refs):
@@ -309,13 +353,16 @@
     second_late = after(second, first_opposite)
     second_up, second_down = mirrored(second_late, "y", 1), mirrored(second_late, "y", -1)
     info = lax.all_to_all(after(info, second).reshape(ny, 2, planes, 4 * slots), Z, 2, 2, tiled=True)
-    gate = gates_call(info, slots)
+    gate = gates_call(after(info, second_up, second_down), slots)
     second_opposite = mirrored(after(second_up, second_down), "y", 1)
-    other_weight = shifted(after(weight, second_opposite, gate), "c", 1)
+    other_weight = shifted(after(weight, gate), "c", 1)
 
     xs = [first, first_up, first_opposite, first_down], [second, second_up, second_opposite, second_down]
-    sums = experts_call(0, pos, xs, weight, gate, rows)
-    partial = experts_call(1, pos, xs, other_weight, gate, rows, sums).reshape(-1, block_width)
+    near, every = (0, 1, 3), (0, 1, 2, 3)
+    sums = (near, experts_call(0, near, pos, xs, weight, gate, rows))
+    sums = (near, sums[1], wait_for(second_opposite, sums[1]))
+    partial = experts_call(1, every, pos, xs, other_weight, gate, rows, (sums,), (2,), weight)
+    partial = partial.reshape(-1, block_width)
     summed = lax.psum_scatter(partial, Z, scatter_dimension=0, tiled=True).reshape(ny, rows, block_width)
     final = [summed[0]] + [mirrored(summed[d], "y", -d) for d in range(1, ny)]
     return place_blocks(pos, final)

time: 231 us -> 231 us (level)
  waiting for transfers between devices: 127 us -> 122 us
  Pallas kernels: 33.4 us -> 36.3 us
    ppermute x9, waiting for transfers between devices: 45.6 us -> 29.5 us  [mirrored(): return lax.ppermute(value, ('c', axis), pairs)]
    all_gather x1, waiting for transfers between devices: 0.01 us -> 9.26 us  [per_device(): weight = lax.all_gather(joined, 'x')]
    pallas_call x2 -> x3, Pallas kernels: 26 us -> 28.8 us  [the longest x2 27.5 us: experts_call(): pl.pallas_call(functools.partial(experts_kernel, core, shifts, [v[0] for...]
  transfers between devices with their start and end apart: 17 -> 17, of which waited for: 11 -> 11; matrix products, arithmetic and copies ran while one was open for 0% -> 0% of each run, Pallas kernels for 8% -> 7%
where the time goes in v10:
time: 231 us; the launch traced here: 229 us
  waiting for transfers between devices  122 us (53%)
  Pallas kernels  36.3 us (16%)
  starting transfers between devices  34 us (15%)
  blocking collectives  14.7 us (6%)
  between operations  13.6 us (6%)
  local copies, waits for them, and re-layouts  6.15 us (3%)
    reduce_scatter x1, waiting for transfers between devices, per_device(): lax.psum_scatter(partial, Z, scatter_dimension=0, tiled=True)  51.7 us
    ppermute x9, waiting for transfers between devices, mirrored(): return lax.ppermute(value, ('c', axis), pairs)  29.5 us
    pallas_call x2, Pallas kernels, experts_call(): pl.pallas_call(functools.partial(experts_kernel, core, shifts, [v[0] for...  27.5 us
    ppermute x4, waiting for transfers between devices, shifted(): lax.ppermute(value, axis, [(i, (i + steps) % count) for i in range(count)])  19.7 us
    all_to_all x1, blocking collectives, per_device(): lax.all_to_all(after(info, second).reshape(ny, 2, planes, 4 * slots), Z,...  14.7 us
    ppermute x9, starting transfers between devices, mirrored(): return lax.ppermute(value, ('c', axis), pairs)  12.7 us
    all_to_all x1, waiting for transfers between devices, per_device(): lax.all_to_all(send(half, after(flat, first, joined), BESIDE), Z, 0, 0, t...  12.2 us
    all_gather x1, waiting for transfers between devices, per_device(): weight = lax.all_gather(joined, 'x')  9.26 us
  transfers between devices with their start and end apart: 17, of which 11 were waited for; matrix products, arithmetic and copies ran while one was open for 0% of the time, Pallas kernels for 7%

profile of v10, /device:TPU:2, one launch (start us, length us, event | category | flops | bytes accessed | tf_op | source)
XLA Modules:
  0.0 229.3 jit_solution(4311104418180046831)
XLA Ops:
  6.5 0.7 reshape.87
  7.3 0.1 eq.31
  7.4 0.8 copy.20
  8.2 0.2 compare_reduce_fusion
  8.4 0.1 reduce_window_sum.11
  8.5 1.2 fusion
  9.7 0.1 reshape.88.flat_ref
  9.8 0.0 copy-start.1
  9.8 1.2 copy-done.1
  11.0 1.7 shard_map.55
  12.7 8.5 %all-to-all-start = ((bf16[8,64,1024]{2,1,0:T(8,128)(2,1)}), bf16[8,64,1024]{2,1,0:T(8,128)(2,1)S(1)}, u32[]{:S(2)}, u32[]{:S(2)}) async-start(bf16[8,64,1024]{2,1,0:T(8,128)(2,1)} %bitcast.6), calls=%async_computation | async-start | bytes 2097152 | tf_op jit(solution)/shard_map/all_to_all | solution.py:337
  21.2 0.0 all-gather.3.cloned.1.call-start
  21.2 0.1 eq.35
  21.3 0.3 select_reduce_fusion
  21.6 0.1 convert_element_type.16
  21.7 0.1 copy.22
  21.8 0.1 broadcast_in_dim.45
  21.9 0.3 select_reduce_fusion.1
  22.2 0.1 reshape_reshape.3
  22.3 0.1 pad_add_fusion.pos_ref
  22.4 0.7 shard_map.56
  23.1 1.7 collective-permute-start.3
  24.7 2.9 %collective-permute-start.4 = (bf16[272,896]{1,0:T(8,128)(2,1)S(1)}, bf16[272,896]{1,0:T(8,128)(2,1)S(1)}, u32[]{:S(2)}, u32[]{:S(2)}) collective-permute-start(bf16[272,896]{1,0:T(8,128)(2,1)S(1)} %get-tuple-element.23), channel_id=1, source_target_pairs={{0,2},{1,3},{2,0},{3,1},{4,6},{5,7},{6,4},{7,5},{8,10},{9,11},{10,... | collective-permute-start | bytes 1462280 | tf_op jit(solution)/shard_map/ppermute | solution.py:19
  27.6 1.3 collective-permute-start.5
  29.0 8.3 %collective-permute-done.3.refs_1_ = bf16[272,896]{1,0:T(8,128)(2,1)S(1)} collective-permute-done((bf16[272,896]{1,0:T(8,128)(2,1)S(1)}, bf16[272,896]{1,0:T(8,128)(2,1)S(1)}, u32[]{:S(2)}, u32[]{:S(2)}) %collective-permute-start.3) | collective-permute-done | bytes 487456 | tf_op jit(solution)/shard_map/ppermute | solution.py:19
  37.3 11.3 %collective-permute-done.4.refs_2_ = bf16[272,896]{1,0:T(8,128)(2,1)S(1)} collective-permute-done((bf16[272,896]{1,0:T(8,128)(2,1)S(1)}, bf16[272,896]{1,0:T(8,128)(2,1)S(1)}, u32[]{:S(2)}, u32[]{:S(2)}) %collective-permute-start.4) | collective-permute-done | bytes 487456 | tf_op jit(solution)/shard_map/ppermute | solution.py:19
  48.6 0.0 collective-permute-done.5.refs_3_
  48.6 2.0 shard_map.57
  50.6 0.0 all-gather.3.cloned.1.call-update
  50.7 2.2 collective-permute-start.1
  52.9 1.7 shard_map.58
  54.6 6.9 %all-to-all-start.1 = ((bf16[8,64,1024]{2,1,0:T(8,128)(2,1)}), bf16[8,64,1024]{2,1,0:T(8,128)(2,1)S(1)}, u32[]{:S(2)}, u32[]{:S(2)}) async-start(bf16[8,64,1024]{2,1,0:T(8,128)(2,1)} %bitcast.12), calls=%async_computation.1 | async-start | bytes 2097152 | tf_op jit(solution)/shard_map/all_to_all | solution.py:351
  61.5 0.0 reduce-scatter.2.cloned.1.call-start
  61.5 14.9 %collective-permute-done.1.refs_2_.refs_3_ = bf16[8,64,1024]{2,1,0:T(8,128)(2,1)} collective-permute-done((bf16[8,64,1024]{2,1,0:T(8,128)(2,1)S(1)}, bf16[8,64,1024]{2,1,0:T(8,128)(2,1)}, u32[]{:S(2)}, u32[]{:S(2)}) %collective-permute-start.1) | collective-permute-done | bytes 1048608 | tf_op jit(solution)/shard_map/ppermute | solution.py:25
  76.4 0.0 collective-permute-done.refs_1_
  76.4 1.6 collective-permute-start.2
  78.0 12.2 %all-to-all-done.1.refs_3_.refs_4_ = bf16[8,64,1024]{2,1,0:T(8,128)(2,1)S(1)} async-done(((bf16[8,64,1024]{2,1,0:T(8,128)(2,1)}), bf16[8,64,1024]{2,1,0:T(8,128)(2,1)S(1)}, u32[]{:S(2)}, u32[]{:S(2)}) %all-to-all-start.1) | async-done | bytes 1048608 | tf_op jit(solution)/shard_map/all_to_all | solution.py:351
  90.2 2.4 %collective-permute-done.2.refs_2_.refs_9_ = bf16[8,64,1024]{2,1,0:T(8,128)(2,1)S(1)} collective-permute-done((bf16[8,64,1024]{2,1,0:T(8,128)(2,1)}, bf16[8,64,1024]{2,1,0:T(8,128)(2,1)S(1)}, u32[]{:S(2)}, u32[]{:S(2)}) %collective-permute-start.2) | collective-permute-done | bytes 1048608 | tf_op jit(solution)/shard_map/ppermute | solution.py:25
  92.6 1.8 collective-permute-start.7
  94.4 0.2 collective-permute-start.6
  94.7 14.7 %all_to_all.15 = bf16[4,2,8,256]{3,1,0,2:T(2,128)(2,1)S(1)} all-to-all(bf16[4,2,8,256]{3,1,0,2:T(2,128)(2,1)S(1)} %copy.25), channel_id=1, replica_groups=mesh['zl'=2,'c'=2,'zh'=4,'x'=4,'y'=4] {'zh','zl'}, dimensions={2} | all-to-all | bytes 65536 | tf_op jit(solution)/shard_map/all_to_all | solution.py:355
  109.3 7.6 %collective-permute-done.7.refs_5_.refs_7_ = bf16[8,64,1024]{2,1,0:T(8,128)(2,1)S(1)} collective-permute-done((bf16[8,64,1024]{2,1,0:T(8,128)(2,1)S(1)}, bf16[8,64,1024]{2,1,0:T(8,128)(2,1)S(1)}, u32[]{:S(2)}, u32[]{:S(2)}) %collective-permute-start.7) | collective-permute-done | bytes 1048608 | tf_op jit(solution)/shard_map/ppermute | solution.py:25
  117.0 0.2 collective-permute-done.6.refs_4_.refs_5_
  117.2 1.2 collective-permute-start.8
  118.3 0.1 shard_map.59.refs_7_.refs_12_
  118.4 0.0 copy-start.3
  118.4 0.6 copy-done.3
  119.1 9.3 %all-gather.3.cloned.1.call-done = bf16[16,256,896]{2,1,0:T(8,128)(2,1)} async-done(((bf16[4,256,896]{2,1,0:T(8,128)(2,1)}), bf16[16,256,896]{2,1,0:T(8,128)(2,1)}) %all-gather.3.cloned.1.call-update) | async-done | bytes 7340048 | tf_op jit(solution)/shard_map/all_gather | solution.py:348
  128.3 0.0 collective-permute-start.9
  128.3 11.2 %shard_map.60.sums_ref.refs_13_ = f32[3,8,64,896]{3,2,1,0:T(8,128)} custom-call(s32[4]{0:T(128)} %copy-done.4, bf16[8,64,1024]{2,1,0:T(8,128)(2,1)} %copy-done.8, bf16[8,64,1024]{2,1,0:T(8,128)(2,1)} %collective-permute-done.refs_1_, bf16[8,64,1024]{2,1,0:T(8,128)(2,1)} %collective-permute-done.1.refs_2_.refs_3_, bf16[8,64,1024]{2,1,0:T(8,128)(2,1)} %copy-done.9, ...), custom_call_target="tpu_custom_call" | custom-call | flops 60000002048 | bytes 98304 | tf_op jit(solution)/shard_map/pallas_call | solution.py:268
  139.6 0.0 collective-permute-done.8.in_ref.refs_6_.refs_10_
  139.6 1.0 copy-done.7
  140.6 1.3 shard_map.61.refs_14_
  141.9 0.0 collective-permute-done.9.refs_8_
  141.9 16.3 %shard_map.62 = bf16[8,4,64,896]{3,2,1,0:T(8,128)(2,1)} custom-call(s32[4]{0:T(128)} %copy-done.4, bf16[8,64,1024]{2,1,0:T(8,128)(2,1)} %copy-done.8, bf16[8,64,1024]{2,1,0:T(8,128)(2,1)} %collective-permute-done.refs_1_, bf16[8,64,1024]{2,1,0:T(8,128)(2,1)} %copy-done.6, bf16[8,64,1024]{2,1,0:T(8,128)(2,1)} %collective-permute-done.1.refs_2_.refs_3_, ...), custom_call_target="tpu_custom_call" | custom-call | flops 3758096384 | bytes 36175872 | tf_op jit(solution)/shard_map/pallas_call | solution.py:268
  158.2 0.0 reduce-scatter.2.cloned.1.call-update
  158.2 51.7 %reduce-scatter.2.cloned.1.call-done = bf16[256,896]{1,0:T(8,128)(2,1)} async-done(((bf16[2048,896]{1,0:T(8,128)(2,1)}), bf16[256,896]{1,0:T(8,128)(2,1)}) %reduce-scatter.2.cloned.1.call-update) | async-done | bytes 458768 | tf_op jit(solution)/shard_map/reduce_scatter | solution.py:366
  209.9 1.1 fusion.5
  211.0 1.6 collective-permute-start.12
  212.6 2.7 %collective-permute-start.11 = (bf16[64,896]{1,0:T(8,128)(2,1)S(1)}, bf16[64,896]{1,0:T(8,128)(2,1)S(1)}, u32[]{:S(2)}, u32[]{:S(2)}) collective-permute-start(bf16[64,896]{1,0:T(8,128)(2,1)S(1)} %get-tuple-element.34), channel_id=1, source_target_pairs={{0,2},{1,3},{2,0},{3,1},{64,66},{65,67},{66,64},{67,65},{4,6},{5,7... | collective-permute-start | bytes 344072 | tf_op jit(solution)/shard_map/ppermute | solution.py:25
  215.3 1.4 collective-permute-start.10
  216.7 0.4 collective-permute-done.12.refs_3_
  217.1 4.0 %collective-permute-done.11.refs_2_ = bf16[64,896]{1,0:T(8,128)(2,1)S(1)} collective-permute-done((bf16[64,896]{1,0:T(8,128)(2,1)S(1)}, bf16[64,896]{1,0:T(8,128)(2,1)S(1)}, u32[]{:S(2)}, u32[]{:S(2)}) %collective-permute-start.11) | collective-permute-done | bytes 114720 | tf_op jit(solution)/shard_map/ppermute | solution.py:25
  221.1 1.4 shard_map.63
  (32 shorter events, 0.1 us)
Async XLA Ops:
  9.8 1.2 copy-start.1
  11.0 10.7 %copy-start.11 = (f32[64,8]{0,1:T(8,128)S(1)}, f32[64,8]{0,1:T(8,128)}, u32[]{:S(2)}) copy-start(f32[64,8]{0,1:T(8,128)} %param.8) | copy-start | bytes 6148
  11.0 11.3 %copy-start = (bf16[1,1,4,64,3584]{4,3,2,1,0:T(8,128)(2,1)S(1)}, bf16[1,1,4,64,3584]{4,3,2,1,0:T(8,128)(2,1)}, u32[]{:S(2)}) copy-start(bf16[1,1,4,64,3584]{4,3,2,1,0:T(8,128)(2,1)} %param.5) | copy-start | bytes 5505028
  12.7 37.9 %all-to-all-start = ((bf16[8,64,1024]{2,1,0:T(8,128)(2,1)}), bf16[8,64,1024]{2,1,0:T(8,128)(2,1)S(1)}, u32[]{:S(2)}, u32[]{:S(2)}) async-start(bf16[8,64,1024]{2,1,0:T(8,128)(2,1)} %bitcast.6), calls=%async_computation | async-start | bytes 2097152 | tf_op jit(solution)/shard_map/all_to_all | solution.py:337
  21.2 107.2 %all-gather.3.cloned.1.call-start = ((), (), s32[]{:S(2)}) async-start(), calls=%async_computation.5 | async-start | bytes 9175040 | tf_op jit(solution)/shard_map/all_gather | solution.py:348
  22.4 28.3 %copy-start.4 = (s32[4]{0:T(128)}, s32[4]{0:T(128)S(1)}, u32[]{:S(2)}) copy-start(s32[4]{0:T(128)S(1)} %pad_add_fusion.pos_ref) | copy-start | bytes 52
  23.1 14.2 %collective-permute-start.3 = (bf16[272,896]{1,0:T(8,128)(2,1)S(1)}, bf16[272,896]{1,0:T(8,128)(2,1)S(1)}, u32[]{:S(2)}, u32[]{:S(2)}) collective-permute-start(bf16[272,896]{1,0:T(8,128)(2,1)S(1)} %get-tuple-element.22), channel_id=1, source_target_pairs={{0,1},{1,2},{2,3},{3,0},{4,5},{5,6},{6,7},{7,4},{8,9},{9,10},{10,1... | collective-permute-start | bytes 1462280 | tf_op jit(solution)/shard_map/ppermute | solution.py:19
  24.7 23.9 %collective-permute-start.4 = (bf16[272,896]{1,0:T(8,128)(2,1)S(1)}, bf16[272,896]{1,0:T(8,128)(2,1)S(1)}, u32[]{:S(2)}, u32[]{:S(2)}) collective-permute-start(bf16[272,896]{1,0:T(8,128)(2,1)S(1)} %get-tuple-element.23), channel_id=1, source_target_pairs={{0,2},{1,3},{2,0},{3,1},{4,6},{5,7},{6,4},{7,5},{8,10},{9,11},{10,... | collective-permute-start | bytes 1462280 | tf_op jit(solution)/shard_map/ppermute | solution.py:19
  27.6 21.0 %collective-permute-start.5 = (bf16[272,896]{1,0:T(8,128)(2,1)S(1)}, bf16[272,896]{1,0:T(8,128)(2,1)S(1)}, u32[]{:S(2)}, u32[]{:S(2)}) collective-permute-start(bf16[272,896]{1,0:T(8,128)(2,1)S(1)} %get-tuple-element.24), channel_id=1, source_target_pairs={{0,3},{1,0},{2,1},{3,2},{4,7},{5,4},{6,5},{7,6},{8,11},{9,8},{10,9... | collective-permute-start | bytes 1462280 | tf_op jit(solution)/shard_map/ppermute | solution.py:19
  48.6 4.3 %copy-start.2 = (bf16[64,8,1024]{2,1,0:T(8,128)(2,1)S(1)}, bf16[64,8,1024]{2,1,0:T(8,128)(2,1)}, u32[]{:S(2)}) copy-start(bf16[64,8,1024]{2,1,0:T(8,128)(2,1)} %param.9) | copy-start | bytes 3145732
  50.7 3.9 %copy-start.8 = (bf16[8,64,1024]{2,1,0:T(8,128)(2,1)}, bf16[8,64,1024]{2,1,0:T(8,128)(2,1)S(1)}, u32[]{:S(2)}) copy-start(bf16[8,64,1024]{2,1,0:T(8,128)(2,1)S(1)} %all-to-all-done.refs_0_) | copy-start | bytes 3145732
  50.7 25.7 %collective-permute-start.1 = (bf16[8,64,1024]{2,1,0:T(8,128)(2,1)S(1)}, bf16[8,64,1024]{2,1,0:T(8,128)(2,1)}, u32[]{:S(2)}, u32[]{:S(2)}) collective-permute-start(bf16[8,64,1024]{2,1,0:T(8,128)(2,1)S(1)} %all-to-all-done.refs_0_), channel_id=1, source_target_pairs={{0,3},{1,0},{2,1},{3,2},{64,65},{65,66},{66,67},{67,64},{4,7},{5,4... | collective-permute-start | bytes 3145736 | tf_op jit(solution)/shard_map/ppermute | solution.py:25
  52.9 23.5 %collective-permute-start = (bf16[8,64,1024]{2,1,0:T(8,128)(2,1)S(1)}, bf16[8,64,1024]{2,1,0:T(8,128)(2,1)}, u32[]{:S(2)}, u32[]{:S(2)}) collective-permute-start(bf16[8,64,1024]{2,1,0:T(8,128)(2,1)S(1)} %all-to-all-done.refs_0_), channel_id=1, source_target_pairs={{0,1},{1,2},{2,3},{3,0},{64,67},{65,64},{66,65},{67,66},{4,5},{5,6... | collective-permute-start | bytes 3145736 | tf_op jit(solution)/shard_map/ppermute | solution.py:25
  54.6 35.6 %all-to-all-start.1 = ((bf16[8,64,1024]{2,1,0:T(8,128)(2,1)}), bf16[8,64,1024]{2,1,0:T(8,128)(2,1)S(1)}, u32[]{:S(2)}, u32[]{:S(2)}) async-start(bf16[8,64,1024]{2,1,0:T(8,128)(2,1)} %bitcast.12), calls=%async_computation.1 | async-start | bytes 2097152 | tf_op jit(solution)/shard_map/all_to_all | solution.py:351
  61.5 148.4 %reduce-scatter.2.cloned.1.call-start = ((), (), s32[]{:S(2)}) async-start(), calls=%async_computation.4 | async-start | bytes 4128768 | tf_op jit(solution)/shard_map/reduce_scatter | solution.py:366
  76.4 16.2 %collective-permute-start.2 = (bf16[8,64,1024]{2,1,0:T(8,128)(2,1)}, bf16[8,64,1024]{2,1,0:T(8,128)(2,1)S(1)}, u32[]{:S(2)}, u32[]{:S(2)}) collective-permute-start(bf16[8,64,1024]{2,1,0:T(8,128)(2,1)} %collective-permute-done.refs_1_), channel_id=1, source_target_pairs={{0,1},{1,2},{2,3},{3,0},{64,67},{65,64},{66,65},{67,66},{4,5},{5,6... | collective-permute-start | bytes 3145736 | tf_op jit(solution)/shard_map/ppermute | solution.py:25
  90.2 27.0 %copy-start.9 = (bf16[8,64,1024]{2,1,0:T(8,128)(2,1)}, bf16[8,64,1024]{2,1,0:T(8,128)(2,1)S(1)}, u32[]{:S(2)}) copy-start(bf16[8,64,1024]{2,1,0:T(8,128)(2,1)S(1)} %all-to-all-done.1.refs_3_.refs_4_) | copy-start | bytes 3145732
  92.6 25.8 %copy-start.6 = (bf16[8,64,1024]{2,1,0:T(8,128)(2,1)}, bf16[8,64,1024]{2,1,0:T(8,128)(2,1)S(1)}, u32[]{:S(2)}) copy-start(bf16[8,64,1024]{2,1,0:T(8,128)(2,1)S(1)} %collective-permute-done.2.refs_2_.refs_9_) | copy-start | bytes 3145732
  92.6 24.3 %collective-permute-start.7 = (bf16[8,64,1024]{2,1,0:T(8,128)(2,1)S(1)}, bf16[8,64,1024]{2,1,0:T(8,128)(2,1)S(1)}, u32[]{:S(2)}, u32[]{:S(2)}) collective-permute-start(bf16[8,64,1024]{2,1,0:T(8,128)(2,1)S(1)} %all-to-all-done.1.refs_3_.refs_4_), channel_id=1, source_target_pairs={{0,3},{1,0},{2,1},{3,2},{64,65},{65,66},{66,67},{67,64},{4,7},{5,4... | collective-permute-start | bytes 3145736 | tf_op jit(solution)/shard_map/ppermute | solution.py:25
  94.4 22.7 %collective-permute-start.6 = (bf16[8,64,1024]{2,1,0:T(8,128)(2,1)S(1)}, bf16[8,64,1024]{2,1,0:T(8,128)(2,1)}, u32[]{:S(2)}, u32[]{:S(2)}) collective-permute-start(bf16[8,64,1024]{2,1,0:T(8,128)(2,1)S(1)} %all-to-all-done.1.refs_3_.refs_4_), channel_id=1, source_target_pairs={{0,1},{1,2},{2,3},{3,0},{64,67},{65,64},{66,65},{67,66},{4,5},{5,6... | collective-permute-start | bytes 3145736 | tf_op jit(solution)/shard_map/ppermute | solution.py:25
  117.0 1.5 copy-start.10
  117.2 22.4 %collective-permute-start.8 = (bf16[8,64,1024]{2,1,0:T(8,128)(2,1)}, bf16[8,64,1024]{2,1,0:T(8,128)(2,1)S(1)}, u32[]{:S(2)}, u32[]{:S(2)}) collective-permute-start(bf16[8,64,1024]{2,1,0:T(8,128)(2,1)} %collective-permute-done.6.refs_4_.refs_5_), channel_id=1, source_target_pairs={{0,1},{1,2},{2,3},{3,0},{64,67},{65,64},{66,65},{67,66},{4,5},{5,6... | collective-permute-start | bytes 3145736 | tf_op jit(solution)/shard_map/ppermute | solution.py:25
  118.4 0.6 copy-start.3
  128.3 13.5 %collective-permute-start.9 = (bf16[4,4,256,896]{3,2,1,0:T(8,128)(2,1)}, bf16[4,4,256,896]{3,2,1,0:T(8,128)(2,1)}, u32[]{:S(2)}, u32[]{:S(2)}) collective-permute-start(bf16[4,4,256,896]{3,2,1,0:T(8,128)(2,1)} %bitcast.27), channel_id=1, source_target_pairs={{0,64},{64,0},{1,65},{65,1},{2,66},{66,2},{3,67},{67,3},{4,68},{68... | collective-permute-start | bytes 22020104 | tf_op jit(solution)/shard_map/ppermute | solution.py:19
  139.6 1.0 copy-start.7
  158.2 62.9 %copy-start.5 = (s32[4]{0:T(128)S(1)}, s32[4]{0:T(128)}, u32[]{:S(2)}) copy-start(s32[4]{0:T(128)} %copy-done.4) | copy-start | bytes 52
  211.0 6.1 %collective-permute-start.12 = (bf16[64,896]{1,0:T(8,128)(2,1)S(1)}, bf16[64,896]{1,0:T(8,128)(2,1)S(1)}, u32[]{:S(2)}, u32[]{:S(2)}) collective-permute-start(bf16[64,896]{1,0:T(8,128)(2,1)S(1)} %get-tuple-element.33), channel_id=1, source_target_pairs={{0,1},{1,2},{2,3},{3,0},{64,67},{65,64},{66,65},{67,66},{4,5},{5,6... | collective-permute-start | bytes 344072 | tf_op jit(solution)/shard_map/ppermute | solution.py:25
  212.6 8.5 %collective-permute-start.11 = (bf16[64,896]{1,0:T(8,128)(2,1)S(1)}, bf16[64,896]{1,0:T(8,128)(2,1)S(1)}, u32[]{:S(2)}, u32[]{:S(2)}) collective-permute-start(bf16[64,896]{1,0:T(8,128)(2,1)S(1)} %get-tuple-element.34), channel_id=1, source_target_pairs={{0,2},{1,3},{2,0},{3,1},{64,66},{65,67},{66,64},{67,65},{4,6},{5,7... | collective-permute-start | bytes 344072 | tf_op jit(solution)/shard_map/ppermute | solution.py:25
  215.3 5.8 %collective-permute-start.10 = (bf16[64,896]{1,0:T(8,128)(2,1)S(1)}, bf16[64,896]{1,0:T(8,128)(2,1)S(1)}, u32[]{:S(2)}, u32[]{:S(2)}) collective-permute-start(bf16[64,896]{1,0:T(8,128)(2,1)S(1)} %get-tuple-element.35), channel_id=1, source_target_pairs={{0,3},{1,0},{2,1},{3,2},{64,65},{65,66},{66,67},{67,64},{4,7},{5,4... | collective-permute-start | bytes 344072 | tf_op jit(solution)/shard_map/ppermute | solution.py:25
Sparse Core Ops, SparseCore 0:
  50.8 77.5 all-gather.2
  158.4 51.4 reduce-scatter.1

commit v11 on v10

--- a/solution.py
+++ b/solution.py
@@ -281,7 +281,7 @@
             pltpu.SemaphoreType.DMA((turns,)),
             pltpu.SemaphoreType.DMA((turns,)),
         ],
-        compiler_params=pltpu.CompilerParams(vmem_limit_bytes=60 << 20),
+        compiler_params=pltpu.CompilerParams(vmem_limit_bytes=(46 if core else 60) << 20),
         cost_estimate=cost(flops, *arrays, total, out) if core else cost(BESIDE, gate),
     )(pos, *arrays, gate, *[v[1] for v in given], *[v[2] for v in given])
 

time: 231 us -> 233 us (level)
  local copies, waits for them, and re-layouts: 6.15 us -> 12.5 us
  Pallas kernels: 36.3 us -> 32.8 us
    unnamed x26 -> x40, local copies, waits for them, and re-layouts: 3.73 us -> 10.1 us
    pallas_call x2, Pallas kernels: 27.5 us -> 25 us  [experts_call(): pl.pallas_call(functools.partial(experts_kernel, core, shifts, [v[0] for...]
  transfers between devices with their start and end apart: 17 -> 17, of which waited for: 11 -> 10; matrix products, arithmetic and copies ran while one was open for 0% -> 0% of each run, Pallas kernels for 7% -> 7%
where the time goes in v11:
time: 233 us; the launch traced here: 231 us
  waiting for transfers between devices  121 us (52%)
  starting transfers between devices  34.2 us (15%)
  Pallas kernels  32.8 us (14%)
  blocking collectives  14.4 us (6%)
  between operations  13.6 us (6%)
  local copies, waits for them, and re-layouts  12.5 us (5%)
    reduce_scatter x1, waiting for transfers between devices, per_device(): lax.psum_scatter(partial, Z, scatter_dimension=0, tiled=True)  51.7 us
    ppermute x9, waiting for transfers between devices, mirrored(): return lax.ppermute(value, ('c', axis), pairs)  29.4 us
    pallas_call x2, Pallas kernels, experts_call(): pl.pallas_call(functools.partial(experts_kernel, core, shifts, [v[0] for...  25 us
    ppermute x4, waiting for transfers between devices, shifted(): lax.ppermute(value, axis, [(i, (i + steps) % count) for i in range(count)])  19.7 us
    all_to_all x1, blocking collectives, per_device(): lax.all_to_all(after(info, second).reshape(ny, 2, planes, 4 * slots), Z,...  14.4 us
    ppermute x9, starting transfers between devices, mirrored(): return lax.ppermute(value, ('c', axis), pairs)  13 us
    all_to_all x1, waiting for transfers between devices, per_device(): lax.all_to_all(send(half, after(flat, first, joined), BESIDE), Z, 0, 0, t...  11.4 us
    unnamed x40, local copies, waits for them, and re-layouts  10.1 us
  transfers between devices with their start and end apart: 17, of which 10 were waited for; matrix products, arithmetic and copies ran while one was open for 0% of the time, Pallas kernels for 7%

profile of v11, /device:TPU:2, one launch (start us, length us, event | category | flops | bytes accessed | tf_op | source)
XLA Modules:
  0.0 231.2 jit_solution(14282063259932231631)
XLA Ops:
  6.5 0.7 reshape.87
  7.3 0.1 eq.31
  7.4 0.8 copy.20
  8.2 0.2 compare_reduce_fusion
  8.4 0.1 reduce_window_sum.11
  8.5 1.2 fusion
  9.7 0.1 reshape.88.flat_ref
  9.8 0.0 copy-start.9
  9.8 1.2 copy-done.9
  11.0 1.8 shard_map.55
  12.8 8.5 %all-to-all-start = ((bf16[8,64,1024]{2,1,0:T(8,128)(2,1)}), bf16[8,64,1024]{2,1,0:T(8,128)(2,1)S(1)}, u32[]{:S(2)}, u32[]{:S(2)}) async-start(bf16[8,64,1024]{2,1,0:T(8,128)(2,1)} %bitcast.6), calls=%async_computation | async-start | bytes 2097152 | tf_op jit(solution)/shard_map/all_to_all | solution.py:337
  21.3 0.0 all-gather.3.cloned.1.call-start
  21.4 0.1 eq.35
  21.4 0.3 select_reduce_fusion
  21.8 0.1 convert_element_type.16
  21.8 0.1 copy.22
  21.9 0.1 broadcast_in_dim.45
  22.0 0.3 select_reduce_fusion.1
  22.3 0.1 reshape_reshape.3
  22.4 0.1 pad_add_fusion.pos_ref
  22.5 0.7 shard_map.56
  23.2 1.7 collective-permute-start.3
  24.8 2.9 %collective-permute-start.4 = (bf16[272,896]{1,0:T(8,128)(2,1)S(1)}, bf16[272,896]{1,0:T(8,128)(2,1)S(1)}, u32[]{:S(2)}, u32[]{:S(2)}) collective-permute-start(bf16[272,896]{1,0:T(8,128)(2,1)S(1)} %get-tuple-element.23), channel_id=1, source_target_pairs={{0,2},{1,3},{2,0},{3,1},{4,6},{5,7},{6,4},{7,5},{8,10},{9,11},{10,... | collective-permute-start | bytes 1462280 | tf_op jit(solution)/shard_map/ppermute | solution.py:19
  27.7 1.3 collective-permute-start.5
  29.1 8.3 %collective-permute-done.3.refs_1_ = bf16[272,896]{1,0:T(8,128)(2,1)S(1)} collective-permute-done((bf16[272,896]{1,0:T(8,128)(2,1)S(1)}, bf16[272,896]{1,0:T(8,128)(2,1)S(1)}, u32[]{:S(2)}, u32[]{:S(2)}) %collective-permute-start.3) | collective-permute-done | bytes 487456 | tf_op jit(solution)/shard_map/ppermute | solution.py:19
  37.4 11.3 %collective-permute-done.4.refs_2_ = bf16[272,896]{1,0:T(8,128)(2,1)S(1)} collective-permute-done((bf16[272,896]{1,0:T(8,128)(2,1)S(1)}, bf16[272,896]{1,0:T(8,128)(2,1)S(1)}, u32[]{:S(2)}, u32[]{:S(2)}) %collective-permute-start.4) | collective-permute-done | bytes 487456 | tf_op jit(solution)/shard_map/ppermute | solution.py:19
  48.8 1.9 shard_map.57
  50.7 0.0 all-gather.3.cloned.1.call-update
  50.7 2.3 collective-permute-start.1
  53.0 0.7 shard_map.58
  53.8 1.1 copy-done.11
  54.9 6.8 %all-to-all-start.1 = ((bf16[8,64,1024]{2,1,0:T(8,128)(2,1)}), bf16[8,64,1024]{2,1,0:T(8,128)(2,1)S(1)}, u32[]{:S(2)}, u32[]{:S(2)}) async-start(bf16[8,64,1024]{2,1,0:T(8,128)(2,1)} %bitcast.23), calls=%async_computation.1 | async-start | bytes 2097152 | tf_op jit(solution)/shard_map/all_to_all | solution.py:351
  61.7 0.0 reduce-scatter.2.cloned.1.call-start
  61.7 14.7 %collective-permute-done.1.refs_2_.refs_3_ = bf16[8,64,1024]{2,1,0:T(8,128)(2,1)S(1)} collective-permute-done((bf16[8,64,1024]{2,1,0:T(8,128)(2,1)S(1)}, bf16[8,64,1024]{2,1,0:T(8,128)(2,1)S(1)}, u32[]{:S(2)}, u32[]{:S(2)}) %collective-permute-start.1) | collective-permute-done | bytes 1048608 | tf_op jit(solution)/shard_map/ppermute | solution.py:25
  76.4 1.0 copy-done.7
  77.4 1.6 collective-permute-start.2
  79.0 11.4 %all-to-all-done.1.refs_3_.refs_4_ = bf16[8,64,1024]{2,1,0:T(8,128)(2,1)S(1)} async-done(((bf16[8,64,1024]{2,1,0:T(8,128)(2,1)}), bf16[8,64,1024]{2,1,0:T(8,128)(2,1)S(1)}, u32[]{:S(2)}, u32[]{:S(2)}) %all-to-all-start.1) | async-done | bytes 1048608 | tf_op jit(solution)/shard_map/all_to_all | solution.py:351
  90.4 3.2 %collective-permute-done.2.refs_2_.refs_9_ = bf16[8,64,1024]{2,1,0:T(8,128)(2,1)S(1)} collective-permute-done((bf16[8,64,1024]{2,1,0:T(8,128)(2,1)}, bf16[8,64,1024]{2,1,0:T(8,128)(2,1)S(1)}, u32[]{:S(2)}, u32[]{:S(2)}) %collective-permute-start.2) | collective-permute-done | bytes 1048608 | tf_op jit(solution)/shard_map/ppermute | solution.py:25
  93.6 1.7 collective-permute-start.7
  95.4 0.3 collective-permute-start.6
  95.7 14.4 %all_to_all.15 = bf16[4,2,8,256]{3,1,0,2:T(2,128)(2,1)S(1)} all-to-all(bf16[4,2,8,256]{3,1,0,2:T(2,128)(2,1)S(1)} %copy.25), channel_id=1, replica_groups=mesh['zl'=2,'c'=2,'zh'=4,'x'=4,'y'=4] {'zh','zl'}, dimensions={2} | all-to-all | bytes 65536 | tf_op jit(solution)/shard_map/all_to_all | solution.py:355
  110.1 7.1 %collective-permute-done.7.refs_5_.refs_7_ = bf16[8,64,1024]{2,1,0:T(8,128)(2,1)S(1)} collective-permute-done((bf16[8,64,1024]{2,1,0:T(8,128)(2,1)S(1)}, bf16[8,64,1024]{2,1,0:T(8,128)(2,1)S(1)}, u32[]{:S(2)}, u32[]{:S(2)}) %collective-permute-start.7) | collective-permute-done | bytes 1048608 | tf_op jit(solution)/shard_map/ppermute | solution.py:25
  117.2 1.4 collective-permute-start.8
  118.5 0.1 shard_map.59.refs_7_.refs_12_
  118.6 0.0 copy-start.12
  118.6 0.6 copy-done.12
  119.3 9.1 %all-gather.3.cloned.1.call-done = bf16[16,256,896]{2,1,0:T(8,128)(2,1)} async-done(((bf16[4,256,896]{2,1,0:T(8,128)(2,1)}), bf16[16,256,896]{2,1,0:T(8,128)(2,1)}) %all-gather.3.cloned.1.call-update) | async-done | bytes 7340048 | tf_op jit(solution)/shard_map/all_gather | solution.py:348
  128.4 11.3 %shard_map.60.sums_ref.refs_13_ = f32[3,8,64,896]{3,2,1,0:T(8,128)} custom-call(s32[4]{0:T(128)} %copy-done.14, bf16[8,64,1024]{2,1,0:T(8,128)(2,1)} %copy-done.2, bf16[8,64,1024]{2,1,0:T(8,128)(2,1)} %collective-permute-done.refs_1_, bf16[8,64,1024]{2,1,0:T(8,128)(2,1)} %copy-done.7, bf16[8,64,1024]{2,1,0:T(8,128)(2,1)} %copy-done.4, ...), custom_call_target="tpu_custom_call" | custom-call | flops 60000002048 | bytes 98304 | tf_op jit(solution)/shard_map/pallas_call | solution.py:268
  139.8 1.0 copy-done
  140.7 1.3 shard_map.61.refs_14_
  142.0 1.2 copy-done.1
  143.3 1.2 copy-done.5
  144.5 1.2 copy-done.8
  145.7 0.7 copy-done.16
  146.4 13.7 %shard_map.62 = bf16[8,4,64,896]{3,2,1,0:T(8,128)(2,1)} custom-call(s32[4]{0:T(128)S(1)} %copy-done.15, bf16[8,64,1024]{2,1,0:T(8,128)(2,1)S(1)} %copy-done.3, bf16[8,64,1024]{2,1,0:T(8,128)(2,1)} %collective-permute-done.refs_1_, bf16[8,64,1024]{2,1,0:T(8,128)(2,1)S(1)} %collective-permute-done.2.refs_2_.refs_9_, bf16[8,64,1024]{2,1,0:T(8,128)(2,1)S(1)} %copy-done.8, ...), custom_call_target="tpu_custom_call" | custom-call | flops 3758096384 | bytes 36175872 | tf_op jit(solution)/shard_map/pallas_call | solution.py:268
  160.1 0.0 reduce-scatter.2.cloned.1.call-update
  160.1 51.7 %reduce-scatter.2.cloned.1.call-done = bf16[256,896]{1,0:T(8,128)(2,1)} async-done(((bf16[2048,896]{1,0:T(8,128)(2,1)}), bf16[256,896]{1,0:T(8,128)(2,1)}) %reduce-scatter.2.cloned.1.call-update) | async-done | bytes 458768 | tf_op jit(solution)/shard_map/reduce_scatter | solution.py:366
  211.8 1.1 fusion.5
  212.9 1.6 collective-permute-start.12
  214.4 2.7 %collective-permute-start.11 = (bf16[64,896]{1,0:T(8,128)(2,1)S(1)}, bf16[64,896]{1,0:T(8,128)(2,1)S(1)}, u32[]{:S(2)}, u32[]{:S(2)}) collective-permute-start(bf16[64,896]{1,0:T(8,128)(2,1)S(1)} %get-tuple-element.34), channel_id=1, source_target_pairs={{0,2},{1,3},{2,0},{3,1},{64,66},{65,67},{66,64},{67,65},{4,6},{5,7... | collective-permute-start | bytes 344072 | tf_op jit(solution)/shard_map/ppermute | solution.py:25
  217.1 1.4 collective-permute-start.10
  218.6 0.4 collective-permute-done.12.refs_3_
  218.9 4.0 %collective-permute-done.11.refs_2_ = bf16[64,896]{1,0:T(8,128)(2,1)S(1)} collective-permute-done((bf16[64,896]{1,0:T(8,128)(2,1)S(1)}, bf16[64,896]{1,0:T(8,128)(2,1)S(1)}, u32[]{:S(2)}, u32[]{:S(2)}) %collective-permute-start.11) | collective-permute-done | bytes 114720 | tf_op jit(solution)/shard_map/ppermute | solution.py:25
  223.0 1.4 shard_map.63
  (46 shorter events, 0.2 us)
Async XLA Ops:
  9.8 1.2 copy-start.9
  11.0 10.8 %copy-start.18 = (f32[64,8]{0,1:T(8,128)S(1)}, f32[64,8]{0,1:T(8,128)}, u32[]{:S(2)}) copy-start(f32[64,8]{0,1:T(8,128)} %param.8) | copy-start | bytes 6148
  11.0 11.4 %copy-start.6 = (bf16[1,1,4,64,3584]{4,3,2,1,0:T(8,128)(2,1)S(1)}, bf16[1,1,4,64,3584]{4,3,2,1,0:T(8,128)(2,1)}, u32[]{:S(2)}) copy-start(bf16[1,1,4,64,3584]{4,3,2,1,0:T(8,128)(2,1)} %param.5) | copy-start | bytes 5505028
  12.8 37.9 %all-to-all-start = ((bf16[8,64,1024]{2,1,0:T(8,128)(2,1)}), bf16[8,64,1024]{2,1,0:T(8,128)(2,1)S(1)}, u32[]{:S(2)}, u32[]{:S(2)}) async-start(bf16[8,64,1024]{2,1,0:T(8,128)(2,1)} %bitcast.6), calls=%async_computation | async-start | bytes 2097152 | tf_op jit(solution)/shard_map/all_to_all | solution.py:337
  21.3 107.1 %all-gather.3.cloned.1.call-start = ((), (), s32[]{:S(2)}) async-start(), calls=%async_computation.5 | async-start | bytes 9175040 | tf_op jit(solution)/shard_map/all_gather | solution.py:348
  22.5 28.2 %copy-start.14 = (s32[4]{0:T(128)}, s32[4]{0:T(128)S(1)}, u32[]{:S(2)}) copy-start(s32[4]{0:T(128)S(1)} %pad_add_fusion.pos_ref) | copy-start | bytes 52
  23.2 14.2 %collective-permute-start.3 = (bf16[272,896]{1,0:T(8,128)(2,1)S(1)}, bf16[272,896]{1,0:T(8,128)(2,1)S(1)}, u32[]{:S(2)}, u32[]{:S(2)}) collective-permute-start(bf16[272,896]{1,0:T(8,128)(2,1)S(1)} %get-tuple-element.22), channel_id=1, source_target_pairs={{0,1},{1,2},{2,3},{3,0},{4,5},{5,6},{6,7},{7,4},{8,9},{9,10},{10,1... | collective-permute-start | bytes 1462280 | tf_op jit(solution)/shard_map/ppermute | solution.py:19
  24.8 23.9 %collective-permute-start.4 = (bf16[272,896]{1,0:T(8,128)(2,1)S(1)}, bf16[272,896]{1,0:T(8,128)(2,1)S(1)}, u32[]{:S(2)}, u32[]{:S(2)}) collective-permute-start(bf16[272,896]{1,0:T(8,128)(2,1)S(1)} %get-tuple-element.23), channel_id=1, source_target_pairs={{0,2},{1,3},{2,0},{3,1},{4,6},{5,7},{6,4},{7,5},{8,10},{9,11},{10,... | collective-permute-start | bytes 1462280 | tf_op jit(solution)/shard_map/ppermute | solution.py:19
  27.7 21.0 %collective-permute-start.5 = (bf16[272,896]{1,0:T(8,128)(2,1)S(1)}, bf16[272,896]{1,0:T(8,128)(2,1)S(1)}, u32[]{:S(2)}, u32[]{:S(2)}) collective-permute-start(bf16[272,896]{1,0:T(8,128)(2,1)S(1)} %get-tuple-element.24), channel_id=1, source_target_pairs={{0,3},{1,0},{2,1},{3,2},{4,7},{5,4},{6,5},{7,6},{8,11},{9,8},{10,9... | collective-permute-start | bytes 1462280 | tf_op jit(solution)/shard_map/ppermute | solution.py:19
  48.8 4.3 %copy-start.10 = (bf16[64,8,1024]{2,1,0:T(8,128)(2,1)S(1)}, bf16[64,8,1024]{2,1,0:T(8,128)(2,1)}, u32[]{:S(2)}) copy-start(bf16[64,8,1024]{2,1,0:T(8,128)(2,1)} %param.9) | copy-start | bytes 3145732
  50.7 3.1 %copy-start.2 = (bf16[8,64,1024]{2,1,0:T(8,128)(2,1)}, bf16[8,64,1024]{2,1,0:T(8,128)(2,1)S(1)}, u32[]{:S(2)}) copy-start(bf16[8,64,1024]{2,1,0:T(8,128)(2,1)S(1)} %all-to-all-done.refs_0_) | copy-start | bytes 3145732
  50.7 25.7 %collective-permute-start.1 = (bf16[8,64,1024]{2,1,0:T(8,128)(2,1)S(1)}, bf16[8,64,1024]{2,1,0:T(8,128)(2,1)S(1)}, u32[]{:S(2)}, u32[]{:S(2)}) collective-permute-start(bf16[8,64,1024]{2,1,0:T(8,128)(2,1)S(1)} %all-to-all-done.refs_0_), channel_id=1, source_target_pairs={{0,3},{1,0},{2,1},{3,2},{64,65},{65,66},{66,67},{67,64},{4,7},{5,4... | collective-permute-start | bytes 3145736 | tf_op jit(solution)/shard_map/ppermute | solution.py:25
  53.0 24.3 %collective-permute-start = (bf16[8,64,1024]{2,1,0:T(8,128)(2,1)S(1)}, bf16[8,64,1024]{2,1,0:T(8,128)(2,1)}, u32[]{:S(2)}, u32[]{:S(2)}) collective-permute-start(bf16[8,64,1024]{2,1,0:T(8,128)(2,1)S(1)} %all-to-all-done.refs_0_), channel_id=1, source_target_pairs={{0,1},{1,2},{2,3},{3,0},{64,67},{65,64},{66,65},{67,66},{4,5},{5,6... | collective-permute-start | bytes 3145736 | tf_op jit(solution)/shard_map/ppermute | solution.py:25
  53.8 1.1 copy-start.11
  54.9 35.5 %all-to-all-start.1 = ((bf16[8,64,1024]{2,1,0:T(8,128)(2,1)}), bf16[8,64,1024]{2,1,0:T(8,128)(2,1)S(1)}, u32[]{:S(2)}, u32[]{:S(2)}) async-start(bf16[8,64,1024]{2,1,0:T(8,128)(2,1)} %bitcast.23), calls=%async_computation.1 | async-start | bytes 2097152 | tf_op jit(solution)/shard_map/all_to_all | solution.py:351
  61.7 150.1 %reduce-scatter.2.cloned.1.call-start = ((), (), s32[]{:S(2)}) async-start(), calls=%async_computation.4 | async-start | bytes 4128768 | tf_op jit(solution)/shard_map/reduce_scatter | solution.py:366
  76.4 1.0 copy-start.7
  77.4 16.2 %collective-permute-start.2 = (bf16[8,64,1024]{2,1,0:T(8,128)(2,1)}, bf16[8,64,1024]{2,1,0:T(8,128)(2,1)S(1)}, u32[]{:S(2)}, u32[]{:S(2)}) collective-permute-start(bf16[8,64,1024]{2,1,0:T(8,128)(2,1)} %collective-permute-done.refs_1_), channel_id=1, source_target_pairs={{0,1},{1,2},{2,3},{3,0},{64,67},{65,64},{66,65},{67,66},{4,5},{5,6... | collective-permute-start | bytes 3145736 | tf_op jit(solution)/shard_map/ppermute | solution.py:25
  90.4 26.8 %copy-start.4 = (bf16[8,64,1024]{2,1,0:T(8,128)(2,1)}, bf16[8,64,1024]{2,1,0:T(8,128)(2,1)S(1)}, u32[]{:S(2)}) copy-start(bf16[8,64,1024]{2,1,0:T(8,128)(2,1)S(1)} %all-to-all-done.1.refs_3_.refs_4_) | copy-start | bytes 3145732
  93.6 23.5 %collective-permute-start.7 = (bf16[8,64,1024]{2,1,0:T(8,128)(2,1)S(1)}, bf16[8,64,1024]{2,1,0:T(8,128)(2,1)S(1)}, u32[]{:S(2)}, u32[]{:S(2)}) collective-permute-start(bf16[8,64,1024]{2,1,0:T(8,128)(2,1)S(1)} %all-to-all-done.1.refs_3_.refs_4_), channel_id=1, source_target_pairs={{0,3},{1,0},{2,1},{3,2},{64,65},{65,66},{66,67},{67,64},{4,7},{5,4... | collective-permute-start | bytes 3145736 | tf_op jit(solution)/shard_map/ppermute | solution.py:25
  95.4 21.8 %collective-permute-start.6 = (bf16[8,64,1024]{2,1,0:T(8,128)(2,1)S(1)}, bf16[8,64,1024]{2,1,0:T(8,128)(2,1)}, u32[]{:S(2)}, u32[]{:S(2)}) collective-permute-start(bf16[8,64,1024]{2,1,0:T(8,128)(2,1)S(1)} %all-to-all-done.1.refs_3_.refs_4_), channel_id=1, source_target_pairs={{0,1},{1,2},{2,3},{3,0},{64,67},{65,64},{66,65},{67,66},{4,5},{5,6... | collective-permute-start | bytes 3145736 | tf_op jit(solution)/shard_map/ppermute | solution.py:25
  117.1 1.5 copy-start.17
  117.2 22.6 %collective-permute-start.8 = (bf16[8,64,1024]{2,1,0:T(8,128)(2,1)}, bf16[8,64,1024]{2,1,0:T(8,128)(2,1)S(1)}, u32[]{:S(2)}, u32[]{:S(2)}) collective-permute-start(bf16[8,64,1024]{2,1,0:T(8,128)(2,1)} %collective-permute-done.6.refs_4_.refs_5_), channel_id=1, source_target_pairs={{0,1},{1,2},{2,3},{3,0},{64,67},{65,64},{66,65},{67,66},{4,5},{5,6... | collective-permute-start | bytes 3145736 | tf_op jit(solution)/shard_map/ppermute | solution.py:25
  118.6 0.6 copy-start.12
  128.4 13.6 %collective-permute-start.9 = (bf16[4,4,256,896]{3,2,1,0:T(8,128)(2,1)}, bf16[4,4,256,896]{3,2,1,0:T(8,128)(2,1)}, u32[]{:S(2)}, u32[]{:S(2)}) collective-permute-start(bf16[4,4,256,896]{3,2,1,0:T(8,128)(2,1)} %bitcast.28), channel_id=1, source_target_pairs={{0,64},{64,0},{1,65},{65,1},{2,66},{66,2},{3,67},{67,3},{4,68},{68... | collective-permute-start | bytes 22020104 | tf_op jit(solution)/shard_map/ppermute | solution.py:19
  139.7 2.3 copy-start.3
  139.7 2.3 copy-start.13
  139.7 2.3 copy-start.15
  139.8 1.0 copy-start
  142.0 1.2 copy-start.1
  143.3 1.2 copy-start.5
  144.5 1.2 copy-start.8
  145.7 0.7 copy-start.16
  212.9 6.1 %collective-permute-start.12 = (bf16[64,896]{1,0:T(8,128)(2,1)S(1)}, bf16[64,896]{1,0:T(8,128)(2,1)S(1)}, u32[]{:S(2)}, u32[]{:S(2)}) collective-permute-start(bf16[64,896]{1,0:T(8,128)(2,1)S(1)} %get-tuple-element.33), channel_id=1, source_target_pairs={{0,1},{1,2},{2,3},{3,0},{64,67},{65,64},{66,65},{67,66},{4,5},{5,6... | collective-permute-start | bytes 344072 | tf_op jit(solution)/shard_map/ppermute | solution.py:25
  214.4 8.5 %collective-permute-start.11 = (bf16[64,896]{1,0:T(8,128)(2,1)S(1)}, bf16[64,896]{1,0:T(8,128)(2,1)S(1)}, u32[]{:S(2)}, u32[]{:S(2)}) collective-permute-start(bf16[64,896]{1,0:T(8,128)(2,1)S(1)} %get-tuple-element.34), channel_id=1, source_target_pairs={{0,2},{1,3},{2,0},{3,1},{64,66},{65,67},{66,64},{67,65},{4,6},{5,7... | collective-permute-start | bytes 344072 | tf_op jit(solution)/shard_map/ppermute | solution.py:25
  217.1 5.8 %collective-permute-start.10 = (bf16[64,896]{1,0:T(8,128)(2,1)S(1)}, bf16[64,896]{1,0:T(8,128)(2,1)S(1)}, u32[]{:S(2)}, u32[]{:S(2)}) collective-permute-start(bf16[64,896]{1,0:T(8,128)(2,1)S(1)} %get-tuple-element.35), channel_id=1, source_target_pairs={{0,3},{1,0},{2,1},{3,2},{64,65},{65,66},{66,67},{67,64},{4,7},{5,4... | collective-permute-start | bytes 344072 | tf_op jit(solution)/shard_map/ppermute | solution.py:25
Sparse Core Ops, SparseCore 0:
  50.8 77.5 all-gather.2
  160.2 51.4 reduce-scatter.1

commit v12 on v10

--- a/solution.py
+++ b/solution.py
@@ -232,7 +232,7 @@
         out_copy(turn).start()
         return 0
 
-    lax.fori_loop(0, turns, combine, 0)
+    lax.fori_loop(0, turns, combine, 0, unroll=True)
     for turn in range(turns):
         out_copy(turn).wait()
 

time: 231 us -> 230 us (level)
  no operation moved by 1% of the time
where the time goes in v12:
time: 230 us; the launch traced here: 229 us
  waiting for transfers between devices  122 us (53%)
  Pallas kernels  35.5 us (15%)
  starting transfers between devices  34 us (15%)
  blocking collectives  14.7 us (6%)
  between operations  13.6 us (6%)
  local copies, waits for them, and re-layouts  6.15 us (3%)
    reduce_scatter x1, waiting for transfers between devices, per_device(): lax.psum_scatter(partial, Z, scatter_dimension=0, tiled=True)  51.7 us
    ppermute x9, waiting for transfers between devices, mirrored(): return lax.ppermute(value, ('c', axis), pairs)  29.5 us
    pallas_call x2, Pallas kernels, experts_call(): pl.pallas_call(functools.partial(experts_kernel, core, shifts, [v[0] for...  26.8 us
    ppermute x4, waiting for transfers between devices, shifted(): lax.ppermute(value, axis, [(i, (i + steps) % count) for i in range(count)])  19.7 us
    all_to_all x1, blocking collectives, per_device(): lax.all_to_all(after(info, second).reshape(ny, 2, planes, 4 * slots), Z,...  14.7 us
    ppermute x9, starting transfers between devices, mirrored(): return lax.ppermute(value, ('c', axis), pairs)  12.7 us
    all_to_all x1, waiting for transfers between devices, per_device(): lax.all_to_all(send(half, after(flat, first, joined), BESIDE), Z, 0, 0, t...  12.2 us
    all_gather x1, waiting for transfers between devices, per_device(): weight = lax.all_gather(joined, 'x')  9.26 us
  transfers between devices with their start and end apart: 17, of which 11 were waited for; matrix products, arithmetic and copies ran while one was open for 0% of the time, Pallas kernels for 7%

profile of v12, /device:TPU:2, one launch (start us, length us, event | category | flops | bytes accessed | tf_op | source)
XLA Modules:
  0.0 228.5 jit_solution(5478022318605287966)
XLA Ops:
  6.5 0.7 reshape.87
  7.3 0.1 eq.31
  7.4 0.8 copy.20
  8.2 0.2 compare_reduce_fusion
  8.4 0.1 reduce_window_sum.11
  8.5 1.2 fusion
  9.7 0.1 reshape.88.flat_ref
  9.8 0.0 copy-start.1
  9.8 1.2 copy-done.1
  11.0 1.7 shard_map.55
  12.7 8.5 %all-to-all-start = ((bf16[8,64,1024]{2,1,0:T(8,128)(2,1)}), bf16[8,64,1024]{2,1,0:T(8,128)(2,1)S(1)}, u32[]{:S(2)}, u32[]{:S(2)}) async-start(bf16[8,64,1024]{2,1,0:T(8,128)(2,1)} %bitcast.6), calls=%async_computation | async-start | bytes 2097152 | tf_op jit(solution)/shard_map/all_to_all | solution.py:337
  21.2 0.0 all-gather.3.cloned.1.call-start
  21.2 0.1 eq.35
  21.3 0.3 select_reduce_fusion
  21.6 0.1 convert_element_type.16
  21.7 0.1 copy.22
  21.8 0.1 broadcast_in_dim.45
  21.9 0.3 select_reduce_fusion.1
  22.2 0.1 reshape_reshape.3
  22.3 0.1 pad_add_fusion.pos_ref
  22.4 0.7 shard_map.56
  23.1 1.7 collective-permute-start.3
  24.7 2.9 %collective-permute-start.4 = (bf16[272,896]{1,0:T(8,128)(2,1)S(1)}, bf16[272,896]{1,0:T(8,128)(2,1)S(1)}, u32[]{:S(2)}, u32[]{:S(2)}) collective-permute-start(bf16[272,896]{1,0:T(8,128)(2,1)S(1)} %get-tuple-element.23), channel_id=1, source_target_pairs={{0,2},{1,3},{2,0},{3,1},{4,6},{5,7},{6,4},{7,5},{8,10},{9,11},{10,... | collective-permute-start | bytes 1462280 | tf_op jit(solution)/shard_map/ppermute | solution.py:19
  27.6 1.3 collective-permute-start.5
  29.0 8.3 %collective-permute-done.3.refs_1_ = bf16[272,896]{1,0:T(8,128)(2,1)S(1)} collective-permute-done((bf16[272,896]{1,0:T(8,128)(2,1)S(1)}, bf16[272,896]{1,0:T(8,128)(2,1)S(1)}, u32[]{:S(2)}, u32[]{:S(2)}) %collective-permute-start.3) | collective-permute-done | bytes 487456 | tf_op jit(solution)/shard_map/ppermute | solution.py:19
  37.3 11.3 %collective-permute-done.4.refs_2_ = bf16[272,896]{1,0:T(8,128)(2,1)S(1)} collective-permute-done((bf16[272,896]{1,0:T(8,128)(2,1)S(1)}, bf16[272,896]{1,0:T(8,128)(2,1)S(1)}, u32[]{:S(2)}, u32[]{:S(2)}) %collective-permute-start.4) | collective-permute-done | bytes 487456 | tf_op jit(solution)/shard_map/ppermute | solution.py:19
  48.6 0.0 collective-permute-done.5.refs_3_
  48.6 2.0 shard_map.57
  50.6 0.0 all-gather.3.cloned.1.call-update
  50.7 2.2 collective-permute-start.1
  52.9 0.0 collective-permute-start
  52.9 1.7 shard_map.58
  54.6 6.9 %all-to-all-start.1 = ((bf16[8,64,1024]{2,1,0:T(8,128)(2,1)}), bf16[8,64,1024]{2,1,0:T(8,128)(2,1)S(1)}, u32[]{:S(2)}, u32[]{:S(2)}) async-start(bf16[8,64,1024]{2,1,0:T(8,128)(2,1)} %bitcast.12), calls=%async_computation.1 | async-start | bytes 2097152 | tf_op jit(solution)/shard_map/all_to_all | solution.py:351
  61.5 0.0 reduce-scatter.2.cloned.1.call-start
  61.5 14.9 %collective-permute-done.1.refs_2_.refs_3_ = bf16[8,64,1024]{2,1,0:T(8,128)(2,1)} collective-permute-done((bf16[8,64,1024]{2,1,0:T(8,128)(2,1)S(1)}, bf16[8,64,1024]{2,1,0:T(8,128)(2,1)}, u32[]{:S(2)}, u32[]{:S(2)}) %collective-permute-start.1) | collective-permute-done | bytes 1048608 | tf_op jit(solution)/shard_map/ppermute | solution.py:25
  76.4 0.0 collective-permute-done.refs_1_
  76.4 1.6 collective-permute-start.2
  78.0 12.2 %all-to-all-done.1.refs_3_.refs_4_ = bf16[8,64,1024]{2,1,0:T(8,128)(2,1)S(1)} async-done(((bf16[8,64,1024]{2,1,0:T(8,128)(2,1)}), bf16[8,64,1024]{2,1,0:T(8,128)(2,1)S(1)}, u32[]{:S(2)}, u32[]{:S(2)}) %all-to-all-start.1) | async-done | bytes 1048608 | tf_op jit(solution)/shard_map/all_to_all | solution.py:351
  90.2 2.4 %collective-permute-done.2.refs_2_.refs_9_ = bf16[8,64,1024]{2,1,0:T(8,128)(2,1)S(1)} collective-permute-done((bf16[8,64,1024]{2,1,0:T(8,128)(2,1)}, bf16[8,64,1024]{2,1,0:T(8,128)(2,1)S(1)}, u32[]{:S(2)}, u32[]{:S(2)}) %collective-permute-start.2) | collective-permute-done | bytes 1048608 | tf_op jit(solution)/shard_map/ppermute | solution.py:25
  92.6 1.8 collective-permute-start.7
  94.4 0.2 collective-permute-start.6
  94.7 14.7 %all_to_all.15 = bf16[4,2,8,256]{3,1,0,2:T(2,128)(2,1)S(1)} all-to-all(bf16[4,2,8,256]{3,1,0,2:T(2,128)(2,1)S(1)} %copy.25), channel_id=1, replica_groups=mesh['zl'=2,'c'=2,'zh'=4,'x'=4,'y'=4] {'zh','zl'}, dimensions={2} | all-to-all | bytes 65536 | tf_op jit(solution)/shard_map/all_to_all | solution.py:355
  109.3 7.6 %collective-permute-done.7.refs_5_.refs_7_ = bf16[8,64,1024]{2,1,0:T(8,128)(2,1)S(1)} collective-permute-done((bf16[8,64,1024]{2,1,0:T(8,128)(2,1)S(1)}, bf16[8,64,1024]{2,1,0:T(8,128)(2,1)S(1)}, u32[]{:S(2)}, u32[]{:S(2)}) %collective-permute-start.7) | collective-permute-done | bytes 1048608 | tf_op jit(solution)/shard_map/ppermute | solution.py:25
  117.0 0.2 collective-permute-done.6.refs_4_.refs_5_
  117.2 1.2 collective-permute-start.8
  118.3 0.1 shard_map.59.refs_7_.refs_12_
  118.4 0.0 copy-start.3
  118.4 0.6 copy-done.3
  119.1 9.3 %all-gather.3.cloned.1.call-done = bf16[16,256,896]{2,1,0:T(8,128)(2,1)} async-done(((bf16[4,256,896]{2,1,0:T(8,128)(2,1)}), bf16[16,256,896]{2,1,0:T(8,128)(2,1)}) %all-gather.3.cloned.1.call-update) | async-done | bytes 7340048 | tf_op jit(solution)/shard_map/all_gather | solution.py:348
  128.3 0.0 collective-permute-start.9
  128.3 10.9 %shard_map.60.sums_ref.refs_13_ = f32[3,8,64,896]{3,2,1,0:T(8,128)} custom-call(s32[4]{0:T(128)} %copy-done.4, bf16[8,64,1024]{2,1,0:T(8,128)(2,1)} %copy-done.8, bf16[8,64,1024]{2,1,0:T(8,128)(2,1)} %collective-permute-done.refs_1_, bf16[8,64,1024]{2,1,0:T(8,128)(2,1)} %collective-permute-done.1.refs_2_.refs_3_, bf16[8,64,1024]{2,1,0:T(8,128)(2,1)} %copy-done.9, ...), custom_call_target="tpu_custom_call" | custom-call | flops 60000002048 | bytes 98304 | tf_op jit(solution)/shard_map/pallas_call | solution.py:268
  139.3 0.0 collective-permute-done.8.in_ref.refs_6_.refs_10_
  139.3 1.0 copy-done.7
  140.3 1.3 shard_map.61.refs_14_
  141.6 15.8 %shard_map.62 = bf16[8,4,64,896]{3,2,1,0:T(8,128)(2,1)} custom-call(s32[4]{0:T(128)} %copy-done.4, bf16[8,64,1024]{2,1,0:T(8,128)(2,1)} %copy-done.8, bf16[8,64,1024]{2,1,0:T(8,128)(2,1)} %collective-permute-done.refs_1_, bf16[8,64,1024]{2,1,0:T(8,128)(2,1)} %copy-done.6, bf16[8,64,1024]{2,1,0:T(8,128)(2,1)} %collective-permute-done.1.refs_2_.refs_3_, ...), custom_call_target="tpu_custom_call" | custom-call | flops 3758096384 | bytes 36175872 | tf_op jit(solution)/shard_map/pallas_call | solution.py:268
  157.4 0.0 reduce-scatter.2.cloned.1.call-update
  157.4 51.7 %reduce-scatter.2.cloned.1.call-done = bf16[256,896]{1,0:T(8,128)(2,1)} async-done(((bf16[2048,896]{1,0:T(8,128)(2,1)}), bf16[256,896]{1,0:T(8,128)(2,1)}) %reduce-scatter.2.cloned.1.call-update) | async-done | bytes 458768 | tf_op jit(solution)/shard_map/reduce_scatter | solution.py:366
  209.1 1.1 fusion.5
  210.2 1.6 collective-permute-start.12
  211.8 2.7 %collective-permute-start.11 = (bf16[64,896]{1,0:T(8,128)(2,1)S(1)}, bf16[64,896]{1,0:T(8,128)(2,1)S(1)}, u32[]{:S(2)}, u32[]{:S(2)}) collective-permute-start(bf16[64,896]{1,0:T(8,128)(2,1)S(1)} %get-tuple-element.34), channel_id=1, source_target_pairs={{0,2},{1,3},{2,0},{3,1},{64,66},{65,67},{66,64},{67,65},{4,6},{5,7... | collective-permute-start | bytes 344072 | tf_op jit(solution)/shard_map/ppermute | solution.py:25
  214.5 1.4 collective-permute-start.10
  215.9 0.4 collective-permute-done.12.refs_3_
  216.3 4.0 %collective-permute-done.11.refs_2_ = bf16[64,896]{1,0:T(8,128)(2,1)S(1)} collective-permute-done((bf16[64,896]{1,0:T(8,128)(2,1)S(1)}, bf16[64,896]{1,0:T(8,128)(2,1)S(1)}, u32[]{:S(2)}, u32[]{:S(2)}) %collective-permute-start.11) | collective-permute-done | bytes 114720 | tf_op jit(solution)/shard_map/ppermute | solution.py:25
  220.3 1.4 shard_map.63
  (32 shorter events, 0.1 us)
Async XLA Ops:
  9.8 1.2 copy-start.1
  11.0 10.7 %copy-start.11 = (f32[64,8]{0,1:T(8,128)S(1)}, f32[64,8]{0,1:T(8,128)}, u32[]{:S(2)}) copy-start(f32[64,8]{0,1:T(8,128)} %param.8) | copy-start | bytes 6148
  11.0 11.3 %copy-start = (bf16[1,1,4,64,3584]{4,3,2,1,0:T(8,128)(2,1)S(1)}, bf16[1,1,4,64,3584]{4,3,2,1,0:T(8,128)(2,1)}, u32[]{:S(2)}) copy-start(bf16[1,1,4,64,3584]{4,3,2,1,0:T(8,128)(2,1)} %param.5) | copy-start | bytes 5505028
  12.7 37.9 %all-to-all-start = ((bf16[8,64,1024]{2,1,0:T(8,128)(2,1)}), bf16[8,64,1024]{2,1,0:T(8,128)(2,1)S(1)}, u32[]{:S(2)}, u32[]{:S(2)}) async-start(bf16[8,64,1024]{2,1,0:T(8,128)(2,1)} %bitcast.6), calls=%async_computation | async-start | bytes 2097152 | tf_op jit(solution)/shard_map/all_to_all | solution.py:337
  21.2 107.2 %all-gather.3.cloned.1.call-start = ((), (), s32[]{:S(2)}) async-start(), calls=%async_computation.5 | async-start | bytes 9175040 | tf_op jit(solution)/shard_map/all_gather | solution.py:348
  22.4 28.3 %copy-start.4 = (s32[4]{0:T(128)}, s32[4]{0:T(128)S(1)}, u32[]{:S(2)}) copy-start(s32[4]{0:T(128)S(1)} %pad_add_fusion.pos_ref) | copy-start | bytes 52
  23.1 14.2 %collective-permute-start.3 = (bf16[272,896]{1,0:T(8,128)(2,1)S(1)}, bf16[272,896]{1,0:T(8,128)(2,1)S(1)}, u32[]{:S(2)}, u32[]{:S(2)}) collective-permute-start(bf16[272,896]{1,0:T(8,128)(2,1)S(1)} %get-tuple-element.22), channel_id=1, source_target_pairs={{0,1},{1,2},{2,3},{3,0},{4,5},{5,6},{6,7},{7,4},{8,9},{9,10},{10,1... | collective-permute-start | bytes 1462280 | tf_op jit(solution)/shard_map/ppermute | solution.py:19
  24.7 23.9 %collective-permute-start.4 = (bf16[272,896]{1,0:T(8,128)(2,1)S(1)}, bf16[272,896]{1,0:T(8,128)(2,1)S(1)}, u32[]{:S(2)}, u32[]{:S(2)}) collective-permute-start(bf16[272,896]{1,0:T(8,128)(2,1)S(1)} %get-tuple-element.23), channel_id=1, source_target_pairs={{0,2},{1,3},{2,0},{3,1},{4,6},{5,7},{6,4},{7,5},{8,10},{9,11},{10,... | collective-permute-start | bytes 1462280 | tf_op jit(solution)/shard_map/ppermute | solution.py:19
  27.6 21.0 %collective-permute-start.5 = (bf16[272,896]{1,0:T(8,128)(2,1)S(1)}, bf16[272,896]{1,0:T(8,128)(2,1)S(1)}, u32[]{:S(2)}, u32[]{:S(2)}) collective-permute-start(bf16[272,896]{1,0:T(8,128)(2,1)S(1)} %get-tuple-element.24), channel_id=1, source_target_pairs={{0,3},{1,0},{2,1},{3,2},{4,7},{5,4},{6,5},{7,6},{8,11},{9,8},{10,9... | collective-permute-start | bytes 1462280 | tf_op jit(solution)/shard_map/ppermute | solution.py:19
  48.6 4.3 %copy-start.2 = (bf16[64,8,1024]{2,1,0:T(8,128)(2,1)S(1)}, bf16[64,8,1024]{2,1,0:T(8,128)(2,1)}, u32[]{:S(2)}) copy-start(bf16[64,8,1024]{2,1,0:T(8,128)(2,1)} %param.9) | copy-start | bytes 3145732
  50.7 3.9 %copy-start.8 = (bf16[8,64,1024]{2,1,0:T(8,128)(2,1)}, bf16[8,64,1024]{2,1,0:T(8,128)(2,1)S(1)}, u32[]{:S(2)}) copy-start(bf16[8,64,1024]{2,1,0:T(8,128)(2,1)S(1)} %all-to-all-done.refs_0_) | copy-start | bytes 3145732
  50.7 25.7 %collective-permute-start.1 = (bf16[8,64,1024]{2,1,0:T(8,128)(2,1)S(1)}, bf16[8,64,1024]{2,1,0:T(8,128)(2,1)}, u32[]{:S(2)}, u32[]{:S(2)}) collective-permute-start(bf16[8,64,1024]{2,1,0:T(8,128)(2,1)S(1)} %all-to-all-done.refs_0_), channel_id=1, source_target_pairs={{0,3},{1,0},{2,1},{3,2},{64,65},{65,66},{66,67},{67,64},{4,7},{5,4... | collective-permute-start | bytes 3145736 | tf_op jit(solution)/shard_map/ppermute | solution.py:25
  52.9 23.5 %collective-permute-start = (bf16[8,64,1024]{2,1,0:T(8,128)(2,1)S(1)}, bf16[8,64,1024]{2,1,0:T(8,128)(2,1)}, u32[]{:S(2)}, u32[]{:S(2)}) collective-permute-start(bf16[8,64,1024]{2,1,0:T(8,128)(2,1)S(1)} %all-to-all-done.refs_0_), channel_id=1, source_target_pairs={{0,1},{1,2},{2,3},{3,0},{64,67},{65,64},{66,65},{67,66},{4,5},{5,6... | collective-permute-start | bytes 3145736 | tf_op jit(solution)/shard_map/ppermute | solution.py:25
  54.6 35.6 %all-to-all-start.1 = ((bf16[8,64,1024]{2,1,0:T(8,128)(2,1)}), bf16[8,64,1024]{2,1,0:T(8,128)(2,1)S(1)}, u32[]{:S(2)}, u32[]{:S(2)}) async-start(bf16[8,64,1024]{2,1,0:T(8,128)(2,1)} %bitcast.12), calls=%async_computation.1 | async-start | bytes 2097152 | tf_op jit(solution)/shard_map/all_to_all | solution.py:351
  61.5 147.6 %reduce-scatter.2.cloned.1.call-start = ((), (), s32[]{:S(2)}) async-start(), calls=%async_computation.4 | async-start | bytes 4128768 | tf_op jit(solution)/shard_map/reduce_scatter | solution.py:366
  76.4 16.2 %collective-permute-start.2 = (bf16[8,64,1024]{2,1,0:T(8,128)(2,1)}, bf16[8,64,1024]{2,1,0:T(8,128)(2,1)S(1)}, u32[]{:S(2)}, u32[]{:S(2)}) collective-permute-start(bf16[8,64,1024]{2,1,0:T(8,128)(2,1)} %collective-permute-done.refs_1_), channel_id=1, source_target_pairs={{0,1},{1,2},{2,3},{3,0},{64,67},{65,64},{66,65},{67,66},{4,5},{5,6... | collective-permute-start | bytes 3145736 | tf_op jit(solution)/shard_map/ppermute | solution.py:25
  90.2 27.0 %copy-start.9 = (bf16[8,64,1024]{2,1,0:T(8,128)(2,1)}, bf16[8,64,1024]{2,1,0:T(8,128)(2,1)S(1)}, u32[]{:S(2)}) copy-start(bf16[8,64,1024]{2,1,0:T(8,128)(2,1)S(1)} %all-to-all-done.1.refs_3_.refs_4_) | copy-start | bytes 3145732
  92.6 25.8 %copy-start.6 = (bf16[8,64,1024]{2,1,0:T(8,128)(2,1)}, bf16[8,64,1024]{2,1,0:T(8,128)(2,1)S(1)}, u32[]{:S(2)}) copy-start(bf16[8,64,1024]{2,1,0:T(8,128)(2,1)S(1)} %collective-permute-done.2.refs_2_.refs_9_) | copy-start | bytes 3145732
  92.6 24.3 %collective-permute-start.7 = (bf16[8,64,1024]{2,1,0:T(8,128)(2,1)S(1)}, bf16[8,64,1024]{2,1,0:T(8,128)(2,1)S(1)}, u32[]{:S(2)}, u32[]{:S(2)}) collective-permute-start(bf16[8,64,1024]{2,1,0:T(8,128)(2,1)S(1)} %all-to-all-done.1.refs_3_.refs_4_), channel_id=1, source_target_pairs={{0,3},{1,0},{2,1},{3,2},{64,65},{65,66},{66,67},{67,64},{4,7},{5,4... | collective-permute-start | bytes 3145736 | tf_op jit(solution)/shard_map/ppermute | solution.py:25
  94.4 22.7 %collective-permute-start.6 = (bf16[8,64,1024]{2,1,0:T(8,128)(2,1)S(1)}, bf16[8,64,1024]{2,1,0:T(8,128)(2,1)}, u32[]{:S(2)}, u32[]{:S(2)}) collective-permute-start(bf16[8,64,1024]{2,1,0:T(8,128)(2,1)S(1)} %all-to-all-done.1.refs_3_.refs_4_), channel_id=1, source_target_pairs={{0,1},{1,2},{2,3},{3,0},{64,67},{65,64},{66,65},{67,66},{4,5},{5,6... | collective-permute-start | bytes 3145736 | tf_op jit(solution)/shard_map/ppermute | solution.py:25
  117.0 1.5 copy-start.10
  117.2 22.1 %collective-permute-start.8 = (bf16[8,64,1024]{2,1,0:T(8,128)(2,1)}, bf16[8,64,1024]{2,1,0:T(8,128)(2,1)S(1)}, u32[]{:S(2)}, u32[]{:S(2)}) collective-permute-start(bf16[8,64,1024]{2,1,0:T(8,128)(2,1)} %collective-permute-done.6.refs_4_.refs_5_), channel_id=1, source_target_pairs={{0,1},{1,2},{2,3},{3,0},{64,67},{65,64},{66,65},{67,66},{4,5},{5,6... | collective-permute-start | bytes 3145736 | tf_op jit(solution)/shard_map/ppermute | solution.py:25
  118.4 0.6 copy-start.3
  128.3 13.2 %collective-permute-start.9 = (bf16[4,4,256,896]{3,2,1,0:T(8,128)(2,1)}, bf16[4,4,256,896]{3,2,1,0:T(8,128)(2,1)}, u32[]{:S(2)}, u32[]{:S(2)}) collective-permute-start(bf16[4,4,256,896]{3,2,1,0:T(8,128)(2,1)} %bitcast.27), channel_id=1, source_target_pairs={{0,64},{64,0},{1,65},{65,1},{2,66},{66,2},{3,67},{67,3},{4,68},{68... | collective-permute-start | bytes 22020104 | tf_op jit(solution)/shard_map/ppermute | solution.py:19
  139.3 1.0 copy-start.7
  157.4 62.9 %copy-start.5 = (s32[4]{0:T(128)S(1)}, s32[4]{0:T(128)}, u32[]{:S(2)}) copy-start(s32[4]{0:T(128)} %copy-done.4) | copy-start | bytes 52
  210.2 6.1 %collective-permute-start.12 = (bf16[64,896]{1,0:T(8,128)(2,1)S(1)}, bf16[64,896]{1,0:T(8,128)(2,1)S(1)}, u32[]{:S(2)}, u32[]{:S(2)}) collective-permute-start(bf16[64,896]{1,0:T(8,128)(2,1)S(1)} %get-tuple-element.33), channel_id=1, source_target_pairs={{0,1},{1,2},{2,3},{3,0},{64,67},{65,64},{66,65},{67,66},{4,5},{5,6... | collective-permute-start | bytes 344072 | tf_op jit(solution)/shard_map/ppermute | solution.py:25
  211.8 8.5 %collective-permute-start.11 = (bf16[64,896]{1,0:T(8,128)(2,1)S(1)}, bf16[64,896]{1,0:T(8,128)(2,1)S(1)}, u32[]{:S(2)}, u32[]{:S(2)}) collective-permute-start(bf16[64,896]{1,0:T(8,128)(2,1)S(1)} %get-tuple-element.34), channel_id=1, source_target_pairs={{0,2},{1,3},{2,0},{3,1},{64,66},{65,67},{66,64},{67,65},{4,6},{5,7... | collective-permute-start | bytes 344072 | tf_op jit(solution)/shard_map/ppermute | solution.py:25
  214.5 5.8 %collective-permute-start.10 = (bf16[64,896]{1,0:T(8,128)(2,1)S(1)}, bf16[64,896]{1,0:T(8,128)(2,1)S(1)}, u32[]{:S(2)}, u32[]{:S(2)}) collective-permute-start(bf16[64,896]{1,0:T(8,128)(2,1)S(1)} %get-tuple-element.35), channel_id=1, source_target_pairs={{0,3},{1,0},{2,1},{3,2},{64,65},{65,66},{66,67},{67,64},{4,7},{5,4... | collective-permute-start | bytes 344072 | tf_op jit(solution)/shard_map/ppermute | solution.py:25
Sparse Core Ops, SparseCore 0:
  50.8 77.5 all-gather.2
  157.6 51.4 reduce-scatter.1

commit v13 on v12

--- a/solution.py
+++ b/solution.py
@@ -281,7 +281,7 @@
             pltpu.SemaphoreType.DMA((turns,)),
             pltpu.SemaphoreType.DMA((turns,)),
         ],
-        compiler_params=pltpu.CompilerParams(vmem_limit_bytes=60 << 20),
+        compiler_params=pltpu.CompilerParams(vmem_limit_bytes=(54 if core else 60) << 20),
         cost_estimate=cost(flops, *arrays, total, out) if core else cost(BESIDE, gate),
     )(pos, *arrays, gate, *[v[1] for v in given], *[v[2] for v in given])
 

time: 230 us -> 230 us (level)
  no operation moved by 1% of the time
where the time goes in v13:
time: 230 us; the launch traced here: 229 us
  waiting for transfers between devices  122 us (53%)
  Pallas kernels  35.5 us (15%)
  starting transfers between devices  34 us (15%)
  blocking collectives  14.7 us (6%)
  between operations  13.6 us (6%)
  local copies, waits for them, and re-layouts  6.15 us (3%)
    reduce_scatter x1, waiting for transfers between devices, per_device(): lax.psum_scatter(partial, Z, scatter_dimension=0, tiled=True)  51.7 us
    ppermute x9, waiting for transfers between devices, mirrored(): return lax.ppermute(value, ('c', axis), pairs)  29.5 us
    pallas_call x2, Pallas kernels, experts_call(): pl.pallas_call(functools.partial(experts_kernel, core, shifts, [v[0] for...  26.8 us
    ppermute x4, waiting for transfers between devices, shifted(): lax.ppermute(value, axis, [(i, (i + steps) % count) for i in range(count)])  19.7 us
    all_to_all x1, blocking collectives, per_device(): lax.all_to_all(after(info, second).reshape(ny, 2, planes, 4 * slots), Z,...  14.7 us
    ppermute x9, starting transfers between devices, mirrored(): return lax.ppermute(value, ('c', axis), pairs)  12.7 us
    all_to_all x1, waiting for transfers between devices, per_device(): lax.all_to_all(send(half, after(flat, first, joined), BESIDE), Z, 0, 0, t...  12.2 us
    all_gather x1, waiting for transfers between devices, per_device(): weight = lax.all_gather(joined, 'x')  9.26 us
  transfers between devices with their start and end apart: 17, of which 11 were waited for; matrix products, arithmetic and copies ran while one was open for 0% of the time, Pallas kernels for 7%

profile of v13, /device:TPU:2, one launch (start us, length us, event | category | flops | bytes accessed | tf_op | source)
XLA Modules:
  0.0 228.5 jit_solution(5478022318605287966)
XLA Ops:
  6.5 0.7 reshape.87
  7.3 0.1 eq.31
  7.4 0.8 copy.20
  8.2 0.2 compare_reduce_fusion
  8.4 0.1 reduce_window_sum.11
  8.5 1.2 fusion
  9.7 0.1 reshape.88.flat_ref
  9.8 0.0 copy-start.1
  9.8 1.2 copy-done.1
  11.0 1.7 shard_map.55
  12.7 8.5 %all-to-all-start = ((bf16[8,64,1024]{2,1,0:T(8,128)(2,1)}), bf16[8,64,1024]{2,1,0:T(8,128)(2,1)S(1)}, u32[]{:S(2)}, u32[]{:S(2)}) async-start(bf16[8,64,1024]{2,1,0:T(8,128)(2,1)} %bitcast.6), calls=%async_computation | async-start | bytes 2097152 | tf_op jit(solution)/shard_map/all_to_all | solution.py:337
  21.2 0.0 all-gather.3.cloned.1.call-start
  21.2 0.1 eq.35
  21.3 0.3 select_reduce_fusion
  21.6 0.1 convert_element_type.16
  21.7 0.1 copy.22
  21.8 0.1 broadcast_in_dim.45
  21.9 0.3 select_reduce_fusion.1
  22.2 0.1 reshape_reshape.3
  22.3 0.1 pad_add_fusion.pos_ref
  22.4 0.7 shard_map.56
  23.1 1.7 collective-permute-start.3
  24.7 2.9 %collective-permute-start.4 = (bf16[272,896]{1,0:T(8,128)(2,1)S(1)}, bf16[272,896]{1,0:T(8,128)(2,1)S(1)}, u32[]{:S(2)}, u32[]{:S(2)}) collective-permute-start(bf16[272,896]{1,0:T(8,128)(2,1)S(1)} %get-tuple-element.23), channel_id=1, source_target_pairs={{0,2},{1,3},{2,0},{3,1},{4,6},{5,7},{6,4},{7,5},{8,10},{9,11},{10,... | collective-permute-start | bytes 1462280 | tf_op jit(solution)/shard_map/ppermute | solution.py:19
  27.6 1.3 collective-permute-start.5
  29.0 8.3 %collective-permute-done.3.refs_1_ = bf16[272,896]{1,0:T(8,128)(2,1)S(1)} collective-permute-done((bf16[272,896]{1,0:T(8,128)(2,1)S(1)}, bf16[272,896]{1,0:T(8,128)(2,1)S(1)}, u32[]{:S(2)}, u32[]{:S(2)}) %collective-permute-start.3) | collective-permute-done | bytes 487456 | tf_op jit(solution)/shard_map/ppermute | solution.py:19
  37.3 11.3 %collective-permute-done.4.refs_2_ = bf16[272,896]{1,0:T(8,128)(2,1)S(1)} collective-permute-done((bf16[272,896]{1,0:T(8,128)(2,1)S(1)}, bf16[272,896]{1,0:T(8,128)(2,1)S(1)}, u32[]{:S(2)}, u32[]{:S(2)}) %collective-permute-start.4) | collective-permute-done | bytes 487456 | tf_op jit(solution)/shard_map/ppermute | solution.py:19
  48.6 0.0 collective-permute-done.5.refs_3_
  48.6 2.0 shard_map.57
  50.6 0.0 all-gather.3.cloned.1.call-update
  50.7 2.2 collective-permute-start.1
  52.9 0.0 collective-permute-start
  52.9 1.7 shard_map.58
  54.6 6.9 %all-to-all-start.1 = ((bf16[8,64,1024]{2,1,0:T(8,128)(2,1)}), bf16[8,64,1024]{2,1,0:T(8,128)(2,1)S(1)}, u32[]{:S(2)}, u32[]{:S(2)}) async-start(bf16[8,64,1024]{2,1,0:T(8,128)(2,1)} %bitcast.12), calls=%async_computation.1 | async-start | bytes 2097152 | tf_op jit(solution)/shard_map/all_to_all | solution.py:351
  61.5 0.0 reduce-scatter.2.cloned.1.call-start
  61.5 14.9 %collective-permute-done.1.refs_2_.refs_3_ = bf16[8,64,1024]{2,1,0:T(8,128)(2,1)} collective-permute-done((bf16[8,64,1024]{2,1,0:T(8,128)(2,1)S(1)}, bf16[8,64,1024]{2,1,0:T(8,128)(2,1)}, u32[]{:S(2)}, u32[]{:S(2)}) %collective-permute-start.1) | collective-permute-done | bytes 1048608 | tf_op jit(solution)/shard_map/ppermute | solution.py:25
  76.4 0.0 collective-permute-done.refs_1_
  76.4 1.6 collective-permute-start.2
  78.0 12.2 %all-to-all-done.1.refs_3_.refs_4_ = bf16[8,64,1024]{2,1,0:T(8,128)(2,1)S(1)} async-done(((bf16[8,64,1024]{2,1,0:T(8,128)(2,1)}), bf16[8,64,1024]{2,1,0:T(8,128)(2,1)S(1)}, u32[]{:S(2)}, u32[]{:S(2)}) %all-to-all-start.1) | async-done | bytes 1048608 | tf_op jit(solution)/shard_map/all_to_all | solution.py:351
  90.2 2.4 %collective-permute-done.2.refs_2_.refs_9_ = bf16[8,64,1024]{2,1,0:T(8,128)(2,1)S(1)} collective-permute-done((bf16[8,64,1024]{2,1,0:T(8,128)(2,1)}, bf16[8,64,1024]{2,1,0:T(8,128)(2,1)S(1)}, u32[]{:S(2)}, u32[]{:S(2)}) %collective-permute-start.2) | collective-permute-done | bytes 1048608 | tf_op jit(solution)/shard_map/ppermute | solution.py:25
  92.6 1.8 collective-permute-start.7
  94.4 0.2 collective-permute-start.6
  94.7 14.7 %all_to_all.15 = bf16[4,2,8,256]{3,1,0,2:T(2,128)(2,1)S(1)} all-to-all(bf16[4,2,8,256]{3,1,0,2:T(2,128)(2,1)S(1)} %copy.25), channel_id=1, replica_groups=mesh['zl'=2,'c'=2,'zh'=4,'x'=4,'y'=4] {'zh','zl'}, dimensions={2} | all-to-all | bytes 65536 | tf_op jit(solution)/shard_map/all_to_all | solution.py:355
  109.3 7.6 %collective-permute-done.7.refs_5_.refs_7_ = bf16[8,64,1024]{2,1,0:T(8,128)(2,1)S(1)} collective-permute-done((bf16[8,64,1024]{2,1,0:T(8,128)(2,1)S(1)}, bf16[8,64,1024]{2,1,0:T(8,128)(2,1)S(1)}, u32[]{:S(2)}, u32[]{:S(2)}) %collective-permute-start.7) | collective-permute-done | bytes 1048608 | tf_op jit(solution)/shard_map/ppermute | solution.py:25
  117.0 0.2 collective-permute-done.6.refs_4_.refs_5_
  117.2 1.2 collective-permute-start.8
  118.3 0.1 shard_map.59.refs_7_.refs_12_
  118.4 0.0 copy-start.3
  118.4 0.6 copy-done.3
  119.1 9.3 %all-gather.3.cloned.1.call-done = bf16[16,256,896]{2,1,0:T(8,128)(2,1)} async-done(((bf16[4,256,896]{2,1,0:T(8,128)(2,1)}), bf16[16,256,896]{2,1,0:T(8,128)(2,1)}) %all-gather.3.cloned.1.call-update) | async-done | bytes 7340048 | tf_op jit(solution)/shard_map/all_gather | solution.py:348
  128.3 0.0 collective-permute-start.9
  128.3 10.9 %shard_map.60.sums_ref.refs_13_ = f32[3,8,64,896]{3,2,1,0:T(8,128)} custom-call(s32[4]{0:T(128)} %copy-done.4, bf16[8,64,1024]{2,1,0:T(8,128)(2,1)} %copy-done.8, bf16[8,64,1024]{2,1,0:T(8,128)(2,1)} %collective-permute-done.refs_1_, bf16[8,64,1024]{2,1,0:T(8,128)(2,1)} %collective-permute-done.1.refs_2_.refs_3_, bf16[8,64,1024]{2,1,0:T(8,128)(2,1)} %copy-done.9, ...), custom_call_target="tpu_custom_call" | custom-call | flops 60000002048 | bytes 98304 | tf_op jit(solution)/shard_map/pallas_call | solution.py:268
  139.3 0.0 collective-permute-done.8.in_ref.refs_6_.refs_10_
  139.3 1.0 copy-done.7
  140.3 1.3 shard_map.61.refs_14_
  141.6 15.8 %shard_map.62 = bf16[8,4,64,896]{3,2,1,0:T(8,128)(2,1)} custom-call(s32[4]{0:T(128)} %copy-done.4, bf16[8,64,1024]{2,1,0:T(8,128)(2,1)} %copy-done.8, bf16[8,64,1024]{2,1,0:T(8,128)(2,1)} %collective-permute-done.refs_1_, bf16[8,64,1024]{2,1,0:T(8,128)(2,1)} %copy-done.6, bf16[8,64,1024]{2,1,0:T(8,128)(2,1)} %collective-permute-done.1.refs_2_.refs_3_, ...), custom_call_target="tpu_custom_call" | custom-call | flops 3758096384 | bytes 36175872 | tf_op jit(solution)/shard_map/pallas_call | solution.py:268
  157.4 0.0 reduce-scatter.2.cloned.1.call-update
  157.4 51.7 %reduce-scatter.2.cloned.1.call-done = bf16[256,896]{1,0:T(8,128)(2,1)} async-done(((bf16[2048,896]{1,0:T(8,128)(2,1)}), bf16[256,896]{1,0:T(8,128)(2,1)}) %reduce-scatter.2.cloned.1.call-update) | async-done | bytes 458768 | tf_op jit(solution)/shard_map/reduce_scatter | solution.py:366
  209.1 1.1 fusion.5
  210.2 1.6 collective-permute-start.12
  211.8 2.7 %collective-permute-start.11 = (bf16[64,896]{1,0:T(8,128)(2,1)S(1)}, bf16[64,896]{1,0:T(8,128)(2,1)S(1)}, u32[]{:S(2)}, u32[]{:S(2)}) collective-permute-start(bf16[64,896]{1,0:T(8,128)(2,1)S(1)} %get-tuple-element.34), channel_id=1, source_target_pairs={{0,2},{1,3},{2,0},{3,1},{64,66},{65,67},{66,64},{67,65},{4,6},{5,7... | collective-permute-start | bytes 344072 | tf_op jit(solution)/shard_map/ppermute | solution.py:25
  214.5 1.4 collective-permute-start.10
  215.9 0.4 collective-permute-done.12.refs_3_
  216.3 4.0 %collective-permute-done.11.refs_2_ = bf16[64,896]{1,0:T(8,128)(2,1)S(1)} collective-permute-done((bf16[64,896]{1,0:T(8,128)(2,1)S(1)}, bf16[64,896]{1,0:T(8,128)(2,1)S(1)}, u32[]{:S(2)}, u32[]{:S(2)}) %collective-permute-start.11) | collective-permute-done | bytes 114720 | tf_op jit(solution)/shard_map/ppermute | solution.py:25
  220.3 1.4 shard_map.63
  (32 shorter events, 0.1 us)
Async XLA Ops:
  9.8 1.2 copy-start.1
  11.0 10.7 %copy-start.11 = (f32[64,8]{0,1:T(8,128)S(1)}, f32[64,8]{0,1:T(8,128)}, u32[]{:S(2)}) copy-start(f32[64,8]{0,1:T(8,128)} %param.8) | copy-start | bytes 6148
  11.0 11.3 %copy-start = (bf16[1,1,4,64,3584]{4,3,2,1,0:T(8,128)(2,1)S(1)}, bf16[1,1,4,64,3584]{4,3,2,1,0:T(8,128)(2,1)}, u32[]{:S(2)}) copy-start(bf16[1,1,4,64,3584]{4,3,2,1,0:T(8,128)(2,1)} %param.5) | copy-start | bytes 5505028
  12.7 37.9 %all-to-all-start = ((bf16[8,64,1024]{2,1,0:T(8,128)(2,1)}), bf16[8,64,1024]{2,1,0:T(8,128)(2,1)S(1)}, u32[]{:S(2)}, u32[]{:S(2)}) async-start(bf16[8,64,1024]{2,1,0:T(8,128)(2,1)} %bitcast.6), calls=%async_computation | async-start | bytes 2097152 | tf_op jit(solution)/shard_map/all_to_all | solution.py:337
  21.2 107.2 %all-gather.3.cloned.1.call-start = ((), (), s32[]{:S(2)}) async-start(), calls=%async_computation.5 | async-start | bytes 9175040 | tf_op jit(solution)/shard_map/all_gather | solution.py:348
  22.4 28.3 %copy-start.4 = (s32[4]{0:T(128)}, s32[4]{0:T(128)S(1)}, u32[]{:S(2)}) copy-start(s32[4]{0:T(128)S(1)} %pad_add_fusion.pos_ref) | copy-start | bytes 52
  23.1 14.2 %collective-permute-start.3 = (bf16[272,896]{1,0:T(8,128)(2,1)S(1)}, bf16[272,896]{1,0:T(8,128)(2,1)S(1)}, u32[]{:S(2)}, u32[]{:S(2)}) collective-permute-start(bf16[272,896]{1,0:T(8,128)(2,1)S(1)} %get-tuple-element.22), channel_id=1, source_target_pairs={{0,1},{1,2},{2,3},{3,0},{4,5},{5,6},{6,7},{7,4},{8,9},{9,10},{10,1... | collective-permute-start | bytes 1462280 | tf_op jit(solution)/shard_map/ppermute | solution.py:19
  24.7 23.9 %collective-permute-start.4 = (bf16[272,896]{1,0:T(8,128)(2,1)S(1)}, bf16[272,896]{1,0:T(8,128)(2,1)S(1)}, u32[]{:S(2)}, u32[]{:S(2)}) collective-permute-start(bf16[272,896]{1,0:T(8,128)(2,1)S(1)} %get-tuple-element.23), channel_id=1, source_target_pairs={{0,2},{1,3},{2,0},{3,1},{4,6},{5,7},{6,4},{7,5},{8,10},{9,11},{10,... | collective-permute-start | bytes 1462280 | tf_op jit(solution)/shard_map/ppermute | solution.py:19
  27.6 21.0 %collective-permute-start.5 = (bf16[272,896]{1,0:T(8,128)(2,1)S(1)}, bf16[272,896]{1,0:T(8,128)(2,1)S(1)}, u32[]{:S(2)}, u32[]{:S(2)}) collective-permute-start(bf16[272,896]{1,0:T(8,128)(2,1)S(1)} %get-tuple-element.24), channel_id=1, source_target_pairs={{0,3},{1,0},{2,1},{3,2},{4,7},{5,4},{6,5},{7,6},{8,11},{9,8},{10,9... | collective-permute-start | bytes 1462280 | tf_op jit(solution)/shard_map/ppermute | solution.py:19
  48.6 4.3 %copy-start.2 = (bf16[64,8,1024]{2,1,0:T(8,128)(2,1)S(1)}, bf16[64,8,1024]{2,1,0:T(8,128)(2,1)}, u32[]{:S(2)}) copy-start(bf16[64,8,1024]{2,1,0:T(8,128)(2,1)} %param.9) | copy-start | bytes 3145732
  50.7 3.9 %copy-start.8 = (bf16[8,64,1024]{2,1,0:T(8,128)(2,1)}, bf16[8,64,1024]{2,1,0:T(8,128)(2,1)S(1)}, u32[]{:S(2)}) copy-start(bf16[8,64,1024]{2,1,0:T(8,128)(2,1)S(1)} %all-to-all-done.refs_0_) | copy-start | bytes 3145732
  50.7 25.7 %collective-permute-start.1 = (bf16[8,64,1024]{2,1,0:T(8,128)(2,1)S(1)}, bf16[8,64,1024]{2,1,0:T(8,128)(2,1)}, u32[]{:S(2)}, u32[]{:S(2)}) collective-permute-start(bf16[8,64,1024]{2,1,0:T(8,128)(2,1)S(1)} %all-to-all-done.refs_0_), channel_id=1, source_target_pairs={{0,3},{1,0},{2,1},{3,2},{64,65},{65,66},{66,67},{67,64},{4,7},{5,4... | collective-permute-start | bytes 3145736 | tf_op jit(solution)/shard_map/ppermute | solution.py:25
  52.9 23.5 %collective-permute-start = (bf16[8,64,1024]{2,1,0:T(8,128)(2,1)S(1)}, bf16[8,64,1024]{2,1,0:T(8,128)(2,1)}, u32[]{:S(2)}, u32[]{:S(2)}) collective-permute-start(bf16[8,64,1024]{2,1,0:T(8,128)(2,1)S(1)} %all-to-all-done.refs_0_), channel_id=1, source_target_pairs={{0,1},{1,2},{2,3},{3,0},{64,67},{65,64},{66,65},{67,66},{4,5},{5,6... | collective-permute-start | bytes 3145736 | tf_op jit(solution)/shard_map/ppermute | solution.py:25
  54.6 35.6 %all-to-all-start.1 = ((bf16[8,64,1024]{2,1,0:T(8,128)(2,1)}), bf16[8,64,1024]{2,1,0:T(8,128)(2,1)S(1)}, u32[]{:S(2)}, u32[]{:S(2)}) async-start(bf16[8,64,1024]{2,1,0:T(8,128)(2,1)} %bitcast.12), calls=%async_computation.1 | async-start | bytes 2097152 | tf_op jit(solution)/shard_map/all_to_all | solution.py:351
  61.5 147.6 %reduce-scatter.2.cloned.1.call-start = ((), (), s32[]{:S(2)}) async-start(), calls=%async_computation.4 | async-start | bytes 4128768 | tf_op jit(solution)/shard_map/reduce_scatter | solution.py:366
  76.4 16.2 %collective-permute-start.2 = (bf16[8,64,1024]{2,1,0:T(8,128)(2,1)}, bf16[8,64,1024]{2,1,0:T(8,128)(2,1)S(1)}, u32[]{:S(2)}, u32[]{:S(2)}) collective-permute-start(bf16[8,64,1024]{2,1,0:T(8,128)(2,1)} %collective-permute-done.refs_1_), channel_id=1, source_target_pairs={{0,1},{1,2},{2,3},{3,0},{64,67},{65,64},{66,65},{67,66},{4,5},{5,6... | collective-permute-start | bytes 3145736 | tf_op jit(solution)/shard_map/ppermute | solution.py:25
  90.2 27.0 %copy-start.9 = (bf16[8,64,1024]{2,1,0:T(8,128)(2,1)}, bf16[8,64,1024]{2,1,0:T(8,128)(2,1)S(1)}, u32[]{:S(2)}) copy-start(bf16[8,64,1024]{2,1,0:T(8,128)(2,1)S(1)} %all-to-all-done.1.refs_3_.refs_4_) | copy-start | bytes 3145732
  92.6 25.8 %copy-start.6 = (bf16[8,64,1024]{2,1,0:T(8,128)(2,1)}, bf16[8,64,1024]{2,1,0:T(8,128)(2,1)S(1)}, u32[]{:S(2)}) copy-start(bf16[8,64,1024]{2,1,0:T(8,128)(2,1)S(1)} %collective-permute-done.2.refs_2_.refs_9_) | copy-start | bytes 3145732
  92.6 24.3 %collective-permute-start.7 = (bf16[8,64,1024]{2,1,0:T(8,128)(2,1)S(1)}, bf16[8,64,1024]{2,1,0:T(8,128)(2,1)S(1)}, u32[]{:S(2)}, u32[]{:S(2)}) collective-permute-start(bf16[8,64,1024]{2,1,0:T(8,128)(2,1)S(1)} %all-to-all-done.1.refs_3_.refs_4_), channel_id=1, source_target_pairs={{0,3},{1,0},{2,1},{3,2},{64,65},{65,66},{66,67},{67,64},{4,7},{5,4... | collective-permute-start | bytes 3145736 | tf_op jit(solution)/shard_map/ppermute | solution.py:25
  94.4 22.7 %collective-permute-start.6 = (bf16[8,64,1024]{2,1,0:T(8,128)(2,1)S(1)}, bf16[8,64,1024]{2,1,0:T(8,128)(2,1)}, u32[]{:S(2)}, u32[]{:S(2)}) collective-permute-start(bf16[8,64,1024]{2,1,0:T(8,128)(2,1)S(1)} %all-to-all-done.1.refs_3_.refs_4_), channel_id=1, source_target_pairs={{0,1},{1,2},{2,3},{3,0},{64,67},{65,64},{66,65},{67,66},{4,5},{5,6... | collective-permute-start | bytes 3145736 | tf_op jit(solution)/shard_map/ppermute | solution.py:25
  117.0 1.5 copy-start.10
  117.2 22.1 %collective-permute-start.8 = (bf16[8,64,1024]{2,1,0:T(8,128)(2,1)}, bf16[8,64,1024]{2,1,0:T(8,128)(2,1)S(1)}, u32[]{:S(2)}, u32[]{:S(2)}) collective-permute-start(bf16[8,64,1024]{2,1,0:T(8,128)(2,1)} %collective-permute-done.6.refs_4_.refs_5_), channel_id=1, source_target_pairs={{0,1},{1,2},{2,3},{3,0},{64,67},{65,64},{66,65},{67,66},{4,5},{5,6... | collective-permute-start | bytes 3145736 | tf_op jit(solution)/shard_map/ppermute | solution.py:25
  118.4 0.6 copy-start.3
  128.3 13.2 %collective-permute-start.9 = (bf16[4,4,256,896]{3,2,1,0:T(8,128)(2,1)}, bf16[4,4,256,896]{3,2,1,0:T(8,128)(2,1)}, u32[]{:S(2)}, u32[]{:S(2)}) collective-permute-start(bf16[4,4,256,896]{3,2,1,0:T(8,128)(2,1)} %bitcast.27), channel_id=1, source_target_pairs={{0,64},{64,0},{1,65},{65,1},{2,66},{66,2},{3,67},{67,3},{4,68},{68... | collective-permute-start | bytes 22020104 | tf_op jit(solution)/shard_map/ppermute | solution.py:19
  139.3 1.0 copy-start.7
  157.4 62.9 %copy-start.5 = (s32[4]{0:T(128)S(1)}, s32[4]{0:T(128)}, u32[]{:S(2)}) copy-start(s32[4]{0:T(128)} %copy-done.4) | copy-start | bytes 52
  210.2 6.1 %collective-permute-start.12 = (bf16[64,896]{1,0:T(8,128)(2,1)S(1)}, bf16[64,896]{1,0:T(8,128)(2,1)S(1)}, u32[]{:S(2)}, u32[]{:S(2)}) collective-permute-start(bf16[64,896]{1,0:T(8,128)(2,1)S(1)} %get-tuple-element.33), channel_id=1, source_target_pairs={{0,1},{1,2},{2,3},{3,0},{64,67},{65,64},{66,65},{67,66},{4,5},{5,6... | collective-permute-start | bytes 344072 | tf_op jit(solution)/shard_map/ppermute | solution.py:25
  211.8 8.5 %collective-permute-start.11 = (bf16[64,896]{1,0:T(8,128)(2,1)S(1)}, bf16[64,896]{1,0:T(8,128)(2,1)S(1)}, u32[]{:S(2)}, u32[]{:S(2)}) collective-permute-start(bf16[64,896]{1,0:T(8,128)(2,1)S(1)} %get-tuple-element.34), channel_id=1, source_target_pairs={{0,2},{1,3},{2,0},{3,1},{64,66},{65,67},{66,64},{67,65},{4,6},{5,7... | collective-permute-start | bytes 344072 | tf_op jit(solution)/shard_map/ppermute | solution.py:25
  214.5 5.8 %collective-permute-start.10 = (bf16[64,896]{1,0:T(8,128)(2,1)S(1)}, bf16[64,896]{1,0:T(8,128)(2,1)S(1)}, u32[]{:S(2)}, u32[]{:S(2)}) collective-permute-start(bf16[64,896]{1,0:T(8,128)(2,1)S(1)} %get-tuple-element.35), channel_id=1, source_target_pairs={{0,3},{1,0},{2,1},{3,2},{64,65},{65,66},{66,67},{67,64},{4,7},{5,4... | collective-permute-start | bytes 344072 | tf_op jit(solution)/shard_map/ppermute | solution.py:25
Sparse Core Ops, SparseCore 0:
  50.8 77.5 all-gather.2
  157.6 51.4 reduce-scatter.1
